TPU v7x, 32 devices: a whole 2x2x4 slice. The times are simulated.
32 devices in a mesh: lat: 2 (over y), chan: 4 (over z), tm: 4 (over x, core).
Axes of the slice: x: 2, y: 2, z: 4, core: 2. Of those that a mesh axis runs over, the one named last changes fastest.
Arguments:
- fields: bfloat16 [32, 1440, 256], P(('tm', 'lat'), None, 'chan'), parts along dimension 0, may hold values from -6 to 6
- disco_weight: bfloat16 [6, 256, 64], P(None, 'chan'), may hold values from -0.25 to 0.25
- support_lat: int32 [8, 9], P('lat'), may hold values from -2 to 2
- support_lon: int32 [8, 9], P('lat'), may hold values from -4 to 4
- support_basis: int32 [8, 9], P('lat'), may hold values from 0 to 5
- support_value: float32 [8, 9], P('lat'), may hold values from 0.25 to 1.5
- w_up: bfloat16 [256, 512], replicated, may hold values from -0.375 to 0.375
- w_down: bfloat16 [512, 256], replicated, may hold values from -0.25 to 0.25
- legendre: bfloat16 [24, 384, 8], P(('lat', 'chan')), may hold values from -2 to 2
Outputs:
- coefficients: bfloat16 [96, 384, 512], P(('tm', 'lat', 'chan')), parts along dimension 0
There are 4 independent parts, one for each index of `tm`. A program takes and returns all parts, laid end to end along the dimension named above; an argument that names none is the same for every part. Nothing has to cross between parts.
All inputs are finite; a program needn't handle non-finite values.
Results may differ from a plain program's by a relative error of at most 0.0076.
Values may be sent and summed in bfloat16 or wider, within the bound.
No kernel may reach another device: no remote copies, remote signals or barrier semaphores. Data moves between devices by JAX's collectives and lax.ppermute only.
A program may use at most 128 MiB of HBM per device.

v0:
```python
import math

import jax
import jax.numpy as jnp
from jax import lax
from jax.sharding import PartitionSpec as P

G = 64
NB = 6
S = 9
HALO = 2
DLON = 4


def with_halo(cells, sides, width):
    for axis, dim in sides:
        count = lax.axis_size(axis)
        ends = count - 1
        head = lax.slice_in_dim(cells, 0, width, axis=dim)
        tail = lax.slice_in_dim(cells, cells.shape[dim] - width, cells.shape[dim], axis=dim)
        cells = jnp.concatenate(
            [
                lax.ppermute(tail, axis, [(i, (i + 1) % count) for i in range(ends)]),
                cells,
                lax.ppermute(head, axis, [((i + 1) % count, i) for i in range(ends)]),
            ],
            axis=dim,
        )
    return cells


def fourier_table(lon_count, mode_count):
    lon_index = jnp.arange(lon_count, dtype=jnp.int32)
    mode_index = jnp.arange(mode_count, dtype=jnp.int32)
    phase = lon_index[:, None] * mode_index[None, :] % lon_count
    angle = phase.astype(jnp.float32) * (2.0 * math.pi / lon_count)
    paired = jnp.stack([jnp.cos(angle), -jnp.sin(angle)], axis=-1) * math.sqrt(2.0 / lon_count)
    return paired.reshape(lon_count, 2 * mode_count).astype(jnp.bfloat16)


def channel_mlp(row_block, w_up, w_down):
    values = row_block.astype(jnp.float32)
    center = values - jnp.mean(values, axis=-1, keepdims=True)
    spread = jnp.mean(center * center, axis=-1, keepdims=True)
    normed = (center * lax.rsqrt(spread + 1e-05)).astype(jnp.bfloat16)
    lifted = jnp.einsum("anc,ch->anh", normed, w_up, preferred_element_type=jnp.float32)
    active = jax.nn.gelu(lifted).astype(jnp.bfloat16)
    lowered = jnp.einsum("anh,hc->anc", active, w_down, preferred_element_type=jnp.float32)
    return (values + lowered).astype(jnp.bfloat16)


def on_device(
    fields,
    disco_weight,
    support_lat,
    support_lon,
    support_basis,
    support_value,
    w_up,
    w_down,
    legendre,
):
    lat_dev, lon_count, chans_dev = fields.shape
    group_count = chans_dev // G
    num_lat = lax.axis_size("lat")
    num_chan = lax.axis_size("chan")
    mode_dev = legendre.shape[0]
    degree_count = legendre.shape[1]
    mode_count = mode_dev * num_lat * num_chan
    padded = with_halo(fields, (("lat", 0),), HALO)
    wrapped = jnp.concatenate([padded[:, lon_count - DLON :], padded, padded[:, :DLON]], axis=1)
    row_ids = jnp.arange(lat_dev, dtype=jnp.int32)
    onehot = (support_basis[:, :, None] == jnp.arange(NB, dtype=jnp.int32)[None, None, :]).astype(
        jnp.float32
    )
    flat_weight = disco_weight.astype(jnp.float32).reshape(NB, chans_dev * G)
    picked = jnp.einsum("asb,bk->ask", onehot, flat_weight, precision=lax.Precision.HIGHEST)
    filters = (
        (picked * support_value[:, :, None])
        .astype(jnp.bfloat16)
        .reshape(lat_dev, S, group_count, G, G)
    )

    def shift_row(source_row, start):
        return lax.dynamic_slice(wrapped, (source_row, start, 0), (1, lon_count, chans_dev))[0]

    accumulated = jnp.zeros((lat_dev, lon_count, group_count, G), jnp.float32)
    for position in range(S):
        source = row_ids + HALO + support_lat[:, position]
        starts = DLON + support_lon[:, position]
        slab = jax.vmap(shift_row)(source, starts).reshape(lat_dev, lon_count, group_count, G)
        accumulated = accumulated + jnp.einsum(
            "anhi,ahoi->anho", slab, filters[:, position], preferred_element_type=jnp.float32
        )
    accumulated = accumulated.reshape(lat_dev, lon_count, chans_dev)
    mixed = (fields.astype(jnp.float32) + accumulated).astype(jnp.bfloat16)
    fourier = fourier_table(lon_count, mode_count)
    mode_start = lax.axis_index(("lat", "chan")) * mode_dev
    mode_ids = mode_start + jnp.arange(mode_dev, dtype=jnp.int32)
    degree = jnp.arange(degree_count, dtype=jnp.int32)
    kept_mask = degree[None, :] >= mode_ids[:, None]
    kept = jnp.where(kept_mask[:, :, None], legendre, jnp.zeros((), jnp.bfloat16))
    mixed_rows = channel_mlp(
        lax.all_to_all(mixed, "chan", split_axis=0, concat_axis=2, tiled=True), w_up, w_down
    )
    banded = lax.all_to_all(mixed_rows, "chan", split_axis=2, concat_axis=0, tiled=True)
    spectrum = jnp.einsum("anc,nk->akc", banded, fourier, preferred_element_type=jnp.float32)
    spectrum = spectrum.astype(jnp.bfloat16).reshape(lat_dev, mode_count, 2 * chans_dev)
    gathered_modes = lax.all_to_all(
        lax.all_to_all(spectrum, "lat", split_axis=1, concat_axis=0, tiled=True),
        "chan",
        split_axis=1,
        concat_axis=0,
        tiled=True,
    )
    gathered_modes = gathered_modes.reshape(num_chan, -1, mode_dev, 2 * chans_dev)
    coefficients = jnp.einsum(
        "mla,jamk->mljk", kept, gathered_modes, preferred_element_type=jnp.float32
    )
    coefficients = coefficients.reshape(mode_dev, degree_count, num_chan, 2, chans_dev)
    coefficients = jnp.transpose(coefficients, (0, 1, 3, 2, 4)).reshape(mode_dev, degree_count, -1)
    return coefficients.astype(jnp.bfloat16)


def solution(mesh):
    in_specs = (
        P(("tm", "lat"), None, "chan"),
        P(None, "chan", None),
        P("lat", None),
        P("lat", None),
        P("lat", None),
        P("lat", None),
        P(),
        P(),
        P(("lat", "chan"), None, None),
    )
    out_specs = P(("tm", "lat", "chan"), None, None)
    return jax.shard_map(
        on_device, mesh=mesh, in_specs=in_specs, out_specs=out_specs, check_vma=False
    )
```

profile of v0, /device:TPU:0, one launch (start us, length us, event | category | flops | bytes accessed | tf_op | source)
XLA Modules:
  0.0 243.2 jit_solution(3471063891435009560)
XLA Ops:
  2.0 5.0 %collective-permute-start = (bf16[2,1440,64]{1,2,0:T(8,128)(2,1)}, bf16[2,1440,64]{1,2,0:T(8,128)(2,1)S(1)}, u32[]{:S(2)}, u32[]{:S(2)}) collective-permute-start(bf16[2,1440,64]{1,2,0:T(8,128)(2,1)} %get-tuple-element.169), channel_id=1, source_target_pairs={{0,16},{1,17},{2,18},{3,19},{4,20},{5,21},{6,22},{7,23},{8,24},{9,... | collective-permute-start | bytes 1105928 | tf_op jit(solution)/shard_map/ppermute | solution.py:23
  11.6 4.1 %collective-permute-done = bf16[2,1440,64]{1,2,0:T(8,128)(2,1)S(1)} collective-permute-done((bf16[2,1440,64]{1,2,0:T(8,128)(2,1)}, bf16[2,1440,64]{1,2,0:T(8,128)(2,1)S(1)}, u32[]{:S(2)}, u32[]{:S(2)}) %collective-permute-start) | collective-permute-done | bytes 368672 | tf_op jit(solution)/shard_map/ppermute | solution.py:23
  16.1 3.6 %collective-permute-done.1 = bf16[2,1440,64]{1,2,0:T(8,128)(2,1)} collective-permute-done((bf16[2,1440,64]{1,2,0:T(8,128)(2,1)S(1)}, bf16[2,1440,64]{1,2,0:T(8,128)(2,1)}, u32[]{:S(2)}, u32[]{:S(2)}) %collective-permute-start.1) | collective-permute-done | bytes 368672 | tf_op jit(solution)/shard_map/ppermute | solution.py:25
  23.2 13.7 %concatenate.34 = bf16[8,1448,64]{2,1,0:T(8,128)(2,1)S(1)} concatenate(bf16[8,4,64]{2,1,0:T(4,128)(2,1)S(1)} %get-tuple-element.168, bf16[8,1440,64]{2,1,0:T(8,128)(2,1)} %copy-done.1, bf16[8,4,64]{2,1,0:T(4,128)(2,1)S(1)} %get-tuple-element.167), dimensions={1} | concatenate | bytes 2965504 | tf_op jit(solution)/shard_map/concatenate | solution.py:71
  38.2 11.3 %while.9 = (s32[]{:T(128)}, bf16[8,1448,64]{2,1,0:T(8,128)(2,1)S(1)}, s32[4,3]{1,0:T(4,128)S(1)}, bf16[4,1,1440,64]{3,2,1,0:T(8,128)(2,1)}, s32[]{:T(128)}) while((s32[]{:T(128)}, bf16[8,1448,64]{2,1,0:T(8,128)(2,1)S(1)}, s32[4,3]{1,0:T(4,128)S(1)}, bf16[4,1,1440,64]{3,2,1,0:T(8,128)(2,1)}, s32[]{:T(128)}) %tuple.166), condition=%wide.while_cond, body=%wide.while_body.sunk | while | flops 2 | bytes 554601 | solution.py:85
  38.9 2.2 bitcast_dynamic-update-slice_fusion.18
  44.6 2.2 bitcast_dynamic-update-slice_fusion.18
  50.9 11.2 %while.10 = (s32[]{:T(128)}, bf16[8,1448,64]{2,1,0:T(8,128)(2,1)S(1)}, s32[4,3]{1,0:T(4,128)S(1)}, bf16[4,1,1440,64]{3,2,1,0:T(8,128)(2,1)}, s32[]{:T(128)}) while((s32[]{:T(128)}, bf16[8,1448,64]{2,1,0:T(8,128)(2,1)S(1)}, s32[4,3]{1,0:T(4,128)S(1)}, bf16[4,1,1440,64]{3,2,1,0:T(8,128)(2,1)}, s32[]{:T(128)}) %tuple.193), condition=%wide.while_cond.1, body=%wide.while_body.1.sunk | while | flops 2 | bytes 554601 | solution.py:85
  54.3 2.2 bitcast_dynamic-update-slice_fusion.19
  57.1 2.2 bitcast_dynamic-update-slice_fusion.19
  63.4 11.2 %while.11 = (s32[]{:T(128)}, bf16[8,1448,64]{2,1,0:T(8,128)(2,1)S(1)}, s32[4,3]{1,0:T(4,128)S(1)}, bf16[4,1,1440,64]{3,2,1,0:T(8,128)(2,1)}, s32[]{:T(128)}) while((s32[]{:T(128)}, bf16[8,1448,64]{2,1,0:T(8,128)(2,1)S(1)}, s32[4,3]{1,0:T(4,128)S(1)}, bf16[4,1,1440,64]{3,2,1,0:T(8,128)(2,1)}, s32[]{:T(128)}) %tuple.194), condition=%wide.while_cond.2, body=%wide.while_body.2.sunk | while | flops 2 | bytes 554601 | solution.py:85
  76.0 11.0 %while.12 = (s32[]{:T(128)}, bf16[8,1448,64]{2,1,0:T(8,128)(2,1)S(1)}, s32[4,3]{1,0:T(4,128)S(1)}, bf16[4,1,1440,64]{3,2,1,0:T(8,128)(2,1)}, s32[]{:T(128)}) while((s32[]{:T(128)}, bf16[8,1448,64]{2,1,0:T(8,128)(2,1)S(1)}, s32[4,3]{1,0:T(4,128)S(1)}, bf16[4,1,1440,64]{3,2,1,0:T(8,128)(2,1)}, s32[]{:T(128)}) %tuple.195), condition=%wide.while_cond.3, body=%wide.while_body.3.sunk | while | flops 2 | bytes 554601 | solution.py:85
  88.3 11.0 %while.13 = (s32[]{:T(128)}, bf16[8,1448,64]{2,1,0:T(8,128)(2,1)S(1)}, s32[4,3]{1,0:T(4,128)S(1)}, bf16[4,1,1440,64]{3,2,1,0:T(8,128)(2,1)}, s32[]{:T(128)}) while((s32[]{:T(128)}, bf16[8,1448,64]{2,1,0:T(8,128)(2,1)S(1)}, s32[4,3]{1,0:T(4,128)S(1)}, bf16[4,1,1440,64]{3,2,1,0:T(8,128)(2,1)}, s32[]{:T(128)}) %tuple.196), condition=%wide.while_cond.4, body=%wide.while_body.4.sunk | while | flops 2 | bytes 554601 | solution.py:85
  100.7 11.5 %while.14 = (s32[]{:T(128)}, bf16[8,1448,64]{2,1,0:T(8,128)(2,1)S(1)}, s32[4,3]{1,0:T(4,128)S(1)}, bf16[4,1,1440,64]{3,2,1,0:T(8,128)(2,1)}, s32[]{:T(128)}) while((s32[]{:T(128)}, bf16[8,1448,64]{2,1,0:T(8,128)(2,1)S(1)}, s32[4,3]{1,0:T(4,128)S(1)}, bf16[4,1,1440,64]{3,2,1,0:T(8,128)(2,1)}, s32[]{:T(128)}) %tuple.197), condition=%wide.while_cond.5, body=%wide.while_body.5.sunk | while | flops 2 | bytes 554601 | solution.py:85
  101.4 2.2 bitcast_dynamic-update-slice_fusion.23
  104.2 2.2 bitcast_dynamic-update-slice_fusion.23
  107.1 2.2 bitcast_dynamic-update-slice_fusion.23
  110.0 2.2 bitcast_dynamic-update-slice_fusion.23
  113.5 10.8 %while.15 = (s32[]{:T(128)}, bf16[8,1448,64]{2,1,0:T(8,128)(2,1)S(1)}, s32[4,3]{1,0:T(4,128)S(1)}, bf16[4,1,1440,64]{3,2,1,0:T(8,128)(2,1)}, s32[]{:T(128)}) while((s32[]{:T(128)}, bf16[8,1448,64]{2,1,0:T(8,128)(2,1)S(1)}, s32[4,3]{1,0:T(4,128)S(1)}, bf16[4,1,1440,64]{3,2,1,0:T(8,128)(2,1)}, s32[]{:T(128)}) %tuple.198), condition=%wide.while_cond.6, body=%wide.while_body.6.sunk | while | flops 2 | bytes 554601 | solution.py:85
  125.6 10.2 %while.16 = (s32[]{:T(128)}, bf16[8,1448,64]{2,1,0:T(8,128)(2,1)S(1)}, s32[4,3]{1,0:T(4,128)S(1)}, bf16[4,1,1440,64]{3,2,1,0:T(8,128)(2,1)}, s32[]{:T(128)}) while((s32[]{:T(128)}, bf16[8,1448,64]{2,1,0:T(8,128)(2,1)S(1)}, s32[4,3]{1,0:T(4,128)S(1)}, bf16[4,1,1440,64]{3,2,1,0:T(8,128)(2,1)}, s32[]{:T(128)}) %tuple.199), condition=%wide.while_cond.7, body=%wide.while_body.7.sunk | while | flops 2 | bytes 554601 | solution.py:85
  137.2 10.9 %while.17 = (s32[]{:T(128)}, bf16[8,1448,64]{2,1,0:T(8,128)(2,1)S(1)}, s32[4,3]{1,0:T(4,128)S(1)}, bf16[4,1,1440,64]{3,2,1,0:T(8,128)(2,1)}, s32[]{:T(128)}) while((s32[]{:T(128)}, bf16[8,1448,64]{2,1,0:T(8,128)(2,1)S(1)}, s32[4,3]{1,0:T(4,128)S(1)}, bf16[4,1,1440,64]{3,2,1,0:T(8,128)(2,1)}, s32[]{:T(128)}) %tuple.200), condition=%wide.while_cond.8, body=%wide.while_body.8.sunk | while | flops 2 | bytes 554601 | solution.py:85
  148.1 2.2 fusion.24
  160.8 23.6 %all_to_all.60 = bf16[4,1440,64]{1,2,0:T(8,128)(2,1)S(1)} all-to-all(bf16[4,1440,64]{1,2,0:T(8,128)(2,1)S(1)} %fusion.11), channel_id=1, replica_groups=mesh['lat'=2,'chan'=4,'tm'=4] {'chan'}, dimensions={0} | all-to-all | bytes 1474560 | tf_op jit(solution)/shard_map/all_to_all | solution.py:104
  185.4 3.2 %fusion.13 = bf16[1,1440,256]{2,1,0:T(8,128)(2,1)} fusion(f32[1440,256]{1,0:T(8,128)S(1)} %copy.144, bf16[512,256]{1,0:T(8,128)(2,1)S(1)} %copy-done, bf16[256,512]{1,0:T(8,128)(2,1)} %param.15, f32[1440,256]{0,1:T(8,128)S(1)} %bitcast.215, f32[1440]{0:T(1024)S(1)} %add_rsqrt_fusion, f32[1440]{0:T(1024)S(1)} %broadcast_multiply_fusion), kind=kOutput, calls=%fused_computation.43 | convolution fusion | flops 763453440 | bytes 4222208 | tf_op jit(solution)/shard_map/anh,hc->anc/dot_general | solution.py:48
  188.5 3.6 %copy.145 = bf16[1,1440,256]{1,0,2:T(2,128)(2,1)S(1)} copy(bf16[1,1440,256]{2,1,0:T(8,128)(2,1)} %fusion.13) | data formatting | bytes 1474560 | tf_op jit(solution)/shard_map/convert_element_type | solution.py:49
  192.7 5.6 %reduce.5 = bf16[256,1440]{1,0:T(8,128)(2,1)S(1)} reduce(bf16[256,1,1440]{2,1,0:T(2,128)(2,1)S(1)} %bitcast.217, bf16[]{:T(256)} %broadcast.411), dimensions={1}, to_apply=%bitcast.151.reduce_sub_computation | reduce | bytes 1474562
  200.3 3.5 %all-to-all-start.1 = ((bf16[4,2,46080]{2,1,0:T(2,128)(2,1)}), bf16[4,2,46080]{2,1,0:T(2,128)(2,1)S(1)}, u32[]{:S(2)}, u32[]{:S(2)}) async-start(bf16[4,2,46080]{2,1,0:T(2,128)(2,1)} %reshape.556), calls=%async_computation.1 | async-start | bytes 1474560 | tf_op jit(solution)/shard_map/all_to_all | solution.py:106
  204.7 17.1 %all-to-all-done.1 = bf16[4,2,46080]{2,1,0:T(2,128)(2,1)S(1)} async-done(((bf16[4,2,46080]{2,1,0:T(2,128)(2,1)}), bf16[4,2,46080]{2,1,0:T(2,128)(2,1)S(1)}, u32[]{:S(2)}, u32[]{:S(2)}) %all-to-all-start.1) | async-done | bytes 737312 | tf_op jit(solution)/shard_map/all_to_all | solution.py:106
  224.3 3.2 %all-to-all-start.2 = ((bf16[4,24,128]{2,0,1:T(4,128)(2,1)}), bf16[4,24,128]{2,0,1:T(4,128)(2,1)S(1)}, u32[]{:S(2)}, u32[]{:S(2)}) async-start(bf16[4,24,128]{2,0,1:T(4,128)(2,1)} %copy.146), calls=%async_computation.2 | async-start | bytes 49152 | tf_op jit(solution)/shard_map/all_to_all | solution.py:110
  227.6 3.9 %all-to-all-done.2 = bf16[4,24,128]{2,0,1:T(4,128)(2,1)S(1)} async-done(((bf16[4,24,128]{2,0,1:T(4,128)(2,1)}), bf16[4,24,128]{2,0,1:T(4,128)(2,1)S(1)}, u32[]{:S(2)}, u32[]{:S(2)}) %all-to-all-start.2) | async-done | bytes 24608 | tf_op jit(solution)/shard_map/all_to_all | solution.py:110
  232.1 3.3 %all-to-all-start.3 = ((bf16[8,12,128]{2,0,1:T(8,128)(2,1)}), bf16[8,12,128]{2,0,1:T(8,128)(2,1)S(1)}, u32[]{:S(2)}, u32[]{:S(2)}) async-start(bf16[8,12,128]{2,0,1:T(8,128)(2,1)} %bitcast.42), calls=%async_computation.3 | async-start | bytes 49152 | tf_op jit(solution)/shard_map/all_to_all | solution.py:109
  235.4 5.5 %all-to-all-done.3 = bf16[8,12,128]{2,0,1:T(8,128)(2,1)S(1)} async-done(((bf16[8,12,128]{2,0,1:T(8,128)(2,1)}), bf16[8,12,128]{2,0,1:T(8,128)(2,1)S(1)}, u32[]{:S(2)}, u32[]{:S(2)}) %all-to-all-start.3) | async-done | bytes 24608 | tf_op jit(solution)/shard_map/all_to_all | solution.py:109
  (194 shorter events, 124.3 us)
Async XLA Ops:
  0.0 185.4 %copy-start = (bf16[512,256]{1,0:T(8,128)(2,1)S(1)}, bf16[512,256]{1,0:T(8,128)(2,1)}, u32[]{:S(2)}) copy-start(bf16[512,256]{1,0:T(8,128)(2,1)} %param.16) | copy-start | bytes 786436
  0.0 8.3 %copy-start.2 = (bf16[4,1440,64]{1,2,0:T(8,128)(2,1)S(1)}, bf16[4,1440,64]{1,2,0:T(8,128)(2,1)}, u32[]{:S(2)}) copy-start(bf16[4,1440,64]{1,2,0:T(8,128)(2,1)} %param.9) | copy-start | bytes 2211844
  2.0 7.2 %copy-start.15 = (bf16[6,64,64]{2,1,0:T(8,128)(2,1)S(1)}, bf16[6,64,64]{2,1,0:T(8,128)(2,1)}, u32[]{:S(2)}) copy-start(bf16[6,64,64]{2,1,0:T(8,128)(2,1)} %param.10) | copy-start | bytes 147460
  2.0 7.3 %copy-start.17 = (f32[4,9]{1,0:T(4,128)S(1)}, f32[4,9]{1,0:T(4,128)}, u32[]{:S(2)}) copy-start(f32[4,9]{1,0:T(4,128)} %param.14) | copy-start | bytes 436
  2.0 7.4 %copy-start.18 = (s32[4,9]{1,0:T(4,128)S(1)}, s32[4,9]{1,0:T(4,128)}, u32[]{:S(2)}) copy-start(s32[4,9]{1,0:T(4,128)} %param.13) | copy-start | bytes 436
  2.0 13.7 %collective-permute-start = (bf16[2,1440,64]{1,2,0:T(8,128)(2,1)}, bf16[2,1440,64]{1,2,0:T(8,128)(2,1)S(1)}, u32[]{:S(2)}, u32[]{:S(2)}) collective-permute-start(bf16[2,1440,64]{1,2,0:T(8,128)(2,1)} %get-tuple-element.169), channel_id=1, source_target_pairs={{0,16},{1,17},{2,18},{3,19},{4,20},{5,21},{6,22},{7,23},{8,24},{9,... | collective-permute-start | bytes 1105928 | tf_op jit(solution)/shard_map/ppermute | solution.py:23
  7.0 12.6 %collective-permute-start.1 = (bf16[2,1440,64]{1,2,0:T(8,128)(2,1)S(1)}, bf16[2,1440,64]{1,2,0:T(8,128)(2,1)}, u32[]{:S(2)}, u32[]{:S(2)}) collective-permute-start(bf16[2,1440,64]{1,2,0:T(8,128)(2,1)S(1)} %get-tuple-element.170), channel_id=1, source_target_pairs={{16,0},{17,1},{18,2},{19,3},{20,4},{21,5},{22,6},{23,7},{24,8},{25... | collective-permute-start | bytes 1105928 | tf_op jit(solution)/shard_map/ppermute | solution.py:25
  9.2 2.1 copy-start.13
  9.2 2.1 copy-start.14
  21.6 1.6 copy-start.1
  148.1 2.2 copy-start.5
  148.1 2.2 copy-start.12
  150.3 1.4 copy-start.6
  151.7 1.4 copy-start.7
  153.0 1.4 copy-start.8
  154.4 1.4 copy-start.9
  155.8 1.4 copy-start.10
  157.2 1.4 copy-start.11
  158.5 1.1 copy-start.3
  158.5 1.6 copy-start.4
  200.3 21.5 %all-to-all-start.1 = ((bf16[4,2,46080]{2,1,0:T(2,128)(2,1)}), bf16[4,2,46080]{2,1,0:T(2,128)(2,1)S(1)}, u32[]{:S(2)}, u32[]{:S(2)}) async-start(bf16[4,2,46080]{2,1,0:T(2,128)(2,1)} %reshape.556), calls=%async_computation.1 | async-start | bytes 1474560 | tf_op jit(solution)/shard_map/all_to_all | solution.py:106
  223.0 17.9 %copy-start.16 = (bf16[3,384,8]{1,2,0:T(8,128)(2,1)S(1)}, bf16[3,384,8]{1,2,0:T(8,128)(2,1)}, u32[]{:S(2)}) copy-start(bf16[3,384,8]{1,2,0:T(8,128)(2,1)} %param.17) | copy-start | bytes 55300
  224.3 7.1 %all-to-all-start.2 = ((bf16[4,24,128]{2,0,1:T(4,128)(2,1)}), bf16[4,24,128]{2,0,1:T(4,128)(2,1)S(1)}, u32[]{:S(2)}, u32[]{:S(2)}) async-start(bf16[4,24,128]{2,0,1:T(4,128)(2,1)} %copy.146), calls=%async_computation.2 | async-start | bytes 49152 | tf_op jit(solution)/shard_map/all_to_all | solution.py:110
  232.1 8.9 %all-to-all-start.3 = ((bf16[8,12,128]{2,0,1:T(8,128)(2,1)}), bf16[8,12,128]{2,0,1:T(8,128)(2,1)S(1)}, u32[]{:S(2)}, u32[]{:S(2)}) async-start(bf16[8,12,128]{2,0,1:T(8,128)(2,1)} %bitcast.42), calls=%async_computation.3 | async-start | bytes 49152 | tf_op jit(solution)/shard_map/all_to_all | solution.py:109
where the time goes:
time: 245 us; the launch traced here: 243 us
  local copies, waits for them, and re-layouts  149 us (61%)
  waiting for transfers between devices  34.1 us (14%)
  blocking collectives  23.6 us (10%)
  starting transfers between devices  16.3 us (7%)
  matrix products  11.8 us (5%)
  other arithmetic  7.93 us (3%)
    gather x108, local copies, waits for them, and re-layouts  99.1 us
    unnamed x52, local copies, waits for them, and re-layouts  23.7 us
    all_to_all x1, blocking collectives, on_device(): lax.all_to_all(mixed, 'chan', split_axis=0, concat_axis=2, tiled=True)  23.6 us
    all_to_all x1, waiting for transfers between devices, on_device(): lax.all_to_all(mixed_rows, 'chan', split_axis=2, concat_axis=0, tiled=True)  17.1 us
    concatenate x1, local copies, waits for them, and re-layouts, on_device(): jnp.concatenate([padded[:, lon_count - DLON:], padded, padded[:, :DLON]],...  13.7 us
    dot_general x9, matrix products, on_device(): jnp.einsum('anhi,ahoi->anho', slab, filters[:, position], preferred_eleme...  7.22 us
    unnamed x1, other arithmetic  5.64 us
    all_to_all x1, waiting for transfers between devices, on_device(): lax.all_to_all(lax.all_to_all(spectrum, 'lat', split_axis=1, concat_axis=...  5.53 us
  transfers between devices with their start and end apart: 5, of which 5 were waited for; matrix products, arithmetic and copies ran while one was open for 2% of the time, Pallas kernels for 0%

commit v1 on v0

v1 whole, which is shorter than its diff:
```python
import functools
import math

import jax
import jax.numpy as jnp
import numpy as np
from jax import lax
from jax.experimental import pallas as pl
from jax.experimental.pallas import tpu as pltpu
from jax.sharding import PartitionSpec as P

G = 64
S = 9
HALO = 2
DLON = 4
TAPS = S + 1
LANES = 128
SLOT = 8
EPS = 1e-05
VMEM_LIMIT = 56 * 1024 * 1024


def ceil_to(value, step):
    return -(-value // step) * step


def conv_kernel(
    chunks,
    has_edge,
    pair_ref,
    lat_ref,
    lon_ref,
    basis_ref,
    value_ref,
    fields_ref,
    *rest,
):
    if has_edge:
        edge_ref, weight_ref, out_ref, rows_ref, taps_ref, filt_ref = rest
    else:
        edge_ref = None
        weight_ref, out_ref, rows_ref, taps_ref, filt_ref = rest
    own, _, lon = fields_ref.shape
    chunk = lon // chunks
    width = out_ref.shape[2]
    total = rows_ref.shape[2]
    pair = pair_ref[0]
    own_at = HALO * (1 - pair)
    edge_at = own * pair

    def place(slot, cells):
        rows_ref[slot, :, LANES : LANES + lon] = cells
        rows_ref[slot, :, 0:LANES] = cells[:, lon - LANES :]
        full = (lon // LANES) * LANES
        tail = total - LANES - lon
        rows_ref[slot, :, LANES + full :] = jnp.concatenate(
            [cells[:, full:], cells[:, :tail]], axis=1
        )

    for row in range(own):
        place(own_at + row, fields_ref[row])
    for row in range(HALO):
        if has_edge:
            place(edge_at + row, edge_ref[row])
        else:
            rows_ref[edge_at + row] = jnp.zeros(rows_ref.shape[1:], rows_ref.dtype)

    lane = lax.broadcasted_iota(jnp.int32, (G, LANES), 1)

    def fill(slot, tap, source, offset):
        for j in range(chunks):
            begin = LANES + chunk * j + offset
            first = lax.div(begin, LANES)
            shift = lax.rem(begin, LANES)
            back = lax.rem(LANES - shift, LANES)
            keep = lane < LANES - shift
            turned = []
            for t in range(width // LANES + 1):
                start = pl.multiple_of((first + t) * LANES, LANES)
                tile = rows_ref[source, :, pl.ds(start, LANES)].astype(jnp.float32)
                turned.append(pltpu.roll(tile, back, 1))
            for t in range(width // LANES):
                moved = jnp.where(keep, turned[t], turned[t + 1]).astype(jnp.bfloat16)
                at = j * width + t * LANES
                taps_ref[slot, pl.ds(pl.multiple_of(tap * G, G), G), at : at + LANES] = moved

    eye = jnp.where(
        lax.broadcasted_iota(jnp.int32, (G, G), 0) == lax.broadcasted_iota(jnp.int32, (G, G), 1),
        1.0,
        0.0,
    ).astype(jnp.bfloat16)
    for i in range(2):
        row = 2 * pair + i

        def one(tap, carry):
            fill(i, tap, HALO + i + lat_ref[row, tap], lon_ref[row, tap])
            return carry

        lax.fori_loop(0, S, one, 0)
        fill(i, S, HALO + i, 0)
        pieces = []
        for tap in range(S):
            picked = weight_ref[basis_ref[row, tap]].astype(jnp.float32) * value_ref[row, tap]
            pieces.append(picked.astype(jnp.bfloat16))
        pieces.append(eye)
        for k in range(TAPS // 2):
            filt_ref[:, k * 2 * G : (k + 1) * 2 * G] = jnp.concatenate(
                [pieces[2 * k], pieces[2 * k + 1]], axis=1
            )
        mixed = jnp.dot(filt_ref[...], taps_ref[i], preferred_element_type=jnp.float32).astype(
            jnp.bfloat16
        )
        for j in range(chunks):
            out_ref[j, i * G : (i + 1) * G, :] = mixed[:, j * width : (j + 1) * width]


def conv_rows(pair, supports, fields, edge, weight, chunks):
    own, chans, lon = fields.shape
    width = ceil_to(lon // chunks, LANES)
    highest = (LANES + lon - lon // chunks + DLON) // LANES
    total = (highest + 1) * LANES + width
    smem = pl.BlockSpec(memory_space=pltpu.SMEM)
    vmem = pl.BlockSpec(memory_space=pltpu.VMEM)
    arrays = [fields] + ([] if edge is None else [edge]) + [weight]
    return pl.pallas_call(
        functools.partial(conv_kernel, chunks, edge is not None),
        out_shape=jax.ShapeDtypeStruct((chunks, 2 * chans, width), jnp.bfloat16),
        in_specs=[smem] * 5 + [vmem] * len(arrays),
        out_specs=vmem,
        scratch_shapes=[
            pltpu.VMEM((own + HALO, chans, total), jnp.bfloat16),
            pltpu.VMEM((2, TAPS * G, chunks * width), jnp.bfloat16),
            pltpu.VMEM((G, TAPS * G), jnp.bfloat16),
        ],
        compiler_params=pltpu.CompilerParams(vmem_limit_bytes=VMEM_LIMIT),
        cost_estimate=pl.CostEstimate(
            flops=4 * G * TAPS * G * chunks * width,
            bytes_accessed=2 * fields.size * 2,
            transcendentals=0,
        ),
        name="conv_rows",
    )(pair, *supports, *arrays)


def mlp_kernel(dests, mixed_ref, up_ref, down_ref, table_ref, *rest):
    if len(rest) == 2:
        earlier_ref, out_ref = rest
    else:
        earlier_ref, out_ref = None, rest[0]
    parts = mixed_ref.shape[0]
    width = mixed_ref.shape[2]
    columns = []
    for i in range(2):
        columns.append(
            jnp.concatenate([mixed_ref[j, i * G : (i + 1) * G, :] for j in range(parts)], axis=0)
        )
    values = jnp.concatenate(columns, axis=1).astype(jnp.float32)
    center = values - jnp.mean(values, axis=0, keepdims=True)
    spread = jnp.mean(center * center, axis=0, keepdims=True)
    normed = (center * lax.rsqrt(spread + EPS)).astype(jnp.bfloat16)
    lifted = lax.dot_general(
        up_ref[...], normed, (((1,), (0,)), ((), ())), preferred_element_type=jnp.float32
    )
    inner = lifted * (
        math.sqrt(2.0 / math.pi) + (math.sqrt(2.0 / math.pi) * 0.044715) * (lifted * lifted)
    )
    half = 0.5 * lifted
    active = (half + half * jnp.tanh(inner)).astype(jnp.bfloat16)
    lowered = lax.dot_general(
        down_ref[...], active, (((1,), (0,)), ((), ())), preferred_element_type=jnp.float32
    )
    result = (values + lowered).astype(jnp.bfloat16)
    found = []
    for i in range(2):
        modes = lax.dot_general(
            table_ref[...],
            result[:, i * width : (i + 1) * width],
            (((1,), (1,)), ((), ())),
            preferred_element_type=jnp.float32,
        )
        found.append(modes.reshape(dests, SLOT, modes.shape[1]))
    block = jnp.concatenate(found, axis=1).astype(jnp.bfloat16)
    if earlier_ref is None:
        out_ref[...] = block
    else:
        out_ref[:, 0 : 2 * SLOT, :] = earlier_ref[...]
        out_ref[:, 2 * SLOT : 4 * SLOT, :] = block


def mlp_rows(mixed, up, down, table, dests, earlier):
    parts, pair_chans, width = mixed.shape
    chan = parts * pair_chans // 2
    rows = 2 * SLOT * (1 if earlier is None else 2)
    vmem = pl.BlockSpec(memory_space=pltpu.VMEM)
    arrays = [mixed, up, down, table] + ([] if earlier is None else [earlier])
    return pl.pallas_call(
        functools.partial(mlp_kernel, dests),
        out_shape=jax.ShapeDtypeStruct((dests, rows, chan), jnp.bfloat16),
        in_specs=[vmem] * len(arrays),
        out_specs=vmem,
        compiler_params=pltpu.CompilerParams(vmem_limit_bytes=VMEM_LIMIT),
        cost_estimate=pl.CostEstimate(
            flops=8 * chan * up.shape[0] * width,
            bytes_accessed=2 * (mixed.size + up.size + down.size + table.size),
            transcendentals=2 * up.shape[0] * width,
        ),
        name="mlp_rows",
    )(*arrays)


def final_kernel(start_ref, legendre_ref, spread_ref, spectrum_ref, out_ref):
    modes, lats, degrees = legendre_ref.shape
    depth = spread_ref.shape[1]
    chan = spectrum_ref.shape[1]
    degree = lax.broadcasted_iota(jnp.int32, (lats, degrees), 1)
    slot = lax.rem(lax.broadcasted_iota(jnp.int32, (degrees, depth), 1), SLOT)
    for m in range(modes):
        kept = jnp.where(degree >= start_ref[0] + m, legendre_ref[m].astype(jnp.float32), 0.0)
        wide = lax.dot_general(
            kept.astype(jnp.bfloat16),
            spread_ref[...],
            (((0,), (0,)), ((), ())),
            preferred_element_type=jnp.float32,
        )
        for r in range(2):
            picked = jnp.where(slot == 2 * m + r, wide, 0.0).astype(jnp.bfloat16)
            out_ref[m, :, r * chan : (r + 1) * chan] = jnp.dot(
                picked, spectrum_ref[...], preferred_element_type=jnp.float32
            ).astype(jnp.bfloat16)


def fourier_blocks(lon, chunks, width, dests, mode_dev):
    chunk = lon // chunks
    index = np.arange(lon, dtype=np.int64)
    mode = np.arange(dests * mode_dev, dtype=np.int64)
    angle = ((mode[:, None] * index[None, :]) % lon) * (2.0 * math.pi / lon)
    paired = np.stack([np.cos(angle), -np.sin(angle)], axis=1) * math.sqrt(2.0 / lon)
    paired = paired.reshape(dests, 2 * mode_dev, chunks, chunk)
    table = np.zeros((chunks, dests, SLOT, width), np.float32)
    table[:, :, : 2 * mode_dev, :chunk] = np.transpose(paired, (2, 0, 1, 3))
    return table.reshape(chunks, dests * SLOT, width).astype(jnp.bfloat16)


def on_device(
    fields,
    disco_weight,
    support_lat,
    support_lon,
    support_basis,
    support_value,
    w_up,
    w_down,
    legendre,
):
    lat_dev, lon, _ = fields.shape
    num_lat = lax.axis_size("lat")
    num_chan = lax.axis_size("chan")
    mode_dev, degrees, lats = legendre.shape
    dests = num_lat * num_chan
    width = ceil_to(lon // num_chan, LANES)
    band = lax.axis_index("lat")
    place = lax.axis_index("chan")
    cells = jnp.swapaxes(fields, 1, 2)
    supports = (support_lat, support_lon, support_basis, support_value)

    two_bands = num_lat == 2
    if two_bands:
        edge_out = lax.dynamic_slice_in_dim(cells, HALO * (1 - band), HALO, axis=0)
        edges = [None, lax.ppermute(edge_out, "lat", [(0, 1), (1, 0)])]
        pairs = [band, 1 - band]
    else:
        ends = num_lat - 1
        edges = [
            lax.ppermute(cells[lat_dev - HALO :], "lat", [(i, i + 1) for i in range(ends)]),
            lax.ppermute(cells[:HALO], "lat", [(i + 1, i) for i in range(ends)]),
        ]
        pairs = [0, 1]

    tables = jnp.asarray(fourier_blocks(lon, num_chan, width, dests, mode_dev))
    table = lax.dynamic_index_in_dim(tables, place, 0, keepdims=False)
    up = w_up.T
    down = w_down.T

    spectrum = None
    received = []
    for edge, pair in zip(edges, pairs):
        mixed = conv_rows(
            jnp.asarray(pair, jnp.int32).reshape(1), supports, cells, edge, disco_weight, num_chan
        )
        received.append(lax.all_to_all(mixed, "chan", split_axis=0, concat_axis=0, tiled=True))
    for block in received:
        spectrum = mlp_rows(block, up, down, table, dests, spectrum)

    gathered = lax.all_to_all(spectrum, ("lat", "chan"), split_axis=0, concat_axis=0, tiled=True)
    depth = dests * 4 * SLOT
    flat = gathered.reshape(depth, gathered.shape[2])

    row = np.arange(depth)
    source_band = row // (4 * SLOT) // num_chan
    phase = (row // (2 * SLOT)) % 2
    source_pair = (phase ^ source_band) if two_bands else phase
    lat_of = lat_dev * source_band + 2 * source_pair + (row // SLOT) % 2
    spread = (lat_of[None, :] == np.arange(lats)[:, None]).astype(jnp.bfloat16)
    start = (lax.axis_index(("lat", "chan")) * mode_dev).astype(jnp.int32).reshape(1)
    vmem = pl.BlockSpec(memory_space=pltpu.VMEM)
    return pl.pallas_call(
        final_kernel,
        out_shape=jax.ShapeDtypeStruct((mode_dev, degrees, 2 * flat.shape[1]), jnp.bfloat16),
        in_specs=[pl.BlockSpec(memory_space=pltpu.SMEM)] + [vmem] * 3,
        out_specs=vmem,
        compiler_params=pltpu.CompilerParams(vmem_limit_bytes=VMEM_LIMIT),
        name="final_sum",
    )(start, jnp.swapaxes(legendre, 1, 2), jnp.asarray(spread), flat)


def solution(mesh):
    in_specs = (
        P(("tm", "lat"), None, "chan"),
        P(None, "chan", None),
        P("lat", None),
        P("lat", None),
        P("lat", None),
        P("lat", None),
        P(),
        P(),
        P(("lat", "chan"), None, None),
    )
    out_specs = P(("tm", "lat", "chan"), None, None)
    return jax.shard_map(
        on_device, mesh=mesh, in_specs=in_specs, out_specs=out_specs, check_vma=False
    )
```

time: 245 us -> 63.4 us (0.26)
  local copies, waits for them, and re-layouts: 149 us -> 5.27 us
  blocking collectives: 23.6 us -> 0 us
  Pallas kernels: 0 us -> 20.4 us
  waiting for transfers between devices: 34.1 us -> 20.8 us
  matrix products: 11.8 us -> 0 us
  other arithmetic: 7.93 us -> 0 us
    gather x108 -> x0, local copies, waits for them, and re-layouts: 99.1 us -> none
    all_to_all x1 -> x0, blocking collectives: 23.6 us -> none  [on_device(): lax.all_to_all(mixed, 'chan', split_axis=0, concat_axis=2, tiled=True)]
    pallas_call x0 -> x5, Pallas kernels: none -> 20.4 us  [the longest x2 11.7 us: conv_rows(): pl.pallas_call(functools.partial(conv_kernel, chunks, edge is not None),...]
    unnamed x52 -> x16, local copies, waits for them, and re-layouts: 23.7 us -> 3.83 us
    all_to_all x3, waiting for transfers between devices: 26.5 us -> 11.7 us  [the longest x1 7.52 us: on_device(): lax.all_to_all(spectrum, ('lat', 'chan'), split_axis=0, concat_axis=0, ti...]
    concatenate x1 -> x0, local copies, waits for them, and re-layouts: 13.7 us -> none  [on_device(): jnp.concatenate([padded[:, lon_count - DLON:], padded, padded[:, :DLON]],...]
    dot_general x12 -> x0, matrix products: 11.2 us -> none  [the longest x9 7.22 us: on_device(): jnp.einsum('anhi,ahoi->anho', slab, filters[:, position], preferred_eleme...]
    convert_element_type x7 -> x0, local copies, waits for them, and re-layouts: 6.07 us -> none  [the longest x1 3.61 us: channel_mlp(): return (values + lowered).astype(jnp.bfloat16)]
  transfers between devices with their start and end apart: 5 -> 4, of which waited for: 5 -> 3; matrix products, arithmetic and copies ran while one was open for 2% -> 5% of each run, Pallas kernels for 0% -> 14%
where the time goes in v1:
time: 63.4 us; the launch traced here: 62.9 us
  waiting for transfers between devices  20.8 us (33%)
  Pallas kernels  20.4 us (32%)
  starting transfers between devices  16.4 us (26%)
  local copies, waits for them, and re-layouts  5.27 us (8%)
    pallas_call x2, Pallas kernels, conv_rows(): pl.pallas_call(functools.partial(conv_kernel, chunks, edge is not None),...  11.7 us
    all_to_all x2, starting transfers between devices, on_device(): lax.all_to_all(mixed, 'chan', split_axis=0, concat_axis=0, tiled=True)  11.1 us
    ppermute x1, waiting for transfers between devices, on_device(): edges = [None, lax.ppermute(edge_out, 'lat', [(0, 1), (1, 0)])]  9.05 us
    all_to_all x1, waiting for transfers between devices, on_device(): lax.all_to_all(spectrum, ('lat', 'chan'), split_axis=0, concat_axis=0, ti...  7.52 us
    pallas_call x2, Pallas kernels, mlp_rows(): pl.pallas_call(functools.partial(mlp_kernel, dests), out_shape=jax.ShapeD...  5.83 us
    all_to_all x2, waiting for transfers between devices, on_device(): lax.all_to_all(mixed, 'chan', split_axis=0, concat_axis=0, tiled=True)  4.21 us
    unnamed x16, local copies, waits for them, and re-layouts  3.83 us
    all_to_all x1, starting transfers between devices, on_device(): lax.all_to_all(spectrum, ('lat', 'chan'), split_axis=0, concat_axis=0, ti...  3.7 us
  transfers between devices with their start and end apart: 4, of which 3 were waited for; matrix products, arithmetic and copies ran while one was open for 5% of the time, Pallas kernels for 14%

profile of v1, /device:TPU:0, one launch (start us, length us, event | category | flops | bytes accessed | tf_op | source)
XLA Modules:
  0.0 62.9 jit_solution(8086583817790146882)
XLA Ops:
  0.0 0.0 copy-start
  0.0 5.8 %conv_rows.3 = bf16[4,128,384]{2,1,0:T(8,128)(2,1)} custom-call(s32[1]{0:T(128)} %bitcast.8.pair_ref, s32[4,9]{1,0:T(4,128)} %lat_ref.3, s32[4,9]{1,0:T(4,128)} %lon_ref.3, s32[4,9]{1,0:T(4,128)} %basis_ref.3, f32[4,9]{1,0:T(4,128)} %value_ref.3, bf16[4,64,1440]{2,1,0:T(8,128)(2,1)} %bitcast.12, bf16[6,64,64]{2,1,0:T(8,128)(2,1)} %rest_0_.1), custom_call_target="tpu_custom_call" | custom-call | flops 251658240 | bytes 1474560 | tf_op jit(solution)/shard_map/conv_rows/pallas_call | solution.py:125
  5.8 6.3 %all-to-all-start.1 = ((bf16[4,128,384]{2,1,0:T(8,128)(2,1)}), bf16[4,128,384]{2,1,0:T(8,128)(2,1)S(1)}, u32[]{:S(2)}, u32[]{:S(2)}) async-start(bf16[4,128,384]{2,1,0:T(8,128)(2,1)} %conv_rows.3), calls=%async_computation.1 | async-start | bytes 786432 | tf_op jit(solution)/shard_map/all_to_all | solution.py:290
  12.1 0.0 copy-done
  12.1 1.6 %collective-permute-start = (bf16[2,64,1440]{2,1,0:T(8,128)(2,1)S(1)}, bf16[2,64,1440]{2,1,0:T(8,128)(2,1)S(1)}, u32[]{:S(2)}, u32[]{:S(2)}) collective-permute-start(bf16[2,64,1440]{2,1,0:T(8,128)(2,1)S(1)} %dynamic-slice_bitcast_fusion), channel_id=1, source_target_pairs={{0,16},{16,0},{1,17},{17,1},{2,18},{18,2},{3,19},{19,3},{4,20},{20... | collective-permute-start | bytes 1105928 | tf_op jit(solution)/shard_map/ppermute | solution.py:269
  13.7 9.1 %collective-permute-done.rest_0_ = bf16[2,64,1440]{2,1,0:T(8,128)(2,1)S(1)} collective-permute-done((bf16[2,64,1440]{2,1,0:T(8,128)(2,1)S(1)}, bf16[2,64,1440]{2,1,0:T(8,128)(2,1)S(1)}, u32[]{:S(2)}, u32[]{:S(2)}) %collective-permute-start) | collective-permute-done | bytes 368672 | tf_op jit(solution)/shard_map/ppermute | solution.py:269
  22.8 0.0 copy-start.4
  22.8 0.7 %copy-done.4 = bf16[2,64,1440]{2,1,0:T(8,128)(2,1)} copy-done((bf16[2,64,1440]{2,1,0:T(8,128)(2,1)}, bf16[2,64,1440]{2,1,0:T(8,128)(2,1)S(1)}, u32[]{:S(2)}) %copy-start.4) | copy-done | bytes 368664
  23.5 0.0 copy-start.5
  23.5 0.0 copy-start.6
  23.5 5.9 %conv_rows.2 = bf16[4,128,384]{2,1,0:T(8,128)(2,1)} custom-call(s32[1]{0:T(128)} %bitcast.2.pair_ref, s32[4,9]{1,0:T(4,128)} %lat_ref.3, s32[4,9]{1,0:T(4,128)} %lon_ref.3, s32[4,9]{1,0:T(4,128)} %basis_ref.3, f32[4,9]{1,0:T(4,128)} %value_ref.3, bf16[4,64,1440]{2,1,0:T(8,128)(2,1)} %bitcast.13, bf16[2,64,1440]{2,1,0:T(8,128)(2,1)} %copy-done.4, ...), custom_call_target="tpu_custom_call" | custom-call | flops 251658240 | bytes 1474560 | tf_op jit(solution)/shard_map/conv_rows/pallas_call | solution.py:125
  29.4 0.0 all-to-all-done.1.mixed_ref
  29.4 0.0 copy-start.2
  29.4 4.8 %all-to-all-start = ((bf16[4,128,384]{2,1,0:T(8,128)(2,1)}), bf16[4,128,384]{2,1,0:T(8,128)(2,1)S(1)}, u32[]{:S(2)}, u32[]{:S(2)}) async-start(bf16[4,128,384]{2,1,0:T(8,128)(2,1)} %conv_rows.2), calls=%async_computation | async-start | bytes 786432 | tf_op jit(solution)/shard_map/all_to_all | solution.py:290
  34.3 0.0 copy-done.5
  34.3 0.8 %copy.12 = bf16[256,512]{0,1:T(8,128)(2,1)} copy(bf16[256,512]{1,0:T(8,128)(2,1)S(1)} %copy-done.5) | data formatting | bytes 524288 | tf_op args[6]
  35.1 0.0 copy-done.6
  35.1 0.8 %copy.13 = bf16[512,256]{0,1:T(8,128)(2,1)} copy(bf16[512,256]{1,0:T(8,128)(2,1)S(1)} %copy-done.6) | data formatting | bytes 524288 | tf_op args[7]
  35.9 1.4 %dynamic-slice_bitcast_fusion.1.table_ref = bf16[64,384]{1,0:T(8,128)(2,1)} fusion(bf16[4,64,384]{2,1,0:T(8,128)(2,1)} %constant.29.clone, s32[]{:T(128)S(6)} %select_n.8), kind=kLoop, calls=%fused_computation.1 | loop fusion | bytes 98308 | tf_op jit(solution)/shard_map/jit(dynamic_index_in_dim)/squeeze | solution.py:280
  37.4 0.0 copy-done.2
  37.4 2.9 %mlp_rows.2.rest_0_ = bf16[8,16,256]{2,1,0:T(8,128)(2,1)} custom-call(bf16[4,128,384]{2,1,0:T(8,128)(2,1)} %copy-done.2, bf16[512,256]{1,0:T(8,128)(2,1)} %bitcast.15, bf16[256,512]{1,0:T(8,128)(2,1)} %bitcast.17, bf16[64,384]{1,0:T(8,128)(2,1)} %dynamic-slice_bitcast_fusion.1.table_ref), custom_call_target="tpu_custom_call" | custom-call | flops 402653184 | bytes 966656 | tf_op jit(solution)/shard_map/mlp_rows/pallas_call | solution.py:196
  40.2 4.2 %all-to-all-done.mixed_ref = bf16[4,128,384]{2,1,0:T(8,128)(2,1)S(1)} async-done(((bf16[4,128,384]{2,1,0:T(8,128)(2,1)}), bf16[4,128,384]{2,1,0:T(8,128)(2,1)S(1)}, u32[]{:S(2)}, u32[]{:S(2)}) %all-to-all-start) | async-done | bytes 393248 | tf_op jit(solution)/shard_map/all_to_all | solution.py:290
  44.5 0.0 copy-start.3
  44.5 0.7 %copy-done.3 = bf16[4,128,384]{2,1,0:T(8,128)(2,1)} copy-done((bf16[4,128,384]{2,1,0:T(8,128)(2,1)}, bf16[4,128,384]{2,1,0:T(8,128)(2,1)S(1)}, u32[]{:S(2)}) %copy-start.3) | copy-done | bytes 393240
  45.2 2.9 %mlp_rows.3 = bf16[8,32,256]{2,1,0:T(8,128)(2,1)} custom-call(bf16[4,128,384]{2,1,0:T(8,128)(2,1)} %copy-done.3, bf16[512,256]{1,0:T(8,128)(2,1)} %bitcast.16, bf16[256,512]{1,0:T(8,128)(2,1)} %bitcast.18, bf16[64,384]{1,0:T(8,128)(2,1)} %dynamic-slice_bitcast_fusion.1.table_ref, bf16[8,16,256]{2,1,0:T(8,128)(2,1)} %mlp_rows.2.rest_0_), custom_call_target="tpu_custom_call" | custom-call | flops 402653184 | bytes 966656 | tf_op jit(solution)/shard_map/mlp_rows/pallas_call | solution.py:196
  48.1 3.7 %all-to-all-start.2 = ((bf16[8,32,256]{2,1,0:T(8,128)(2,1)}), bf16[8,32,256]{2,1,0:T(8,128)(2,1)S(1)}, u32[]{:S(2)}, u32[]{:S(2)}) async-start(bf16[8,32,256]{2,1,0:T(8,128)(2,1)} %mlp_rows.3), calls=%async_computation.2 | async-start | bytes 262144 | tf_op jit(solution)/shard_map/all_to_all | solution.py:294
  51.9 7.5 %all-to-all-done.2 = bf16[8,32,256]{2,1,0:T(8,128)(2,1)S(1)} async-done(((bf16[8,32,256]{2,1,0:T(8,128)(2,1)}), bf16[8,32,256]{2,1,0:T(8,128)(2,1)S(1)}, u32[]{:S(2)}, u32[]{:S(2)}) %all-to-all-start.2) | async-done | bytes 131104 | tf_op jit(solution)/shard_map/all_to_all | solution.py:294
  59.4 0.0 copy-start.1
  59.4 0.6 %copy-done.1 = bf16[8,32,256]{2,1,0:T(8,128)(2,1)} copy-done((bf16[8,32,256]{2,1,0:T(8,128)(2,1)}, bf16[8,32,256]{2,1,0:T(8,128)(2,1)S(1)}, u32[]{:S(2)}) %copy-start.1) | copy-done | bytes 131096
  60.0 2.9 %final_sum.1 = bf16[3,384,512]{2,1,0:T(8,128)(2,1)} custom-call(s32[1]{0:T(128)} %bitcast.start_ref, bf16[3,8,384]{2,1,0:T(8,128)(2,1)} %bitcast.19, bf16[8,256]{1,0:T(8,128)(2,1)} %constant.30.clone.spread_ref, bf16[256,256]{1,0:T(8,128)(2,1)} %bitcast.14), custom_call_target="tpu_custom_call" | custom-call | tf_op jit(solution)/shard_map/final_sum/pallas_call | solution.py:306
  (1 shorter events, 0.0 us)
Async XLA Ops:
  0.0 12.1 %copy-start = (bf16[4,1440,64]{1,2,0:T(8,128)(2,1)S(1)}, bf16[4,1440,64]{1,2,0:T(8,128)(2,1)}, u32[]{:S(2)}) copy-start(bf16[4,1440,64]{1,2,0:T(8,128)(2,1)} %param.11) | copy-start | bytes 2211844
  5.8 23.6 %all-to-all-start.1 = ((bf16[4,128,384]{2,1,0:T(8,128)(2,1)}), bf16[4,128,384]{2,1,0:T(8,128)(2,1)S(1)}, u32[]{:S(2)}, u32[]{:S(2)}) async-start(bf16[4,128,384]{2,1,0:T(8,128)(2,1)} %conv_rows.3), calls=%async_computation.1 | async-start | bytes 786432 | tf_op jit(solution)/shard_map/all_to_all | solution.py:290
  12.1 10.6 %collective-permute-start = (bf16[2,64,1440]{2,1,0:T(8,128)(2,1)S(1)}, bf16[2,64,1440]{2,1,0:T(8,128)(2,1)S(1)}, u32[]{:S(2)}, u32[]{:S(2)}) collective-permute-start(bf16[2,64,1440]{2,1,0:T(8,128)(2,1)S(1)} %dynamic-slice_bitcast_fusion), channel_id=1, source_target_pairs={{0,16},{16,0},{1,17},{17,1},{2,18},{18,2},{3,19},{19,3},{4,20},{20... | collective-permute-start | bytes 1105928 | tf_op jit(solution)/shard_map/ppermute | solution.py:269
  22.8 0.7 %copy-start.4 = (bf16[2,64,1440]{2,1,0:T(8,128)(2,1)}, bf16[2,64,1440]{2,1,0:T(8,128)(2,1)S(1)}, u32[]{:S(2)}) copy-start(bf16[2,64,1440]{2,1,0:T(8,128)(2,1)S(1)} %collective-permute-done.rest_0_) | copy-start | bytes 1105924
  23.5 10.7 %copy-start.5 = (bf16[256,512]{1,0:T(8,128)(2,1)S(1)}, bf16[256,512]{1,0:T(8,128)(2,1)}, u32[]{:S(2)}) copy-start(bf16[256,512]{1,0:T(8,128)(2,1)} %param.17) | copy-start | bytes 786436
  23.5 11.6 %copy-start.6 = (bf16[512,256]{1,0:T(8,128)(2,1)S(1)}, bf16[512,256]{1,0:T(8,128)(2,1)}, u32[]{:S(2)}) copy-start(bf16[512,256]{1,0:T(8,128)(2,1)} %param.18) | copy-start | bytes 786436
  29.4 7.9 %copy-start.2 = (bf16[4,128,384]{2,1,0:T(8,128)(2,1)}, bf16[4,128,384]{2,1,0:T(8,128)(2,1)S(1)}, u32[]{:S(2)}) copy-start(bf16[4,128,384]{2,1,0:T(8,128)(2,1)S(1)} %all-to-all-done.1.mixed_ref) | copy-start | bytes 1179652
  29.4 15.0 %all-to-all-start = ((bf16[4,128,384]{2,1,0:T(8,128)(2,1)}), bf16[4,128,384]{2,1,0:T(8,128)(2,1)S(1)}, u32[]{:S(2)}, u32[]{:S(2)}) async-start(bf16[4,128,384]{2,1,0:T(8,128)(2,1)} %conv_rows.2), calls=%async_computation | async-start | bytes 786432 | tf_op jit(solution)/shard_map/all_to_all | solution.py:290
  44.5 0.7 %copy-start.3 = (bf16[4,128,384]{2,1,0:T(8,128)(2,1)}, bf16[4,128,384]{2,1,0:T(8,128)(2,1)S(1)}, u32[]{:S(2)}) copy-start(bf16[4,128,384]{2,1,0:T(8,128)(2,1)S(1)} %all-to-all-done.mixed_ref) | copy-start | bytes 1179652
  48.1 11.2 %all-to-all-start.2 = ((bf16[8,32,256]{2,1,0:T(8,128)(2,1)}), bf16[8,32,256]{2,1,0:T(8,128)(2,1)S(1)}, u32[]{:S(2)}, u32[]{:S(2)}) async-start(bf16[8,32,256]{2,1,0:T(8,128)(2,1)} %mlp_rows.3), calls=%async_computation.2 | async-start | bytes 262144 | tf_op jit(solution)/shard_map/all_to_all | solution.py:294
  59.4 0.7 %copy-start.1 = (bf16[8,32,256]{2,1,0:T(8,128)(2,1)}, bf16[8,32,256]{2,1,0:T(8,128)(2,1)S(1)}, u32[]{:S(2)}) copy-start(bf16[8,32,256]{2,1,0:T(8,128)(2,1)S(1)} %all-to-all-done.2) | copy-start | bytes 393220

commit v2 on v1

v2 whole, which is shorter than its diff:
```python
import functools
import math

import jax
import jax.numpy as jnp
import numpy as np
from jax import lax
from jax.experimental import pallas as pl
from jax.experimental.pallas import tpu as pltpu
from jax.sharding import PartitionSpec as P

G = 64
S = 9
HALO = 2
DLON = 4
TAPS = S + 1
LANES = 128
SLOT = 8
EPS = 1e-05
FEW = 8
MIB = 1024 * 1024
FLOPS_PER_US = 1_000_000_000

SMEM = pl.BlockSpec(memory_space=pltpu.SMEM)
VMEM = pl.BlockSpec(memory_space=pltpu.VMEM)


def ceil_to(value, step):
    return -(-value // step) * step


def params(mib):
    return pltpu.CompilerParams(vmem_limit_bytes=mib * MIB)


def takes(micros):
    return pl.CostEstimate(flops=micros * FLOPS_PER_US, bytes_accessed=0, transcendentals=0)


def conv_kernel(
    has_edge, pair_ref, place_ref, lat_ref, lon_ref, basis_ref, value_ref, fields_ref, *rest
):
    if has_edge:
        edge_ref, weight_ref, *rest = rest
    else:
        edge_ref, (weight_ref, *rest) = None, rest
    *out_refs, rows_ref, taps_ref, filt_ref = rest
    own, _, lon = fields_ref.shape
    chunks = len(out_refs)
    chunk = lon // chunks
    width = out_refs[0].shape[1]
    total = rows_ref.shape[2]
    pair = pair_ref[0]
    own_at = HALO * (1 - pair)
    edge_at = own * pair

    def put(slot, cells):
        rows_ref[slot, :, LANES : LANES + lon] = cells
        rows_ref[slot, :, 0:LANES] = cells[:, lon - LANES :]
        full = (lon // LANES) * LANES
        tail = total - LANES - lon
        rows_ref[slot, :, LANES + full :] = jnp.concatenate(
            [cells[:, full:], cells[:, :tail]], axis=1
        )

    for row in range(own):
        put(own_at + row, fields_ref[row])
    for row in range(HALO):
        if has_edge:
            put(edge_at + row, edge_ref[row])
        else:
            rows_ref[edge_at + row] = jnp.zeros(rows_ref.shape[1:], rows_ref.dtype)

    lane = lax.broadcasted_iota(jnp.int32, (G, LANES), 1)
    begins = [LANES + chunk * lax.rem(place_ref[0] + k, chunks) for k in range(chunks)]

    def fill(slot, tap, source, offset):
        for k in range(chunks):
            begin = begins[k] + offset
            first = lax.div(begin, LANES)
            shift = lax.rem(begin, LANES)
            back = lax.rem(LANES - shift, LANES)
            keep = lane < LANES - shift
            turned = []
            for t in range(width // LANES + 1):
                start = pl.multiple_of((first + t) * LANES, LANES)
                tile = rows_ref[source, :, pl.ds(start, LANES)]
                turned.append(pltpu.roll(tile, back, 1))
            for t in range(width // LANES):
                at = k * width + t * LANES
                taps_ref[slot, tap * G : (tap + 1) * G, at : at + LANES] = jnp.where(
                    keep, turned[t], turned[t + 1]
                )

    eye = jnp.where(
        lax.broadcasted_iota(jnp.int32, (G, G), 0) == lax.broadcasted_iota(jnp.int32, (G, G), 1),
        1.0,
        0.0,
    ).astype(jnp.bfloat16)
    for i in range(2):
        row = 2 * pair + i
        pieces = []
        for tap in range(S):
            picked = weight_ref[basis_ref[row, tap]].astype(jnp.float32) * value_ref[row, tap]
            pieces.append(picked.astype(jnp.bfloat16))
        pieces.append(eye)
        for k in range(TAPS // 2):
            filt_ref[i, :, k * 2 * G : (k + 1) * 2 * G] = jnp.concatenate(
                [pieces[2 * k], pieces[2 * k + 1]], axis=1
            )
        for tap in range(S):
            fill(i, tap, HALO + i + lat_ref[row, tap], lon_ref[row, tap])
        fill(i, S, HALO + i, 0)
        mixed = jnp.dot(filt_ref[i], taps_ref[i], preferred_element_type=jnp.float32).astype(
            jnp.bfloat16
        )
        for k in range(chunks):
            out_refs[k][i * G : (i + 1) * G, :] = mixed[:, k * width : (k + 1) * width]


def conv_rows(pair, place, supports, fields, edge, weight, chunks):
    own, chans, lon = fields.shape
    width = ceil_to(lon // chunks, LANES)
    highest = (LANES + lon - lon // chunks + DLON) // LANES
    total = (highest + 1) * LANES + width
    arrays = [fields] + ([] if edge is None else [edge]) + [weight]
    return pl.pallas_call(
        functools.partial(conv_kernel, edge is not None),
        out_shape=[jax.ShapeDtypeStruct((2 * chans, width), jnp.bfloat16)] * chunks,
        in_specs=[SMEM] * 6 + [VMEM] * len(arrays),
        out_specs=[VMEM] * chunks,
        scratch_shapes=[
            pltpu.VMEM((own + HALO, chans, total), jnp.bfloat16),
            pltpu.VMEM((2, TAPS * G, chunks * width), jnp.bfloat16),
            pltpu.VMEM((2, G, TAPS * G), jnp.bfloat16),
        ],
        compiler_params=params(20),
        cost_estimate=takes(4),
        name="conv_rows",
    )(pair, place, *supports, *arrays)


def mlp_kernel(parts, last, me_ref, place_ref, *rest):
    blocks, rest = rest[:parts], rest[parts:]
    up_ref, down_ref, table_ref, *rest = rest
    *rest, cells_ref = rest
    if last:
        earlier_ref, *out_refs, gather_ref = rest
    else:
        (out_ref,) = rest
    width = blocks[0].shape[1]
    place = place_ref[0]
    for k in range(parts):
        source = pl.multiple_of(lax.rem(place - k + parts, parts) * G, G)
        for i in range(2):
            cells_ref[pl.ds(source, G), i * width : (i + 1) * width] = blocks[k][
                i * G : (i + 1) * G, :
            ]
    values = cells_ref[...].astype(jnp.float32)
    center = values - jnp.mean(values, axis=0, keepdims=True)
    spread = jnp.mean(center * center, axis=0, keepdims=True)
    normed = (center * lax.rsqrt(spread + EPS)).astype(jnp.bfloat16)
    lifted = jnp.dot(up_ref[...], normed, preferred_element_type=jnp.float32)
    scale = math.sqrt(2.0 / math.pi)
    inner = lifted * (scale + (scale * 0.044715) * (lifted * lifted))
    half = 0.5 * lifted
    active = (half + half * jnp.tanh(inner)).astype(jnp.bfloat16)
    lowered = jnp.dot(down_ref[...], active, preferred_element_type=jnp.float32)
    result = (values + lowered).astype(jnp.bfloat16)
    found = []
    for i in range(2):
        modes = lax.dot_general(
            table_ref[place],
            result[:, i * width : (i + 1) * width],
            (((1,), (1,)), ((), ())),
            preferred_element_type=jnp.float32,
        )
        found.append(modes.reshape(modes.shape[0] // SLOT, SLOT, modes.shape[1]))
    block = jnp.concatenate(found, axis=1).astype(jnp.bfloat16)
    if not last:
        out_ref[...] = block
        return
    gather_ref[:, 0 : 2 * SLOT, :] = earlier_ref[...]
    gather_ref[:, 2 * SLOT : 4 * SLOT, :] = block
    if len(out_refs) == 1:
        out_refs[0][...] = gather_ref[...]
        return
    dests = len(out_refs)
    for k in range(dests):
        out_refs[k][...] = gather_ref[lax.rem(me_ref[0] + k, dests)]


def mlp_rows(me, place, blocks, up, down, tables, earlier, dests):
    pair_chans, width = blocks[0].shape
    chan = len(blocks) * pair_chans // 2
    last = earlier is not None
    arrays = [*blocks, up, down, tables] + ([earlier] if last else [])
    shape = (dests, 2 * SLOT, chan)
    scratch = []
    if last:
        shape = (dests, 4 * SLOT, chan)
        scratch = [pltpu.VMEM(shape, jnp.bfloat16)]
    outs = jax.ShapeDtypeStruct(shape, jnp.bfloat16)
    out_specs = VMEM
    if last and dests <= FEW:
        outs = [jax.ShapeDtypeStruct(shape[1:], jnp.bfloat16)] * dests
        out_specs = [VMEM] * dests
    return pl.pallas_call(
        functools.partial(mlp_kernel, len(blocks), last),
        out_shape=outs,
        in_specs=[SMEM] * 2 + [VMEM] * len(arrays),
        out_specs=out_specs,
        scratch_shapes=scratch + [pltpu.VMEM((chan, 2 * width), jnp.bfloat16)],
        compiler_params=params(20 if dests <= FEW else 40),
        cost_estimate=takes(3),
        name="mlp_rows",
    )(me, place, *arrays)


def expand_kernel(start_ref, legendre_ref, spread_ref, out_ref):
    _, lats, degrees = legendre_ref.shape
    m = pl.program_id(0)
    degree = lax.broadcasted_iota(jnp.int32, (lats, degrees), 1)
    kept = jnp.where(degree >= start_ref[0] + m, legendre_ref[0].astype(jnp.float32), 0.0)
    wide = lax.dot_general(
        kept.astype(jnp.bfloat16),
        spread_ref[...],
        (((0,), (0,)), ((), ())),
        preferred_element_type=jnp.float32,
    )
    slot = lax.rem(lax.broadcasted_iota(jnp.int32, wide.shape, 1), SLOT)
    for r in range(2):
        out_ref[0, r] = jnp.where(slot == 2 * m + r, wide, 0.0).astype(jnp.bfloat16)


def expand(start, legendre, spread):
    modes, lats, degrees = legendre.shape
    depth = spread.shape[1]
    return pl.pallas_call(
        expand_kernel,
        out_shape=jax.ShapeDtypeStruct((modes, 2, degrees, depth), jnp.bfloat16),
        grid=(modes,),
        in_specs=[
            SMEM,
            pl.BlockSpec((1, lats, degrees), lambda m: (m, 0, 0)),
            pl.BlockSpec((lats, depth), lambda m: (0, 0)),
        ],
        out_specs=pl.BlockSpec((1, 2, degrees, depth), lambda m: (m, 0, 0, 0)),
        compiler_params=params(10 if depth <= 512 else 48),
        cost_estimate=takes(2),
        name="expand",
    )(start, legendre, spread)


def final_kernel(me_ref, left_ref, *rest):
    *blocks, out_ref, spectrum_ref = rest
    depth, chan = spectrum_ref.shape
    count = len(blocks)
    rows = depth // count

    @pl.when(pl.program_id(0) == 0)
    def _():
        for k in range(count):
            source = lax.rem(me_ref[0] - k + count, count) * rows
            spectrum_ref[pl.ds(pl.multiple_of(source, rows), rows), :] = blocks[k][...]

    for r in range(2):
        out_ref[0, :, r * chan : (r + 1) * chan] = jnp.dot(
            left_ref[0, r], spectrum_ref[...], preferred_element_type=jnp.float32
        ).astype(jnp.bfloat16)


def final_sum(me, left, blocks):
    modes, _, degrees, depth = left.shape
    rows, chan = blocks[0].shape
    return pl.pallas_call(
        final_kernel,
        out_shape=jax.ShapeDtypeStruct((modes, degrees, 2 * chan), jnp.bfloat16),
        grid=(modes,),
        in_specs=[SMEM, pl.BlockSpec((1, 2, degrees, depth), lambda m: (m, 0, 0, 0))]
        + [pl.BlockSpec((rows, chan), lambda m: (0, 0))] * len(blocks),
        out_specs=pl.BlockSpec((1, degrees, 2 * chan), lambda m: (m, 0, 0)),
        scratch_shapes=[pltpu.VMEM((depth, chan), jnp.bfloat16)],
        compiler_params=params(10 if depth <= 512 else 48),
        cost_estimate=takes(2),
        name="final_sum",
    )(me, left, *blocks)


def fourier_blocks(lon, chunks, width, dests, mode_dev):
    chunk = lon // chunks
    index = np.arange(lon, dtype=np.int64)
    mode = np.arange(dests * mode_dev, dtype=np.int64)
    angle = ((mode[:, None] * index[None, :]) % lon) * (2.0 * math.pi / lon)
    paired = np.stack([np.cos(angle), -np.sin(angle)], axis=1) * math.sqrt(2.0 / lon)
    paired = paired.reshape(dests, 2 * mode_dev, chunks, chunk)
    table = np.zeros((chunks, dests, SLOT, width), np.float32)
    table[:, :, : 2 * mode_dev, :chunk] = np.transpose(paired, (2, 0, 1, 3))
    return table.reshape(chunks, dests * SLOT, width).astype(jnp.bfloat16)


def turn(block, axis, count, step):
    return lax.ppermute(block, axis, [(i, (i + step) % count) for i in range(count)])


def scalar(value):
    return jnp.asarray(value, jnp.int32).reshape(1)


def on_device(
    fields,
    disco_weight,
    support_lat,
    support_lon,
    support_basis,
    support_value,
    w_up,
    w_down,
    legendre,
):
    lat_dev, lon, _ = fields.shape
    num_lat = lax.axis_size("lat")
    num_chan = lax.axis_size("chan")
    mode_dev, _, lats = legendre.shape
    dests = num_lat * num_chan
    width = ceil_to(lon // num_chan, LANES)
    band = lax.axis_index("lat")
    place = scalar(lax.axis_index("chan"))
    index = lax.axis_index(("lat", "chan"))
    me = scalar(index)
    cells = jnp.swapaxes(fields, 1, 2)
    supports = (support_lat, support_lon, support_basis, support_value)

    two_bands = num_lat == 2
    if two_bands:
        edge_out = lax.dynamic_slice_in_dim(cells, HALO * (1 - band), HALO, axis=0)
        edges = [None, lax.ppermute(edge_out, "lat", [(0, 1), (1, 0)])]
        pairs = [band, 1 - band]
    else:
        ends = num_lat - 1
        edges = [
            lax.ppermute(cells[lat_dev - HALO :], "lat", [(i, i + 1) for i in range(ends)]),
            lax.ppermute(cells[:HALO], "lat", [(i + 1, i) for i in range(ends)]),
        ]
        pairs = [0, 1]

    tables = jnp.asarray(fourier_blocks(lon, num_chan, width, dests, mode_dev))
    up = w_up.T
    down = w_down.T

    depth = dests * 4 * SLOT
    row = np.arange(depth)
    source_band = row // (4 * SLOT) // num_chan
    phase = (row // (2 * SLOT)) % 2
    source_pair = (phase ^ source_band) if two_bands else phase
    lat_of = lat_dev * source_band + 2 * source_pair + (row // SLOT) % 2
    spread = (lat_of[None, :] == np.arange(lats)[:, None]).astype(jnp.bfloat16)
    left = expand(scalar(index * mode_dev), jnp.swapaxes(legendre, 1, 2), jnp.asarray(spread))

    received = []
    for edge, pair in zip(edges, pairs):
        mixed = conv_rows(scalar(pair), place, supports, cells, edge, disco_weight, num_chan)
        received.append(
            [mixed[0]] + [turn(mixed[k], "chan", num_chan, k) for k in range(1, num_chan)]
        )
    spectrum = None
    for blocks in received:
        spectrum = mlp_rows(me, place, blocks, up, down, tables, spectrum, dests)

    both = ("lat", "chan")
    if dests <= FEW:
        blocks = [spectrum[0]] + [turn(spectrum[k], both, dests, k) for k in range(1, dests)]
    else:
        whole = lax.all_to_all(spectrum, both, split_axis=0, concat_axis=0, tiled=True)
        blocks = [whole.reshape(depth, whole.shape[2])]
    return final_sum(me, left, blocks)


def solution(mesh):
    in_specs = (
        P(("tm", "lat"), None, "chan"),
        P(None, "chan", None),
        P("lat", None),
        P("lat", None),
        P("lat", None),
        P("lat", None),
        P(),
        P(),
        P(("lat", "chan"), None, None),
    )
    out_specs = P(("tm", "lat", "chan"), None, None)
    return jax.shard_map(
        on_device, mesh=mesh, in_specs=in_specs, out_specs=out_specs, check_vma=False
    )
```

time: 63.4 us -> 48 us (0.76)
  waiting for transfers between devices: 20.8 us -> 6.76 us
  Pallas kernels: 20.4 us -> 11.1 us
  starting transfers between devices: 16.4 us -> 23.5 us
  local copies, waits for them, and re-layouts: 5.27 us -> 6.09 us
    ppermute x0 -> x13, starting transfers between devices: none -> 20.4 us  [turn(): lax.ppermute(block, axis, [(i, (i + step) % count) for i in range(count)])]
    all_to_all x3 -> x0, starting transfers between devices: 14.8 us -> none  [the longest x2 11.1 us: on_device(): lax.all_to_all(mixed, 'chan', split_axis=0, concat_axis=0, tiled=True)]
    all_to_all x3 -> x0, waiting for transfers between devices: 11.7 us -> none  [the longest x1 7.52 us: on_device(): lax.all_to_all(spectrum, ('lat', 'chan'), split_axis=0, concat_axis=0, ti...]
    pallas_call x5 -> x6, Pallas kernels: 20.4 us -> 11.1 us  [the longest x2 5.94 us: conv_rows(): pl.pallas_call(functools.partial(conv_kernel, edge is not None), out_shap...]
    ppermute x1, waiting for transfers between devices: 9.05 us -> 0.01 us  [on_device(): edges = [None, lax.ppermute(edge_out, 'lat', [(0, 1), (1, 0)])]]
    ppermute x0 -> x13, waiting for transfers between devices: none -> 6.75 us  [turn(): lax.ppermute(block, axis, [(i, (i + step) % count) for i in range(count)])]
    ppermute x1, starting transfers between devices: 1.59 us -> 3.03 us  [on_device(): edges = [None, lax.ppermute(edge_out, 'lat', [(0, 1), (1, 0)])]]
    squeeze x1 -> x0, local copies, waits for them, and re-layouts: 1.42 us -> none  [on_device(): table = lax.dynamic_index_in_dim(tables, place, 0, keepdims=False)]
  transfers between devices with their start and end apart: 4 -> 14, of which waited for: 3 -> 4; matrix products, arithmetic and copies ran while one was open for 5% -> 1% of each run, Pallas kernels for 14% -> 17%
where the time goes in v2:
time: 48 us; the launch traced here: 47.7 us
  starting transfers between devices  23.5 us (49%)
  Pallas kernels  11.1 us (23%)
  waiting for transfers between devices  6.76 us (14%)
  local copies, waits for them, and re-layouts  6.09 us (13%)
    ppermute x13, starting transfers between devices, turn(): lax.ppermute(block, axis, [(i, (i + step) % count) for i in range(count)])  20.4 us
    ppermute x13, waiting for transfers between devices, turn(): lax.ppermute(block, axis, [(i, (i + step) % count) for i in range(count)])  6.75 us
    pallas_call x2, Pallas kernels, conv_rows(): pl.pallas_call(functools.partial(conv_kernel, edge is not None), out_shap...  5.94 us
    unnamed x36, local copies, waits for them, and re-layouts  5.07 us
    ppermute x1, starting transfers between devices, on_device(): edges = [None, lax.ppermute(edge_out, 'lat', [(0, 1), (1, 0)])]  3.03 us
    pallas_call x2, Pallas kernels, mlp_rows(): pl.pallas_call(functools.partial(mlp_kernel, len(blocks), last), out_shap...  2.35 us
    pallas_call x1, Pallas kernels, final_sum(): pl.pallas_call(final_kernel, out_shape=jax.ShapeDtypeStruct((modes, degre...  2.05 us
    dynamic_slice x1, local copies, waits for them, and re-layouts, on_device(): edge_out = lax.dynamic_slice_in_dim(cells, HALO * (1 - band), HALO, axis=0)  1.02 us
  transfers between devices with their start and end apart: 14, of which 4 were waited for; matrix products, arithmetic and copies ran while one was open for 1% of the time, Pallas kernels for 17%

profile of v2, /device:TPU:0, one launch (start us, length us, event | category | flops | bytes accessed | tf_op | source)
XLA Modules:
  0.0 47.7 jit_solution(9604170170113197028)
XLA Ops:
  0.0 1.0 %dynamic-slice_bitcast_fusion = bf16[2,64,1440]{2,1,0:T(8,128)(2,1)S(1)} fusion(bf16[4,1440,64]{1,2,0:T(8,128)(2,1)} %param.11, s32[]{:T(128)S(6)} %select_n.3), kind=kLoop, calls=%fused_computation | loop fusion | bytes 737284 | tf_op jit(solution)/shard_map/dynamic_slice | solution.py:336
  1.0 3.0 %collective-permute-start = (bf16[2,64,1440]{2,1,0:T(8,128)(2,1)S(1)}, bf16[2,64,1440]{2,1,0:T(8,128)(2,1)S(1)}, u32[]{:S(2)}, u32[]{:S(2)}) collective-permute-start(bf16[2,64,1440]{2,1,0:T(8,128)(2,1)S(1)} %dynamic-slice_bitcast_fusion), channel_id=1, source_target_pairs={{0,16},{16,0},{1,17},{17,1},{2,18},{18,2},{3,19},{19,3},{4,20},{20... | collective-permute-start | bytes 1105928 | tf_op jit(solution)/shard_map/ppermute | solution.py:337
  4.1 1.1 %copy-done = bf16[4,1440,64]{1,2,0:T(8,128)(2,1)S(1)} copy-done((bf16[4,1440,64]{1,2,0:T(8,128)(2,1)S(1)}, bf16[4,1440,64]{1,2,0:T(8,128)(2,1)}, u32[]{:S(2)}) %copy-start) | copy-done | bytes 737304
  5.2 0.9 %copy-done.2 = bf16[6,64,64]{2,1,0:T(8,128)(2,1)S(1)} copy-done((bf16[6,64,64]{2,1,0:T(8,128)(2,1)S(1)}, bf16[6,64,64]{2,1,0:T(8,128)(2,1)}, u32[]{:S(2)}) %copy-start.2) | copy-done | bytes 49176
  6.1 0.7 %copy-done.5 = s32[4,9]{1,0:T(4,128)S(1)} copy-done((s32[4,9]{1,0:T(4,128)S(1)}, s32[4,9]{1,0:T(4,128)}, u32[]{:S(2)}) %copy-start.5) | copy-done | bytes 168
  6.8 0.7 %copy-done.7 = s32[4,9]{1,0:T(4,128)S(1)} copy-done((s32[4,9]{1,0:T(4,128)S(1)}, s32[4,9]{1,0:T(4,128)}, u32[]{:S(2)}) %copy-start.7) | copy-done | bytes 168
  7.5 0.7 %copy-done.9 = s32[4,9]{1,0:T(4,128)S(1)} copy-done((s32[4,9]{1,0:T(4,128)S(1)}, s32[4,9]{1,0:T(4,128)}, u32[]{:S(2)}) %copy-start.9) | copy-done | bytes 168
  8.1 0.7 %copy-done.11 = f32[4,9]{1,0:T(4,128)S(1)} copy-done((f32[4,9]{1,0:T(4,128)S(1)}, f32[4,9]{1,0:T(4,128)}, u32[]{:S(2)}) %copy-start.11) | copy-done | bytes 168
  8.9 2.9 %conv_rows.3 = (bf16[128,384]{1,0:T(8,128)(2,1)S(1)}, bf16[128,384]{1,0:T(8,128)(2,1)S(1)}, bf16[128,384]{1,0:T(8,128)(2,1)S(1)}, bf16[128,384]{1,0:T(8,128)(2,1)S(1)}) custom-call(s32[1]{0:T(128)} %bitcast.9.pair_ref, s32[1]{0:T(128)} %bitcast.3.place_ref, s32[4,9]{1,0:T(4,128)S(1)} %copy-done.5, s32[4,9]{1,0:T(4,128)S(1)} %copy-done.7, ...), custom_call_target="tpu_custom_call" | custom-call | flops 4000000000 | tf_op jit(solution)/shard_map/conv_rows/pallas_call | solution.py:127
  11.8 1.6 %collective-permute-start.4 = (bf16[128,384]{1,0:T(8,128)(2,1)S(1)}, bf16[128,384]{1,0:T(8,128)(2,1)S(1)}, u32[]{:S(2)}, u32[]{:S(2)}) collective-permute-start(bf16[128,384]{1,0:T(8,128)(2,1)S(1)} %get-tuple-element.26), channel_id=1, source_target_pairs={{0,4},{4,8},{8,12},{12,0},{1,5},{5,9},{9,13},{13,1},{2,6},{6,10},{... | collective-permute-start | bytes 294920 | tf_op jit(solution)/shard_map/ppermute | solution.py:303
  13.4 2.6 %collective-permute-start.5 = (bf16[128,384]{1,0:T(8,128)(2,1)S(1)}, bf16[128,384]{1,0:T(8,128)(2,1)S(1)}, u32[]{:S(2)}, u32[]{:S(2)}) collective-permute-start(bf16[128,384]{1,0:T(8,128)(2,1)S(1)} %get-tuple-element.27), channel_id=1, source_target_pairs={{0,8},{4,12},{8,0},{12,4},{1,9},{5,13},{9,1},{13,5},{2,10},{6,14},... | collective-permute-start | bytes 294920 | tf_op jit(solution)/shard_map/ppermute | solution.py:303
  16.0 1.3 %collective-permute-start.6 = (bf16[128,384]{1,0:T(8,128)(2,1)S(1)}, bf16[128,384]{1,0:T(8,128)(2,1)S(1)}, u32[]{:S(2)}, u32[]{:S(2)}) collective-permute-start(bf16[128,384]{1,0:T(8,128)(2,1)S(1)} %get-tuple-element.28), channel_id=1, source_target_pairs={{0,12},{4,0},{8,4},{12,8},{1,13},{5,1},{9,5},{13,9},{2,14},{6,2},{... | collective-permute-start | bytes 294920 | tf_op jit(solution)/shard_map/ppermute | solution.py:303
  17.5 0.1 copy.13
  17.8 3.0 %conv_rows.2 = (bf16[128,384]{1,0:T(8,128)(2,1)S(1)}, bf16[128,384]{1,0:T(8,128)(2,1)S(1)}, bf16[128,384]{1,0:T(8,128)(2,1)S(1)}, bf16[128,384]{1,0:T(8,128)(2,1)S(1)}) custom-call(s32[1]{0:T(128)} %bitcast.4.pair_ref, s32[1]{0:T(128)} %bitcast.3.place_ref, s32[4,9]{1,0:T(4,128)S(1)} %copy-done.6, s32[4,9]{1,0:T(4,128)S(1)} %copy-done.8, ...), custom_call_target="tpu_custom_call" | custom-call | flops 4000000000 | tf_op jit(solution)/shard_map/conv_rows/pallas_call | solution.py:127
  20.8 0.7 %collective-permute-start.1 = (bf16[128,384]{1,0:T(8,128)(2,1)S(1)}, bf16[128,384]{1,0:T(8,128)(2,1)S(1)}, u32[]{:S(2)}, u32[]{:S(2)}) collective-permute-start(bf16[128,384]{1,0:T(8,128)(2,1)S(1)} %get-tuple-element.22), channel_id=1, source_target_pairs={{0,4},{4,8},{8,12},{12,0},{1,5},{5,9},{9,13},{13,1},{2,6},{6,10},{... | collective-permute-start | bytes 294920 | tf_op jit(solution)/shard_map/ppermute | solution.py:303
  21.5 0.3 collective-permute-start.2
  21.8 2.8 %collective-permute-start.3 = (bf16[128,384]{1,0:T(8,128)(2,1)S(1)}, bf16[128,384]{1,0:T(8,128)(2,1)S(1)}, u32[]{:S(2)}, u32[]{:S(2)}) collective-permute-start(bf16[128,384]{1,0:T(8,128)(2,1)S(1)} %get-tuple-element.24), channel_id=1, source_target_pairs={{0,12},{4,0},{8,4},{12,8},{1,13},{5,1},{9,5},{13,9},{2,14},{6,2},{... | collective-permute-start | bytes 294920 | tf_op jit(solution)/shard_map/ppermute | solution.py:303
  24.7 1.2 %mlp_rows.2.rest_7_ = bf16[8,16,256]{2,1,0:T(8,128)(2,1)S(1)} custom-call(s32[1]{0:T(128)} %bitcast.me_ref, s32[1]{0:T(128)} %bitcast.3.place_ref, bf16[128,384]{1,0:T(8,128)(2,1)S(1)} %get-tuple-element.25.rest_0_, bf16[128,384]{1,0:T(8,128)(2,1)S(1)} %collective-permute-done.4.rest_1_, bf16[128,384]{1,0:T(8,128)(2,1)S(1)} %collective-permute-done.5.rest_2_, ...), custom_call_target="tpu_custom_call" | custom-call | flops 3000000000 | tf_op jit(solution)/shard_map/mlp_rows/pallas_call | solution.py:208
  25.8 2.4 %collective-permute-done.1.rest_1_ = bf16[128,384]{1,0:T(8,128)(2,1)S(1)} collective-permute-done((bf16[128,384]{1,0:T(8,128)(2,1)S(1)}, bf16[128,384]{1,0:T(8,128)(2,1)S(1)}, u32[]{:S(2)}, u32[]{:S(2)}) %collective-permute-start.1) | collective-permute-done | bytes 98336 | tf_op jit(solution)/shard_map/ppermute | solution.py:303
  28.2 2.7 %collective-permute-done.2.rest_2_ = bf16[128,384]{1,0:T(8,128)(2,1)S(1)} collective-permute-done((bf16[128,384]{1,0:T(8,128)(2,1)S(1)}, bf16[128,384]{1,0:T(8,128)(2,1)S(1)}, u32[]{:S(2)}, u32[]{:S(2)}) %collective-permute-start.2) | collective-permute-done | bytes 98336 | tf_op jit(solution)/shard_map/ppermute | solution.py:303
  30.9 1.2 %mlp_rows.3 = (bf16[32,256]{1,0:T(8,128)(2,1)S(1)}, bf16[32,256]{1,0:T(8,128)(2,1)S(1)}, bf16[32,256]{1,0:T(8,128)(2,1)S(1)}, bf16[32,256]{1,0:T(8,128)(2,1)S(1)...) custom-call(s32[1]{0:T(128)} %bitcast.me_ref, ...), custom_call_target="tpu_custom_call" | custom-call | flops 3000000000 | tf_op jit(solution)/shard_map/mlp_rows/pallas_call | solution.py:208
  32.1 2.4 %collective-permute-start.7 = (bf16[32,256]{1,0:T(8,128)(2,1)S(1)}, bf16[32,256]{1,0:T(8,128)(2,1)S(1)}, u32[]{:S(2)}, u32[]{:S(2)}) collective-permute-start(bf16[32,256]{1,0:T(8,128)(2,1)S(1)} %get-tuple-element.30), channel_id=1, source_target_pairs={{0,4},{4,8},{8,12},{12,16},{16,20},{20,24},{24,28},{28,0},{1,5},{5... | collective-permute-start | bytes 49160 | tf_op jit(solution)/shard_map/ppermute | solution.py:303
  34.5 1.7 %collective-permute-start.8 = (bf16[32,256]{1,0:T(8,128)(2,1)S(1)}, bf16[32,256]{1,0:T(8,128)(2,1)S(1)}, u32[]{:S(2)}, u32[]{:S(2)}) collective-permute-start(bf16[32,256]{1,0:T(8,128)(2,1)S(1)} %get-tuple-element.31), channel_id=1, source_target_pairs={{0,8},{4,12},{8,16},{12,20},{16,24},{20,28},{24,0},{28,4},{1,9},{5... | collective-permute-start | bytes 49160 | tf_op jit(solution)/shard_map/ppermute | solution.py:303
  36.3 0.7 %collective-permute-start.9 = (bf16[32,256]{1,0:T(8,128)(2,1)S(1)}, bf16[32,256]{1,0:T(8,128)(2,1)S(1)}, u32[]{:S(2)}, u32[]{:S(2)}) collective-permute-start(bf16[32,256]{1,0:T(8,128)(2,1)S(1)} %get-tuple-element.32), channel_id=1, source_target_pairs={{0,12},{4,16},{8,20},{12,24},{16,28},{20,0},{24,4},{28,8},{1,13},{... | collective-permute-start | bytes 49160 | tf_op jit(solution)/shard_map/ppermute | solution.py:303
  37.0 1.5 %collective-permute-start.10 = (bf16[32,256]{1,0:T(8,128)(2,1)S(1)}, bf16[32,256]{1,0:T(8,128)(2,1)S(1)}, u32[]{:S(2)}, u32[]{:S(2)}) collective-permute-start(bf16[32,256]{1,0:T(8,128)(2,1)S(1)} %get-tuple-element.33), channel_id=1, source_target_pairs={{0,16},{4,20},{8,24},{12,28},{16,0},{20,4},{24,8},{28,12},{1,17},{... | collective-permute-start | bytes 49160 | tf_op jit(solution)/shard_map/ppermute | solution.py:303
  38.4 1.3 %collective-permute-start.11 = (bf16[32,256]{1,0:T(8,128)(2,1)S(1)}, bf16[32,256]{1,0:T(8,128)(2,1)S(1)}, u32[]{:S(2)}, u32[]{:S(2)}) collective-permute-start(bf16[32,256]{1,0:T(8,128)(2,1)S(1)} %get-tuple-element.34), channel_id=1, source_target_pairs={{0,20},{4,24},{8,28},{12,0},{16,4},{20,8},{24,12},{28,16},{1,21},{... | collective-permute-start | bytes 49160 | tf_op jit(solution)/shard_map/ppermute | solution.py:303
  39.7 2.2 %collective-permute-start.12 = (bf16[32,256]{1,0:T(8,128)(2,1)S(1)}, bf16[32,256]{1,0:T(8,128)(2,1)S(1)}, u32[]{:S(2)}, u32[]{:S(2)}) collective-permute-start(bf16[32,256]{1,0:T(8,128)(2,1)S(1)} %get-tuple-element.35), channel_id=1, source_target_pairs={{0,24},{4,28},{8,0},{12,4},{16,8},{20,12},{24,16},{28,20},{1,25},{... | collective-permute-start | bytes 49160 | tf_op jit(solution)/shard_map/ppermute | solution.py:303
  41.9 1.3 %collective-permute-start.13 = (bf16[32,256]{1,0:T(8,128)(2,1)S(1)}, bf16[32,256]{1,0:T(8,128)(2,1)S(1)}, u32[]{:S(2)}, u32[]{:S(2)}) collective-permute-start(bf16[32,256]{1,0:T(8,128)(2,1)S(1)} %get-tuple-element.36), channel_id=1, source_target_pairs={{0,28},{4,0},{8,4},{12,8},{16,12},{20,16},{24,20},{28,24},{1,29},{... | collective-permute-start | bytes 49160 | tf_op jit(solution)/shard_map/ppermute | solution.py:303
  43.1 0.8 %expand.1.left_ref = bf16[3,2,384,256]{3,2,1,0:T(8,128)(2,1)S(1)} custom-call(s32[1]{0:T(128)} %bitcast.1.start_ref, bf16[3,8,384]{2,1,0:T(8,128)(2,1)S(1)} %bitcast.17, bf16[8,256]{1,0:T(8,128)(2,1)S(1)} %copy-done.14), custom_call_target="tpu_custom_call" | custom-call | flops 2000000000 | tf_op jit(solution)/shard_map/expand/pallas_call | solution.py:239
  44.0 0.4 collective-permute-done.12.rest_6_
  44.3 1.3 %collective-permute-done.13.rest_7_ = bf16[32,256]{1,0:T(8,128)(2,1)S(1)} collective-permute-done((bf16[32,256]{1,0:T(8,128)(2,1)S(1)}, bf16[32,256]{1,0:T(8,128)(2,1)S(1)}, u32[]{:S(2)}, u32[]{:S(2)}) %collective-permute-start.13) | collective-permute-done | bytes 16416 | tf_op jit(solution)/shard_map/ppermute | solution.py:303
  45.6 2.1 %final_sum.1 = bf16[3,384,512]{2,1,0:T(8,128)(2,1)} custom-call(s32[1]{0:T(128)} %bitcast.me_ref, bf16[3,2,384,256]{3,2,1,0:T(8,128)(2,1)S(1)} %expand.1.left_ref, bf16[32,256]{1,0:T(8,128)(2,1)S(1)} %get-tuple-element.29.rest_0_, bf16[32,256]{1,0:T(8,128)(2,1)S(1)} %collective-permute-done.7.rest_1_, bf16[32,256]{1,0:T(8,128)(2,1)S(1)} %collective-permute-done.8.rest_2_, ...), custom_call_target="tpu_custom_call" | custom-call | flops 2000000000 | tf_op jit(solution)/shard_map/final_sum/pallas_call | solution.py:276
  (39 shorter events, 0.2 us)
Async XLA Ops:
  1.0 16.7 %collective-permute-start = (bf16[2,64,1440]{2,1,0:T(8,128)(2,1)S(1)}, bf16[2,64,1440]{2,1,0:T(8,128)(2,1)S(1)}, u32[]{:S(2)}, u32[]{:S(2)}) collective-permute-start(bf16[2,64,1440]{2,1,0:T(8,128)(2,1)S(1)} %dynamic-slice_bitcast_fusion), channel_id=1, source_target_pairs={{0,16},{16,0},{1,17},{17,1},{2,18},{18,2},{3,19},{19,3},{4,20},{20... | collective-permute-start | bytes 1105928 | tf_op jit(solution)/shard_map/ppermute | solution.py:337
  4.1 1.1 %copy-start = (bf16[4,1440,64]{1,2,0:T(8,128)(2,1)S(1)}, bf16[4,1440,64]{1,2,0:T(8,128)(2,1)}, u32[]{:S(2)}) copy-start(bf16[4,1440,64]{1,2,0:T(8,128)(2,1)} %param.11) | copy-start | bytes 2211844
  5.2 0.9 %copy-start.2 = (bf16[6,64,64]{2,1,0:T(8,128)(2,1)S(1)}, bf16[6,64,64]{2,1,0:T(8,128)(2,1)}, u32[]{:S(2)}) copy-start(bf16[6,64,64]{2,1,0:T(8,128)(2,1)} %rest_0_.1) | copy-start | bytes 147460
  6.1 0.7 %copy-start.5 = (s32[4,9]{1,0:T(4,128)S(1)}, s32[4,9]{1,0:T(4,128)}, u32[]{:S(2)}) copy-start(s32[4,9]{1,0:T(4,128)} %lat_ref.3) | copy-start | bytes 436
  6.8 0.7 %copy-start.7 = (s32[4,9]{1,0:T(4,128)S(1)}, s32[4,9]{1,0:T(4,128)}, u32[]{:S(2)}) copy-start(s32[4,9]{1,0:T(4,128)} %lon_ref.3) | copy-start | bytes 436
  7.4 0.7 %copy-start.9 = (s32[4,9]{1,0:T(4,128)S(1)}, s32[4,9]{1,0:T(4,128)}, u32[]{:S(2)}) copy-start(s32[4,9]{1,0:T(4,128)} %basis_ref.3) | copy-start | bytes 436
  8.1 0.7 %copy-start.11 = (f32[4,9]{1,0:T(4,128)S(1)}, f32[4,9]{1,0:T(4,128)}, u32[]{:S(2)}) copy-start(f32[4,9]{1,0:T(4,128)} %value_ref.3) | copy-start | bytes 436
  8.8 8.6 %copy-start.15 = (bf16[256,512]{1,0:T(8,128)(2,1)S(1)}, bf16[256,512]{1,0:T(8,128)(2,1)}, u32[]{:S(2)}) copy-start(bf16[256,512]{1,0:T(8,128)(2,1)} %param.17) | copy-start | bytes 786436
  8.8 8.7 %copy-start.16 = (bf16[512,256]{1,0:T(8,128)(2,1)S(1)}, bf16[512,256]{1,0:T(8,128)(2,1)}, u32[]{:S(2)}) copy-start(bf16[512,256]{1,0:T(8,128)(2,1)} %param.18) | copy-start | bytes 786436
  8.8 8.9 %copy-start.1 = (bf16[4,1440,64]{1,2,0:T(8,128)(2,1)S(1)}, bf16[4,1440,64]{1,2,0:T(8,128)(2,1)}, u32[]{:S(2)}) copy-start(bf16[4,1440,64]{1,2,0:T(8,128)(2,1)} %param.11) | copy-start | bytes 2211844
  8.8 8.9 %copy-start.3 = (bf16[6,64,64]{2,1,0:T(8,128)(2,1)S(1)}, bf16[6,64,64]{2,1,0:T(8,128)(2,1)}, u32[]{:S(2)}) copy-start(bf16[6,64,64]{2,1,0:T(8,128)(2,1)} %rest_0_.1) | copy-start | bytes 147460
  8.8 8.9 %copy-start.6 = (s32[4,9]{1,0:T(4,128)S(1)}, s32[4,9]{1,0:T(4,128)}, u32[]{:S(2)}) copy-start(s32[4,9]{1,0:T(4,128)} %lat_ref.3) | copy-start | bytes 436
  8.8 8.9 %copy-start.8 = (s32[4,9]{1,0:T(4,128)S(1)}, s32[4,9]{1,0:T(4,128)}, u32[]{:S(2)}) copy-start(s32[4,9]{1,0:T(4,128)} %lon_ref.3) | copy-start | bytes 436
  8.8 8.9 %copy-start.10 = (s32[4,9]{1,0:T(4,128)S(1)}, s32[4,9]{1,0:T(4,128)}, u32[]{:S(2)}) copy-start(s32[4,9]{1,0:T(4,128)} %basis_ref.3) | copy-start | bytes 436
  8.9 8.9 %copy-start.12 = (f32[4,9]{1,0:T(4,128)S(1)}, f32[4,9]{1,0:T(4,128)}, u32[]{:S(2)}) copy-start(f32[4,9]{1,0:T(4,128)} %value_ref.3) | copy-start | bytes 436
  11.8 10.0 %collective-permute-start.4 = (bf16[128,384]{1,0:T(8,128)(2,1)S(1)}, bf16[128,384]{1,0:T(8,128)(2,1)S(1)}, u32[]{:S(2)}, u32[]{:S(2)}) collective-permute-start(bf16[128,384]{1,0:T(8,128)(2,1)S(1)} %get-tuple-element.26), channel_id=1, source_target_pairs={{0,4},{4,8},{8,12},{12,0},{1,5},{5,9},{9,13},{13,1},{2,6},{6,10},{... | collective-permute-start | bytes 294920 | tf_op jit(solution)/shard_map/ppermute | solution.py:303
  13.4 11.2 %collective-permute-start.5 = (bf16[128,384]{1,0:T(8,128)(2,1)S(1)}, bf16[128,384]{1,0:T(8,128)(2,1)S(1)}, u32[]{:S(2)}, u32[]{:S(2)}) collective-permute-start(bf16[128,384]{1,0:T(8,128)(2,1)S(1)} %get-tuple-element.27), channel_id=1, source_target_pairs={{0,8},{4,12},{8,0},{12,4},{1,9},{5,13},{9,1},{13,5},{2,10},{6,14},... | collective-permute-start | bytes 294920 | tf_op jit(solution)/shard_map/ppermute | solution.py:303
  16.0 8.6 %collective-permute-start.6 = (bf16[128,384]{1,0:T(8,128)(2,1)S(1)}, bf16[128,384]{1,0:T(8,128)(2,1)S(1)}, u32[]{:S(2)}, u32[]{:S(2)}) collective-permute-start(bf16[128,384]{1,0:T(8,128)(2,1)S(1)} %get-tuple-element.28), channel_id=1, source_target_pairs={{0,12},{4,0},{8,4},{12,8},{1,13},{5,1},{9,5},{13,9},{2,14},{6,2},{... | collective-permute-start | bytes 294920 | tf_op jit(solution)/shard_map/ppermute | solution.py:303
  17.7 6.9 %copy-start.13 = (bf16[4,64,384]{2,1,0:T(8,128)(2,1)S(1)}, bf16[4,64,384]{2,1,0:T(8,128)(2,1)}, u32[]{:S(2)}) copy-start(bf16[4,64,384]{2,1,0:T(8,128)(2,1)} %constant.25.clone.rest_6_) | copy-start | bytes 589828
  20.8 7.5 %collective-permute-start.1 = (bf16[128,384]{1,0:T(8,128)(2,1)S(1)}, bf16[128,384]{1,0:T(8,128)(2,1)S(1)}, u32[]{:S(2)}, u32[]{:S(2)}) collective-permute-start(bf16[128,384]{1,0:T(8,128)(2,1)S(1)} %get-tuple-element.22), channel_id=1, source_target_pairs={{0,4},{4,8},{8,12},{12,0},{1,5},{5,9},{9,13},{13,1},{2,6},{6,10},{... | collective-permute-start | bytes 294920 | tf_op jit(solution)/shard_map/ppermute | solution.py:303
  21.5 9.4 %collective-permute-start.2 = (bf16[128,384]{1,0:T(8,128)(2,1)S(1)}, bf16[128,384]{1,0:T(8,128)(2,1)S(1)}, u32[]{:S(2)}, u32[]{:S(2)}) collective-permute-start(bf16[128,384]{1,0:T(8,128)(2,1)S(1)} %get-tuple-element.23), channel_id=1, source_target_pairs={{0,8},{4,12},{8,0},{12,4},{1,9},{5,13},{9,1},{13,5},{2,10},{6,14},... | collective-permute-start | bytes 294920 | tf_op jit(solution)/shard_map/ppermute | solution.py:303
  21.8 9.1 %collective-permute-start.3 = (bf16[128,384]{1,0:T(8,128)(2,1)S(1)}, bf16[128,384]{1,0:T(8,128)(2,1)S(1)}, u32[]{:S(2)}, u32[]{:S(2)}) collective-permute-start(bf16[128,384]{1,0:T(8,128)(2,1)S(1)} %get-tuple-element.24), channel_id=1, source_target_pairs={{0,12},{4,0},{8,4},{12,8},{1,13},{5,1},{9,5},{13,9},{2,14},{6,2},{... | collective-permute-start | bytes 294920 | tf_op jit(solution)/shard_map/ppermute | solution.py:303
  30.9 12.2 %copy-start.4 = (bf16[3,384,8]{1,2,0:T(8,128)(2,1)S(1)}, bf16[3,384,8]{1,2,0:T(8,128)(2,1)}, u32[]{:S(2)}) copy-start(bf16[3,384,8]{1,2,0:T(8,128)(2,1)} %param.19) | copy-start | bytes 55300
  30.9 12.2 %copy-start.14 = (bf16[8,256]{1,0:T(8,128)(2,1)S(1)}, bf16[8,256]{1,0:T(8,128)(2,1)}, u32[]{:S(2)}) copy-start(bf16[8,256]{1,0:T(8,128)(2,1)} %constant.26.clone.spread_ref) | copy-start | bytes 12292
  32.1 7.6 %collective-permute-start.7 = (bf16[32,256]{1,0:T(8,128)(2,1)S(1)}, bf16[32,256]{1,0:T(8,128)(2,1)S(1)}, u32[]{:S(2)}, u32[]{:S(2)}) collective-permute-start(bf16[32,256]{1,0:T(8,128)(2,1)S(1)} %get-tuple-element.30), channel_id=1, source_target_pairs={{0,4},{4,8},{8,12},{12,16},{16,20},{20,24},{24,28},{28,0},{1,5},{5... | collective-permute-start | bytes 49160 | tf_op jit(solution)/shard_map/ppermute | solution.py:303
  34.5 7.3 %collective-permute-start.8 = (bf16[32,256]{1,0:T(8,128)(2,1)S(1)}, bf16[32,256]{1,0:T(8,128)(2,1)S(1)}, u32[]{:S(2)}, u32[]{:S(2)}) collective-permute-start(bf16[32,256]{1,0:T(8,128)(2,1)S(1)} %get-tuple-element.31), channel_id=1, source_target_pairs={{0,8},{4,12},{8,16},{12,20},{16,24},{20,28},{24,0},{28,4},{1,9},{5... | collective-permute-start | bytes 49160 | tf_op jit(solution)/shard_map/ppermute | solution.py:303
  36.3 7.7 %collective-permute-start.9 = (bf16[32,256]{1,0:T(8,128)(2,1)S(1)}, bf16[32,256]{1,0:T(8,128)(2,1)S(1)}, u32[]{:S(2)}, u32[]{:S(2)}) collective-permute-start(bf16[32,256]{1,0:T(8,128)(2,1)S(1)} %get-tuple-element.32), channel_id=1, source_target_pairs={{0,12},{4,16},{8,20},{12,24},{16,28},{20,0},{24,4},{28,8},{1,13},{... | collective-permute-start | bytes 49160 | tf_op jit(solution)/shard_map/ppermute | solution.py:303
  37.0 7.0 %collective-permute-start.10 = (bf16[32,256]{1,0:T(8,128)(2,1)S(1)}, bf16[32,256]{1,0:T(8,128)(2,1)S(1)}, u32[]{:S(2)}, u32[]{:S(2)}) collective-permute-start(bf16[32,256]{1,0:T(8,128)(2,1)S(1)} %get-tuple-element.33), channel_id=1, source_target_pairs={{0,16},{4,20},{8,24},{12,28},{16,0},{20,4},{24,8},{28,12},{1,17},{... | collective-permute-start | bytes 49160 | tf_op jit(solution)/shard_map/ppermute | solution.py:303
  38.4 5.5 %collective-permute-start.11 = (bf16[32,256]{1,0:T(8,128)(2,1)S(1)}, bf16[32,256]{1,0:T(8,128)(2,1)S(1)}, u32[]{:S(2)}, u32[]{:S(2)}) collective-permute-start(bf16[32,256]{1,0:T(8,128)(2,1)S(1)} %get-tuple-element.34), channel_id=1, source_target_pairs={{0,20},{4,24},{8,28},{12,0},{16,4},{20,8},{24,12},{28,16},{1,21},{... | collective-permute-start | bytes 49160 | tf_op jit(solution)/shard_map/ppermute | solution.py:303
  39.7 4.6 %collective-permute-start.12 = (bf16[32,256]{1,0:T(8,128)(2,1)S(1)}, bf16[32,256]{1,0:T(8,128)(2,1)S(1)}, u32[]{:S(2)}, u32[]{:S(2)}) collective-permute-start(bf16[32,256]{1,0:T(8,128)(2,1)S(1)} %get-tuple-element.35), channel_id=1, source_target_pairs={{0,24},{4,28},{8,0},{12,4},{16,8},{20,12},{24,16},{28,20},{1,25},{... | collective-permute-start | bytes 49160 | tf_op jit(solution)/shard_map/ppermute | solution.py:303
  41.9 3.7 %collective-permute-start.13 = (bf16[32,256]{1,0:T(8,128)(2,1)S(1)}, bf16[32,256]{1,0:T(8,128)(2,1)S(1)}, u32[]{:S(2)}, u32[]{:S(2)}) collective-permute-start(bf16[32,256]{1,0:T(8,128)(2,1)S(1)} %get-tuple-element.36), channel_id=1, source_target_pairs={{0,28},{4,0},{8,4},{12,8},{16,12},{20,16},{24,20},{28,24},{1,29},{... | collective-permute-start | bytes 49160 | tf_op jit(solution)/shard_map/ppermute | solution.py:303

commit v3 on v2

--- a/solution.py
+++ b/solution.py
@@ -23,6 +23,7 @@
 
 SMEM = pl.BlockSpec(memory_space=pltpu.SMEM)
 VMEM = pl.BlockSpec(memory_space=pltpu.VMEM)
+HBM = pl.BlockSpec(memory_space=pltpu.HBM)
 
 
 def ceil_to(value, step):
@@ -134,20 +135,19 @@
             pltpu.VMEM((2, TAPS * G, chunks * width), jnp.bfloat16),
             pltpu.VMEM((2, G, TAPS * G), jnp.bfloat16),
         ],
-        compiler_params=params(20),
+        compiler_params=params(56 if edge is None else 20),
         cost_estimate=takes(4),
         name="conv_rows",
     )(pair, place, *supports, *arrays)
 
 
-def mlp_kernel(parts, last, me_ref, place_ref, *rest):
+def mlp_kernel(parts, last, place_ref, *rest):
     blocks, rest = rest[:parts], rest[parts:]
     up_ref, down_ref, table_ref, *rest = rest
-    *rest, cells_ref = rest
     if last:
-        earlier_ref, *out_refs, gather_ref = rest
+        earlier_ref, out_ref, cells_ref = rest
     else:
-        (out_ref,) = rest
+        out_ref, cells_ref = rest
     width = blocks[0].shape[1]
     place = place_ref[0]
     for k in range(parts):
@@ -177,44 +177,29 @@
         )
         found.append(modes.reshape(modes.shape[0] // SLOT, SLOT, modes.shape[1]))
     block = jnp.concatenate(found, axis=1).astype(jnp.bfloat16)
-    if not last:
+    if last:
+        out_ref[:, 0 : 2 * SLOT, :] = earlier_ref[...]
+        out_ref[:, 2 * SLOT : 4 * SLOT, :] = block
+    else:
         out_ref[...] = block
-        return
-    gather_ref[:, 0 : 2 * SLOT, :] = earlier_ref[...]
-    gather_ref[:, 2 * SLOT : 4 * SLOT, :] = block
-    if len(out_refs) == 1:
-        out_refs[0][...] = gather_ref[...]
-        return
-    dests = len(out_refs)
-    for k in range(dests):
-        out_refs[k][...] = gather_ref[lax.rem(me_ref[0] + k, dests)]
-
-
-def mlp_rows(me, place, blocks, up, down, tables, earlier, dests):
+
+
+def mlp_rows(place, blocks, up, down, tables, earlier, dests):
     pair_chans, width = blocks[0].shape
     chan = len(blocks) * pair_chans // 2
     last = earlier is not None
     arrays = [*blocks, up, down, tables] + ([earlier] if last else [])
-    shape = (dests, 2 * SLOT, chan)
-    scratch = []
-    if last:
-        shape = (dests, 4 * SLOT, chan)
-        scratch = [pltpu.VMEM(shape, jnp.bfloat16)]
-    outs = jax.ShapeDtypeStruct(shape, jnp.bfloat16)
-    out_specs = VMEM
-    if last and dests <= FEW:
-        outs = [jax.ShapeDtypeStruct(shape[1:], jnp.bfloat16)] * dests
-        out_specs = [VMEM] * dests
+    rows = (4 if last else 2) * SLOT
     return pl.pallas_call(
         functools.partial(mlp_kernel, len(blocks), last),
-        out_shape=outs,
-        in_specs=[SMEM] * 2 + [VMEM] * len(arrays),
-        out_specs=out_specs,
-        scratch_shapes=scratch + [pltpu.VMEM((chan, 2 * width), jnp.bfloat16)],
+        out_shape=jax.ShapeDtypeStruct((dests, rows, chan), jnp.bfloat16),
+        in_specs=[SMEM] + [VMEM] * len(arrays),
+        out_specs=VMEM,
+        scratch_shapes=[pltpu.VMEM((chan, 2 * width), jnp.bfloat16)],
         compiler_params=params(20 if dests <= FEW else 40),
-        cost_estimate=takes(3),
+        cost_estimate=takes(2),
         name="mlp_rows",
-    )(me, place, *arrays)
+    )(place, *arrays)
 
 
 def expand_kernel(start_ref, legendre_ref, spread_ref, out_ref):
@@ -252,39 +237,34 @@
     )(start, legendre, spread)
 
 
-def final_kernel(me_ref, left_ref, *rest):
-    *blocks, out_ref, spectrum_ref = rest
-    depth, chan = spectrum_ref.shape
-    count = len(blocks)
-    rows = depth // count
-
-    @pl.when(pl.program_id(0) == 0)
-    def _():
-        for k in range(count):
-            source = lax.rem(me_ref[0] - k + count, count) * rows
-            spectrum_ref[pl.ds(pl.multiple_of(source, rows), rows), :] = blocks[k][...]
-
-    for r in range(2):
-        out_ref[0, :, r * chan : (r + 1) * chan] = jnp.dot(
-            left_ref[0, r], spectrum_ref[...], preferred_element_type=jnp.float32
-        ).astype(jnp.bfloat16)
-
-
-def final_sum(me, left, blocks):
+def final_kernel(left_ref, spectrum_ref, out_ref, result_ref, sems):
+    modes = left_ref.shape[0]
+    chan = spectrum_ref.shape[1]
+    copies = []
+    for m in range(modes):
+        for r in range(2):
+            result_ref[m, :, r * chan : (r + 1) * chan] = jnp.dot(
+                left_ref[m, r], spectrum_ref[...], preferred_element_type=jnp.float32
+            ).astype(jnp.bfloat16)
+        copies.append(pltpu.make_async_copy(result_ref.at[m], out_ref.at[m], sems.at[m]))
+        copies[-1].start()
+    for copy in copies:
+        copy.wait()
+
+
+def final_sum(left, spectrum):
     modes, _, degrees, depth = left.shape
-    rows, chan = blocks[0].shape
+    shape = (modes, degrees, 2 * spectrum.shape[1])
     return pl.pallas_call(
         final_kernel,
-        out_shape=jax.ShapeDtypeStruct((modes, degrees, 2 * chan), jnp.bfloat16),
-        grid=(modes,),
-        in_specs=[SMEM, pl.BlockSpec((1, 2, degrees, depth), lambda m: (m, 0, 0, 0))]
-        + [pl.BlockSpec((rows, chan), lambda m: (0, 0))] * len(blocks),
-        out_specs=pl.BlockSpec((1, degrees, 2 * chan), lambda m: (m, 0, 0)),
-        scratch_shapes=[pltpu.VMEM((depth, chan), jnp.bfloat16)],
-        compiler_params=params(10 if depth <= 512 else 48),
-        cost_estimate=takes(2),
+        out_shape=jax.ShapeDtypeStruct(shape, jnp.bfloat16),
+        in_specs=[VMEM, VMEM],
+        out_specs=HBM,
+        scratch_shapes=[pltpu.VMEM(shape, jnp.bfloat16), pltpu.SemaphoreType.DMA((modes,))],
+        compiler_params=params(8 if depth <= 512 else 48),
+        cost_estimate=takes(1),
         name="final_sum",
-    )(me, left, *blocks)
+    )(left, spectrum)
 
 
 def fourier_blocks(lon, chunks, width, dests, mode_dev):
@@ -327,11 +307,10 @@
     band = lax.axis_index("lat")
     place = scalar(lax.axis_index("chan"))
     index = lax.axis_index(("lat", "chan"))
-    me = scalar(index)
+    supports = (support_lat, support_lon, support_basis, support_value)
+
+    two_bands = num_lat == 2
     cells = jnp.swapaxes(fields, 1, 2)
-    supports = (support_lat, support_lon, support_basis, support_value)
-
-    two_bands = num_lat == 2
     if two_bands:
         edge_out = lax.dynamic_slice_in_dim(cells, HALO * (1 - band), HALO, axis=0)
         edges = [None, lax.ppermute(edge_out, "lat", [(0, 1), (1, 0)])]
@@ -365,15 +344,11 @@
         )
     spectrum = None
     for blocks in received:
-        spectrum = mlp_rows(me, place, blocks, up, down, tables, spectrum, dests)
+        spectrum = mlp_rows(place, blocks, up, down, tables, spectrum, dests)
 
     both = ("lat", "chan")
-    if dests <= FEW:
-        blocks = [spectrum[0]] + [turn(spectrum[k], both, dests, k) for k in range(1, dests)]
-    else:
-        whole = lax.all_to_all(spectrum, both, split_axis=0, concat_axis=0, tiled=True)
-        blocks = [whole.reshape(depth, whole.shape[2])]
-    return final_sum(me, left, blocks)
+    gathered = lax.all_to_all(spectrum, both, split_axis=0, concat_axis=0, tiled=True)
+    return final_sum(left, gathered.reshape(depth, gathered.shape[2]))
 
 
 def solution(mesh):

time: 48 us -> 43.2 us (0.900)
  starting transfers between devices: 23.5 us -> 18.1 us
  local copies, waits for them, and re-layouts: 6.09 us -> 1.35 us
  waiting for transfers between devices: 6.76 us -> 11 us
  Pallas kernels: 11.1 us -> 12.3 us
    ppermute x13 -> x6, starting transfers between devices: 20.4 us -> 10.3 us  [turn(): lax.ppermute(block, axis, [(i, (i + step) % count) for i in range(count)])]
    all_to_all x0 -> x1, waiting for transfers between devices: none -> 6.68 us  [on_device(): lax.all_to_all(spectrum, both, split_axis=0, concat_axis=0, tiled=True)]
    unnamed x36 -> x26, local copies, waits for them, and re-layouts: 5.07 us -> 0.33 us
    all_to_all x0 -> x1, starting transfers between devices: none -> 4.73 us  [on_device(): lax.all_to_all(spectrum, both, split_axis=0, concat_axis=0, tiled=True)]
    ppermute x13 -> x6, waiting for transfers between devices: 6.75 us -> 4.36 us  [turn(): lax.ppermute(block, axis, [(i, (i + step) % count) for i in range(count)])]
    pallas_call x2, Pallas kernels: 5.94 us -> 7.17 us  [conv_rows(): pl.pallas_call(functools.partial(conv_kernel, edge is not None), out_shap...]
    pallas_call x1, Pallas kernels: 2.05 us -> 1.3 us  [final_sum(): pl.pallas_call(final_kernel, out_shape=jax.ShapeDtypeStruct(shape, jnp.bf...]
    pallas_call x2, Pallas kernels: 2.35 us -> 2.99 us  [mlp_rows(): pl.pallas_call(functools.partial(mlp_kernel, len(blocks), last), out_shap...]
  transfers between devices with their start and end apart: 14 -> 8, of which waited for: 4 -> 3; matrix products, arithmetic and copies ran while one was open for 1% -> 1% of each run, Pallas kernels for 17% -> 21%
where the time goes in v3:
time: 43.2 us; the launch traced here: 42.9 us
  starting transfers between devices  18.1 us (42%)
  Pallas kernels  12.3 us (28%)
  waiting for transfers between devices  11 us (25%)
  local copies, waits for them, and re-layouts  1.35 us (3%)
    ppermute x6, starting transfers between devices, turn(): lax.ppermute(block, axis, [(i, (i + step) % count) for i in range(count)])  10.3 us
    pallas_call x2, Pallas kernels, conv_rows(): pl.pallas_call(functools.partial(conv_kernel, edge is not None), out_shap...  7.17 us
    all_to_all x1, waiting for transfers between devices, on_device(): lax.all_to_all(spectrum, both, split_axis=0, concat_axis=0, tiled=True)  6.68 us
    all_to_all x1, starting transfers between devices, on_device(): lax.all_to_all(spectrum, both, split_axis=0, concat_axis=0, tiled=True)  4.73 us
    ppermute x6, waiting for transfers between devices, turn(): lax.ppermute(block, axis, [(i, (i + step) % count) for i in range(count)])  4.36 us
    ppermute x1, starting transfers between devices, on_device(): edges = [None, lax.ppermute(edge_out, 'lat', [(0, 1), (1, 0)])]  3.03 us
    pallas_call x2, Pallas kernels, mlp_rows(): pl.pallas_call(functools.partial(mlp_kernel, len(blocks), last), out_shap...  2.99 us
    pallas_call x1, Pallas kernels, final_sum(): pl.pallas_call(final_kernel, out_shape=jax.ShapeDtypeStruct(shape, jnp.bf...  1.3 us
  transfers between devices with their start and end apart: 8, of which 3 were waited for; matrix products, arithmetic and copies ran while one was open for 1% of the time, Pallas kernels for 21%

profile of v3, /device:TPU:0, one launch (start us, length us, event | category | flops | bytes accessed | tf_op | source)
XLA Modules:
  0.0 42.9 jit_solution(11811267296517814322)
XLA Ops:
  0.0 1.0 %dynamic-slice_bitcast_fusion = bf16[2,64,1440]{2,1,0:T(8,128)(2,1)S(1)} fusion(bf16[4,1440,64]{1,2,0:T(8,128)(2,1)} %param.11, s32[]{:T(128)S(6)} %select_n.3), kind=kLoop, calls=%fused_computation | loop fusion | bytes 737284 | tf_op jit(solution)/shard_map/dynamic_slice | solution.py:315
  1.0 3.0 %collective-permute-start = (bf16[2,64,1440]{2,1,0:T(8,128)(2,1)S(1)}, bf16[2,64,1440]{2,1,0:T(8,128)(2,1)S(1)}, u32[]{:S(2)}, u32[]{:S(2)}) collective-permute-start(bf16[2,64,1440]{2,1,0:T(8,128)(2,1)S(1)} %dynamic-slice_bitcast_fusion), channel_id=1, source_target_pairs={{0,16},{16,0},{1,17},{17,1},{2,18},{18,2},{3,19},{19,3},{4,20},{20... | collective-permute-start | bytes 1105928 | tf_op jit(solution)/shard_map/ppermute | solution.py:316
  4.1 0.0 copy-start.3
  4.1 0.0 copy-start.4
  4.1 0.0 copy-start.5
  4.1 0.0 copy-start.6
  4.1 4.2 %conv_rows.3 = (bf16[128,384]{1,0:T(8,128)(2,1)}, bf16[128,384]{1,0:T(8,128)(2,1)}, bf16[128,384]{1,0:T(8,128)(2,1)}, bf16[128,384]{1,0:T(8,128)(2,1)}) custom-call(s32[1]{0:T(128)} %bitcast.8.pair_ref, s32[1]{0:T(128)} %bitcast.2.place_ref, s32[4,9]{1,0:T(4,128)} %lat_ref.3, s32[4,9]{1,0:T(4,128)} %lon_ref.3, s32[4,9]{1,0:T(4,128)} %basis_ref.3, ...), custom_call_target="tpu_custom_call" | custom-call | flops 4000000000 | tf_op jit(solution)/shard_map/conv_rows/pallas_call | solution.py:128
  8.3 1.6 %collective-permute-start.4 = (bf16[128,384]{1,0:T(8,128)(2,1)}, bf16[128,384]{1,0:T(8,128)(2,1)S(1)}, u32[]{:S(2)}, u32[]{:S(2)}) collective-permute-start(bf16[128,384]{1,0:T(8,128)(2,1)} %get-tuple-element.18), channel_id=1, source_target_pairs={{0,4},{4,8},{8,12},{12,0},{1,5},{5,9},{9,13},{13,1},{2,6},{6,10},{... | collective-permute-start | bytes 294920 | tf_op jit(solution)/shard_map/ppermute | solution.py:283
  9.9 2.6 %collective-permute-start.5 = (bf16[128,384]{1,0:T(8,128)(2,1)}, bf16[128,384]{1,0:T(8,128)(2,1)S(1)}, u32[]{:S(2)}, u32[]{:S(2)}) collective-permute-start(bf16[128,384]{1,0:T(8,128)(2,1)} %get-tuple-element.19), channel_id=1, source_target_pairs={{0,8},{4,12},{8,0},{12,4},{1,9},{5,13},{9,1},{13,5},{2,10},{6,14},... | collective-permute-start | bytes 294920 | tf_op jit(solution)/shard_map/ppermute | solution.py:283
  12.5 1.3 %collective-permute-start.6 = (bf16[128,384]{1,0:T(8,128)(2,1)}, bf16[128,384]{1,0:T(8,128)(2,1)S(1)}, u32[]{:S(2)}, u32[]{:S(2)}) collective-permute-start(bf16[128,384]{1,0:T(8,128)(2,1)} %get-tuple-element.20), channel_id=1, source_target_pairs={{0,12},{4,0},{8,4},{12,8},{1,13},{5,1},{9,5},{13,9},{2,14},{6,2},{... | collective-permute-start | bytes 294920 | tf_op jit(solution)/shard_map/ppermute | solution.py:283
  13.8 0.0 copy-done.10
  13.8 0.1 copy.12
  14.0 0.1 copy.13
  14.1 0.0 collective-permute-done.rest_0_
  14.2 0.0 copy-start.7
  14.2 0.0 copy-start.9
  14.2 3.0 %conv_rows.2 = (bf16[128,384]{1,0:T(8,128)(2,1)S(1)}, bf16[128,384]{1,0:T(8,128)(2,1)S(1)}, bf16[128,384]{1,0:T(8,128)(2,1)S(1)}, bf16[128,384]{1,0:T(8,128)(2,1)S(1)}) custom-call(s32[1]{0:T(128)} %bitcast.3.pair_ref, s32[1]{0:T(128)} %bitcast.2.place_ref, s32[4,9]{1,0:T(4,128)S(1)} %copy-done.3, s32[4,9]{1,0:T(4,128)S(1)} %copy-done.4, ...), custom_call_target="tpu_custom_call" | custom-call | flops 4000000000 | tf_op jit(solution)/shard_map/conv_rows/pallas_call | solution.py:128
  17.2 0.9 %collective-permute-start.1 = (bf16[128,384]{1,0:T(8,128)(2,1)S(1)}, bf16[128,384]{1,0:T(8,128)(2,1)S(1)}, u32[]{:S(2)}, u32[]{:S(2)}) collective-permute-start(bf16[128,384]{1,0:T(8,128)(2,1)S(1)} %get-tuple-element.14), channel_id=1, source_target_pairs={{0,4},{4,8},{8,12},{12,0},{1,5},{5,9},{9,13},{13,1},{2,6},{6,10},{... | collective-permute-start | bytes 294920 | tf_op jit(solution)/shard_map/ppermute | solution.py:283
  18.1 2.6 %collective-permute-start.2 = (bf16[128,384]{1,0:T(8,128)(2,1)S(1)}, bf16[128,384]{1,0:T(8,128)(2,1)S(1)}, u32[]{:S(2)}, u32[]{:S(2)}) collective-permute-start(bf16[128,384]{1,0:T(8,128)(2,1)S(1)} %get-tuple-element.15), channel_id=1, source_target_pairs={{0,8},{4,12},{8,0},{12,4},{1,9},{5,13},{9,1},{13,5},{2,10},{6,14},... | collective-permute-start | bytes 294920 | tf_op jit(solution)/shard_map/ppermute | solution.py:283
  20.7 0.0 collective-permute-done.4.rest_1_
  20.7 1.3 %collective-permute-start.3 = (bf16[128,384]{1,0:T(8,128)(2,1)S(1)}, bf16[128,384]{1,0:T(8,128)(2,1)S(1)}, u32[]{:S(2)}, u32[]{:S(2)}) collective-permute-start(bf16[128,384]{1,0:T(8,128)(2,1)S(1)} %get-tuple-element.16), channel_id=1, source_target_pairs={{0,12},{4,0},{8,4},{12,8},{1,13},{5,1},{9,5},{13,9},{2,14},{6,2},{... | collective-permute-start | bytes 294920 | tf_op jit(solution)/shard_map/ppermute | solution.py:283
  22.0 0.0 collective-permute-done.5.rest_2_
  22.0 0.0 collective-permute-done.6.rest_3_
  22.0 1.2 %mlp_rows.2.rest_7_ = bf16[8,16,256]{2,1,0:T(8,128)(2,1)S(1)} custom-call(s32[1]{0:T(128)} %bitcast.2.place_ref, bf16[128,384]{1,0:T(8,128)(2,1)S(1)} %copy-done.9, bf16[128,384]{1,0:T(8,128)(2,1)S(1)} %collective-permute-done.4.rest_1_, bf16[128,384]{1,0:T(8,128)(2,1)S(1)} %collective-permute-done.5.rest_2_, ...), custom_call_target="tpu_custom_call" | custom-call | flops 2000000000 | tf_op jit(solution)/shard_map/mlp_rows/pallas_call | solution.py:193
  23.2 1.4 %collective-permute-done.1.rest_1_ = bf16[128,384]{1,0:T(8,128)(2,1)S(1)} collective-permute-done((bf16[128,384]{1,0:T(8,128)(2,1)S(1)}, bf16[128,384]{1,0:T(8,128)(2,1)S(1)}, u32[]{:S(2)}, u32[]{:S(2)}) %collective-permute-start.1) | collective-permute-done | bytes 98336 | tf_op jit(solution)/shard_map/ppermute | solution.py:283
  24.7 2.9 %collective-permute-done.2.rest_2_ = bf16[128,384]{1,0:T(8,128)(2,1)S(1)} collective-permute-done((bf16[128,384]{1,0:T(8,128)(2,1)S(1)}, bf16[128,384]{1,0:T(8,128)(2,1)S(1)}, u32[]{:S(2)}, u32[]{:S(2)}) %collective-permute-start.2) | collective-permute-done | bytes 98336 | tf_op jit(solution)/shard_map/ppermute | solution.py:283
  27.6 0.0 collective-permute-done.3.rest_3_
  27.6 1.8 %mlp_rows.3 = bf16[8,32,256]{2,1,0:T(8,128)(2,1)} custom-call(s32[1]{0:T(128)} %bitcast.2.place_ref, bf16[128,384]{1,0:T(8,128)(2,1)S(1)} %get-tuple-element.13.rest_0_, bf16[128,384]{1,0:T(8,128)(2,1)S(1)} %collective-permute-done.1.rest_1_, bf16[128,384]{1,0:T(8,128)(2,1)S(1)} %collective-permute-done.2.rest_2_, ...), custom_call_target="tpu_custom_call" | custom-call | flops 2000000000 | tf_op jit(solution)/shard_map/mlp_rows/pallas_call | solution.py:193
  29.4 4.7 %all-to-all-start = ((bf16[8,32,256]{2,1,0:T(8,128)(2,1)}), bf16[8,32,256]{2,1,0:T(8,128)(2,1)S(1)}, u32[]{:S(2)}, u32[]{:S(2)}) async-start(bf16[8,32,256]{2,1,0:T(8,128)(2,1)} %mlp_rows.3), calls=%async_computation | async-start | bytes 262144 | tf_op jit(solution)/shard_map/all_to_all | solution.py:350
  34.1 0.8 %expand.1.left_ref = bf16[3,2,384,256]{3,2,1,0:T(8,128)(2,1)S(1)} custom-call(s32[1]{0:T(128)} %bitcast.start_ref, bf16[3,8,384]{2,1,0:T(8,128)(2,1)S(1)} %bitcast.18, bf16[8,256]{1,0:T(8,128)(2,1)S(1)} %copy-done.8), custom_call_target="tpu_custom_call" | custom-call | flops 2000000000 | tf_op jit(solution)/shard_map/expand/pallas_call | solution.py:224
  35.0 6.7 %all-to-all-done = bf16[8,32,256]{2,1,0:T(8,128)(2,1)S(1)} async-done(((bf16[8,32,256]{2,1,0:T(8,128)(2,1)}), bf16[8,32,256]{2,1,0:T(8,128)(2,1)S(1)}, u32[]{:S(2)}, u32[]{:S(2)}) %all-to-all-start) | async-done | bytes 131104 | tf_op jit(solution)/shard_map/all_to_all | solution.py:350
  41.6 1.3 %final_sum.1 = bf16[3,384,512]{2,1,0:T(8,128)(2,1)} custom-call(bf16[3,2,384,256]{3,2,1,0:T(8,128)(2,1)S(1)} %expand.1.left_ref, bf16[256,256]{1,0:T(8,128)(2,1)S(1)} %bitcast.17), custom_call_target="tpu_custom_call" | custom-call | flops 1000000000 | tf_op jit(solution)/shard_map/final_sum/pallas_call | solution.py:258
  (17 shorter events, 0.0 us)
Async XLA Ops:
  1.0 13.1 %collective-permute-start = (bf16[2,64,1440]{2,1,0:T(8,128)(2,1)S(1)}, bf16[2,64,1440]{2,1,0:T(8,128)(2,1)S(1)}, u32[]{:S(2)}, u32[]{:S(2)}) collective-permute-start(bf16[2,64,1440]{2,1,0:T(8,128)(2,1)S(1)} %dynamic-slice_bitcast_fusion), channel_id=1, source_target_pairs={{0,16},{16,0},{1,17},{17,1},{2,18},{18,2},{3,19},{19,3},{4,20},{20... | collective-permute-start | bytes 1105928 | tf_op jit(solution)/shard_map/ppermute | solution.py:316
  4.1 9.8 %copy-start.10 = (bf16[256,512]{1,0:T(8,128)(2,1)S(1)}, bf16[256,512]{1,0:T(8,128)(2,1)}, u32[]{:S(2)}) copy-start(bf16[256,512]{1,0:T(8,128)(2,1)} %param.17) | copy-start | bytes 786436
  4.1 9.9 %copy-start.11 = (bf16[512,256]{1,0:T(8,128)(2,1)S(1)}, bf16[512,256]{1,0:T(8,128)(2,1)}, u32[]{:S(2)}) copy-start(bf16[512,256]{1,0:T(8,128)(2,1)} %param.18) | copy-start | bytes 786436
  4.1 10.1 %copy-start = (bf16[4,1440,64]{1,2,0:T(8,128)(2,1)S(1)}, bf16[4,1440,64]{1,2,0:T(8,128)(2,1)}, u32[]{:S(2)}) copy-start(bf16[4,1440,64]{1,2,0:T(8,128)(2,1)} %param.11) | copy-start | bytes 2211844
  4.1 10.1 %copy-start.1 = (bf16[6,64,64]{2,1,0:T(8,128)(2,1)S(1)}, bf16[6,64,64]{2,1,0:T(8,128)(2,1)}, u32[]{:S(2)}) copy-start(bf16[6,64,64]{2,1,0:T(8,128)(2,1)} %rest_0_.1) | copy-start | bytes 147460
  4.1 10.1 %copy-start.3 = (s32[4,9]{1,0:T(4,128)S(1)}, s32[4,9]{1,0:T(4,128)}, u32[]{:S(2)}) copy-start(s32[4,9]{1,0:T(4,128)} %lat_ref.3) | copy-start | bytes 436
  4.1 10.1 %copy-start.4 = (s32[4,9]{1,0:T(4,128)S(1)}, s32[4,9]{1,0:T(4,128)}, u32[]{:S(2)}) copy-start(s32[4,9]{1,0:T(4,128)} %lon_ref.3) | copy-start | bytes 436
  4.1 10.1 %copy-start.5 = (s32[4,9]{1,0:T(4,128)S(1)}, s32[4,9]{1,0:T(4,128)}, u32[]{:S(2)}) copy-start(s32[4,9]{1,0:T(4,128)} %basis_ref.3) | copy-start | bytes 436
  4.1 10.1 %copy-start.6 = (f32[4,9]{1,0:T(4,128)S(1)}, f32[4,9]{1,0:T(4,128)}, u32[]{:S(2)}) copy-start(f32[4,9]{1,0:T(4,128)} %value_ref.3) | copy-start | bytes 436
  8.3 12.4 %collective-permute-start.4 = (bf16[128,384]{1,0:T(8,128)(2,1)}, bf16[128,384]{1,0:T(8,128)(2,1)S(1)}, u32[]{:S(2)}, u32[]{:S(2)}) collective-permute-start(bf16[128,384]{1,0:T(8,128)(2,1)} %get-tuple-element.18), channel_id=1, source_target_pairs={{0,4},{4,8},{8,12},{12,0},{1,5},{5,9},{9,13},{13,1},{2,6},{6,10},{... | collective-permute-start | bytes 294920 | tf_op jit(solution)/shard_map/ppermute | solution.py:283
  9.9 12.1 %collective-permute-start.5 = (bf16[128,384]{1,0:T(8,128)(2,1)}, bf16[128,384]{1,0:T(8,128)(2,1)S(1)}, u32[]{:S(2)}, u32[]{:S(2)}) collective-permute-start(bf16[128,384]{1,0:T(8,128)(2,1)} %get-tuple-element.19), channel_id=1, source_target_pairs={{0,8},{4,12},{8,0},{12,4},{1,9},{5,13},{9,1},{13,5},{2,10},{6,14},... | collective-permute-start | bytes 294920 | tf_op jit(solution)/shard_map/ppermute | solution.py:283
  12.5 9.6 %collective-permute-start.6 = (bf16[128,384]{1,0:T(8,128)(2,1)}, bf16[128,384]{1,0:T(8,128)(2,1)S(1)}, u32[]{:S(2)}, u32[]{:S(2)}) collective-permute-start(bf16[128,384]{1,0:T(8,128)(2,1)} %get-tuple-element.20), channel_id=1, source_target_pairs={{0,12},{4,0},{8,4},{12,8},{1,13},{5,1},{9,5},{13,9},{2,14},{6,2},{... | collective-permute-start | bytes 294920 | tf_op jit(solution)/shard_map/ppermute | solution.py:283
  14.2 7.8 %copy-start.7 = (bf16[4,64,384]{2,1,0:T(8,128)(2,1)S(1)}, bf16[4,64,384]{2,1,0:T(8,128)(2,1)}, u32[]{:S(2)}) copy-start(bf16[4,64,384]{2,1,0:T(8,128)(2,1)} %constant.25.clone.rest_6_) | copy-start | bytes 589828
  14.2 7.8 %copy-start.9 = (bf16[128,384]{1,0:T(8,128)(2,1)S(1)}, bf16[128,384]{1,0:T(8,128)(2,1)}, u32[]{:S(2)}) copy-start(bf16[128,384]{1,0:T(8,128)(2,1)} %get-tuple-element.17.rest_0_) | copy-start | bytes 294916
  17.2 7.5 %collective-permute-start.1 = (bf16[128,384]{1,0:T(8,128)(2,1)S(1)}, bf16[128,384]{1,0:T(8,128)(2,1)S(1)}, u32[]{:S(2)}, u32[]{:S(2)}) collective-permute-start(bf16[128,384]{1,0:T(8,128)(2,1)S(1)} %get-tuple-element.14), channel_id=1, source_target_pairs={{0,4},{4,8},{8,12},{12,0},{1,5},{5,9},{9,13},{13,1},{2,6},{6,10},{... | collective-permute-start | bytes 294920 | tf_op jit(solution)/shard_map/ppermute | solution.py:283
  18.1 9.5 %collective-permute-start.2 = (bf16[128,384]{1,0:T(8,128)(2,1)S(1)}, bf16[128,384]{1,0:T(8,128)(2,1)S(1)}, u32[]{:S(2)}, u32[]{:S(2)}) collective-permute-start(bf16[128,384]{1,0:T(8,128)(2,1)S(1)} %get-tuple-element.15), channel_id=1, source_target_pairs={{0,8},{4,12},{8,0},{12,4},{1,9},{5,13},{9,1},{13,5},{2,10},{6,14},... | collective-permute-start | bytes 294920 | tf_op jit(solution)/shard_map/ppermute | solution.py:283
  20.7 6.9 %collective-permute-start.3 = (bf16[128,384]{1,0:T(8,128)(2,1)S(1)}, bf16[128,384]{1,0:T(8,128)(2,1)S(1)}, u32[]{:S(2)}, u32[]{:S(2)}) collective-permute-start(bf16[128,384]{1,0:T(8,128)(2,1)S(1)} %get-tuple-element.16), channel_id=1, source_target_pairs={{0,12},{4,0},{8,4},{12,8},{1,13},{5,1},{9,5},{13,9},{2,14},{6,2},{... | collective-permute-start | bytes 294920 | tf_op jit(solution)/shard_map/ppermute | solution.py:283
  27.6 6.6 %copy-start.2 = (bf16[3,384,8]{1,2,0:T(8,128)(2,1)S(1)}, bf16[3,384,8]{1,2,0:T(8,128)(2,1)}, u32[]{:S(2)}) copy-start(bf16[3,384,8]{1,2,0:T(8,128)(2,1)} %param.19) | copy-start | bytes 55300
  27.6 6.6 %copy-start.8 = (bf16[8,256]{1,0:T(8,128)(2,1)S(1)}, bf16[8,256]{1,0:T(8,128)(2,1)}, u32[]{:S(2)}) copy-start(bf16[8,256]{1,0:T(8,128)(2,1)} %constant.26.clone.spread_ref) | copy-start | bytes 12292
  29.4 12.3 %all-to-all-start = ((bf16[8,32,256]{2,1,0:T(8,128)(2,1)}), bf16[8,32,256]{2,1,0:T(8,128)(2,1)S(1)}, u32[]{:S(2)}, u32[]{:S(2)}) async-start(bf16[8,32,256]{2,1,0:T(8,128)(2,1)} %mlp_rows.3), calls=%async_computation | async-start | bytes 262144 | tf_op jit(solution)/shard_map/all_to_all | solution.py:350

commit v4 on v3

--- a/solution.py
+++ b/solution.py
@@ -45,53 +45,61 @@
         edge_ref, weight_ref, *rest = rest
     else:
         edge_ref, (weight_ref, *rest) = None, rest
-    *out_refs, rows_ref, taps_ref, filt_ref = rest
+    *out_refs, wrap_ref, rows_ref, taps_ref, filt_ref = rest
     own, _, lon = fields_ref.shape
     chunks = len(out_refs)
     chunk = lon // chunks
     width = out_refs[0].shape[1]
-    total = rows_ref.shape[2]
+    total = wrap_ref.shape[2]
     pair = pair_ref[0]
     own_at = HALO * (1 - pair)
     edge_at = own * pair
 
-    def put(slot, cells):
-        rows_ref[slot, :, LANES : LANES + lon] = cells
-        rows_ref[slot, :, 0:LANES] = cells[:, lon - LANES :]
+    lane = lax.broadcasted_iota(jnp.int32, (G, LANES), 1)
+    begins = [LANES + chunk * lax.rem(place_ref[0] + k, chunks) - DLON for k in range(chunks)]
+
+    def put(slot, room, cells):
+        wrap_ref[room, :, LANES : LANES + lon] = cells
+        wrap_ref[room, :, 0:LANES] = cells[:, lon - LANES :]
         full = (lon // LANES) * LANES
         tail = total - LANES - lon
-        rows_ref[slot, :, LANES + full :] = jnp.concatenate(
+        wrap_ref[room, :, LANES + full :] = jnp.concatenate(
             [cells[:, full:], cells[:, :tail]], axis=1
         )
-
-    for row in range(own):
-        put(own_at + row, fields_ref[row])
-    for row in range(HALO):
-        if has_edge:
-            put(edge_at + row, edge_ref[row])
-        else:
-            rows_ref[edge_at + row] = jnp.zeros(rows_ref.shape[1:], rows_ref.dtype)
-
-    lane = lax.broadcasted_iota(jnp.int32, (G, LANES), 1)
-    begins = [LANES + chunk * lax.rem(place_ref[0] + k, chunks) for k in range(chunks)]
-
-    def fill(slot, tap, source, offset):
         for k in range(chunks):
-            begin = begins[k] + offset
-            first = lax.div(begin, LANES)
-            shift = lax.rem(begin, LANES)
+            first = lax.div(begins[k], LANES)
+            shift = lax.rem(begins[k], LANES)
             back = lax.rem(LANES - shift, LANES)
             keep = lane < LANES - shift
             turned = []
             for t in range(width // LANES + 1):
                 start = pl.multiple_of((first + t) * LANES, LANES)
-                tile = rows_ref[source, :, pl.ds(start, LANES)]
-                turned.append(pltpu.roll(tile, back, 1))
+                turned.append(pltpu.roll(wrap_ref[room, :, pl.ds(start, LANES)], back, 1))
             for t in range(width // LANES):
                 at = k * width + t * LANES
-                taps_ref[slot, tap * G : (tap + 1) * G, at : at + LANES] = jnp.where(
-                    keep, turned[t], turned[t + 1]
-                )
+                rows_ref[slot, :, at : at + LANES] = jnp.where(keep, turned[t], turned[t + 1])
+
+    for row in range(own):
+        put(own_at + row, row, fields_ref[row])
+    for row in range(HALO):
+        if has_edge:
+            put(edge_at + row, own + row, edge_ref[row])
+        else:
+            rows_ref[edge_at + row] = jnp.zeros(rows_ref.shape[1:], rows_ref.dtype)
+
+    def fill(slot, tap, source, offset):
+        shift = offset + DLON
+        back = lax.rem(LANES - shift, LANES)
+        keep = lane < LANES - shift
+        for k in range(chunks):
+            turned = []
+            for at in range(k * width, (k + 1) * width, LANES):
+                turned.append(pltpu.roll(rows_ref[source, :, at : at + LANES], back, 1))
+            for t, tile in enumerate(turned):
+                if t + 1 < len(turned):
+                    tile = jnp.where(keep, tile, turned[t + 1])
+                at = k * width + t * LANES
+                taps_ref[slot, tap * G : (tap + 1) * G, at : at + LANES] = tile
 
     eye = jnp.where(
         lax.broadcasted_iota(jnp.int32, (G, G), 0) == lax.broadcasted_iota(jnp.int32, (G, G), 1),
@@ -121,8 +129,8 @@
 
 def conv_rows(pair, place, supports, fields, edge, weight, chunks):
     own, chans, lon = fields.shape
-    width = ceil_to(lon // chunks, LANES)
-    highest = (LANES + lon - lon // chunks + DLON) // LANES
+    width = ceil_to(lon // chunks + 2 * DLON, LANES)
+    highest = (LANES + lon - lon // chunks - DLON) // LANES
     total = (highest + 1) * LANES + width
     arrays = [fields] + ([] if edge is None else [edge]) + [weight]
     return pl.pallas_call(
@@ -132,6 +140,7 @@
         out_specs=[VMEM] * chunks,
         scratch_shapes=[
             pltpu.VMEM((own + HALO, chans, total), jnp.bfloat16),
+            pltpu.VMEM((own + HALO, chans, chunks * width), jnp.bfloat16),
             pltpu.VMEM((2, TAPS * G, chunks * width), jnp.bfloat16),
             pltpu.VMEM((2, G, TAPS * G), jnp.bfloat16),
         ],
@@ -303,7 +312,7 @@
     num_chan = lax.axis_size("chan")
     mode_dev, _, lats = legendre.shape
     dests = num_lat * num_chan
-    width = ceil_to(lon // num_chan, LANES)
+    width = ceil_to(lon // num_chan + 2 * DLON, LANES)
     band = lax.axis_index("lat")
     place = scalar(lax.axis_index("chan"))
     index = lax.axis_index(("lat", "chan"))

time: 43.2 us -> 43.4 us (level)
  transfers between devices with their start and end apart: 8 -> 8, of which waited for: 3 -> 3; matrix products, arithmetic and copies ran while one was open for 1% -> 1% of each run, Pallas kernels for 21% -> 22%
where the time goes in v4:
time: 43.4 us; the launch traced here: 43.2 us
  starting transfers between devices  18.3 us (42%)
  Pallas kernels  12.6 us (29%)
  waiting for transfers between devices  10.8 us (25%)
  local copies, waits for them, and re-layouts  1.35 us (3%)
    ppermute x6, starting transfers between devices, turn(): lax.ppermute(block, axis, [(i, (i + step) % count) for i in range(count)])  10.3 us
    pallas_call x2, Pallas kernels, conv_rows(): pl.pallas_call(functools.partial(conv_kernel, edge is not None), out_shap...  7.46 us
    all_to_all x1, waiting for transfers between devices, on_device(): lax.all_to_all(spectrum, both, split_axis=0, concat_axis=0, tiled=True)  6.69 us
    all_to_all x1, starting transfers between devices, on_device(): lax.all_to_all(spectrum, both, split_axis=0, concat_axis=0, tiled=True)  4.92 us
    ppermute x6, waiting for transfers between devices, turn(): lax.ppermute(block, axis, [(i, (i + step) % count) for i in range(count)])  4.12 us
    ppermute x1, starting transfers between devices, on_device(): edges = [None, lax.ppermute(edge_out, 'lat', [(0, 1), (1, 0)])]  3.03 us
    pallas_call x2, Pallas kernels, mlp_rows(): pl.pallas_call(functools.partial(mlp_kernel, len(blocks), last), out_shap...  2.99 us
    pallas_call x1, Pallas kernels, final_sum(): pl.pallas_call(final_kernel, out_shape=jax.ShapeDtypeStruct(shape, jnp.bf...  1.3 us
  transfers between devices with their start and end apart: 8, of which 3 were waited for; matrix products, arithmetic and copies ran while one was open for 1% of the time, Pallas kernels for 22%

profile of v4, /device:TPU:0, one launch (start us, length us, event | category | flops | bytes accessed | tf_op | source)
XLA Modules:
  0.0 43.2 jit_solution(1279807605052591454)
XLA Ops:
  0.0 1.0 %dynamic-slice_bitcast_fusion = bf16[2,64,1440]{2,1,0:T(8,128)(2,1)S(1)} fusion(bf16[4,1440,64]{1,2,0:T(8,128)(2,1)} %param.11, s32[]{:T(128)S(6)} %select_n.3), kind=kLoop, calls=%fused_computation | loop fusion | bytes 737284 | tf_op jit(solution)/shard_map/dynamic_slice | solution.py:324
  1.0 3.0 %collective-permute-start = (bf16[2,64,1440]{2,1,0:T(8,128)(2,1)S(1)}, bf16[2,64,1440]{2,1,0:T(8,128)(2,1)S(1)}, u32[]{:S(2)}, u32[]{:S(2)}) collective-permute-start(bf16[2,64,1440]{2,1,0:T(8,128)(2,1)S(1)} %dynamic-slice_bitcast_fusion), channel_id=1, source_target_pairs={{0,16},{16,0},{1,17},{17,1},{2,18},{18,2},{3,19},{19,3},{4,20},{20... | collective-permute-start | bytes 1105928 | tf_op jit(solution)/shard_map/ppermute | solution.py:325
  4.1 0.0 copy-start.3
  4.1 0.0 copy-start.4
  4.1 0.0 copy-start.5
  4.1 0.0 copy-start.6
  4.1 4.2 %conv_rows.3 = (bf16[128,384]{1,0:T(8,128)(2,1)}, bf16[128,384]{1,0:T(8,128)(2,1)}, bf16[128,384]{1,0:T(8,128)(2,1)}, bf16[128,384]{1,0:T(8,128)(2,1)}) custom-call(s32[1]{0:T(128)} %bitcast.8.pair_ref, s32[1]{0:T(128)} %bitcast.2.place_ref, s32[4,9]{1,0:T(4,128)} %lat_ref.3, s32[4,9]{1,0:T(4,128)} %lon_ref.3, s32[4,9]{1,0:T(4,128)} %basis_ref.3, ...), custom_call_target="tpu_custom_call" | custom-call | flops 4000000000 | tf_op jit(solution)/shard_map/conv_rows/pallas_call | solution.py:136
  8.3 1.6 %collective-permute-start.4 = (bf16[128,384]{1,0:T(8,128)(2,1)}, bf16[128,384]{1,0:T(8,128)(2,1)S(1)}, u32[]{:S(2)}, u32[]{:S(2)}) collective-permute-start(bf16[128,384]{1,0:T(8,128)(2,1)} %get-tuple-element.18), channel_id=1, source_target_pairs={{0,4},{4,8},{8,12},{12,0},{1,5},{5,9},{9,13},{13,1},{2,6},{6,10},{... | collective-permute-start | bytes 294920 | tf_op jit(solution)/shard_map/ppermute | solution.py:292
  9.9 2.6 %collective-permute-start.5 = (bf16[128,384]{1,0:T(8,128)(2,1)}, bf16[128,384]{1,0:T(8,128)(2,1)S(1)}, u32[]{:S(2)}, u32[]{:S(2)}) collective-permute-start(bf16[128,384]{1,0:T(8,128)(2,1)} %get-tuple-element.19), channel_id=1, source_target_pairs={{0,8},{4,12},{8,0},{12,4},{1,9},{5,13},{9,1},{13,5},{2,10},{6,14},... | collective-permute-start | bytes 294920 | tf_op jit(solution)/shard_map/ppermute | solution.py:292
  12.5 1.3 %collective-permute-start.6 = (bf16[128,384]{1,0:T(8,128)(2,1)}, bf16[128,384]{1,0:T(8,128)(2,1)S(1)}, u32[]{:S(2)}, u32[]{:S(2)}) collective-permute-start(bf16[128,384]{1,0:T(8,128)(2,1)} %get-tuple-element.20), channel_id=1, source_target_pairs={{0,12},{4,0},{8,4},{12,8},{1,13},{5,1},{9,5},{13,9},{2,14},{6,2},{... | collective-permute-start | bytes 294920 | tf_op jit(solution)/shard_map/ppermute | solution.py:292
  13.8 0.0 copy-done.10
  13.9 0.1 copy.12
  14.0 0.1 copy.13
  14.1 0.0 collective-permute-done.rest_0_
  14.2 0.0 copy-start.7
  14.2 0.0 copy-start.9
  14.2 3.2 %conv_rows.2 = (bf16[128,384]{1,0:T(8,128)(2,1)S(1)}, bf16[128,384]{1,0:T(8,128)(2,1)S(1)}, bf16[128,384]{1,0:T(8,128)(2,1)S(1)}, bf16[128,384]{1,0:T(8,128)(2,1)S(1)}) custom-call(s32[1]{0:T(128)} %bitcast.3.pair_ref, s32[1]{0:T(128)} %bitcast.2.place_ref, s32[4,9]{1,0:T(4,128)S(1)} %copy-done.3, s32[4,9]{1,0:T(4,128)S(1)} %copy-done.4, ...), custom_call_target="tpu_custom_call" | custom-call | flops 4000000000 | tf_op jit(solution)/shard_map/conv_rows/pallas_call | solution.py:136
  17.5 0.8 %collective-permute-start.1 = (bf16[128,384]{1,0:T(8,128)(2,1)S(1)}, bf16[128,384]{1,0:T(8,128)(2,1)S(1)}, u32[]{:S(2)}, u32[]{:S(2)}) collective-permute-start(bf16[128,384]{1,0:T(8,128)(2,1)S(1)} %get-tuple-element.14), channel_id=1, source_target_pairs={{0,4},{4,8},{8,12},{12,0},{1,5},{5,9},{9,13},{13,1},{2,6},{6,10},{... | collective-permute-start | bytes 294920 | tf_op jit(solution)/shard_map/ppermute | solution.py:292
  18.3 2.6 %collective-permute-start.2 = (bf16[128,384]{1,0:T(8,128)(2,1)S(1)}, bf16[128,384]{1,0:T(8,128)(2,1)S(1)}, u32[]{:S(2)}, u32[]{:S(2)}) collective-permute-start(bf16[128,384]{1,0:T(8,128)(2,1)S(1)} %get-tuple-element.15), channel_id=1, source_target_pairs={{0,8},{4,12},{8,0},{12,4},{1,9},{5,13},{9,1},{13,5},{2,10},{6,14},... | collective-permute-start | bytes 294920 | tf_op jit(solution)/shard_map/ppermute | solution.py:292
  20.9 0.0 collective-permute-done.4.rest_1_
  20.9 1.3 %collective-permute-start.3 = (bf16[128,384]{1,0:T(8,128)(2,1)S(1)}, bf16[128,384]{1,0:T(8,128)(2,1)S(1)}, u32[]{:S(2)}, u32[]{:S(2)}) collective-permute-start(bf16[128,384]{1,0:T(8,128)(2,1)S(1)} %get-tuple-element.16), channel_id=1, source_target_pairs={{0,12},{4,0},{8,4},{12,8},{1,13},{5,1},{9,5},{13,9},{2,14},{6,2},{... | collective-permute-start | bytes 294920 | tf_op jit(solution)/shard_map/ppermute | solution.py:292
  22.3 0.0 collective-permute-done.5.rest_2_
  22.3 0.0 collective-permute-done.6.rest_3_
  22.3 1.2 %mlp_rows.2.rest_7_ = bf16[8,16,256]{2,1,0:T(8,128)(2,1)S(1)} custom-call(s32[1]{0:T(128)} %bitcast.2.place_ref, bf16[128,384]{1,0:T(8,128)(2,1)S(1)} %copy-done.9, bf16[128,384]{1,0:T(8,128)(2,1)S(1)} %collective-permute-done.4.rest_1_, bf16[128,384]{1,0:T(8,128)(2,1)S(1)} %collective-permute-done.5.rest_2_, ...), custom_call_target="tpu_custom_call" | custom-call | flops 2000000000 | tf_op jit(solution)/shard_map/mlp_rows/pallas_call | solution.py:202
  23.5 1.5 %collective-permute-done.1.rest_1_ = bf16[128,384]{1,0:T(8,128)(2,1)S(1)} collective-permute-done((bf16[128,384]{1,0:T(8,128)(2,1)S(1)}, bf16[128,384]{1,0:T(8,128)(2,1)S(1)}, u32[]{:S(2)}, u32[]{:S(2)}) %collective-permute-start.1) | collective-permute-done | bytes 98336 | tf_op jit(solution)/shard_map/ppermute | solution.py:292
  25.0 2.6 %collective-permute-done.2.rest_2_ = bf16[128,384]{1,0:T(8,128)(2,1)S(1)} collective-permute-done((bf16[128,384]{1,0:T(8,128)(2,1)S(1)}, bf16[128,384]{1,0:T(8,128)(2,1)S(1)}, u32[]{:S(2)}, u32[]{:S(2)}) %collective-permute-start.2) | collective-permute-done | bytes 98336 | tf_op jit(solution)/shard_map/ppermute | solution.py:292
  27.6 0.0 collective-permute-done.3.rest_3_
  27.6 1.8 %mlp_rows.3 = bf16[8,32,256]{2,1,0:T(8,128)(2,1)} custom-call(s32[1]{0:T(128)} %bitcast.2.place_ref, bf16[128,384]{1,0:T(8,128)(2,1)S(1)} %get-tuple-element.13.rest_0_, bf16[128,384]{1,0:T(8,128)(2,1)S(1)} %collective-permute-done.1.rest_1_, bf16[128,384]{1,0:T(8,128)(2,1)S(1)} %collective-permute-done.2.rest_2_, ...), custom_call_target="tpu_custom_call" | custom-call | flops 2000000000 | tf_op jit(solution)/shard_map/mlp_rows/pallas_call | solution.py:202
  29.4 4.9 %all-to-all-start = ((bf16[8,32,256]{2,1,0:T(8,128)(2,1)}), bf16[8,32,256]{2,1,0:T(8,128)(2,1)S(1)}, u32[]{:S(2)}, u32[]{:S(2)}) async-start(bf16[8,32,256]{2,1,0:T(8,128)(2,1)} %mlp_rows.3), calls=%async_computation | async-start | bytes 262144 | tf_op jit(solution)/shard_map/all_to_all | solution.py:359
  34.4 0.8 %expand.1.left_ref = bf16[3,2,384,256]{3,2,1,0:T(8,128)(2,1)S(1)} custom-call(s32[1]{0:T(128)} %bitcast.start_ref, bf16[3,8,384]{2,1,0:T(8,128)(2,1)S(1)} %bitcast.18, bf16[8,256]{1,0:T(8,128)(2,1)S(1)} %copy-done.8), custom_call_target="tpu_custom_call" | custom-call | flops 2000000000 | tf_op jit(solution)/shard_map/expand/pallas_call | solution.py:233
  35.2 6.7 %all-to-all-done = bf16[8,32,256]{2,1,0:T(8,128)(2,1)S(1)} async-done(((bf16[8,32,256]{2,1,0:T(8,128)(2,1)}), bf16[8,32,256]{2,1,0:T(8,128)(2,1)S(1)}, u32[]{:S(2)}, u32[]{:S(2)}) %all-to-all-start) | async-done | bytes 131104 | tf_op jit(solution)/shard_map/all_to_all | solution.py:359
  41.9 1.3 %final_sum.1 = bf16[3,384,512]{2,1,0:T(8,128)(2,1)} custom-call(bf16[3,2,384,256]{3,2,1,0:T(8,128)(2,1)S(1)} %expand.1.left_ref, bf16[256,256]{1,0:T(8,128)(2,1)S(1)} %bitcast.17), custom_call_target="tpu_custom_call" | custom-call | flops 1000000000 | tf_op jit(solution)/shard_map/final_sum/pallas_call | solution.py:267
  (17 shorter events, 0.0 us)
Async XLA Ops:
  1.0 13.1 %collective-permute-start = (bf16[2,64,1440]{2,1,0:T(8,128)(2,1)S(1)}, bf16[2,64,1440]{2,1,0:T(8,128)(2,1)S(1)}, u32[]{:S(2)}, u32[]{:S(2)}) collective-permute-start(bf16[2,64,1440]{2,1,0:T(8,128)(2,1)S(1)} %dynamic-slice_bitcast_fusion), channel_id=1, source_target_pairs={{0,16},{16,0},{1,17},{17,1},{2,18},{18,2},{3,19},{19,3},{4,20},{20... | collective-permute-start | bytes 1105928 | tf_op jit(solution)/shard_map/ppermute | solution.py:325
  4.1 9.8 %copy-start.10 = (bf16[256,512]{1,0:T(8,128)(2,1)S(1)}, bf16[256,512]{1,0:T(8,128)(2,1)}, u32[]{:S(2)}) copy-start(bf16[256,512]{1,0:T(8,128)(2,1)} %param.17) | copy-start | bytes 786436
  4.1 9.9 %copy-start.11 = (bf16[512,256]{1,0:T(8,128)(2,1)S(1)}, bf16[512,256]{1,0:T(8,128)(2,1)}, u32[]{:S(2)}) copy-start(bf16[512,256]{1,0:T(8,128)(2,1)} %param.18) | copy-start | bytes 786436
  4.1 10.1 %copy-start = (bf16[4,1440,64]{1,2,0:T(8,128)(2,1)S(1)}, bf16[4,1440,64]{1,2,0:T(8,128)(2,1)}, u32[]{:S(2)}) copy-start(bf16[4,1440,64]{1,2,0:T(8,128)(2,1)} %param.11) | copy-start | bytes 2211844
  4.1 10.1 %copy-start.1 = (bf16[6,64,64]{2,1,0:T(8,128)(2,1)S(1)}, bf16[6,64,64]{2,1,0:T(8,128)(2,1)}, u32[]{:S(2)}) copy-start(bf16[6,64,64]{2,1,0:T(8,128)(2,1)} %rest_0_.1) | copy-start | bytes 147460
  4.1 10.1 %copy-start.3 = (s32[4,9]{1,0:T(4,128)S(1)}, s32[4,9]{1,0:T(4,128)}, u32[]{:S(2)}) copy-start(s32[4,9]{1,0:T(4,128)} %lat_ref.3) | copy-start | bytes 436
  4.1 10.1 %copy-start.4 = (s32[4,9]{1,0:T(4,128)S(1)}, s32[4,9]{1,0:T(4,128)}, u32[]{:S(2)}) copy-start(s32[4,9]{1,0:T(4,128)} %lon_ref.3) | copy-start | bytes 436
  4.1 10.1 %copy-start.5 = (s32[4,9]{1,0:T(4,128)S(1)}, s32[4,9]{1,0:T(4,128)}, u32[]{:S(2)}) copy-start(s32[4,9]{1,0:T(4,128)} %basis_ref.3) | copy-start | bytes 436
  4.1 10.1 %copy-start.6 = (f32[4,9]{1,0:T(4,128)S(1)}, f32[4,9]{1,0:T(4,128)}, u32[]{:S(2)}) copy-start(f32[4,9]{1,0:T(4,128)} %value_ref.3) | copy-start | bytes 436
  8.3 12.6 %collective-permute-start.4 = (bf16[128,384]{1,0:T(8,128)(2,1)}, bf16[128,384]{1,0:T(8,128)(2,1)S(1)}, u32[]{:S(2)}, u32[]{:S(2)}) collective-permute-start(bf16[128,384]{1,0:T(8,128)(2,1)} %get-tuple-element.18), channel_id=1, source_target_pairs={{0,4},{4,8},{8,12},{12,0},{1,5},{5,9},{9,13},{13,1},{2,6},{6,10},{... | collective-permute-start | bytes 294920 | tf_op jit(solution)/shard_map/ppermute | solution.py:292
  9.9 12.4 %collective-permute-start.5 = (bf16[128,384]{1,0:T(8,128)(2,1)}, bf16[128,384]{1,0:T(8,128)(2,1)S(1)}, u32[]{:S(2)}, u32[]{:S(2)}) collective-permute-start(bf16[128,384]{1,0:T(8,128)(2,1)} %get-tuple-element.19), channel_id=1, source_target_pairs={{0,8},{4,12},{8,0},{12,4},{1,9},{5,13},{9,1},{13,5},{2,10},{6,14},... | collective-permute-start | bytes 294920 | tf_op jit(solution)/shard_map/ppermute | solution.py:292
  12.5 9.8 %collective-permute-start.6 = (bf16[128,384]{1,0:T(8,128)(2,1)}, bf16[128,384]{1,0:T(8,128)(2,1)S(1)}, u32[]{:S(2)}, u32[]{:S(2)}) collective-permute-start(bf16[128,384]{1,0:T(8,128)(2,1)} %get-tuple-element.20), channel_id=1, source_target_pairs={{0,12},{4,0},{8,4},{12,8},{1,13},{5,1},{9,5},{13,9},{2,14},{6,2},{... | collective-permute-start | bytes 294920 | tf_op jit(solution)/shard_map/ppermute | solution.py:292
  14.2 8.1 %copy-start.7 = (bf16[4,64,384]{2,1,0:T(8,128)(2,1)S(1)}, bf16[4,64,384]{2,1,0:T(8,128)(2,1)}, u32[]{:S(2)}) copy-start(bf16[4,64,384]{2,1,0:T(8,128)(2,1)} %constant.25.clone.rest_6_) | copy-start | bytes 589828
  14.2 8.1 %copy-start.9 = (bf16[128,384]{1,0:T(8,128)(2,1)S(1)}, bf16[128,384]{1,0:T(8,128)(2,1)}, u32[]{:S(2)}) copy-start(bf16[128,384]{1,0:T(8,128)(2,1)} %get-tuple-element.17.rest_0_) | copy-start | bytes 294916
  17.5 7.5 %collective-permute-start.1 = (bf16[128,384]{1,0:T(8,128)(2,1)S(1)}, bf16[128,384]{1,0:T(8,128)(2,1)S(1)}, u32[]{:S(2)}, u32[]{:S(2)}) collective-permute-start(bf16[128,384]{1,0:T(8,128)(2,1)S(1)} %get-tuple-element.14), channel_id=1, source_target_pairs={{0,4},{4,8},{8,12},{12,0},{1,5},{5,9},{9,13},{13,1},{2,6},{6,10},{... | collective-permute-start | bytes 294920 | tf_op jit(solution)/shard_map/ppermute | solution.py:292
  18.3 9.3 %collective-permute-start.2 = (bf16[128,384]{1,0:T(8,128)(2,1)S(1)}, bf16[128,384]{1,0:T(8,128)(2,1)S(1)}, u32[]{:S(2)}, u32[]{:S(2)}) collective-permute-start(bf16[128,384]{1,0:T(8,128)(2,1)S(1)} %get-tuple-element.15), channel_id=1, source_target_pairs={{0,8},{4,12},{8,0},{12,4},{1,9},{5,13},{9,1},{13,5},{2,10},{6,14},... | collective-permute-start | bytes 294920 | tf_op jit(solution)/shard_map/ppermute | solution.py:292
  20.9 6.7 %collective-permute-start.3 = (bf16[128,384]{1,0:T(8,128)(2,1)S(1)}, bf16[128,384]{1,0:T(8,128)(2,1)S(1)}, u32[]{:S(2)}, u32[]{:S(2)}) collective-permute-start(bf16[128,384]{1,0:T(8,128)(2,1)S(1)} %get-tuple-element.16), channel_id=1, source_target_pairs={{0,12},{4,0},{8,4},{12,8},{1,13},{5,1},{9,5},{13,9},{2,14},{6,2},{... | collective-permute-start | bytes 294920 | tf_op jit(solution)/shard_map/ppermute | solution.py:292
  27.6 6.8 %copy-start.2 = (bf16[3,384,8]{1,2,0:T(8,128)(2,1)S(1)}, bf16[3,384,8]{1,2,0:T(8,128)(2,1)}, u32[]{:S(2)}) copy-start(bf16[3,384,8]{1,2,0:T(8,128)(2,1)} %param.19) | copy-start | bytes 55300
  27.6 6.8 %copy-start.8 = (bf16[8,256]{1,0:T(8,128)(2,1)S(1)}, bf16[8,256]{1,0:T(8,128)(2,1)}, u32[]{:S(2)}) copy-start(bf16[8,256]{1,0:T(8,128)(2,1)} %constant.26.clone.spread_ref) | copy-start | bytes 12292
  29.4 12.4 %all-to-all-start = ((bf16[8,32,256]{2,1,0:T(8,128)(2,1)}), bf16[8,32,256]{2,1,0:T(8,128)(2,1)S(1)}, u32[]{:S(2)}, u32[]{:S(2)}) async-start(bf16[8,32,256]{2,1,0:T(8,128)(2,1)} %mlp_rows.3), calls=%async_computation | async-start | bytes 262144 | tf_op jit(solution)/shard_map/all_to_all | solution.py:359

commit v5 on v3

--- a/solution.py
+++ b/solution.py
@@ -19,10 +19,11 @@
 EPS = 1e-05
 FEW = 8
 MIB = 1024 * 1024
-FLOPS_PER_US = 1_000_000_000
+FLOPS_PER_US = 100_000_000
 
 SMEM = pl.BlockSpec(memory_space=pltpu.SMEM)
 VMEM = pl.BlockSpec(memory_space=pltpu.VMEM)
+ANY = pl.BlockSpec(memory_space=pl.ANY)
 HBM = pl.BlockSpec(memory_space=pltpu.HBM)
 
 
@@ -35,25 +36,45 @@
 
 
 def takes(micros):
-    return pl.CostEstimate(flops=micros * FLOPS_PER_US, bytes_accessed=0, transcendentals=0)
+    return pl.CostEstimate(flops=int(micros * FLOPS_PER_US), bytes_accessed=0, transcendentals=0)
 
 
 def conv_kernel(
-    has_edge, pair_ref, place_ref, lat_ref, lon_ref, basis_ref, value_ref, fields_ref, *rest
+    step,
+    edges,
+    emit,
+    after,
+    pair_ref,
+    place_ref,
+    lat_ref,
+    lon_ref,
+    basis_ref,
+    value_ref,
+    fields_ref,
+    weight_ref,
+    *rest,
 ):
-    if has_edge:
-        edge_ref, weight_ref, *rest = rest
-    else:
-        edge_ref, (weight_ref, *rest) = None, rest
+    edge_refs, rest = rest[:edges], rest[edges + after :]
     *out_refs, rows_ref, taps_ref, filt_ref = rest
     own, _, lon = fields_ref.shape
+    pair = pair_ref[0]
+    if emit:
+        *out_refs, near_ref, far_ref = out_refs
+        near_ref[...] = fields_ref[(own - 1) * (1 - pair)]
+        far_ref[...] = fields_ref[(own - 2) * (1 - pair) + pair]
     chunks = len(out_refs)
     chunk = lon // chunks
     width = out_refs[0].shape[1]
     total = rows_ref.shape[2]
-    pair = pair_ref[0]
     own_at = HALO * (1 - pair)
-    edge_at = own * pair
+    edge_at = [own * pair + 1 - pair, (own + 1) * pair]
+    if edges == 0:
+        i = step
+    elif step == 0:
+        i = 1 - pair
+    else:
+        i = pair
+    row = 2 * pair + i
 
     def put(slot, cells):
         rows_ref[slot, :, LANES : LANES + lon] = cells
@@ -64,18 +85,18 @@
             [cells[:, full:], cells[:, :tail]], axis=1
         )
 
-    for row in range(own):
-        put(own_at + row, fields_ref[row])
-    for row in range(HALO):
-        if has_edge:
-            put(edge_at + row, edge_ref[row])
+    for k in range(own):
+        put(own_at + k, fields_ref[k])
+    for k in range(HALO):
+        if k < edges:
+            put(edge_at[k], edge_refs[k][...])
         else:
-            rows_ref[edge_at + row] = jnp.zeros(rows_ref.shape[1:], rows_ref.dtype)
+            rows_ref[edge_at[k]] = jnp.zeros(rows_ref.shape[1:], rows_ref.dtype)
 
     lane = lax.broadcasted_iota(jnp.int32, (G, LANES), 1)
     begins = [LANES + chunk * lax.rem(place_ref[0] + k, chunks) for k in range(chunks)]
 
-    def fill(slot, tap, source, offset):
+    def fill(tap, source, offset):
         for k in range(chunks):
             begin = begins[k] + offset
             first = lax.div(begin, LANES)
@@ -89,7 +110,7 @@
                 turned.append(pltpu.roll(tile, back, 1))
             for t in range(width // LANES):
                 at = k * width + t * LANES
-                taps_ref[slot, tap * G : (tap + 1) * G, at : at + LANES] = jnp.where(
+                taps_ref[tap * G : (tap + 1) * G, at : at + LANES] = jnp.where(
                     keep, turned[t], turned[t + 1]
                 )
 
@@ -98,64 +119,59 @@
         1.0,
         0.0,
     ).astype(jnp.bfloat16)
-    for i in range(2):
-        row = 2 * pair + i
-        pieces = []
-        for tap in range(S):
-            picked = weight_ref[basis_ref[row, tap]].astype(jnp.float32) * value_ref[row, tap]
-            pieces.append(picked.astype(jnp.bfloat16))
-        pieces.append(eye)
-        for k in range(TAPS // 2):
-            filt_ref[i, :, k * 2 * G : (k + 1) * 2 * G] = jnp.concatenate(
-                [pieces[2 * k], pieces[2 * k + 1]], axis=1
-            )
-        for tap in range(S):
-            fill(i, tap, HALO + i + lat_ref[row, tap], lon_ref[row, tap])
-        fill(i, S, HALO + i, 0)
-        mixed = jnp.dot(filt_ref[i], taps_ref[i], preferred_element_type=jnp.float32).astype(
-            jnp.bfloat16
+    pieces = []
+    for tap in range(S):
+        picked = weight_ref[basis_ref[row, tap]].astype(jnp.float32) * value_ref[row, tap]
+        pieces.append(picked.astype(jnp.bfloat16))
+    pieces.append(eye)
+    for k in range(TAPS // 2):
+        filt_ref[:, k * 2 * G : (k + 1) * 2 * G] = jnp.concatenate(
+            [pieces[2 * k], pieces[2 * k + 1]], axis=1
         )
-        for k in range(chunks):
-            out_refs[k][i * G : (i + 1) * G, :] = mixed[:, k * width : (k + 1) * width]
-
-
-def conv_rows(pair, place, supports, fields, edge, weight, chunks):
+    for tap in range(S):
+        fill(tap, HALO + i + lat_ref[row, tap], lon_ref[row, tap])
+    fill(S, HALO + i, 0)
+    mixed = jnp.dot(filt_ref[...], taps_ref[...], preferred_element_type=jnp.float32).astype(
+        jnp.bfloat16
+    )
+    for k in range(chunks):
+        out_refs[k][...] = mixed[:, k * width : (k + 1) * width]
+
+
+def conv_row(step, emit, pair, place, supports, fields, weight, edges, after, chunks):
     own, chans, lon = fields.shape
     width = ceil_to(lon // chunks, LANES)
     highest = (LANES + lon - lon // chunks + DLON) // LANES
     total = (highest + 1) * LANES + width
-    arrays = [fields] + ([] if edge is None else [edge]) + [weight]
+    outs = [jax.ShapeDtypeStruct((chans, width), jnp.bfloat16)] * chunks
+    if emit:
+        outs += [jax.ShapeDtypeStruct((chans, lon), jnp.bfloat16)] * HALO
     return pl.pallas_call(
-        functools.partial(conv_kernel, edge is not None),
-        out_shape=[jax.ShapeDtypeStruct((2 * chans, width), jnp.bfloat16)] * chunks,
-        in_specs=[SMEM] * 6 + [VMEM] * len(arrays),
-        out_specs=[VMEM] * chunks,
+        functools.partial(conv_kernel, step, len(edges), emit, len(after)),
+        out_shape=outs,
+        in_specs=[SMEM] * 6 + [VMEM] * (2 + len(edges)) + [ANY] * len(after),
+        out_specs=[VMEM] * len(outs),
         scratch_shapes=[
             pltpu.VMEM((own + HALO, chans, total), jnp.bfloat16),
-            pltpu.VMEM((2, TAPS * G, chunks * width), jnp.bfloat16),
-            pltpu.VMEM((2, G, TAPS * G), jnp.bfloat16),
+            pltpu.VMEM((TAPS * G, chunks * width), jnp.bfloat16),
+            pltpu.VMEM((G, TAPS * G), jnp.bfloat16),
         ],
-        compiler_params=params(56 if edge is None else 20),
-        cost_estimate=takes(4),
-        name="conv_rows",
-    )(pair, place, *supports, *arrays)
-
-
-def mlp_kernel(parts, last, place_ref, *rest):
-    blocks, rest = rest[:parts], rest[parts:]
+        compiler_params=params(56 if emit else 16),
+        cost_estimate=takes(2),
+        name="conv_row",
+    )(pair, place, *supports, fields, weight, *edges, *after)
+
+
+def mlp_kernel(parts, rows, joins, wide, place_ref, *rest):
+    blocks, rest = rest[: parts * rows], rest[parts * rows :]
     up_ref, down_ref, table_ref, *rest = rest
-    if last:
-        earlier_ref, out_ref, cells_ref = rest
-    else:
-        out_ref, cells_ref = rest
+    earlier, (out_ref, cells_ref) = rest[:joins], rest[-2:]
     width = blocks[0].shape[1]
     place = place_ref[0]
     for k in range(parts):
         source = pl.multiple_of(lax.rem(place - k + parts, parts) * G, G)
-        for i in range(2):
-            cells_ref[pl.ds(source, G), i * width : (i + 1) * width] = blocks[k][
-                i * G : (i + 1) * G, :
-            ]
+        for i in range(rows):
+            cells_ref[pl.ds(source, G), i * width : (i + 1) * width] = blocks[i * parts + k][...]
     values = cells_ref[...].astype(jnp.float32)
     center = values - jnp.mean(values, axis=0, keepdims=True)
     spread = jnp.mean(center * center, axis=0, keepdims=True)
@@ -168,7 +184,7 @@
     lowered = jnp.dot(down_ref[...], active, preferred_element_type=jnp.float32)
     result = (values + lowered).astype(jnp.bfloat16)
     found = []
-    for i in range(2):
+    for i in range(rows):
         modes = lax.dot_general(
             table_ref[place],
             result[:, i * width : (i + 1) * width],
@@ -176,30 +192,36 @@
             preferred_element_type=jnp.float32,
         )
         found.append(modes.reshape(modes.shape[0] // SLOT, SLOT, modes.shape[1]))
-    block = jnp.concatenate(found, axis=1).astype(jnp.bfloat16)
-    if last:
-        out_ref[:, 0 : 2 * SLOT, :] = earlier_ref[...]
-        out_ref[:, 2 * SLOT : 4 * SLOT, :] = block
+    if wide:
+        out_ref[...] = found[0]
+    elif joins:
+        first_ref, second_ref = earlier
+        out_ref[:, 0 : 2 * SLOT, :] = first_ref[...]
+        out_ref[:, 2 * SLOT : 4 * SLOT, :] = jnp.concatenate(
+            [second_ref[...], *found], axis=1
+        ).astype(jnp.bfloat16)
     else:
-        out_ref[...] = block
-
-
-def mlp_rows(place, blocks, up, down, tables, earlier, dests):
-    pair_chans, width = blocks[0].shape
-    chan = len(blocks) * pair_chans // 2
-    last = earlier is not None
-    arrays = [*blocks, up, down, tables] + ([earlier] if last else [])
-    rows = (4 if last else 2) * SLOT
+        out_ref[...] = jnp.concatenate(found, axis=1).astype(jnp.bfloat16)
+
+
+def mlp_rows(place, rows, up, down, tables, earlier, wide, after=()):
+    parts = len(rows[0])
+    chans, width = rows[0][0].shape
+    chan = parts * chans
+    dests = tables.shape[1] // SLOT
+    arrays = [*(block for row in rows for block in row), up, down, tables, *earlier]
+    slots = 4 if earlier else len(rows)
+    kind = jnp.float32 if wide else jnp.bfloat16
     return pl.pallas_call(
-        functools.partial(mlp_kernel, len(blocks), last),
-        out_shape=jax.ShapeDtypeStruct((dests, rows, chan), jnp.bfloat16),
-        in_specs=[SMEM] + [VMEM] * len(arrays),
+        functools.partial(mlp_kernel, parts, len(rows), len(earlier), wide),
+        out_shape=jax.ShapeDtypeStruct((dests, slots * SLOT, chan), kind),
+        in_specs=[SMEM] + [VMEM] * len(arrays) + [ANY] * len(after),
         out_specs=VMEM,
-        scratch_shapes=[pltpu.VMEM((chan, 2 * width), jnp.bfloat16)],
+        scratch_shapes=[pltpu.VMEM((chan, len(rows) * width), jnp.bfloat16)],
         compiler_params=params(20 if dests <= FEW else 40),
-        cost_estimate=takes(2),
+        cost_estimate=takes(1),
         name="mlp_rows",
-    )(place, *arrays)
+    )(place, *arrays, *after)
 
 
 def expand_kernel(start_ref, legendre_ref, spread_ref, out_ref):
@@ -311,17 +333,7 @@
 
     two_bands = num_lat == 2
     cells = jnp.swapaxes(fields, 1, 2)
-    if two_bands:
-        edge_out = lax.dynamic_slice_in_dim(cells, HALO * (1 - band), HALO, axis=0)
-        edges = [None, lax.ppermute(edge_out, "lat", [(0, 1), (1, 0)])]
-        pairs = [band, 1 - band]
-    else:
-        ends = num_lat - 1
-        edges = [
-            lax.ppermute(cells[lat_dev - HALO :], "lat", [(i, i + 1) for i in range(ends)]),
-            lax.ppermute(cells[:HALO], "lat", [(i + 1, i) for i in range(ends)]),
-        ]
-        pairs = [0, 1]
+    two_bands = num_lat == 2
 
     tables = jnp.asarray(fourier_blocks(lon, num_chan, width, dests, mode_dev))
     up = w_up.T
@@ -330,21 +342,47 @@
     depth = dests * 4 * SLOT
     row = np.arange(depth)
     source_band = row // (4 * SLOT) // num_chan
+    step = (row // SLOT) % 2
     phase = (row // (2 * SLOT)) % 2
     source_pair = (phase ^ source_band) if two_bands else phase
-    lat_of = lat_dev * source_band + 2 * source_pair + (row // SLOT) % 2
+    edged = (phase == 1) if two_bands else np.ones_like(phase, bool)
+    source_row = np.where(edged, np.where(step == 0, 1 - source_pair, source_pair), step)
+    lat_of = lat_dev * source_band + 2 * source_pair + source_row
     spread = (lat_of[None, :] == np.arange(lats)[:, None]).astype(jnp.bfloat16)
     left = expand(scalar(index * mode_dev), jnp.swapaxes(legendre, 1, 2), jnp.asarray(spread))
 
-    received = []
-    for edge, pair in zip(edges, pairs):
-        mixed = conv_rows(scalar(pair), place, supports, cells, edge, disco_weight, num_chan)
-        received.append(
-            [mixed[0]] + [turn(mixed[k], "chan", num_chan, k) for k in range(1, num_chan)]
+    def send(step, pair, edges, emit=False, after=()):
+        outs = conv_row(
+            step, emit, scalar(pair), place, supports, cells, disco_weight, edges, after, num_chan
         )
-    spectrum = None
-    for blocks in received:
-        spectrum = mlp_rows(place, blocks, up, down, tables, spectrum, dests)
+        outs = list(outs)
+        row = outs[:1] + [turn(outs[k], "chan", num_chan, k) for k in range(1, num_chan)]
+        return (row, *outs[num_chan:])
+
+    if two_bands:
+        row_a, near, far = send(0, band, [], emit=True)
+        edges = [lax.ppermute(edge, "lat", [(0, 1), (1, 0)]) for edge in (near, far)]
+        (row_b,) = send(1, band, [], after=[near])
+        last = 1 - band
+    else:
+        ends = num_lat - 1
+        up_edges = [
+            lax.ppermute(cells[lat_dev - 1 - k], "lat", [(i, i + 1) for i in range(ends)])
+            for k in range(HALO)
+        ]
+        edges = [
+            lax.ppermute(cells[k], "lat", [(i + 1, i) for i in range(ends)]) for k in range(HALO)
+        ]
+        (row_a,) = send(0, 0, up_edges[:1])
+        (row_b,) = send(1, 0, up_edges)
+        last = 1
+    (row_c,) = send(0, last, edges[:1], after=row_a[1:])
+    (row_d,) = send(1, last, edges)
+    first = mlp_rows(
+        place, [row_a, row_b], up, down, tables, [], False, after=[row_c[0], edges[1]]
+    )
+    second = mlp_rows(place, [row_c], up, down, tables, [], True)
+    spectrum = mlp_rows(place, [row_d], up, down, tables, [first, second], False)
 
     both = ("lat", "chan")
     gathered = lax.all_to_all(spectrum, both, split_axis=0, concat_axis=0, tiled=True)

time: 43.2 us -> 55 us (1.27)
  starting transfers between devices: 18.1 us -> 27.4 us
  waiting for transfers between devices: 11 us -> 6.87 us
  local copies, waits for them, and re-layouts: 1.35 us -> 4.88 us
  Pallas kernels: 12.3 us -> 15.3 us
    ppermute x6 -> x12, starting transfers between devices: 10.3 us -> 18.7 us  [turn(): lax.ppermute(block, axis, [(i, (i + step) % count) for i in range(count)])]
    unnamed x26 -> x38, local copies, waits for them, and re-layouts: 0.33 us -> 4.88 us
    ppermute x6 -> x12, waiting for transfers between devices: 4.36 us -> 0.18 us  [turn(): lax.ppermute(block, axis, [(i, (i + step) % count) for i in range(count)])]
    pallas_call x4 -> x7, Pallas kernels: 10.2 us -> 13.2 us  [the longest x4 9.62 us: conv_row(): pl.pallas_call(functools.partial(conv_kernel, step, len(edges), emit, len...]
    dynamic_slice x1 -> x0, local copies, waits for them, and re-layouts: 1.02 us -> none  [on_device(): edge_out = lax.dynamic_slice_in_dim(cells, HALO * (1 - band), HALO, axis=0)]
    all_to_all x1, starting transfers between devices: 4.73 us -> 5.54 us  [on_device(): lax.all_to_all(spectrum, both, split_axis=0, concat_axis=0, tiled=True)]
    ppermute x1 -> x2, starting transfers between devices: 3.03 us -> 3.07 us  [on_device(): lax.ppermute(edge, 'lat', [(0, 1), (1, 0)])]
  transfers between devices with their start and end apart: 8 -> 15, of which waited for: 3 -> 2; matrix products, arithmetic and copies ran while one was open for 1% -> 0% of each run, Pallas kernels for 21% -> 17%
where the time goes in v5:
time: 55 us; the launch traced here: 54.6 us
  starting transfers between devices  27.4 us (50%)
  Pallas kernels  15.3 us (28%)
  waiting for transfers between devices  6.87 us (12%)
  local copies, waits for them, and re-layouts  4.88 us (9%)
    ppermute x12, starting transfers between devices, turn(): lax.ppermute(block, axis, [(i, (i + step) % count) for i in range(count)])  18.7 us
    pallas_call x4, Pallas kernels, conv_row(): pl.pallas_call(functools.partial(conv_kernel, step, len(edges), emit, len...  9.62 us
    all_to_all x1, waiting for transfers between devices, on_device(): lax.all_to_all(spectrum, both, split_axis=0, concat_axis=0, tiled=True)  6.68 us
    all_to_all x1, starting transfers between devices, on_device(): lax.all_to_all(spectrum, both, split_axis=0, concat_axis=0, tiled=True)  5.54 us
    unnamed x38, local copies, waits for them, and re-layouts  4.88 us
    pallas_call x3, Pallas kernels, mlp_rows(): pl.pallas_call(functools.partial(mlp_kernel, parts, len(rows), len(earlie...  3.54 us
    ppermute x2, starting transfers between devices, on_device(): lax.ppermute(edge, 'lat', [(0, 1), (1, 0)])  3.07 us
    pallas_call x1, Pallas kernels, final_sum(): pl.pallas_call(final_kernel, out_shape=jax.ShapeDtypeStruct(shape, jnp.bf...  1.3 us
  transfers between devices with their start and end apart: 15, of which 2 were waited for; matrix products, arithmetic and copies ran while one was open for 0% of the time, Pallas kernels for 17%

profile of v5, /device:TPU:0, one launch (start us, length us, event | category | flops | bytes accessed | tf_op | source)
XLA Modules:
  0.0 54.6 jit_solution(14425775545495027966)
XLA Ops:
  0.0 3.4 %conv_row.4 = (bf16[64,384]{1,0:T(8,128)(2,1)}, bf16[64,384]{1,0:T(8,128)(2,1)}, bf16[64,384]{1,0:T(8,128)(2,1)}, bf16[64,384]{1,0:T(8,128)(2,1)}, bf16[64,1440]{1,0:T(8,128)(2,1)}, /*index=5*/bf16[64,1440]{1,0:T(8,128)(2,1)}) custom-call(s32[1]{0:T(128)} %bitcast.5.pair_ref, s32[1]{0:T(128)} %bitcast.2.place_ref, s32[4,9]{1,0:T(4,128)} %lat_ref.7, ...), custom_call_target="tpu_custom_call" | custom-call | flops 200000000 | tf_op jit(solution)/shard_map/conv_row/pallas_call | solution.py:149
  3.4 3.0 %collective-permute-start = (bf16[64,1440]{1,0:T(8,128)(2,1)}, bf16[64,1440]{1,0:T(8,128)(2,1)S(1)}, u32[]{:S(2)}, u32[]{:S(2)}) collective-permute-start(bf16[64,1440]{1,0:T(8,128)(2,1)} %get-tuple-element.23.rest_0_), channel_id=1, source_target_pairs={{0,16},{16,0},{1,17},{17,1},{2,18},{18,2},{3,19},{19,3},{4,20},{20... | collective-permute-start | bytes 552968 | tf_op jit(solution)/shard_map/ppermute | solution.py:364
  6.5 2.0 %collective-permute-start.5 = (bf16[64,384]{1,0:T(8,128)(2,1)}, bf16[64,384]{1,0:T(8,128)(2,1)S(1)}, u32[]{:S(2)}, u32[]{:S(2)}) collective-permute-start(bf16[64,384]{1,0:T(8,128)(2,1)} %get-tuple-element.30), channel_id=1, source_target_pairs={{0,4},{4,8},{8,12},{12,0},{1,5},{5,9},{9,13},{13,1},{2,6},{6,10},{... | collective-permute-start | bytes 147464 | tf_op jit(solution)/shard_map/ppermute | solution.py:305
  8.5 2.6 %collective-permute-start.6 = (bf16[64,384]{1,0:T(8,128)(2,1)}, bf16[64,384]{1,0:T(8,128)(2,1)S(1)}, u32[]{:S(2)}, u32[]{:S(2)}) collective-permute-start(bf16[64,384]{1,0:T(8,128)(2,1)} %get-tuple-element.31), channel_id=1, source_target_pairs={{0,8},{4,12},{8,0},{12,4},{1,9},{5,13},{9,1},{13,5},{2,10},{6,14},... | collective-permute-start | bytes 147464 | tf_op jit(solution)/shard_map/ppermute | solution.py:305
  11.1 1.3 %collective-permute-start.7 = (bf16[64,384]{1,0:T(8,128)(2,1)}, bf16[64,384]{1,0:T(8,128)(2,1)S(1)}, u32[]{:S(2)}, u32[]{:S(2)}) collective-permute-start(bf16[64,384]{1,0:T(8,128)(2,1)} %get-tuple-element.32), channel_id=1, source_target_pairs={{0,12},{4,0},{8,4},{12,8},{1,13},{5,1},{9,5},{13,9},{2,14},{6,2},{... | collective-permute-start | bytes 147464 | tf_op jit(solution)/shard_map/ppermute | solution.py:305
  12.4 0.9 %copy-done.2 = bf16[6,64,64]{2,1,0:T(8,128)(2,1)S(1)} copy-done((bf16[6,64,64]{2,1,0:T(8,128)(2,1)S(1)}, bf16[6,64,64]{2,1,0:T(8,128)(2,1)}, u32[]{:S(2)}) %copy-start.2) | copy-done | bytes 49176
  13.3 0.9 %copy-done.4 = bf16[64,1440]{1,0:T(8,128)(2,1)S(1)} copy-done((bf16[64,1440]{1,0:T(8,128)(2,1)S(1)}, bf16[64,1440]{1,0:T(8,128)(2,1)}, u32[]{:S(2)}) %copy-start.4) | copy-done | bytes 184344
  14.2 0.7 %copy-done.6 = s32[4,9]{1,0:T(4,128)S(1)} copy-done((s32[4,9]{1,0:T(4,128)S(1)}, s32[4,9]{1,0:T(4,128)}, u32[]{:S(2)}) %copy-start.6) | copy-done | bytes 168
  14.9 0.7 %copy-done.8 = s32[4,9]{1,0:T(4,128)S(1)} copy-done((s32[4,9]{1,0:T(4,128)S(1)}, s32[4,9]{1,0:T(4,128)}, u32[]{:S(2)}) %copy-start.8) | copy-done | bytes 168
  15.6 0.7 %copy-done.10 = s32[4,9]{1,0:T(4,128)S(1)} copy-done((s32[4,9]{1,0:T(4,128)S(1)}, s32[4,9]{1,0:T(4,128)}, u32[]{:S(2)}) %copy-start.10) | copy-done | bytes 168
  16.3 0.7 %copy-done.12 = f32[4,9]{1,0:T(4,128)S(1)} copy-done((f32[4,9]{1,0:T(4,128)S(1)}, f32[4,9]{1,0:T(4,128)}, u32[]{:S(2)}) %copy-start.12) | copy-done | bytes 168
  17.0 2.1 %conv_row.6 = (bf16[64,384]{1,0:T(8,128)(2,1)S(1)}, bf16[64,384]{1,0:T(8,128)(2,1)S(1)}, bf16[64,384]{1,0:T(8,128)(2,1)S(1)}, bf16[64,384]{1,0:T(8,128)(2,1)S(1)}) custom-call(s32[1]{0:T(128)} %bitcast.5.pair_ref, s32[1]{0:T(128)} %bitcast.2.place_ref, s32[4,9]{1,0:T(4,128)S(1)} %copy-done.6, s32[4,9]{1,0:T(4,128)S(1)} %copy-done.8, s32[4,9]{1,0:T(4,128)S(1)} %copy-done.10, ...), custom_call_target="tpu_custom_call" | custom-call | flops 200000000 | tf_op jit(solution)/shard_map/conv_row/pallas_call | solution.py:149
  19.1 0.7 %collective-permute-start.8 = (bf16[64,384]{1,0:T(8,128)(2,1)S(1)}, bf16[64,384]{1,0:T(8,128)(2,1)S(1)}, u32[]{:S(2)}, u32[]{:S(2)}) collective-permute-start(bf16[64,384]{1,0:T(8,128)(2,1)S(1)} %get-tuple-element.34), channel_id=1, source_target_pairs={{0,4},{4,8},{8,12},{12,0},{1,5},{5,9},{9,13},{13,1},{2,6},{6,10},{... | collective-permute-start | bytes 147464 | tf_op jit(solution)/shard_map/ppermute | solution.py:305
  19.8 0.3 collective-permute-start.9
  20.1 2.9 %collective-permute-start.10 = (bf16[64,384]{1,0:T(8,128)(2,1)S(1)}, bf16[64,384]{1,0:T(8,128)(2,1)S(1)}, u32[]{:S(2)}, u32[]{:S(2)}) collective-permute-start(bf16[64,384]{1,0:T(8,128)(2,1)S(1)} %get-tuple-element.36), channel_id=1, source_target_pairs={{0,12},{4,0},{8,4},{12,8},{1,13},{5,1},{9,5},{13,9},{2,14},{6,2},{... | collective-permute-start | bytes 147464 | tf_op jit(solution)/shard_map/ppermute | solution.py:305
  23.1 2.1 %conv_row.7 = (bf16[64,384]{1,0:T(8,128)(2,1)S(1)}, bf16[64,384]{1,0:T(8,128)(2,1)S(1)}, bf16[64,384]{1,0:T(8,128)(2,1)S(1)}, bf16[64,384]{1,0:T(8,128)(2,1)S(1)}) custom-call(s32[1]{0:T(128)} %bitcast.3.pair_ref, s32[1]{0:T(128)} %bitcast.2.place_ref, s32[4,9]{1,0:T(4,128)S(1)} %copy-done.7, s32[4,9]{1,0:T(4,128)S(1)} %copy-done.9, s32[4,9]{1,0:T(4,128)S(1)} %copy-done.11, ...), custom_call_target="tpu_custom_call" | custom-call | flops 200000000 | tf_op jit(solution)/shard_map/conv_row/pallas_call | solution.py:149
  25.2 0.6 %collective-permute-start.11 = (bf16[64,384]{1,0:T(8,128)(2,1)S(1)}, bf16[64,384]{1,0:T(8,128)(2,1)S(1)}, u32[]{:S(2)}, u32[]{:S(2)}) collective-permute-start(bf16[64,384]{1,0:T(8,128)(2,1)S(1)} %get-tuple-element.38), channel_id=1, source_target_pairs={{0,4},{4,8},{8,12},{12,0},{1,5},{5,9},{9,13},{13,1},{2,6},{6,10},{... | collective-permute-start | bytes 147464 | tf_op jit(solution)/shard_map/ppermute | solution.py:305
  25.8 1.5 %collective-permute-start.12 = (bf16[64,384]{1,0:T(8,128)(2,1)S(1)}, bf16[64,384]{1,0:T(8,128)(2,1)S(1)}, u32[]{:S(2)}, u32[]{:S(2)}) collective-permute-start(bf16[64,384]{1,0:T(8,128)(2,1)S(1)} %get-tuple-element.39), channel_id=1, source_target_pairs={{0,8},{4,12},{8,0},{12,4},{1,9},{5,13},{9,1},{13,5},{2,10},{6,14},... | collective-permute-start | bytes 147464 | tf_op jit(solution)/shard_map/ppermute | solution.py:305
  27.3 2.8 %collective-permute-start.13 = (bf16[64,384]{1,0:T(8,128)(2,1)S(1)}, bf16[64,384]{1,0:T(8,128)(2,1)S(1)}, u32[]{:S(2)}, u32[]{:S(2)}) collective-permute-start(bf16[64,384]{1,0:T(8,128)(2,1)S(1)} %get-tuple-element.40), channel_id=1, source_target_pairs={{0,12},{4,0},{8,4},{12,8},{1,13},{5,1},{9,5},{13,9},{2,14},{6,2},{... | collective-permute-start | bytes 147464 | tf_op jit(solution)/shard_map/ppermute | solution.py:305
  30.2 2.1 %conv_row.5 = (bf16[64,384]{1,0:T(8,128)(2,1)S(1)}, bf16[64,384]{1,0:T(8,128)(2,1)S(1)}, bf16[64,384]{1,0:T(8,128)(2,1)S(1)}, bf16[64,384]{1,0:T(8,128)(2,1)S(1)}) custom-call(s32[1]{0:T(128)} %bitcast.3.pair_ref, s32[1]{0:T(128)} %bitcast.2.place_ref, s32[4,9]{1,0:T(4,128)S(1)} %copy-done.7, s32[4,9]{1,0:T(4,128)S(1)} %copy-done.9, s32[4,9]{1,0:T(4,128)S(1)} %copy-done.11, ...), custom_call_target="tpu_custom_call" | custom-call | flops 200000000 | tf_op jit(solution)/shard_map/conv_row/pallas_call | solution.py:149
  32.3 1.0 %collective-permute-start.3 = (bf16[64,384]{1,0:T(8,128)(2,1)S(1)}, bf16[64,384]{1,0:T(8,128)(2,1)S(1)}, u32[]{:S(2)}, u32[]{:S(2)}) collective-permute-start(bf16[64,384]{1,0:T(8,128)(2,1)S(1)} %get-tuple-element.27), channel_id=1, source_target_pairs={{0,8},{4,12},{8,0},{12,4},{1,9},{5,13},{9,1},{13,5},{2,10},{6,14},... | collective-permute-start | bytes 147464 | tf_op jit(solution)/shard_map/ppermute | solution.py:305
  33.3 2.8 %collective-permute-start.4 = (bf16[64,384]{1,0:T(8,128)(2,1)S(1)}, bf16[64,384]{1,0:T(8,128)(2,1)S(1)}, u32[]{:S(2)}, u32[]{:S(2)}) collective-permute-start(bf16[64,384]{1,0:T(8,128)(2,1)S(1)} %get-tuple-element.28), channel_id=1, source_target_pairs={{0,12},{4,0},{8,4},{12,8},{1,13},{5,1},{9,5},{13,9},{2,14},{6,2},{... | collective-permute-start | bytes 147464 | tf_op jit(solution)/shard_map/ppermute | solution.py:305
  36.2 0.1 copy.12
  36.3 0.1 copy.13
  36.5 1.2 %mlp_rows.3.rest_7_ = bf16[8,16,256]{2,1,0:T(8,128)(2,1)S(1)} custom-call(s32[1]{0:T(128)} %bitcast.2.place_ref, bf16[64,384]{1,0:T(8,128)(2,1)S(1)} %copy-done.5, bf16[64,384]{1,0:T(8,128)(2,1)S(1)} %collective-permute-done.5.rest_1_, bf16[64,384]{1,0:T(8,128)(2,1)S(1)} %collective-permute-done.6.rest_2_, ...), custom_call_target="tpu_custom_call" | custom-call | flops 100000000 | tf_op jit(solution)/shard_map/mlp_rows/pallas_call | solution.py:215
  37.7 0.9 %mlp_rows.4.rest_8_ = f32[8,8,256]{2,1,0:T(8,128)S(1)} custom-call(s32[1]{0:T(128)} %bitcast.2.place_ref, bf16[64,384]{1,0:T(8,128)(2,1)S(1)} %get-tuple-element.37.rest_11_.rest_0_, bf16[64,384]{1,0:T(8,128)(2,1)S(1)} %collective-permute-done.11.rest_1_, bf16[64,384]{1,0:T(8,128)(2,1)S(1)} %collective-permute-done.12.rest_2_, ...), custom_call_target="tpu_custom_call" | custom-call | flops 100000000 | tf_op jit(solution)/shard_map/mlp_rows/pallas_call | solution.py:215
  38.6 0.2 collective-permute-done.4.rest_3_
  38.8 1.5 %mlp_rows.5 = bf16[8,32,256]{2,1,0:T(8,128)(2,1)} custom-call(s32[1]{0:T(128)} %bitcast.2.place_ref, bf16[64,384]{1,0:T(8,128)(2,1)S(1)} %get-tuple-element.25.rest_0_, bf16[64,384]{1,0:T(8,128)(2,1)S(1)} %collective-permute-done.2.rest_1_, bf16[64,384]{1,0:T(8,128)(2,1)S(1)} %collective-permute-done.3.rest_2_, ...), custom_call_target="tpu_custom_call" | custom-call | flops 100000000 | tf_op jit(solution)/shard_map/mlp_rows/pallas_call | solution.py:215
  40.3 5.5 %all-to-all-start = ((bf16[8,32,256]{2,1,0:T(8,128)(2,1)}), bf16[8,32,256]{2,1,0:T(8,128)(2,1)S(1)}, u32[]{:S(2)}, u32[]{:S(2)}) async-start(bf16[8,32,256]{2,1,0:T(8,128)(2,1)} %mlp_rows.5), calls=%async_computation | async-start | bytes 262144 | tf_op jit(solution)/shard_map/all_to_all | solution.py:388
  45.8 0.8 %expand.1.left_ref = bf16[3,2,384,256]{3,2,1,0:T(8,128)(2,1)S(1)} custom-call(s32[1]{0:T(128)} %bitcast.start_ref, bf16[3,8,384]{2,1,0:T(8,128)(2,1)S(1)} %bitcast.20, bf16[8,256]{1,0:T(8,128)(2,1)S(1)} %copy-done.15), custom_call_target="tpu_custom_call" | custom-call | flops 200000000 | tf_op jit(solution)/shard_map/expand/pallas_call | solution.py:246
  46.7 6.7 %all-to-all-done = bf16[8,32,256]{2,1,0:T(8,128)(2,1)S(1)} async-done(((bf16[8,32,256]{2,1,0:T(8,128)(2,1)}), bf16[8,32,256]{2,1,0:T(8,128)(2,1)S(1)}, u32[]{:S(2)}, u32[]{:S(2)}) %all-to-all-start) | async-done | bytes 131104 | tf_op jit(solution)/shard_map/all_to_all | solution.py:388
  53.3 1.3 %final_sum.1 = bf16[3,384,512]{2,1,0:T(8,128)(2,1)} custom-call(bf16[3,2,384,256]{3,2,1,0:T(8,128)(2,1)S(1)} %expand.1.left_ref, bf16[256,256]{1,0:T(8,128)(2,1)S(1)} %bitcast.19), custom_call_target="tpu_custom_call" | custom-call | flops 100000000 | tf_op jit(solution)/shard_map/final_sum/pallas_call | solution.py:280
  (45 shorter events, 0.2 us)
Async XLA Ops:
  0.0 23.0 %copy-start.13 = (f32[4,9]{1,0:T(4,128)S(1)}, f32[4,9]{1,0:T(4,128)}, u32[]{:S(2)}) copy-start(f32[4,9]{1,0:T(4,128)} %value_ref.7) | copy-start | bytes 436
  0.0 23.0 %copy-start.11 = (s32[4,9]{1,0:T(4,128)S(1)}, s32[4,9]{1,0:T(4,128)}, u32[]{:S(2)}) copy-start(s32[4,9]{1,0:T(4,128)} %basis_ref.7) | copy-start | bytes 436
  0.0 23.0 %copy-start.9 = (s32[4,9]{1,0:T(4,128)S(1)}, s32[4,9]{1,0:T(4,128)}, u32[]{:S(2)}) copy-start(s32[4,9]{1,0:T(4,128)} %lon_ref.7) | copy-start | bytes 436
  0.0 23.0 %copy-start.7 = (s32[4,9]{1,0:T(4,128)S(1)}, s32[4,9]{1,0:T(4,128)}, u32[]{:S(2)}) copy-start(s32[4,9]{1,0:T(4,128)} %lat_ref.7) | copy-start | bytes 436
  0.0 23.0 %copy-start.3 = (bf16[6,64,64]{2,1,0:T(8,128)(2,1)S(1)}, bf16[6,64,64]{2,1,0:T(8,128)(2,1)}, u32[]{:S(2)}) copy-start(bf16[6,64,64]{2,1,0:T(8,128)(2,1)} %weight_ref.7) | copy-start | bytes 147460
  0.0 12.4 %copy-start = (bf16[4,1440,64]{1,2,0:T(8,128)(2,1)S(1)}, bf16[4,1440,64]{1,2,0:T(8,128)(2,1)}, u32[]{:S(2)}) copy-start(bf16[4,1440,64]{1,2,0:T(8,128)(2,1)} %param.11) | copy-start | bytes 2211844
  3.4 19.6 %collective-permute-start = (bf16[64,1440]{1,0:T(8,128)(2,1)}, bf16[64,1440]{1,0:T(8,128)(2,1)S(1)}, u32[]{:S(2)}, u32[]{:S(2)}) collective-permute-start(bf16[64,1440]{1,0:T(8,128)(2,1)} %get-tuple-element.23.rest_0_), channel_id=1, source_target_pairs={{0,16},{16,0},{1,17},{17,1},{2,18},{18,2},{3,19},{19,3},{4,20},{20... | collective-permute-start | bytes 552968 | tf_op jit(solution)/shard_map/ppermute | solution.py:364
  6.4 20.9 %collective-permute-start.1 = (bf16[64,1440]{1,0:T(8,128)(2,1)}, bf16[64,1440]{1,0:T(8,128)(2,1)S(1)}, u32[]{:S(2)}, u32[]{:S(2)}) collective-permute-start(bf16[64,1440]{1,0:T(8,128)(2,1)} %get-tuple-element.24), channel_id=1, source_target_pairs={{0,16},{16,0},{1,17},{17,1},{2,18},{18,2},{3,19},{19,3},{4,20},{20... | collective-permute-start | bytes 552968 | tf_op jit(solution)/shard_map/ppermute | solution.py:364
  6.5 12.6 %collective-permute-start.5 = (bf16[64,384]{1,0:T(8,128)(2,1)}, bf16[64,384]{1,0:T(8,128)(2,1)S(1)}, u32[]{:S(2)}, u32[]{:S(2)}) collective-permute-start(bf16[64,384]{1,0:T(8,128)(2,1)} %get-tuple-element.30), channel_id=1, source_target_pairs={{0,4},{4,8},{8,12},{12,0},{1,5},{5,9},{9,13},{13,1},{2,6},{6,10},{... | collective-permute-start | bytes 147464 | tf_op jit(solution)/shard_map/ppermute | solution.py:305
  8.5 11.3 %collective-permute-start.6 = (bf16[64,384]{1,0:T(8,128)(2,1)}, bf16[64,384]{1,0:T(8,128)(2,1)S(1)}, u32[]{:S(2)}, u32[]{:S(2)}) collective-permute-start(bf16[64,384]{1,0:T(8,128)(2,1)} %get-tuple-element.31), channel_id=1, source_target_pairs={{0,8},{4,12},{8,0},{12,4},{1,9},{5,13},{9,1},{13,5},{2,10},{6,14},... | collective-permute-start | bytes 147464 | tf_op jit(solution)/shard_map/ppermute | solution.py:305
  11.1 9.1 %collective-permute-start.7 = (bf16[64,384]{1,0:T(8,128)(2,1)}, bf16[64,384]{1,0:T(8,128)(2,1)S(1)}, u32[]{:S(2)}, u32[]{:S(2)}) collective-permute-start(bf16[64,384]{1,0:T(8,128)(2,1)} %get-tuple-element.32), channel_id=1, source_target_pairs={{0,12},{4,0},{8,4},{12,8},{1,13},{5,1},{9,5},{13,9},{2,14},{6,2},{... | collective-permute-start | bytes 147464 | tf_op jit(solution)/shard_map/ppermute | solution.py:305
  12.4 0.9 %copy-start.2 = (bf16[6,64,64]{2,1,0:T(8,128)(2,1)S(1)}, bf16[6,64,64]{2,1,0:T(8,128)(2,1)}, u32[]{:S(2)}) copy-start(bf16[6,64,64]{2,1,0:T(8,128)(2,1)} %weight_ref.7) | copy-start | bytes 147460
  13.3 0.9 %copy-start.4 = (bf16[64,1440]{1,0:T(8,128)(2,1)S(1)}, bf16[64,1440]{1,0:T(8,128)(2,1)}, u32[]{:S(2)}) copy-start(bf16[64,1440]{1,0:T(8,128)(2,1)} %get-tuple-element.23.rest_0_) | copy-start | bytes 552964
  14.2 0.7 %copy-start.6 = (s32[4,9]{1,0:T(4,128)S(1)}, s32[4,9]{1,0:T(4,128)}, u32[]{:S(2)}) copy-start(s32[4,9]{1,0:T(4,128)} %lat_ref.7) | copy-start | bytes 436
  14.9 0.7 %copy-start.8 = (s32[4,9]{1,0:T(4,128)S(1)}, s32[4,9]{1,0:T(4,128)}, u32[]{:S(2)}) copy-start(s32[4,9]{1,0:T(4,128)} %lon_ref.7) | copy-start | bytes 436
  15.6 0.7 %copy-start.10 = (s32[4,9]{1,0:T(4,128)S(1)}, s32[4,9]{1,0:T(4,128)}, u32[]{:S(2)}) copy-start(s32[4,9]{1,0:T(4,128)} %basis_ref.7) | copy-start | bytes 436
  19.1 6.7 %collective-permute-start.8 = (bf16[64,384]{1,0:T(8,128)(2,1)S(1)}, bf16[64,384]{1,0:T(8,128)(2,1)S(1)}, u32[]{:S(2)}, u32[]{:S(2)}) collective-permute-start(bf16[64,384]{1,0:T(8,128)(2,1)S(1)} %get-tuple-element.34), channel_id=1, source_target_pairs={{0,4},{4,8},{8,12},{12,0},{1,5},{5,9},{9,13},{13,1},{2,6},{6,10},{... | collective-permute-start | bytes 147464 | tf_op jit(solution)/shard_map/ppermute | solution.py:305
  19.8 12.4 %collective-permute-start.9 = (bf16[64,384]{1,0:T(8,128)(2,1)S(1)}, bf16[64,384]{1,0:T(8,128)(2,1)S(1)}, u32[]{:S(2)}, u32[]{:S(2)}) collective-permute-start(bf16[64,384]{1,0:T(8,128)(2,1)S(1)} %get-tuple-element.35), channel_id=1, source_target_pairs={{0,8},{4,12},{8,0},{12,4},{1,9},{5,13},{9,1},{13,5},{2,10},{6,14},... | collective-permute-start | bytes 147464 | tf_op jit(solution)/shard_map/ppermute | solution.py:305
  20.1 12.2 %collective-permute-start.10 = (bf16[64,384]{1,0:T(8,128)(2,1)S(1)}, bf16[64,384]{1,0:T(8,128)(2,1)S(1)}, u32[]{:S(2)}, u32[]{:S(2)}) collective-permute-start(bf16[64,384]{1,0:T(8,128)(2,1)S(1)} %get-tuple-element.36), channel_id=1, source_target_pairs={{0,12},{4,0},{8,4},{12,8},{1,13},{5,1},{9,5},{13,9},{2,14},{6,2},{... | collective-permute-start | bytes 147464 | tf_op jit(solution)/shard_map/ppermute | solution.py:305
  23.1 13.1 %copy-start.16 = (bf16[256,512]{1,0:T(8,128)(2,1)S(1)}, bf16[256,512]{1,0:T(8,128)(2,1)}, u32[]{:S(2)}) copy-start(bf16[256,512]{1,0:T(8,128)(2,1)} %param.17) | copy-start | bytes 786436
  25.2 11.2 %copy-start.17 = (bf16[512,256]{1,0:T(8,128)(2,1)S(1)}, bf16[512,256]{1,0:T(8,128)(2,1)}, u32[]{:S(2)}) copy-start(bf16[512,256]{1,0:T(8,128)(2,1)} %param.18) | copy-start | bytes 786436
  25.2 11.3 %copy-start.1 = (bf16[4,64,384]{2,1,0:T(8,128)(2,1)S(1)}, bf16[4,64,384]{2,1,0:T(8,128)(2,1)}, u32[]{:S(2)}) copy-start(bf16[4,64,384]{2,1,0:T(8,128)(2,1)} %constant.21.clone.rest_10_.rest_6_) | copy-start | bytes 589828
  25.2 11.3 %copy-start.5 = (bf16[64,384]{1,0:T(8,128)(2,1)S(1)}, bf16[64,384]{1,0:T(8,128)(2,1)}, u32[]{:S(2)}) copy-start(bf16[64,384]{1,0:T(8,128)(2,1)} %get-tuple-element.29.rest_0_) | copy-start | bytes 147460
  25.2 8.2 %collective-permute-start.11 = (bf16[64,384]{1,0:T(8,128)(2,1)S(1)}, bf16[64,384]{1,0:T(8,128)(2,1)S(1)}, u32[]{:S(2)}, u32[]{:S(2)}) collective-permute-start(bf16[64,384]{1,0:T(8,128)(2,1)S(1)} %get-tuple-element.38), channel_id=1, source_target_pairs={{0,4},{4,8},{8,12},{12,0},{1,5},{5,9},{9,13},{13,1},{2,6},{6,10},{... | collective-permute-start | bytes 147464 | tf_op jit(solution)/shard_map/ppermute | solution.py:305
  25.8 11.9 %collective-permute-start.12 = (bf16[64,384]{1,0:T(8,128)(2,1)S(1)}, bf16[64,384]{1,0:T(8,128)(2,1)S(1)}, u32[]{:S(2)}, u32[]{:S(2)}) collective-permute-start(bf16[64,384]{1,0:T(8,128)(2,1)S(1)} %get-tuple-element.39), channel_id=1, source_target_pairs={{0,8},{4,12},{8,0},{12,4},{1,9},{5,13},{9,1},{13,5},{2,10},{6,14},... | collective-permute-start | bytes 147464 | tf_op jit(solution)/shard_map/ppermute | solution.py:305
  27.3 10.4 %collective-permute-start.13 = (bf16[64,384]{1,0:T(8,128)(2,1)S(1)}, bf16[64,384]{1,0:T(8,128)(2,1)S(1)}, u32[]{:S(2)}, u32[]{:S(2)}) collective-permute-start(bf16[64,384]{1,0:T(8,128)(2,1)S(1)} %get-tuple-element.40), channel_id=1, source_target_pairs={{0,12},{4,0},{8,4},{12,8},{1,13},{5,1},{9,5},{13,9},{2,14},{6,2},{... | collective-permute-start | bytes 147464 | tf_op jit(solution)/shard_map/ppermute | solution.py:305
  32.2 6.3 %collective-permute-start.2 = (bf16[64,384]{1,0:T(8,128)(2,1)S(1)}, bf16[64,384]{1,0:T(8,128)(2,1)S(1)}, u32[]{:S(2)}, u32[]{:S(2)}) collective-permute-start(bf16[64,384]{1,0:T(8,128)(2,1)S(1)} %get-tuple-element.26), channel_id=1, source_target_pairs={{0,4},{4,8},{8,12},{12,0},{1,5},{5,9},{9,13},{13,1},{2,6},{6,10},{... | collective-permute-start | bytes 147464 | tf_op jit(solution)/shard_map/ppermute | solution.py:305
  32.3 6.3 %collective-permute-start.3 = (bf16[64,384]{1,0:T(8,128)(2,1)S(1)}, bf16[64,384]{1,0:T(8,128)(2,1)S(1)}, u32[]{:S(2)}, u32[]{:S(2)}) collective-permute-start(bf16[64,384]{1,0:T(8,128)(2,1)S(1)} %get-tuple-element.27), channel_id=1, source_target_pairs={{0,8},{4,12},{8,0},{12,4},{1,9},{5,13},{9,1},{13,5},{2,10},{6,14},... | collective-permute-start | bytes 147464 | tf_op jit(solution)/shard_map/ppermute | solution.py:305
  33.3 5.4 %collective-permute-start.4 = (bf16[64,384]{1,0:T(8,128)(2,1)S(1)}, bf16[64,384]{1,0:T(8,128)(2,1)S(1)}, u32[]{:S(2)}, u32[]{:S(2)}) collective-permute-start(bf16[64,384]{1,0:T(8,128)(2,1)S(1)} %get-tuple-element.28), channel_id=1, source_target_pairs={{0,12},{4,0},{8,4},{12,8},{1,13},{5,1},{9,5},{13,9},{2,14},{6,2},{... | collective-permute-start | bytes 147464 | tf_op jit(solution)/shard_map/ppermute | solution.py:305
  37.7 8.1 %copy-start.14 = (bf16[3,384,8]{1,2,0:T(8,128)(2,1)S(1)}, bf16[3,384,8]{1,2,0:T(8,128)(2,1)}, u32[]{:S(2)}) copy-start(bf16[3,384,8]{1,2,0:T(8,128)(2,1)} %param.19) | copy-start | bytes 55300
  37.7 8.1 %copy-start.15 = (bf16[8,256]{1,0:T(8,128)(2,1)S(1)}, bf16[8,256]{1,0:T(8,128)(2,1)}, u32[]{:S(2)}) copy-start(bf16[8,256]{1,0:T(8,128)(2,1)} %constant.22.clone.spread_ref) | copy-start | bytes 12292
  40.3 13.1 %all-to-all-start = ((bf16[8,32,256]{2,1,0:T(8,128)(2,1)}), bf16[8,32,256]{2,1,0:T(8,128)(2,1)S(1)}, u32[]{:S(2)}, u32[]{:S(2)}) async-start(bf16[8,32,256]{2,1,0:T(8,128)(2,1)} %mlp_rows.5), calls=%async_computation | async-start | bytes 262144 | tf_op jit(solution)/shard_map/all_to_all | solution.py:388
  (1 other events, 0.7 us)

commit v6 on v5

--- a/solution.py
+++ b/solution.py
@@ -19,7 +19,7 @@
 EPS = 1e-05
 FEW = 8
 MIB = 1024 * 1024
-FLOPS_PER_US = 100_000_000
+FLOPS_PER_US = 1_000_000_000
 
 SMEM = pl.BlockSpec(memory_space=pltpu.SMEM)
 VMEM = pl.BlockSpec(memory_space=pltpu.VMEM)
@@ -40,7 +40,7 @@
 
 
 def conv_kernel(
-    step,
+    steps,
     edges,
     emit,
     after,
@@ -68,14 +68,6 @@
     total = rows_ref.shape[2]
     own_at = HALO * (1 - pair)
     edge_at = [own * pair + 1 - pair, (own + 1) * pair]
-    if edges == 0:
-        i = step
-    elif step == 0:
-        i = 1 - pair
-    else:
-        i = pair
-    row = 2 * pair + i
-
     def put(slot, cells):
         rows_ref[slot, :, LANES : LANES + lon] = cells
         rows_ref[slot, :, 0:LANES] = cells[:, lon - LANES :]
@@ -96,7 +88,7 @@
     lane = lax.broadcasted_iota(jnp.int32, (G, LANES), 1)
     begins = [LANES + chunk * lax.rem(place_ref[0] + k, chunks) for k in range(chunks)]
 
-    def fill(tap, source, offset):
+    def fill(slot, tap, source, offset):
         for k in range(chunks):
             begin = begins[k] + offset
             first = lax.div(begin, LANES)
@@ -110,7 +102,7 @@
                 turned.append(pltpu.roll(tile, back, 1))
             for t in range(width // LANES):
                 at = k * width + t * LANES
-                taps_ref[tap * G : (tap + 1) * G, at : at + LANES] = jnp.where(
+                taps_ref[slot, tap * G : (tap + 1) * G, at : at + LANES] = jnp.where(
                     keep, turned[t], turned[t + 1]
                 )
 
@@ -119,51 +111,57 @@
         1.0,
         0.0,
     ).astype(jnp.bfloat16)
-    pieces = []
-    for tap in range(S):
-        picked = weight_ref[basis_ref[row, tap]].astype(jnp.float32) * value_ref[row, tap]
-        pieces.append(picked.astype(jnp.bfloat16))
-    pieces.append(eye)
-    for k in range(TAPS // 2):
-        filt_ref[:, k * 2 * G : (k + 1) * 2 * G] = jnp.concatenate(
-            [pieces[2 * k], pieces[2 * k + 1]], axis=1
+    for n, step in enumerate(steps):
+        i = step
+        if edges:
+            i = pair if step else 1 - pair
+        row = 2 * pair + i
+        pieces = []
+        for tap in range(S):
+            picked = weight_ref[basis_ref[row, tap]].astype(jnp.float32) * value_ref[row, tap]
+            pieces.append(picked.astype(jnp.bfloat16))
+        pieces.append(eye)
+        for k in range(TAPS // 2):
+            filt_ref[n, :, k * 2 * G : (k + 1) * 2 * G] = jnp.concatenate(
+                [pieces[2 * k], pieces[2 * k + 1]], axis=1
+            )
+        for tap in range(S):
+            fill(n, tap, HALO + i + lat_ref[row, tap], lon_ref[row, tap])
+        fill(n, S, HALO + i, 0)
+        mixed = jnp.dot(filt_ref[n], taps_ref[n], preferred_element_type=jnp.float32).astype(
+            jnp.bfloat16
         )
-    for tap in range(S):
-        fill(tap, HALO + i + lat_ref[row, tap], lon_ref[row, tap])
-    fill(S, HALO + i, 0)
-    mixed = jnp.dot(filt_ref[...], taps_ref[...], preferred_element_type=jnp.float32).astype(
-        jnp.bfloat16
-    )
-    for k in range(chunks):
-        out_refs[k][...] = mixed[:, k * width : (k + 1) * width]
-
-
-def conv_row(step, emit, pair, place, supports, fields, weight, edges, after, chunks):
+        for k in range(chunks):
+            out_refs[k][n * G : (n + 1) * G, :] = mixed[:, k * width : (k + 1) * width]
+
+
+def conv_rows(steps, emit, pair, place, supports, fields, weight, edges, after, chunks):
     own, chans, lon = fields.shape
     width = ceil_to(lon // chunks, LANES)
     highest = (LANES + lon - lon // chunks + DLON) // LANES
     total = (highest + 1) * LANES + width
-    outs = [jax.ShapeDtypeStruct((chans, width), jnp.bfloat16)] * chunks
+    count = len(steps)
+    outs = [jax.ShapeDtypeStruct((count * chans, width), jnp.bfloat16)] * chunks
     if emit:
         outs += [jax.ShapeDtypeStruct((chans, lon), jnp.bfloat16)] * HALO
     return pl.pallas_call(
-        functools.partial(conv_kernel, step, len(edges), emit, len(after)),
+        functools.partial(conv_kernel, steps, len(edges), emit, len(after)),
         out_shape=outs,
         in_specs=[SMEM] * 6 + [VMEM] * (2 + len(edges)) + [ANY] * len(after),
         out_specs=[VMEM] * len(outs),
         scratch_shapes=[
             pltpu.VMEM((own + HALO, chans, total), jnp.bfloat16),
-            pltpu.VMEM((TAPS * G, chunks * width), jnp.bfloat16),
-            pltpu.VMEM((G, TAPS * G), jnp.bfloat16),
+            pltpu.VMEM((count, TAPS * G, chunks * width), jnp.bfloat16),
+            pltpu.VMEM((count, G, TAPS * G), jnp.bfloat16),
         ],
         compiler_params=params(56 if emit else 16),
         cost_estimate=takes(2),
-        name="conv_row",
+        name="conv_rows",
     )(pair, place, *supports, fields, weight, *edges, *after)
 
 
 def mlp_kernel(parts, rows, joins, wide, place_ref, *rest):
-    blocks, rest = rest[: parts * rows], rest[parts * rows :]
+    blocks, rest = rest[:parts], rest[parts:]
     up_ref, down_ref, table_ref, *rest = rest
     earlier, (out_ref, cells_ref) = rest[:joins], rest[-2:]
     width = blocks[0].shape[1]
@@ -171,7 +169,9 @@
     for k in range(parts):
         source = pl.multiple_of(lax.rem(place - k + parts, parts) * G, G)
         for i in range(rows):
-            cells_ref[pl.ds(source, G), i * width : (i + 1) * width] = blocks[i * parts + k][...]
+            cells_ref[pl.ds(source, G), i * width : (i + 1) * width] = blocks[k][
+                i * G : (i + 1) * G, :
+            ]
     values = cells_ref[...].astype(jnp.float32)
     center = values - jnp.mean(values, axis=0, keepdims=True)
     spread = jnp.mean(center * center, axis=0, keepdims=True)
@@ -204,20 +204,21 @@
         out_ref[...] = jnp.concatenate(found, axis=1).astype(jnp.bfloat16)
 
 
-def mlp_rows(place, rows, up, down, tables, earlier, wide, after=()):
-    parts = len(rows[0])
-    chans, width = rows[0][0].shape
-    chan = parts * chans
+def mlp_rows(place, blocks, up, down, tables, earlier, wide, after=()):
+    parts = len(blocks)
+    chans, width = blocks[0].shape
+    rows = chans // G
+    chan = parts * G
     dests = tables.shape[1] // SLOT
-    arrays = [*(block for row in rows for block in row), up, down, tables, *earlier]
-    slots = 4 if earlier else len(rows)
+    arrays = [*blocks, up, down, tables, *earlier]
+    slots = 4 if earlier else rows
     kind = jnp.float32 if wide else jnp.bfloat16
     return pl.pallas_call(
-        functools.partial(mlp_kernel, parts, len(rows), len(earlier), wide),
+        functools.partial(mlp_kernel, parts, rows, len(earlier), wide),
         out_shape=jax.ShapeDtypeStruct((dests, slots * SLOT, chan), kind),
         in_specs=[SMEM] + [VMEM] * len(arrays) + [ANY] * len(after),
         out_specs=VMEM,
-        scratch_shapes=[pltpu.VMEM((chan, len(rows) * width), jnp.bfloat16)],
+        scratch_shapes=[pltpu.VMEM((chan, rows * width), jnp.bfloat16)],
         compiler_params=params(20 if dests <= FEW else 40),
         cost_estimate=takes(1),
         name="mlp_rows",
@@ -345,24 +346,24 @@
     step = (row // SLOT) % 2
     phase = (row // (2 * SLOT)) % 2
     source_pair = (phase ^ source_band) if two_bands else phase
-    edged = (phase == 1) if two_bands else np.ones_like(phase, bool)
-    source_row = np.where(edged, np.where(step == 0, 1 - source_pair, source_pair), step)
+    plain = (phase == 0) if two_bands else np.zeros_like(phase, bool)
+    source_row = np.where(plain, step, np.where(step == 0, 1 - source_pair, source_pair))
     lat_of = lat_dev * source_band + 2 * source_pair + source_row
     spread = (lat_of[None, :] == np.arange(lats)[:, None]).astype(jnp.bfloat16)
     left = expand(scalar(index * mode_dev), jnp.swapaxes(legendre, 1, 2), jnp.asarray(spread))
 
-    def send(step, pair, edges, emit=False, after=()):
-        outs = conv_row(
-            step, emit, scalar(pair), place, supports, cells, disco_weight, edges, after, num_chan
+    def send(steps, pair, edges, emit=False, after=()):
+        outs = list(
+            conv_rows(
+                steps, emit, scalar(pair), place, supports, cells, disco_weight, edges, after, num_chan
+            )
         )
-        outs = list(outs)
-        row = outs[:1] + [turn(outs[k], "chan", num_chan, k) for k in range(1, num_chan)]
-        return (row, *outs[num_chan:])
+        blocks = outs[:1] + [turn(outs[k], "chan", num_chan, k) for k in range(1, num_chan)]
+        return (blocks, *outs[num_chan:])
 
     if two_bands:
-        row_a, near, far = send(0, band, [], emit=True)
+        blocks, near, far = send((0, 1), band, [], emit=True)
         edges = [lax.ppermute(edge, "lat", [(0, 1), (1, 0)]) for edge in (near, far)]
-        (row_b,) = send(1, band, [], after=[near])
         last = 1 - band
     else:
         ends = num_lat - 1
@@ -373,16 +374,13 @@
         edges = [
             lax.ppermute(cells[k], "lat", [(i + 1, i) for i in range(ends)]) for k in range(HALO)
         ]
-        (row_a,) = send(0, 0, up_edges[:1])
-        (row_b,) = send(1, 0, up_edges)
+        (blocks,) = send((0, 1), 0, up_edges)
         last = 1
-    (row_c,) = send(0, last, edges[:1], after=row_a[1:])
-    (row_d,) = send(1, last, edges)
-    first = mlp_rows(
-        place, [row_a, row_b], up, down, tables, [], False, after=[row_c[0], edges[1]]
-    )
-    second = mlp_rows(place, [row_c], up, down, tables, [], True)
-    spectrum = mlp_rows(place, [row_d], up, down, tables, [first, second], False)
+    (row_c,) = send((0,), last, edges[:1])
+    (row_d,) = send((1,), last, edges, after=blocks[1:])
+    first = mlp_rows(place, blocks, up, down, tables, [], False, after=row_c[:1])
+    second = mlp_rows(place, row_c, up, down, tables, [], True)
+    spectrum = mlp_rows(place, row_d, up, down, tables, [first, second], False)
 
     both = ("lat", "chan")
     gathered = lax.all_to_all(spectrum, both, split_axis=0, concat_axis=0, tiled=True)

time: 55 us -> 48.2 us (0.88)
  local copies, waits for them, and re-layouts: 4.88 us -> 0.32 us
  starting transfers between devices: 27.4 us -> 24.8 us
  waiting for transfers between devices: 6.87 us -> 8.45 us
  Pallas kernels: 15.3 us -> 14.1 us
    unnamed x38 -> x26, local copies, waits for them, and re-layouts: 4.88 us -> 0.32 us
    ppermute x12 -> x9, starting transfers between devices: 18.7 us -> 16.8 us  [turn(): lax.ppermute(block, axis, [(i, (i + step) % count) for i in range(count)])]
    ppermute x12 -> x9, waiting for transfers between devices: 0.18 us -> 1.76 us  [turn(): lax.ppermute(block, axis, [(i, (i + step) % count) for i in range(count)])]
    pallas_call x7 -> x6, Pallas kernels: 13.2 us -> 12 us  [the longest x3 8.45 us: conv_rows(): pl.pallas_call(functools.partial(conv_kernel, steps, len(edges), emit, le...]
    all_to_all x1, starting transfers between devices: 5.54 us -> 4.54 us  [on_device(): lax.all_to_all(spectrum, both, split_axis=0, concat_axis=0, tiled=True)]
  transfers between devices with their start and end apart: 15 -> 12, of which waited for: 2 -> 2; matrix products, arithmetic and copies ran while one was open for 0% -> 1% of each run, Pallas kernels for 17% -> 15%
where the time goes in v6:
time: 48.2 us; the launch traced here: 47.9 us
  starting transfers between devices  24.8 us (51%)
  Pallas kernels  14.1 us (29%)
  waiting for transfers between devices  8.45 us (18%)
    ppermute x9, starting transfers between devices, turn(): lax.ppermute(block, axis, [(i, (i + step) % count) for i in range(count)])  16.8 us
    pallas_call x3, Pallas kernels, conv_rows(): pl.pallas_call(functools.partial(conv_kernel, steps, len(edges), emit, le...  8.45 us
    all_to_all x1, waiting for transfers between devices, on_device(): lax.all_to_all(spectrum, both, split_axis=0, concat_axis=0, tiled=True)  6.69 us
    all_to_all x1, starting transfers between devices, on_device(): lax.all_to_all(spectrum, both, split_axis=0, concat_axis=0, tiled=True)  4.54 us
    pallas_call x3, Pallas kernels, mlp_rows(): pl.pallas_call(functools.partial(mlp_kernel, parts, rows, len(earlier), w...  3.53 us
    ppermute x2, starting transfers between devices, on_device(): lax.ppermute(edge, 'lat', [(0, 1), (1, 0)])  3.48 us
    ppermute x9, waiting for transfers between devices, turn(): lax.ppermute(block, axis, [(i, (i + step) % count) for i in range(count)])  1.76 us
    pallas_call x1, Pallas kernels, final_sum(): pl.pallas_call(final_kernel, out_shape=jax.ShapeDtypeStruct(shape, jnp.bf...  1.3 us
  transfers between devices with their start and end apart: 12, of which 2 were waited for; matrix products, arithmetic and copies ran while one was open for 1% of the time, Pallas kernels for 15%

profile of v6, /device:TPU:0, one launch (start us, length us, event | category | flops | bytes accessed | tf_op | source)
XLA Modules:
  0.0 47.9 jit_solution(6238360034207321519)
XLA Ops:
  0.0 4.3 %conv_rows.3 = (bf16[128,384]{1,0:T(8,128)(2,1)}, bf16[128,384]{1,0:T(8,128)(2,1)}, bf16[128,384]{1,0:T(8,128)(2,1)}, bf16[128,384]{1,0:T(8,128)(2,1)}, bf16[64,...) custom-call(s32[1]{0:T(128)} %bitcast.5.pair_ref, s32[1]{0:T(128)} %bitcast.2.place_ref, s32[4,9]{1,0:T(4,128)} %lat_ref.5, ...), custom_call_target="tpu_custom_call" | custom-call | flops 2000000000 | tf_op jit(solution)/shard_map/conv_rows/pallas_call | solution.py:147
  4.3 3.0 %collective-permute-start = (bf16[64,1440]{1,0:T(8,128)(2,1)}, bf16[64,1440]{1,0:T(8,128)(2,1)S(1)}, u32[]{:S(2)}, u32[]{:S(2)}) collective-permute-start(bf16[64,1440]{1,0:T(8,128)(2,1)} %get-tuple-element.19), channel_id=1, source_target_pairs={{0,16},{16,0},{1,17},{17,1},{2,18},{18,2},{3,19},{19,3},{4,20},{20... | collective-permute-start | bytes 552968 | tf_op jit(solution)/shard_map/ppermute | solution.py:366
  7.3 1.6 %collective-permute-start.2 = (bf16[128,384]{1,0:T(8,128)(2,1)}, bf16[128,384]{1,0:T(8,128)(2,1)S(1)}, u32[]{:S(2)}, u32[]{:S(2)}) collective-permute-start(bf16[128,384]{1,0:T(8,128)(2,1)} %get-tuple-element.21), channel_id=1, source_target_pairs={{0,4},{4,8},{8,12},{12,0},{1,5},{5,9},{9,13},{13,1},{2,6},{6,10},{... | collective-permute-start | bytes 294920 | tf_op jit(solution)/shard_map/ppermute | solution.py:306
  8.9 2.6 %collective-permute-start.3 = (bf16[128,384]{1,0:T(8,128)(2,1)}, bf16[128,384]{1,0:T(8,128)(2,1)S(1)}, u32[]{:S(2)}, u32[]{:S(2)}) collective-permute-start(bf16[128,384]{1,0:T(8,128)(2,1)} %get-tuple-element.22), channel_id=1, source_target_pairs={{0,8},{4,12},{8,0},{12,4},{1,9},{5,13},{9,1},{13,5},{2,10},{6,14},... | collective-permute-start | bytes 294920 | tf_op jit(solution)/shard_map/ppermute | solution.py:306
  11.5 1.4 %collective-permute-start.4 = (bf16[128,384]{1,0:T(8,128)(2,1)}, bf16[128,384]{1,0:T(8,128)(2,1)S(1)}, u32[]{:S(2)}, u32[]{:S(2)}) collective-permute-start(bf16[128,384]{1,0:T(8,128)(2,1)} %get-tuple-element.23), channel_id=1, source_target_pairs={{0,12},{4,0},{8,4},{12,8},{1,13},{5,1},{9,5},{13,9},{2,14},{6,2},{... | collective-permute-start | bytes 294920 | tf_op jit(solution)/shard_map/ppermute | solution.py:306
  12.8 0.5 %collective-permute-start.1 = (bf16[64,1440]{1,0:T(8,128)(2,1)}, bf16[64,1440]{1,0:T(8,128)(2,1)S(1)}, u32[]{:S(2)}, u32[]{:S(2)}) collective-permute-start(bf16[64,1440]{1,0:T(8,128)(2,1)} %get-tuple-element.20), channel_id=1, source_target_pairs={{0,16},{16,0},{1,17},{17,1},{2,18},{18,2},{3,19},{19,3},{4,20},{20... | collective-permute-start | bytes 552968 | tf_op jit(solution)/shard_map/ppermute | solution.py:366
  13.3 0.1 copy.12
  13.5 0.1 copy.13
  13.6 0.0 collective-permute-done.rest_0_
  13.7 2.1 %conv_rows.5 = (bf16[64,384]{1,0:T(8,128)(2,1)S(1)}, bf16[64,384]{1,0:T(8,128)(2,1)S(1)}, bf16[64,384]{1,0:T(8,128)(2,1)S(1)}, bf16[64,384]{1,0:T(8,128)(2,1)S(1)}) custom-call(s32[1]{0:T(128)} %bitcast.3.pair_ref, s32[1]{0:T(128)} %bitcast.2.place_ref, s32[4,9]{1,0:T(4,128)S(1)} %copy-done.3, s32[4,9]{1,0:T(4,128)S(1)} %copy-done.4, s32[4,9]{1,0:T(4,128)S(1)} %copy-done.5, ...), custom_call_target="tpu_custom_call" | custom-call | flops 2000000000 | tf_op jit(solution)/shard_map/conv_rows/pallas_call | solution.py:147
  15.8 0.7 %collective-permute-start.8 = (bf16[64,384]{1,0:T(8,128)(2,1)S(1)}, bf16[64,384]{1,0:T(8,128)(2,1)S(1)}, u32[]{:S(2)}, u32[]{:S(2)}) collective-permute-start(bf16[64,384]{1,0:T(8,128)(2,1)S(1)} %get-tuple-element.30), channel_id=1, source_target_pairs={{0,4},{4,8},{8,12},{12,0},{1,5},{5,9},{9,13},{13,1},{2,6},{6,10},{... | collective-permute-start | bytes 147464 | tf_op jit(solution)/shard_map/ppermute | solution.py:306
  16.5 0.0 collective-permute-done.2.rest_2_.rest_1_
  16.5 3.6 %collective-permute-start.9 = (bf16[64,384]{1,0:T(8,128)(2,1)S(1)}, bf16[64,384]{1,0:T(8,128)(2,1)S(1)}, u32[]{:S(2)}, u32[]{:S(2)}) collective-permute-start(bf16[64,384]{1,0:T(8,128)(2,1)S(1)} %get-tuple-element.31), channel_id=1, source_target_pairs={{0,8},{4,12},{8,0},{12,4},{1,9},{5,13},{9,1},{13,5},{2,10},{6,14},... | collective-permute-start | bytes 147464 | tf_op jit(solution)/shard_map/ppermute | solution.py:306
  20.1 0.0 collective-permute-done.3.rest_3_.rest_2_
  20.1 3.0 %collective-permute-start.10 = (bf16[64,384]{1,0:T(8,128)(2,1)S(1)}, bf16[64,384]{1,0:T(8,128)(2,1)S(1)}, u32[]{:S(2)}, u32[]{:S(2)}) collective-permute-start(bf16[64,384]{1,0:T(8,128)(2,1)S(1)} %get-tuple-element.32), channel_id=1, source_target_pairs={{0,12},{4,0},{8,4},{12,8},{1,13},{5,1},{9,5},{13,9},{2,14},{6,2},{... | collective-permute-start | bytes 147464 | tf_op jit(solution)/shard_map/ppermute | solution.py:306
  23.2 0.0 collective-permute-done.4.rest_4_.rest_3_
  23.2 0.0 collective-permute-done.1.rest_1_
  23.2 2.1 %conv_rows.4 = (bf16[64,384]{1,0:T(8,128)(2,1)S(1)}, bf16[64,384]{1,0:T(8,128)(2,1)S(1)}, bf16[64,384]{1,0:T(8,128)(2,1)S(1)}, bf16[64,384]{1,0:T(8,128)(2,1)S(1)}) custom-call(s32[1]{0:T(128)} %bitcast.3.pair_ref, s32[1]{0:T(128)} %bitcast.2.place_ref, s32[4,9]{1,0:T(4,128)S(1)} %copy-done.3, s32[4,9]{1,0:T(4,128)S(1)} %copy-done.4, s32[4,9]{1,0:T(4,128)S(1)} %copy-done.5, ...), custom_call_target="tpu_custom_call" | custom-call | flops 2000000000 | tf_op jit(solution)/shard_map/conv_rows/pallas_call | solution.py:147
  25.3 0.1 collective-permute-start.5
  25.3 0.6 %collective-permute-start.6 = (bf16[64,384]{1,0:T(8,128)(2,1)S(1)}, bf16[64,384]{1,0:T(8,128)(2,1)S(1)}, u32[]{:S(2)}, u32[]{:S(2)}) collective-permute-start(bf16[64,384]{1,0:T(8,128)(2,1)S(1)} %get-tuple-element.26), channel_id=1, source_target_pairs={{0,8},{4,12},{8,0},{12,4},{1,9},{5,13},{9,1},{13,5},{2,10},{6,14},... | collective-permute-start | bytes 147464 | tf_op jit(solution)/shard_map/ppermute | solution.py:306
  25.9 1.2 %mlp_rows.3.rest_7_ = bf16[8,16,256]{2,1,0:T(8,128)(2,1)S(1)} custom-call(s32[1]{0:T(128)} %bitcast.2.place_ref, bf16[128,384]{1,0:T(8,128)(2,1)S(1)} %copy-done.9, bf16[128,384]{1,0:T(8,128)(2,1)S(1)} %collective-permute-done.2.rest_2_.rest_1_, bf16[128,384]{1,0:T(8,128)(2,1)S(1)} %collective-permute-done.3.rest_3_.rest_2_, ...), custom_call_target="tpu_custom_call" | custom-call | flops 1000000000 | tf_op jit(solution)/shard_map/mlp_rows/pallas_call | solution.py:216
  27.1 0.0 collective-permute-done.8.rest_1_
  27.1 3.3 %collective-permute-start.7 = (bf16[64,384]{1,0:T(8,128)(2,1)S(1)}, bf16[64,384]{1,0:T(8,128)(2,1)S(1)}, u32[]{:S(2)}, u32[]{:S(2)}) collective-permute-start(bf16[64,384]{1,0:T(8,128)(2,1)S(1)} %get-tuple-element.27), channel_id=1, source_target_pairs={{0,12},{4,0},{8,4},{12,8},{1,13},{5,1},{9,5},{13,9},{2,14},{6,2},{... | collective-permute-start | bytes 147464 | tf_op jit(solution)/shard_map/ppermute | solution.py:306
  30.4 0.0 collective-permute-done.9.rest_2_
  30.4 0.9 %mlp_rows.4.rest_8_ = f32[8,8,256]{2,1,0:T(8,128)S(1)} custom-call(s32[1]{0:T(128)} %bitcast.2.place_ref, bf16[64,384]{1,0:T(8,128)(2,1)S(1)} %get-tuple-element.29.rest_7_.rest_0_, bf16[64,384]{1,0:T(8,128)(2,1)S(1)} %collective-permute-done.8.rest_1_, bf16[64,384]{1,0:T(8,128)(2,1)S(1)} %collective-permute-done.9.rest_2_, ...), custom_call_target="tpu_custom_call" | custom-call | flops 1000000000 | tf_op jit(solution)/shard_map/mlp_rows/pallas_call | solution.py:216
  31.2 0.0 collective-permute-done.5.rest_1_
  31.3 1.7 %collective-permute-done.7.rest_3_ = bf16[64,384]{1,0:T(8,128)(2,1)S(1)} collective-permute-done((bf16[64,384]{1,0:T(8,128)(2,1)S(1)}, bf16[64,384]{1,0:T(8,128)(2,1)S(1)}, u32[]{:S(2)}, u32[]{:S(2)}) %collective-permute-start.7) | collective-permute-done | bytes 49184 | tf_op jit(solution)/shard_map/ppermute | solution.py:306
  33.0 1.5 %mlp_rows.5 = bf16[8,32,256]{2,1,0:T(8,128)(2,1)} custom-call(s32[1]{0:T(128)} %bitcast.2.place_ref, bf16[64,384]{1,0:T(8,128)(2,1)S(1)} %get-tuple-element.24.rest_0_, bf16[64,384]{1,0:T(8,128)(2,1)S(1)} %collective-permute-done.5.rest_1_, bf16[64,384]{1,0:T(8,128)(2,1)S(1)} %collective-permute-done.6.rest_2_, ...), custom_call_target="tpu_custom_call" | custom-call | flops 1000000000 | tf_op jit(solution)/shard_map/mlp_rows/pallas_call | solution.py:216
  34.5 4.5 %all-to-all-start = ((bf16[8,32,256]{2,1,0:T(8,128)(2,1)}), bf16[8,32,256]{2,1,0:T(8,128)(2,1)S(1)}, u32[]{:S(2)}, u32[]{:S(2)}) async-start(bf16[8,32,256]{2,1,0:T(8,128)(2,1)} %mlp_rows.5), calls=%async_computation | async-start | bytes 262144 | tf_op jit(solution)/shard_map/all_to_all | solution.py:386
  39.1 0.8 %expand.1.left_ref = bf16[3,2,384,256]{3,2,1,0:T(8,128)(2,1)S(1)} custom-call(s32[1]{0:T(128)} %bitcast.start_ref, bf16[3,8,384]{2,1,0:T(8,128)(2,1)S(1)} %bitcast.19, bf16[8,256]{1,0:T(8,128)(2,1)S(1)} %copy-done.8), custom_call_target="tpu_custom_call" | custom-call | flops 2000000000 | tf_op jit(solution)/shard_map/expand/pallas_call | solution.py:247
  39.9 6.7 %all-to-all-done = bf16[8,32,256]{2,1,0:T(8,128)(2,1)S(1)} async-done(((bf16[8,32,256]{2,1,0:T(8,128)(2,1)}), bf16[8,32,256]{2,1,0:T(8,128)(2,1)S(1)}, u32[]{:S(2)}, u32[]{:S(2)}) %all-to-all-start) | async-done | bytes 131104 | tf_op jit(solution)/shard_map/all_to_all | solution.py:386
  46.6 1.3 %final_sum.1 = bf16[3,384,512]{2,1,0:T(8,128)(2,1)} custom-call(bf16[3,2,384,256]{3,2,1,0:T(8,128)(2,1)S(1)} %expand.1.left_ref, bf16[256,256]{1,0:T(8,128)(2,1)S(1)} %bitcast.15), custom_call_target="tpu_custom_call" | custom-call | flops 1000000000 | tf_op jit(solution)/shard_map/final_sum/pallas_call | solution.py:281
  (26 shorter events, 0.1 us)
Async XLA Ops:
  0.0 13.3 %copy-start.10 = (bf16[256,512]{1,0:T(8,128)(2,1)S(1)}, bf16[256,512]{1,0:T(8,128)(2,1)}, u32[]{:S(2)}) copy-start(bf16[256,512]{1,0:T(8,128)(2,1)} %param.17) | copy-start | bytes 786436
  0.0 13.5 %copy-start.11 = (bf16[512,256]{1,0:T(8,128)(2,1)S(1)}, bf16[512,256]{1,0:T(8,128)(2,1)}, u32[]{:S(2)}) copy-start(bf16[512,256]{1,0:T(8,128)(2,1)} %param.18) | copy-start | bytes 786436
  0.0 13.6 %copy-start = (bf16[4,1440,64]{1,2,0:T(8,128)(2,1)S(1)}, bf16[4,1440,64]{1,2,0:T(8,128)(2,1)}, u32[]{:S(2)}) copy-start(bf16[4,1440,64]{1,2,0:T(8,128)(2,1)} %param.11) | copy-start | bytes 2211844
  0.0 13.6 %copy-start.1 = (bf16[6,64,64]{2,1,0:T(8,128)(2,1)S(1)}, bf16[6,64,64]{2,1,0:T(8,128)(2,1)}, u32[]{:S(2)}) copy-start(bf16[6,64,64]{2,1,0:T(8,128)(2,1)} %weight_ref.5) | copy-start | bytes 147460
  0.0 13.6 %copy-start.3 = (s32[4,9]{1,0:T(4,128)S(1)}, s32[4,9]{1,0:T(4,128)}, u32[]{:S(2)}) copy-start(s32[4,9]{1,0:T(4,128)} %lat_ref.5) | copy-start | bytes 436
  0.0 13.7 %copy-start.4 = (s32[4,9]{1,0:T(4,128)S(1)}, s32[4,9]{1,0:T(4,128)}, u32[]{:S(2)}) copy-start(s32[4,9]{1,0:T(4,128)} %lon_ref.5) | copy-start | bytes 436
  0.0 13.7 %copy-start.5 = (s32[4,9]{1,0:T(4,128)S(1)}, s32[4,9]{1,0:T(4,128)}, u32[]{:S(2)}) copy-start(s32[4,9]{1,0:T(4,128)} %basis_ref.5) | copy-start | bytes 436
  0.0 13.7 %copy-start.6 = (f32[4,9]{1,0:T(4,128)S(1)}, f32[4,9]{1,0:T(4,128)}, u32[]{:S(2)}) copy-start(f32[4,9]{1,0:T(4,128)} %value_ref.5) | copy-start | bytes 436
  4.3 9.3 %collective-permute-start = (bf16[64,1440]{1,0:T(8,128)(2,1)}, bf16[64,1440]{1,0:T(8,128)(2,1)S(1)}, u32[]{:S(2)}, u32[]{:S(2)}) collective-permute-start(bf16[64,1440]{1,0:T(8,128)(2,1)} %get-tuple-element.19), channel_id=1, source_target_pairs={{0,16},{16,0},{1,17},{17,1},{2,18},{18,2},{3,19},{19,3},{4,20},{20... | collective-permute-start | bytes 552968 | tf_op jit(solution)/shard_map/ppermute | solution.py:366
  7.3 9.2 %collective-permute-start.2 = (bf16[128,384]{1,0:T(8,128)(2,1)}, bf16[128,384]{1,0:T(8,128)(2,1)S(1)}, u32[]{:S(2)}, u32[]{:S(2)}) collective-permute-start(bf16[128,384]{1,0:T(8,128)(2,1)} %get-tuple-element.21), channel_id=1, source_target_pairs={{0,4},{4,8},{8,12},{12,0},{1,5},{5,9},{9,13},{13,1},{2,6},{6,10},{... | collective-permute-start | bytes 294920 | tf_op jit(solution)/shard_map/ppermute | solution.py:306
  8.9 11.3 %collective-permute-start.3 = (bf16[128,384]{1,0:T(8,128)(2,1)}, bf16[128,384]{1,0:T(8,128)(2,1)S(1)}, u32[]{:S(2)}, u32[]{:S(2)}) collective-permute-start(bf16[128,384]{1,0:T(8,128)(2,1)} %get-tuple-element.22), channel_id=1, source_target_pairs={{0,8},{4,12},{8,0},{12,4},{1,9},{5,13},{9,1},{13,5},{2,10},{6,14},... | collective-permute-start | bytes 294920 | tf_op jit(solution)/shard_map/ppermute | solution.py:306
  11.5 11.7 %collective-permute-start.4 = (bf16[128,384]{1,0:T(8,128)(2,1)}, bf16[128,384]{1,0:T(8,128)(2,1)S(1)}, u32[]{:S(2)}, u32[]{:S(2)}) collective-permute-start(bf16[128,384]{1,0:T(8,128)(2,1)} %get-tuple-element.23), channel_id=1, source_target_pairs={{0,12},{4,0},{8,4},{12,8},{1,13},{5,1},{9,5},{13,9},{2,14},{6,2},{... | collective-permute-start | bytes 294920 | tf_op jit(solution)/shard_map/ppermute | solution.py:306
  12.8 10.3 %collective-permute-start.1 = (bf16[64,1440]{1,0:T(8,128)(2,1)}, bf16[64,1440]{1,0:T(8,128)(2,1)S(1)}, u32[]{:S(2)}, u32[]{:S(2)}) collective-permute-start(bf16[64,1440]{1,0:T(8,128)(2,1)} %get-tuple-element.20), channel_id=1, source_target_pairs={{0,16},{16,0},{1,17},{17,1},{2,18},{18,2},{3,19},{19,3},{4,20},{20... | collective-permute-start | bytes 552968 | tf_op jit(solution)/shard_map/ppermute | solution.py:366
  15.8 11.3 %collective-permute-start.8 = (bf16[64,384]{1,0:T(8,128)(2,1)S(1)}, bf16[64,384]{1,0:T(8,128)(2,1)S(1)}, u32[]{:S(2)}, u32[]{:S(2)}) collective-permute-start(bf16[64,384]{1,0:T(8,128)(2,1)S(1)} %get-tuple-element.30), channel_id=1, source_target_pairs={{0,4},{4,8},{8,12},{12,0},{1,5},{5,9},{9,13},{13,1},{2,6},{6,10},{... | collective-permute-start | bytes 147464 | tf_op jit(solution)/shard_map/ppermute | solution.py:306
  16.5 13.9 %collective-permute-start.9 = (bf16[64,384]{1,0:T(8,128)(2,1)S(1)}, bf16[64,384]{1,0:T(8,128)(2,1)S(1)}, u32[]{:S(2)}, u32[]{:S(2)}) collective-permute-start(bf16[64,384]{1,0:T(8,128)(2,1)S(1)} %get-tuple-element.31), channel_id=1, source_target_pairs={{0,8},{4,12},{8,0},{12,4},{1,9},{5,13},{9,1},{13,5},{2,10},{6,14},... | collective-permute-start | bytes 147464 | tf_op jit(solution)/shard_map/ppermute | solution.py:306
  20.1 5.7 %copy-start.7 = (bf16[4,64,384]{2,1,0:T(8,128)(2,1)S(1)}, bf16[4,64,384]{2,1,0:T(8,128)(2,1)}, u32[]{:S(2)}) copy-start(bf16[4,64,384]{2,1,0:T(8,128)(2,1)} %constant.21.clone.rest_6_) | copy-start | bytes 589828
  20.1 5.8 %copy-start.9 = (bf16[128,384]{1,0:T(8,128)(2,1)S(1)}, bf16[128,384]{1,0:T(8,128)(2,1)}, u32[]{:S(2)}) copy-start(bf16[128,384]{1,0:T(8,128)(2,1)} %get-tuple-element.28.rest_0_) | copy-start | bytes 294916
  20.1 10.2 %collective-permute-start.10 = (bf16[64,384]{1,0:T(8,128)(2,1)S(1)}, bf16[64,384]{1,0:T(8,128)(2,1)S(1)}, u32[]{:S(2)}, u32[]{:S(2)}) collective-permute-start(bf16[64,384]{1,0:T(8,128)(2,1)S(1)} %get-tuple-element.32), channel_id=1, source_target_pairs={{0,12},{4,0},{8,4},{12,8},{1,13},{5,1},{9,5},{13,9},{2,14},{6,2},{... | collective-permute-start | bytes 147464 | tf_op jit(solution)/shard_map/ppermute | solution.py:306
  25.3 6.0 %collective-permute-start.5 = (bf16[64,384]{1,0:T(8,128)(2,1)S(1)}, bf16[64,384]{1,0:T(8,128)(2,1)S(1)}, u32[]{:S(2)}, u32[]{:S(2)}) collective-permute-start(bf16[64,384]{1,0:T(8,128)(2,1)S(1)} %get-tuple-element.25), channel_id=1, source_target_pairs={{0,4},{4,8},{8,12},{12,0},{1,5},{5,9},{9,13},{13,1},{2,6},{6,10},{... | collective-permute-start | bytes 147464 | tf_op jit(solution)/shard_map/ppermute | solution.py:306
  25.3 5.9 %collective-permute-start.6 = (bf16[64,384]{1,0:T(8,128)(2,1)S(1)}, bf16[64,384]{1,0:T(8,128)(2,1)S(1)}, u32[]{:S(2)}, u32[]{:S(2)}) collective-permute-start(bf16[64,384]{1,0:T(8,128)(2,1)S(1)} %get-tuple-element.26), channel_id=1, source_target_pairs={{0,8},{4,12},{8,0},{12,4},{1,9},{5,13},{9,1},{13,5},{2,10},{6,14},... | collective-permute-start | bytes 147464 | tf_op jit(solution)/shard_map/ppermute | solution.py:306
  27.1 5.9 %collective-permute-start.7 = (bf16[64,384]{1,0:T(8,128)(2,1)S(1)}, bf16[64,384]{1,0:T(8,128)(2,1)S(1)}, u32[]{:S(2)}, u32[]{:S(2)}) collective-permute-start(bf16[64,384]{1,0:T(8,128)(2,1)S(1)} %get-tuple-element.27), channel_id=1, source_target_pairs={{0,12},{4,0},{8,4},{12,8},{1,13},{5,1},{9,5},{13,9},{2,14},{6,2},{... | collective-permute-start | bytes 147464 | tf_op jit(solution)/shard_map/ppermute | solution.py:306
  33.0 6.1 %copy-start.2 = (bf16[3,384,8]{1,2,0:T(8,128)(2,1)S(1)}, bf16[3,384,8]{1,2,0:T(8,128)(2,1)}, u32[]{:S(2)}) copy-start(bf16[3,384,8]{1,2,0:T(8,128)(2,1)} %param.19) | copy-start | bytes 55300
  33.0 6.1 %copy-start.8 = (bf16[8,256]{1,0:T(8,128)(2,1)S(1)}, bf16[8,256]{1,0:T(8,128)(2,1)}, u32[]{:S(2)}) copy-start(bf16[8,256]{1,0:T(8,128)(2,1)} %constant.22.clone.spread_ref) | copy-start | bytes 12292
  34.5 12.1 %all-to-all-start = ((bf16[8,32,256]{2,1,0:T(8,128)(2,1)}), bf16[8,32,256]{2,1,0:T(8,128)(2,1)S(1)}, u32[]{:S(2)}, u32[]{:S(2)}) async-start(bf16[8,32,256]{2,1,0:T(8,128)(2,1)} %mlp_rows.5), calls=%async_computation | async-start | bytes 262144 | tf_op jit(solution)/shard_map/all_to_all | solution.py:386

commit v7 on v3

--- a/solution.py
+++ b/solution.py
@@ -23,6 +23,7 @@
 
 SMEM = pl.BlockSpec(memory_space=pltpu.SMEM)
 VMEM = pl.BlockSpec(memory_space=pltpu.VMEM)
+ANY = pl.BlockSpec(memory_space=pl.ANY)
 HBM = pl.BlockSpec(memory_space=pltpu.HBM)
 
 
@@ -35,19 +36,37 @@
 
 
 def takes(micros):
-    return pl.CostEstimate(flops=micros * FLOPS_PER_US, bytes_accessed=0, transcendentals=0)
+    return pl.CostEstimate(flops=int(micros * FLOPS_PER_US), bytes_accessed=0, transcendentals=0)
+
+
+def edge_kernel(start_ref, fields_ref, out_ref, sem):
+    copy = pltpu.make_async_copy(fields_ref.at[pl.ds(start_ref[0], HALO)], out_ref, sem)
+    copy.start()
+    copy.wait()
+
+
+def edge_rows(start, fields):
+    return pl.pallas_call(
+        edge_kernel,
+        out_shape=jax.ShapeDtypeStruct((HALO, *fields.shape[1:]), fields.dtype),
+        in_specs=[SMEM, ANY],
+        out_specs=ANY,
+        scratch_shapes=[pltpu.SemaphoreType.DMA],
+        compiler_params=params(56),
+        cost_estimate=takes(1),
+        name="edge_rows",
+    )(start, fields)
 
 
 def conv_kernel(
-    has_edge, pair_ref, place_ref, lat_ref, lon_ref, basis_ref, value_ref, fields_ref, *rest
+    chunks, picks, has_edge, after, pair_ref, place_ref, lat_ref, lon_ref, basis_ref, value_ref, fields_ref, *rest
 ):
     if has_edge:
         edge_ref, weight_ref, *rest = rest
     else:
         edge_ref, (weight_ref, *rest) = None, rest
-    *out_refs, rows_ref, taps_ref, filt_ref = rest
+    *out_refs, rows_ref, taps_ref, filt_ref = rest[after:]
     own, _, lon = fields_ref.shape
-    chunks = len(out_refs)
     chunk = lon // chunks
     width = out_refs[0].shape[1]
     total = rows_ref.shape[2]
@@ -73,11 +92,11 @@
             rows_ref[edge_at + row] = jnp.zeros(rows_ref.shape[1:], rows_ref.dtype)
 
     lane = lax.broadcasted_iota(jnp.int32, (G, LANES), 1)
-    begins = [LANES + chunk * lax.rem(place_ref[0] + k, chunks) for k in range(chunks)]
+    begins = [LANES + chunk * lax.rem(place_ref[0] + k, chunks) for k in picks]
 
     def fill(slot, tap, source, offset):
-        for k in range(chunks):
-            begin = begins[k] + offset
+        for k, origin in enumerate(begins):
+            begin = origin + offset
             first = lax.div(begin, LANES)
             shift = lax.rem(begin, LANES)
             back = lax.rem(LANES - shift, LANES)
@@ -115,35 +134,36 @@
         mixed = jnp.dot(filt_ref[i], taps_ref[i], preferred_element_type=jnp.float32).astype(
             jnp.bfloat16
         )
-        for k in range(chunks):
+        for k in range(len(picks)):
             out_refs[k][i * G : (i + 1) * G, :] = mixed[:, k * width : (k + 1) * width]
 
 
-def conv_rows(pair, place, supports, fields, edge, weight, chunks):
+def conv_rows(pair, place, supports, fields, edge, weight, chunks, picks, after, roomy):
     own, chans, lon = fields.shape
     width = ceil_to(lon // chunks, LANES)
     highest = (LANES + lon - lon // chunks + DLON) // LANES
     total = (highest + 1) * LANES + width
     arrays = [fields] + ([] if edge is None else [edge]) + [weight]
     return pl.pallas_call(
-        functools.partial(conv_kernel, edge is not None),
-        out_shape=[jax.ShapeDtypeStruct((2 * chans, width), jnp.bfloat16)] * chunks,
-        in_specs=[SMEM] * 6 + [VMEM] * len(arrays),
-        out_specs=[VMEM] * chunks,
+        functools.partial(conv_kernel, chunks, picks, edge is not None, len(after)),
+        out_shape=[jax.ShapeDtypeStruct((2 * chans, width), jnp.bfloat16)] * len(picks),
+        in_specs=[SMEM] * 6 + [VMEM] * len(arrays) + [ANY] * len(after),
+        out_specs=[VMEM] * len(picks),
         scratch_shapes=[
             pltpu.VMEM((own + HALO, chans, total), jnp.bfloat16),
-            pltpu.VMEM((2, TAPS * G, chunks * width), jnp.bfloat16),
+            pltpu.VMEM((2, TAPS * G, len(picks) * width), jnp.bfloat16),
             pltpu.VMEM((2, G, TAPS * G), jnp.bfloat16),
         ],
-        compiler_params=params(56 if edge is None else 20),
-        cost_estimate=takes(4),
+        compiler_params=params(56 if roomy else 20),
+        cost_estimate=takes(1 if len(picks) > 1 else 0.2),
         name="conv_rows",
-    )(pair, place, *supports, *arrays)
-
-
-def mlp_kernel(parts, last, place_ref, *rest):
+    )(pair, place, *supports, *arrays, *after)
+
+
+def mlp_kernel(parts, last, after, place_ref, *rest):
     blocks, rest = rest[:parts], rest[parts:]
     up_ref, down_ref, table_ref, *rest = rest
+    rest = rest[after:]
     if last:
         earlier_ref, out_ref, cells_ref = rest
     else:
@@ -184,20 +204,23 @@
         out_ref[...] = block
 
 
-def mlp_rows(place, blocks, up, down, tables, earlier, dests):
+def mlp_rows(place, blocks, up, down, tables, earlier, dests, after):
     pair_chans, width = blocks[0].shape
     chan = len(blocks) * pair_chans // 2
     last = earlier is not None
-    arrays = [*blocks, up, down, tables] + ([earlier] if last else [])
+    arrays = [*blocks, up, down, tables, *after] + ([earlier] if last else [])
     rows = (4 if last else 2) * SLOT
     return pl.pallas_call(
-        functools.partial(mlp_kernel, len(blocks), last),
+        functools.partial(mlp_kernel, len(blocks), last, len(after)),
         out_shape=jax.ShapeDtypeStruct((dests, rows, chan), jnp.bfloat16),
-        in_specs=[SMEM] + [VMEM] * len(arrays),
+        in_specs=[SMEM]
+        + [VMEM] * (len(blocks) + 3)
+        + [ANY] * len(after)
+        + [VMEM] * last,
         out_specs=VMEM,
         scratch_shapes=[pltpu.VMEM((chan, 2 * width), jnp.bfloat16)],
         compiler_params=params(20 if dests <= FEW else 40),
-        cost_estimate=takes(2),
+        cost_estimate=takes(1),
         name="mlp_rows",
     )(place, *arrays)
 
@@ -232,7 +255,7 @@
         ],
         out_specs=pl.BlockSpec((1, 2, degrees, depth), lambda m: (m, 0, 0, 0)),
         compiler_params=params(10 if depth <= 512 else 48),
-        cost_estimate=takes(2),
+        cost_estimate=takes(0.2),
         name="expand",
     )(start, legendre, spread)
 
@@ -312,7 +335,7 @@
     two_bands = num_lat == 2
     cells = jnp.swapaxes(fields, 1, 2)
     if two_bands:
-        edge_out = lax.dynamic_slice_in_dim(cells, HALO * (1 - band), HALO, axis=0)
+        edge_out = edge_rows(scalar(HALO * (1 - band)), cells)
         edges = [None, lax.ppermute(edge_out, "lat", [(0, 1), (1, 0)])]
         pairs = [band, 1 - band]
     else:
@@ -337,14 +360,20 @@
     left = expand(scalar(index * mode_dev), jnp.swapaxes(legendre, 1, 2), jnp.asarray(spread))
 
     received = []
+    after = [edge_out] if two_bands else []
     for edge, pair in zip(edges, pairs):
-        mixed = conv_rows(scalar(pair), place, supports, cells, edge, disco_weight, num_chan)
+        shared = (scalar(pair), place, supports, cells, edge, disco_weight, num_chan)
+        sent = conv_rows(*shared, tuple(range(1, num_chan)), after, edge is None)
+        kept = conv_rows(*shared, (0,), sent[:1], False)
         received.append(
-            [mixed[0]] + [turn(mixed[k], "chan", num_chan, k) for k in range(1, num_chan)]
+            list(kept) + [turn(block, "chan", num_chan, k + 1) for k, block in enumerate(sent)]
         )
+        after = kept
     spectrum = None
+    after = list(after)
     for blocks in received:
-        spectrum = mlp_rows(place, blocks, up, down, tables, spectrum, dests)
+        spectrum = mlp_rows(place, blocks, up, down, tables, spectrum, dests, after)
+        after = []
 
     both = ("lat", "chan")
     gathered = lax.all_to_all(spectrum, both, split_axis=0, concat_axis=0, tiled=True)

time: 43.2 us -> 54.7 us (1.27)
  Pallas kernels: 12.3 us -> 27.3 us
  starting transfers between devices: 18.1 us -> 15.3 us
  waiting for transfers between devices: 11 us -> 10.4 us
    pallas_call x4 -> x7, Pallas kernels: 10.2 us -> 25.1 us  [the longest x1 13 us: edge_rows(): pl.pallas_call(edge_kernel, out_shape=jax.ShapeDtypeStruct((HALO, *fields...]
    ppermute x6, starting transfers between devices: 10.3 us -> 8.62 us  [turn(): lax.ppermute(block, axis, [(i, (i + step) % count) for i in range(count)])]
    all_to_all x1, starting transfers between devices: 4.73 us -> 3.67 us  [on_device(): lax.all_to_all(spectrum, both, split_axis=0, concat_axis=0, tiled=True)]
    dynamic_slice x1 -> x0, local copies, waits for them, and re-layouts: 1.02 us -> none  [on_device(): edge_out = lax.dynamic_slice_in_dim(cells, HALO * (1 - band), HALO, axis=0)]
    unnamed x26, local copies, waits for them, and re-layouts: 0.33 us -> 1.22 us
    ppermute x6, waiting for transfers between devices: 4.36 us -> 3.76 us  [turn(): lax.ppermute(block, axis, [(i, (i + step) % count) for i in range(count)])]
  transfers between devices with their start and end apart: 8 -> 8, of which waited for: 3 -> 3; matrix products, arithmetic and copies ran while one was open for 1% -> 1% of each run, Pallas kernels for 21% -> 20%
where the time goes in v7:
time: 54.7 us; the launch traced here: 54.5 us
  Pallas kernels  27.3 us (50%)
  starting transfers between devices  15.3 us (28%)
  waiting for transfers between devices  10.4 us (19%)
  local copies, waits for them, and re-layouts  1.22 us (2%)
    pallas_call x1, Pallas kernels, edge_rows(): pl.pallas_call(edge_kernel, out_shape=jax.ShapeDtypeStruct((HALO, *fields...  13 us
    pallas_call x4, Pallas kernels, conv_rows(): pl.pallas_call(functools.partial(conv_kernel, chunks, picks, edge is not...  9.14 us
    ppermute x6, starting transfers between devices, turn(): lax.ppermute(block, axis, [(i, (i + step) % count) for i in range(count)])  8.62 us
    all_to_all x1, waiting for transfers between devices, on_device(): lax.all_to_all(spectrum, both, split_axis=0, concat_axis=0, tiled=True)  6.68 us
    ppermute x6, waiting for transfers between devices, turn(): lax.ppermute(block, axis, [(i, (i + step) % count) for i in range(count)])  3.76 us
    all_to_all x1, starting transfers between devices, on_device(): lax.all_to_all(spectrum, both, split_axis=0, concat_axis=0, tiled=True)  3.67 us
    ppermute x1, starting transfers between devices, on_device(): edges = [None, lax.ppermute(edge_out, 'lat', [(0, 1), (1, 0)])]  3.03 us
    pallas_call x2, Pallas kernels, mlp_rows(): pl.pallas_call(functools.partial(mlp_kernel, len(blocks), last, len(after...  2.99 us
  transfers between devices with their start and end apart: 8, of which 3 were waited for; matrix products, arithmetic and copies ran while one was open for 1% of the time, Pallas kernels for 20%

profile of v7, /device:TPU:0, one launch (start us, length us, event | category | flops | bytes accessed | tf_op | source)
XLA Modules:
  0.0 54.5 jit_solution(2236115805828118497)
XLA Ops:
  0.0 13.0 %edge_rows.1.rest_1_ = bf16[2,64,1440]{2,1,0:T(8,128)(2,1)} custom-call(s32[1]{0:T(128)} %bitcast.5.start_ref, bf16[4,64,1440]{2,1,0:T(8,128)(2,1)} %bitcast.10), custom_call_target="tpu_custom_call" | custom-call | flops 1000000000 | tf_op jit(solution)/shard_map/edge_rows/pallas_call | solution.py:49
  13.0 3.0 %collective-permute-start = (bf16[2,64,1440]{2,1,0:T(8,128)(2,1)}, bf16[2,64,1440]{2,1,0:T(8,128)(2,1)S(1)}, u32[]{:S(2)}, u32[]{:S(2)}) collective-permute-start(bf16[2,64,1440]{2,1,0:T(8,128)(2,1)} %edge_rows.1.rest_1_), channel_id=1, source_target_pairs={{0,16},{16,0},{1,17},{17,1},{2,18},{18,2},{3,19},{19,3},{4,20},{20... | collective-permute-start | bytes 1105928 | tf_op jit(solution)/shard_map/ppermute | solution.py:339
  16.1 0.0 copy-start.6
  16.1 0.0 copy-start.7
  16.1 0.0 copy-start.10
  16.1 0.0 copy-start.11
  16.1 3.7 %conv_rows.4 = (bf16[128,384]{1,0:T(8,128)(2,1)}, bf16[128,384]{1,0:T(8,128)(2,1)}, bf16[128,384]{1,0:T(8,128)(2,1)}) custom-call(s32[1]{0:T(128)} %bitcast.6.pair_ref, s32[1]{0:T(128)} %bitcast.2.place_ref, s32[4,9]{1,0:T(4,128)} %lat_ref.7, s32[4,9]{1,0:T(4,128)} %lon_ref.7, s32[4,9]{1,0:T(4,128)} %basis_ref.7, f32[4,9]{1,0:T(4,128)} %value_ref.7, ...), custom_call_target="tpu_custom_call" | custom-call | flops 1000000000 | tf_op jit(solution)/shard_map/conv_rows/pallas_call | solution.py:147
  19.8 2.6 %collective-permute-start.5 = (bf16[128,384]{1,0:T(8,128)(2,1)}, bf16[128,384]{1,0:T(8,128)(2,1)S(1)}, u32[]{:S(2)}, u32[]{:S(2)}) collective-permute-start(bf16[128,384]{1,0:T(8,128)(2,1)} %get-tuple-element.15), channel_id=1, source_target_pairs={{0,8},{4,12},{8,0},{12,4},{1,9},{5,13},{9,1},{13,5},{2,10},{6,14},... | collective-permute-start | bytes 294920 | tf_op jit(solution)/shard_map/ppermute | solution.py:306
  22.4 1.4 %collective-permute-start.6 = (bf16[128,384]{1,0:T(8,128)(2,1)}, bf16[128,384]{1,0:T(8,128)(2,1)S(1)}, u32[]{:S(2)}, u32[]{:S(2)}) collective-permute-start(bf16[128,384]{1,0:T(8,128)(2,1)} %get-tuple-element.16), channel_id=1, source_target_pairs={{0,12},{4,0},{8,4},{12,8},{1,13},{5,1},{9,5},{13,9},{2,14},{6,2},{... | collective-permute-start | bytes 294920 | tf_op jit(solution)/shard_map/ppermute | solution.py:306
  23.7 0.7 %collective-permute-start.4 = (bf16[128,384]{1,0:T(8,128)(2,1)}, bf16[128,384]{1,0:T(8,128)(2,1)S(1)}, u32[]{:S(2)}, u32[]{:S(2)}) collective-permute-start(bf16[128,384]{1,0:T(8,128)(2,1)} %get-tuple-element.11.rest_1_), channel_id=1, source_target_pairs={{0,4},{4,8},{8,12},{12,0},{1,5},{5,9},{9,13},{13,1},{2,6},{6,10},{... | collective-permute-start | bytes 294920 | tf_op jit(solution)/shard_map/ppermute | solution.py:306
  24.4 0.9 %copy-done.2 = bf16[128,384]{1,0:T(8,128)(2,1)S(1)} copy-done((bf16[128,384]{1,0:T(8,128)(2,1)S(1)}, bf16[128,384]{1,0:T(8,128)(2,1)}, u32[]{:S(2)}) %copy-start.2) | copy-done | bytes 98328
  25.3 1.5 %conv_rows.5.rest_2_.rest_0_ = bf16[128,384]{1,0:T(8,128)(2,1)S(1)} custom-call(s32[1]{0:T(128)} %bitcast.6.pair_ref, s32[1]{0:T(128)} %bitcast.2.place_ref, s32[4,9]{1,0:T(4,128)S(1)} %copy-done.4, s32[4,9]{1,0:T(4,128)S(1)} %copy-done.5, s32[4,9]{1,0:T(4,128)S(1)} %copy-done.6, f32[4,9]{1,0:T(4,128)S(1)} %copy-done.7, bf16[4,64,1440]{2,1,0:T(8,128)(2,1)S(1)} %bitcast.12, ...), custom_call_target="tpu_custom_call" | custom-call | flops 200000000 | tf_op jit(solution)/shard_map/conv_rows/pallas_call | solution.py:147
  26.9 0.1 copy.12
  27.0 0.1 copy.13
  27.1 0.0 collective-permute-done.rest_0_
  27.2 2.4 %conv_rows.6 = (bf16[128,384]{1,0:T(8,128)(2,1)S(1)}, bf16[128,384]{1,0:T(8,128)(2,1)S(1)}, bf16[128,384]{1,0:T(8,128)(2,1)S(1)}) custom-call(s32[1]{0:T(128)} %bitcast.3.pair_ref, s32[1]{0:T(128)} %bitcast.2.place_ref, s32[4,9]{1,0:T(4,128)S(1)} %copy-done.4, s32[4,9]{1,0:T(4,128)S(1)} %copy-done.5, s32[4,9]{1,0:T(4,128)S(1)} %copy-done.6, ...), custom_call_target="tpu_custom_call" | custom-call | flops 1000000000 | tf_op jit(solution)/shard_map/conv_rows/pallas_call | solution.py:147
  29.6 0.0 copy-start.9
  29.6 1.1 %collective-permute-start.2 = (bf16[128,384]{1,0:T(8,128)(2,1)S(1)}, bf16[128,384]{1,0:T(8,128)(2,1)S(1)}, u32[]{:S(2)}, u32[]{:S(2)}) collective-permute-start(bf16[128,384]{1,0:T(8,128)(2,1)S(1)} %get-tuple-element.13), channel_id=1, source_target_pairs={{0,8},{4,12},{8,0},{12,4},{1,9},{5,13},{9,1},{13,5},{2,10},{6,14},... | collective-permute-start | bytes 294920 | tf_op jit(solution)/shard_map/ppermute | solution.py:306
  30.7 2.9 %collective-permute-start.3 = (bf16[128,384]{1,0:T(8,128)(2,1)S(1)}, bf16[128,384]{1,0:T(8,128)(2,1)S(1)}, u32[]{:S(2)}, u32[]{:S(2)}) collective-permute-start(bf16[128,384]{1,0:T(8,128)(2,1)S(1)} %get-tuple-element.14), channel_id=1, source_target_pairs={{0,12},{4,0},{8,4},{12,8},{1,13},{5,1},{9,5},{13,9},{2,14},{6,2},{... | collective-permute-start | bytes 294920 | tf_op jit(solution)/shard_map/ppermute | solution.py:306
  33.6 0.0 collective-permute-done.5.rest_2_
  33.6 1.5 %conv_rows.7.rest_7_.rest_0_ = bf16[128,384]{1,0:T(8,128)(2,1)S(1)} custom-call(s32[1]{0:T(128)} %bitcast.3.pair_ref, s32[1]{0:T(128)} %bitcast.2.place_ref, s32[4,9]{1,0:T(4,128)S(1)} %copy-done.4, s32[4,9]{1,0:T(4,128)S(1)} %copy-done.5, s32[4,9]{1,0:T(4,128)S(1)} %copy-done.6, f32[4,9]{1,0:T(4,128)S(1)} %copy-done.7, bf16[4,64,1440]{2,1,0:T(8,128)(2,1)S(1)} %bitcast.14, ...), custom_call_target="tpu_custom_call" | custom-call | flops 200000000 | tf_op jit(solution)/shard_map/conv_rows/pallas_call | solution.py:147
  35.2 0.0 collective-permute-done.6.rest_3_
  35.2 1.2 %mlp_rows.2.rest_7_ = bf16[8,16,256]{2,1,0:T(8,128)(2,1)S(1)} custom-call(s32[1]{0:T(128)} %bitcast.2.place_ref, bf16[128,384]{1,0:T(8,128)(2,1)S(1)} %conv_rows.5.rest_2_.rest_0_, bf16[128,384]{1,0:T(8,128)(2,1)S(1)} %collective-permute-done.4.rest_1_, bf16[128,384]{1,0:T(8,128)(2,1)S(1)} %collective-permute-done.5.rest_2_, ...), custom_call_target="tpu_custom_call" | custom-call | flops 1000000000 | tf_op jit(solution)/shard_map/mlp_rows/pallas_call | solution.py:213
  36.4 0.0 copy-start.3
  36.4 0.0 copy-start.8
  36.4 1.7 %collective-permute-done.2.rest_2_ = bf16[128,384]{1,0:T(8,128)(2,1)S(1)} collective-permute-done((bf16[128,384]{1,0:T(8,128)(2,1)S(1)}, bf16[128,384]{1,0:T(8,128)(2,1)S(1)}, u32[]{:S(2)}, u32[]{:S(2)}) %collective-permute-start.2) | collective-permute-done | bytes 98336 | tf_op jit(solution)/shard_map/ppermute | solution.py:306
  38.1 2.0 %collective-permute-done.1.rest_1_ = bf16[128,384]{1,0:T(8,128)(2,1)S(1)} collective-permute-done((bf16[128,384]{1,0:T(8,128)(2,1)S(1)}, bf16[128,384]{1,0:T(8,128)(2,1)S(1)}, u32[]{:S(2)}, u32[]{:S(2)}) %collective-permute-start.1) | collective-permute-done | bytes 98336 | tf_op jit(solution)/shard_map/ppermute | solution.py:306
  40.2 1.8 %mlp_rows.3 = bf16[8,32,256]{2,1,0:T(8,128)(2,1)} custom-call(s32[1]{0:T(128)} %bitcast.2.place_ref, bf16[128,384]{1,0:T(8,128)(2,1)S(1)} %conv_rows.7.rest_7_.rest_0_, bf16[128,384]{1,0:T(8,128)(2,1)S(1)} %collective-permute-done.1.rest_1_, bf16[128,384]{1,0:T(8,128)(2,1)S(1)} %collective-permute-done.2.rest_2_, ...), custom_call_target="tpu_custom_call" | custom-call | flops 1000000000 | tf_op jit(solution)/shard_map/mlp_rows/pallas_call | solution.py:213
  42.0 3.7 %all-to-all-start = ((bf16[8,32,256]{2,1,0:T(8,128)(2,1)}), bf16[8,32,256]{2,1,0:T(8,128)(2,1)S(1)}, u32[]{:S(2)}, u32[]{:S(2)}) async-start(bf16[8,32,256]{2,1,0:T(8,128)(2,1)} %mlp_rows.3), calls=%async_computation | async-start | bytes 262144 | tf_op jit(solution)/shard_map/all_to_all | solution.py:379
  45.7 0.8 %expand.1.left_ref = bf16[3,2,384,256]{3,2,1,0:T(8,128)(2,1)S(1)} custom-call(s32[1]{0:T(128)} %bitcast.start_ref, bf16[3,8,384]{2,1,0:T(8,128)(2,1)S(1)} %bitcast.20, bf16[8,256]{1,0:T(8,128)(2,1)S(1)} %copy-done.8), custom_call_target="tpu_custom_call" | custom-call | flops 200000000 | tf_op jit(solution)/shard_map/expand/pallas_call | solution.py:247
  46.5 6.7 %all-to-all-done = bf16[8,32,256]{2,1,0:T(8,128)(2,1)S(1)} async-done(((bf16[8,32,256]{2,1,0:T(8,128)(2,1)}), bf16[8,32,256]{2,1,0:T(8,128)(2,1)S(1)}, u32[]{:S(2)}, u32[]{:S(2)}) %all-to-all-start) | async-done | bytes 131104 | tf_op jit(solution)/shard_map/all_to_all | solution.py:379
  53.2 1.3 %final_sum.1 = bf16[3,384,512]{2,1,0:T(8,128)(2,1)} custom-call(bf16[3,2,384,256]{3,2,1,0:T(8,128)(2,1)S(1)} %expand.1.left_ref, bf16[256,256]{1,0:T(8,128)(2,1)S(1)} %bitcast.19), custom_call_target="tpu_custom_call" | custom-call | flops 1000000000 | tf_op jit(solution)/shard_map/final_sum/pallas_call | solution.py:281
  (19 shorter events, 0.0 us)
Async XLA Ops:
  13.0 14.1 %collective-permute-start = (bf16[2,64,1440]{2,1,0:T(8,128)(2,1)}, bf16[2,64,1440]{2,1,0:T(8,128)(2,1)S(1)}, u32[]{:S(2)}, u32[]{:S(2)}) collective-permute-start(bf16[2,64,1440]{2,1,0:T(8,128)(2,1)} %edge_rows.1.rest_1_), channel_id=1, source_target_pairs={{0,16},{16,0},{1,17},{17,1},{2,18},{18,2},{3,19},{19,3},{4,20},{20... | collective-permute-start | bytes 1105928 | tf_op jit(solution)/shard_map/ppermute | solution.py:339
  16.1 8.3 %copy-start = (bf16[4,1440,64]{1,2,0:T(8,128)(2,1)S(1)}, bf16[4,1440,64]{1,2,0:T(8,128)(2,1)}, u32[]{:S(2)}) copy-start(bf16[4,1440,64]{1,2,0:T(8,128)(2,1)} %param.11) | copy-start | bytes 2211844
  16.1 8.3 %copy-start.1 = (bf16[6,64,64]{2,1,0:T(8,128)(2,1)S(1)}, bf16[6,64,64]{2,1,0:T(8,128)(2,1)}, u32[]{:S(2)}) copy-start(bf16[6,64,64]{2,1,0:T(8,128)(2,1)} %rest_1_.3) | copy-start | bytes 147460
  16.1 8.3 %copy-start.4 = (s32[4,9]{1,0:T(4,128)S(1)}, s32[4,9]{1,0:T(4,128)}, u32[]{:S(2)}) copy-start(s32[4,9]{1,0:T(4,128)} %lat_ref.7) | copy-start | bytes 436
  16.1 8.3 %copy-start.5 = (s32[4,9]{1,0:T(4,128)S(1)}, s32[4,9]{1,0:T(4,128)}, u32[]{:S(2)}) copy-start(s32[4,9]{1,0:T(4,128)} %lon_ref.7) | copy-start | bytes 436
  16.1 8.3 %copy-start.6 = (s32[4,9]{1,0:T(4,128)S(1)}, s32[4,9]{1,0:T(4,128)}, u32[]{:S(2)}) copy-start(s32[4,9]{1,0:T(4,128)} %basis_ref.7) | copy-start | bytes 436
  16.1 8.3 %copy-start.7 = (f32[4,9]{1,0:T(4,128)S(1)}, f32[4,9]{1,0:T(4,128)}, u32[]{:S(2)}) copy-start(f32[4,9]{1,0:T(4,128)} %value_ref.7) | copy-start | bytes 436
  16.1 10.7 %copy-start.10 = (bf16[256,512]{1,0:T(8,128)(2,1)S(1)}, bf16[256,512]{1,0:T(8,128)(2,1)}, u32[]{:S(2)}) copy-start(bf16[256,512]{1,0:T(8,128)(2,1)} %param.17) | copy-start | bytes 786436
  16.1 10.9 %copy-start.11 = (bf16[512,256]{1,0:T(8,128)(2,1)S(1)}, bf16[512,256]{1,0:T(8,128)(2,1)}, u32[]{:S(2)}) copy-start(bf16[512,256]{1,0:T(8,128)(2,1)} %param.18) | copy-start | bytes 786436
  19.8 13.9 %collective-permute-start.5 = (bf16[128,384]{1,0:T(8,128)(2,1)}, bf16[128,384]{1,0:T(8,128)(2,1)S(1)}, u32[]{:S(2)}, u32[]{:S(2)}) collective-permute-start(bf16[128,384]{1,0:T(8,128)(2,1)} %get-tuple-element.15), channel_id=1, source_target_pairs={{0,8},{4,12},{8,0},{12,4},{1,9},{5,13},{9,1},{13,5},{2,10},{6,14},... | collective-permute-start | bytes 294920 | tf_op jit(solution)/shard_map/ppermute | solution.py:306
  22.4 12.8 %collective-permute-start.6 = (bf16[128,384]{1,0:T(8,128)(2,1)}, bf16[128,384]{1,0:T(8,128)(2,1)S(1)}, u32[]{:S(2)}, u32[]{:S(2)}) collective-permute-start(bf16[128,384]{1,0:T(8,128)(2,1)} %get-tuple-element.16), channel_id=1, source_target_pairs={{0,12},{4,0},{8,4},{12,8},{1,13},{5,1},{9,5},{13,9},{2,14},{6,2},{... | collective-permute-start | bytes 294920 | tf_op jit(solution)/shard_map/ppermute | solution.py:306
  23.7 11.5 %collective-permute-start.4 = (bf16[128,384]{1,0:T(8,128)(2,1)}, bf16[128,384]{1,0:T(8,128)(2,1)S(1)}, u32[]{:S(2)}, u32[]{:S(2)}) collective-permute-start(bf16[128,384]{1,0:T(8,128)(2,1)} %get-tuple-element.11.rest_1_), channel_id=1, source_target_pairs={{0,4},{4,8},{8,12},{12,0},{1,5},{5,9},{9,13},{13,1},{2,6},{6,10},{... | collective-permute-start | bytes 294920 | tf_op jit(solution)/shard_map/ppermute | solution.py:306
  24.4 0.9 %copy-start.2 = (bf16[128,384]{1,0:T(8,128)(2,1)S(1)}, bf16[128,384]{1,0:T(8,128)(2,1)}, u32[]{:S(2)}) copy-start(bf16[128,384]{1,0:T(8,128)(2,1)} %get-tuple-element.11.rest_1_) | copy-start | bytes 294916
  29.6 5.6 %copy-start.9 = (bf16[4,64,384]{2,1,0:T(8,128)(2,1)S(1)}, bf16[4,64,384]{2,1,0:T(8,128)(2,1)}, u32[]{:S(2)}) copy-start(bf16[4,64,384]{2,1,0:T(8,128)(2,1)} %constant.23.clone.rest_6_) | copy-start | bytes 589828
  29.6 8.5 %collective-permute-start.2 = (bf16[128,384]{1,0:T(8,128)(2,1)S(1)}, bf16[128,384]{1,0:T(8,128)(2,1)S(1)}, u32[]{:S(2)}, u32[]{:S(2)}) collective-permute-start(bf16[128,384]{1,0:T(8,128)(2,1)S(1)} %get-tuple-element.13), channel_id=1, source_target_pairs={{0,8},{4,12},{8,0},{12,4},{1,9},{5,13},{9,1},{13,5},{2,10},{6,14},... | collective-permute-start | bytes 294920 | tf_op jit(solution)/shard_map/ppermute | solution.py:306
  30.7 7.4 %collective-permute-start.3 = (bf16[128,384]{1,0:T(8,128)(2,1)S(1)}, bf16[128,384]{1,0:T(8,128)(2,1)S(1)}, u32[]{:S(2)}, u32[]{:S(2)}) collective-permute-start(bf16[128,384]{1,0:T(8,128)(2,1)S(1)} %get-tuple-element.14), channel_id=1, source_target_pairs={{0,12},{4,0},{8,4},{12,8},{1,13},{5,1},{9,5},{13,9},{2,14},{6,2},{... | collective-permute-start | bytes 294920 | tf_op jit(solution)/shard_map/ppermute | solution.py:306
  33.6 6.5 %collective-permute-start.1 = (bf16[128,384]{1,0:T(8,128)(2,1)S(1)}, bf16[128,384]{1,0:T(8,128)(2,1)S(1)}, u32[]{:S(2)}, u32[]{:S(2)}) collective-permute-start(bf16[128,384]{1,0:T(8,128)(2,1)S(1)} %get-tuple-element.12.rest_2_), channel_id=1, source_target_pairs={{0,4},{4,8},{8,12},{12,0},{1,5},{5,9},{9,13},{13,1},{2,6},{6,10},{... | collective-permute-start | bytes 294920 | tf_op jit(solution)/shard_map/ppermute | solution.py:306
  36.4 9.3 %copy-start.3 = (bf16[3,384,8]{1,2,0:T(8,128)(2,1)S(1)}, bf16[3,384,8]{1,2,0:T(8,128)(2,1)}, u32[]{:S(2)}) copy-start(bf16[3,384,8]{1,2,0:T(8,128)(2,1)} %param.19) | copy-start | bytes 55300
  36.4 9.3 %copy-start.8 = (bf16[8,256]{1,0:T(8,128)(2,1)S(1)}, bf16[8,256]{1,0:T(8,128)(2,1)}, u32[]{:S(2)}) copy-start(bf16[8,256]{1,0:T(8,128)(2,1)} %constant.24.clone.spread_ref) | copy-start | bytes 12292
  42.0 11.2 %all-to-all-start = ((bf16[8,32,256]{2,1,0:T(8,128)(2,1)}), bf16[8,32,256]{2,1,0:T(8,128)(2,1)S(1)}, u32[]{:S(2)}, u32[]{:S(2)}) async-start(bf16[8,32,256]{2,1,0:T(8,128)(2,1)} %mlp_rows.3), calls=%async_computation | async-start | bytes 262144 | tf_op jit(solution)/shard_map/all_to_all | solution.py:379

commit v8 on v7

--- a/solution.py
+++ b/solution.py
@@ -37,25 +37,6 @@
 
 def takes(micros):
     return pl.CostEstimate(flops=int(micros * FLOPS_PER_US), bytes_accessed=0, transcendentals=0)
-
-
-def edge_kernel(start_ref, fields_ref, out_ref, sem):
-    copy = pltpu.make_async_copy(fields_ref.at[pl.ds(start_ref[0], HALO)], out_ref, sem)
-    copy.start()
-    copy.wait()
-
-
-def edge_rows(start, fields):
-    return pl.pallas_call(
-        edge_kernel,
-        out_shape=jax.ShapeDtypeStruct((HALO, *fields.shape[1:]), fields.dtype),
-        in_specs=[SMEM, ANY],
-        out_specs=ANY,
-        scratch_shapes=[pltpu.SemaphoreType.DMA],
-        compiler_params=params(56),
-        cost_estimate=takes(1),
-        name="edge_rows",
-    )(start, fields)
 
 
 def conv_kernel(
@@ -335,7 +316,7 @@
     two_bands = num_lat == 2
     cells = jnp.swapaxes(fields, 1, 2)
     if two_bands:
-        edge_out = edge_rows(scalar(HALO * (1 - band)), cells)
+        edge_out = lax.dynamic_slice_in_dim(cells, HALO * (1 - band), HALO, axis=0)
         edges = [None, lax.ppermute(edge_out, "lat", [(0, 1), (1, 0)])]
         pairs = [band, 1 - band]
     else:
@@ -360,14 +341,13 @@
     left = expand(scalar(index * mode_dev), jnp.swapaxes(legendre, 1, 2), jnp.asarray(spread))
 
     received = []
-    after = [edge_out] if two_bands else []
+    after = []
     for edge, pair in zip(edges, pairs):
         shared = (scalar(pair), place, supports, cells, edge, disco_weight, num_chan)
         sent = conv_rows(*shared, tuple(range(1, num_chan)), after, edge is None)
-        kept = conv_rows(*shared, (0,), sent[:1], False)
-        received.append(
-            list(kept) + [turn(block, "chan", num_chan, k + 1) for k, block in enumerate(sent)]
-        )
+        moved = [turn(block, "chan", num_chan, k + 1) for k, block in enumerate(sent)]
+        kept = conv_rows(*shared, (0,), sent[-1:], False)
+        received.append([*kept, *moved])
         after = kept
     spectrum = None
     after = list(after)

time: 54.7 us -> 43.5 us (0.80)
  Pallas kernels: 27.3 us -> 14.2 us
  starting transfers between devices: 15.3 us -> 16.8 us
  local copies, waits for them, and re-layouts: 1.22 us -> 2.24 us
  waiting for transfers between devices: 10.4 us -> 9.68 us
    pallas_call x1 -> x0, Pallas kernels: 13 us -> none  [edge_rows(): pl.pallas_call(edge_kernel, out_shape=jax.ShapeDtypeStruct((HALO, *fields...]
    dynamic_slice x0 -> x1, local copies, waits for them, and re-layouts: none -> 1.02 us  [on_device(): edge_out = lax.dynamic_slice_in_dim(cells, HALO * (1 - band), HALO, axis=0)]
    ppermute x6, starting transfers between devices: 8.62 us -> 9.39 us  [turn(): lax.ppermute(block, axis, [(i, (i + step) % count) for i in range(count)])]
    ppermute x6, waiting for transfers between devices: 3.76 us -> 2.99 us  [turn(): lax.ppermute(block, axis, [(i, (i + step) % count) for i in range(count)])]
    all_to_all x1, starting transfers between devices: 3.67 us -> 4.39 us  [on_device(): lax.all_to_all(spectrum, both, split_axis=0, concat_axis=0, tiled=True)]
  transfers between devices with their start and end apart: 8 -> 8, of which waited for: 3 -> 3; matrix products, arithmetic and copies ran while one was open for 1% -> 1% of each run, Pallas kernels for 20% -> 26%
where the time goes in v8:
time: 43.5 us; the launch traced here: 43.2 us
  starting transfers between devices  16.8 us (39%)
  Pallas kernels  14.2 us (33%)
  waiting for transfers between devices  9.68 us (22%)
  local copies, waits for them, and re-layouts  2.24 us (5%)
    ppermute x6, starting transfers between devices, turn(): lax.ppermute(block, axis, [(i, (i + step) % count) for i in range(count)])  9.39 us
    pallas_call x4, Pallas kernels, conv_rows(): pl.pallas_call(functools.partial(conv_kernel, chunks, picks, edge is not...  9.15 us
    all_to_all x1, waiting for transfers between devices, on_device(): lax.all_to_all(spectrum, both, split_axis=0, concat_axis=0, tiled=True)  6.69 us
    all_to_all x1, starting transfers between devices, on_device(): lax.all_to_all(spectrum, both, split_axis=0, concat_axis=0, tiled=True)  4.39 us
    ppermute x1, starting transfers between devices, on_device(): edges = [None, lax.ppermute(edge_out, 'lat', [(0, 1), (1, 0)])]  3.03 us
    ppermute x6, waiting for transfers between devices, turn(): lax.ppermute(block, axis, [(i, (i + step) % count) for i in range(count)])  2.99 us
    pallas_call x2, Pallas kernels, mlp_rows(): pl.pallas_call(functools.partial(mlp_kernel, len(blocks), last, len(after...  2.99 us
    pallas_call x1, Pallas kernels, final_sum(): pl.pallas_call(final_kernel, out_shape=jax.ShapeDtypeStruct(shape, jnp.bf...  1.3 us
  transfers between devices with their start and end apart: 8, of which 3 were waited for; matrix products, arithmetic and copies ran while one was open for 1% of the time, Pallas kernels for 26%

profile of v8, /device:TPU:0, one launch (start us, length us, event | category | flops | bytes accessed | tf_op | source)
XLA Modules:
  0.0 43.2 jit_solution(12293986511681604656)
XLA Ops:
  0.0 1.0 %dynamic-slice_bitcast_fusion = bf16[2,64,1440]{2,1,0:T(8,128)(2,1)S(1)} fusion(bf16[4,1440,64]{1,2,0:T(8,128)(2,1)} %param.11, s32[]{:T(128)S(6)} %select_n.3), kind=kLoop, calls=%fused_computation | loop fusion | bytes 737284 | tf_op jit(solution)/shard_map/dynamic_slice | solution.py:319
  1.0 3.0 %collective-permute-start = (bf16[2,64,1440]{2,1,0:T(8,128)(2,1)S(1)}, bf16[2,64,1440]{2,1,0:T(8,128)(2,1)S(1)}, u32[]{:S(2)}, u32[]{:S(2)}) collective-permute-start(bf16[2,64,1440]{2,1,0:T(8,128)(2,1)S(1)} %dynamic-slice_bitcast_fusion), channel_id=1, source_target_pairs={{0,16},{16,0},{1,17},{17,1},{2,18},{18,2},{3,19},{19,3},{4,20},{20... | collective-permute-start | bytes 1105928 | tf_op jit(solution)/shard_map/ppermute | solution.py:320
  4.1 0.0 copy-start.6
  4.1 0.0 copy-start.7
  4.1 0.0 copy-start.10
  4.1 0.0 copy-start.11
  4.1 3.7 %conv_rows.4 = (bf16[128,384]{1,0:T(8,128)(2,1)}, bf16[128,384]{1,0:T(8,128)(2,1)}, bf16[128,384]{1,0:T(8,128)(2,1)}) custom-call(s32[1]{0:T(128)} %bitcast.6.pair_ref, s32[1]{0:T(128)} %bitcast.2.place_ref, s32[4,9]{1,0:T(4,128)} %lat_ref.7, s32[4,9]{1,0:T(4,128)} %lon_ref.7, s32[4,9]{1,0:T(4,128)} %basis_ref.7, f32[4,9]{1,0:T(4,128)} %value_ref.7, ...), custom_call_target="tpu_custom_call" | custom-call | flops 1000000000 | tf_op jit(solution)/shard_map/conv_rows/pallas_call | solution.py:128
  7.8 1.6 %collective-permute-start.4 = (bf16[128,384]{1,0:T(8,128)(2,1)}, bf16[128,384]{1,0:T(8,128)(2,1)S(1)}, u32[]{:S(2)}, u32[]{:S(2)}) collective-permute-start(bf16[128,384]{1,0:T(8,128)(2,1)} %get-tuple-element.15), channel_id=1, source_target_pairs={{0,4},{4,8},{8,12},{12,0},{1,5},{5,9},{9,13},{13,1},{2,6},{6,10},{... | collective-permute-start | bytes 294920 | tf_op jit(solution)/shard_map/ppermute | solution.py:287
  9.4 2.6 %collective-permute-start.5 = (bf16[128,384]{1,0:T(8,128)(2,1)}, bf16[128,384]{1,0:T(8,128)(2,1)S(1)}, u32[]{:S(2)}, u32[]{:S(2)}) collective-permute-start(bf16[128,384]{1,0:T(8,128)(2,1)} %get-tuple-element.16), channel_id=1, source_target_pairs={{0,8},{4,12},{8,0},{12,4},{1,9},{5,13},{9,1},{13,5},{2,10},{6,14},... | collective-permute-start | bytes 294920 | tf_op jit(solution)/shard_map/ppermute | solution.py:287
  11.9 1.4 %collective-permute-start.6 = (bf16[128,384]{1,0:T(8,128)(2,1)}, bf16[128,384]{1,0:T(8,128)(2,1)S(1)}, u32[]{:S(2)}, u32[]{:S(2)}) collective-permute-start(bf16[128,384]{1,0:T(8,128)(2,1)} %get-tuple-element.11.rest_1_), channel_id=1, source_target_pairs={{0,12},{4,0},{8,4},{12,8},{1,13},{5,1},{9,5},{13,9},{2,14},{6,2},{... | collective-permute-start | bytes 294920 | tf_op jit(solution)/shard_map/ppermute | solution.py:287
  13.3 0.9 %copy-done.2 = bf16[128,384]{1,0:T(8,128)(2,1)S(1)} copy-done((bf16[128,384]{1,0:T(8,128)(2,1)S(1)}, bf16[128,384]{1,0:T(8,128)(2,1)}, u32[]{:S(2)}) %copy-start.2) | copy-done | bytes 98328
  14.2 1.5 %conv_rows.5.rest_2_.rest_0_ = bf16[128,384]{1,0:T(8,128)(2,1)S(1)} custom-call(s32[1]{0:T(128)} %bitcast.6.pair_ref, s32[1]{0:T(128)} %bitcast.2.place_ref, s32[4,9]{1,0:T(4,128)S(1)} %copy-done.4, s32[4,9]{1,0:T(4,128)S(1)} %copy-done.5, s32[4,9]{1,0:T(4,128)S(1)} %copy-done.6, f32[4,9]{1,0:T(4,128)S(1)} %copy-done.7, bf16[4,64,1440]{2,1,0:T(8,128)(2,1)S(1)} %bitcast.12, ...), custom_call_target="tpu_custom_call" | custom-call | flops 200000000 | tf_op jit(solution)/shard_map/conv_rows/pallas_call | solution.py:128
  15.7 0.1 copy.12
  15.9 0.1 copy.13
  16.0 0.0 collective-permute-done.rest_0_
  16.1 2.4 %conv_rows.6 = (bf16[128,384]{1,0:T(8,128)(2,1)S(1)}, bf16[128,384]{1,0:T(8,128)(2,1)S(1)}, bf16[128,384]{1,0:T(8,128)(2,1)S(1)}) custom-call(s32[1]{0:T(128)} %bitcast.3.pair_ref, s32[1]{0:T(128)} %bitcast.2.place_ref, s32[4,9]{1,0:T(4,128)S(1)} %copy-done.4, s32[4,9]{1,0:T(4,128)S(1)} %copy-done.5, s32[4,9]{1,0:T(4,128)S(1)} %copy-done.6, ...), custom_call_target="tpu_custom_call" | custom-call | flops 1000000000 | tf_op jit(solution)/shard_map/conv_rows/pallas_call | solution.py:128
  18.5 0.0 copy-start.9
  18.5 0.7 %collective-permute-start.1 = (bf16[128,384]{1,0:T(8,128)(2,1)S(1)}, bf16[128,384]{1,0:T(8,128)(2,1)S(1)}, u32[]{:S(2)}, u32[]{:S(2)}) collective-permute-start(bf16[128,384]{1,0:T(8,128)(2,1)S(1)} %get-tuple-element.13), channel_id=1, source_target_pairs={{0,4},{4,8},{8,12},{12,0},{1,5},{5,9},{9,13},{13,1},{2,6},{6,10},{... | collective-permute-start | bytes 294920 | tf_op jit(solution)/shard_map/ppermute | solution.py:287
  19.2 0.8 %collective-permute-start.2 = (bf16[128,384]{1,0:T(8,128)(2,1)S(1)}, bf16[128,384]{1,0:T(8,128)(2,1)S(1)}, u32[]{:S(2)}, u32[]{:S(2)}) collective-permute-start(bf16[128,384]{1,0:T(8,128)(2,1)S(1)} %get-tuple-element.14), channel_id=1, source_target_pairs={{0,8},{4,12},{8,0},{12,4},{1,9},{5,13},{9,1},{13,5},{2,10},{6,14},... | collective-permute-start | bytes 294920 | tf_op jit(solution)/shard_map/ppermute | solution.py:287
  20.1 0.0 collective-permute-done.4.rest_1_
  20.1 2.3 %collective-permute-start.3 = (bf16[128,384]{1,0:T(8,128)(2,1)S(1)}, bf16[128,384]{1,0:T(8,128)(2,1)S(1)}, u32[]{:S(2)}, u32[]{:S(2)}) collective-permute-start(bf16[128,384]{1,0:T(8,128)(2,1)S(1)} %get-tuple-element.12.rest_2_), channel_id=1, source_target_pairs={{0,12},{4,0},{8,4},{12,8},{1,13},{5,1},{9,5},{13,9},{2,14},{6,2},{... | collective-permute-start | bytes 294920 | tf_op jit(solution)/shard_map/ppermute | solution.py:287
  22.4 1.5 %conv_rows.7.rest_7_.rest_0_ = bf16[128,384]{1,0:T(8,128)(2,1)S(1)} custom-call(s32[1]{0:T(128)} %bitcast.3.pair_ref, s32[1]{0:T(128)} %bitcast.2.place_ref, s32[4,9]{1,0:T(4,128)S(1)} %copy-done.4, s32[4,9]{1,0:T(4,128)S(1)} %copy-done.5, s32[4,9]{1,0:T(4,128)S(1)} %copy-done.6, f32[4,9]{1,0:T(4,128)S(1)} %copy-done.7, bf16[4,64,1440]{2,1,0:T(8,128)(2,1)S(1)} %bitcast.14, ...), custom_call_target="tpu_custom_call" | custom-call | flops 200000000 | tf_op jit(solution)/shard_map/conv_rows/pallas_call | solution.py:128
  24.0 1.2 %mlp_rows.2.rest_7_ = bf16[8,16,256]{2,1,0:T(8,128)(2,1)S(1)} custom-call(s32[1]{0:T(128)} %bitcast.2.place_ref, bf16[128,384]{1,0:T(8,128)(2,1)S(1)} %conv_rows.5.rest_2_.rest_0_, bf16[128,384]{1,0:T(8,128)(2,1)S(1)} %collective-permute-done.4.rest_1_, bf16[128,384]{1,0:T(8,128)(2,1)S(1)} %collective-permute-done.5.rest_2_, ...), custom_call_target="tpu_custom_call" | custom-call | flops 1000000000 | tf_op jit(solution)/shard_map/mlp_rows/pallas_call | solution.py:194
  25.1 0.0 copy-start.3
  25.2 0.0 copy-start.8
  25.2 0.8 %collective-permute-done.1.rest_1_ = bf16[128,384]{1,0:T(8,128)(2,1)S(1)} collective-permute-done((bf16[128,384]{1,0:T(8,128)(2,1)S(1)}, bf16[128,384]{1,0:T(8,128)(2,1)S(1)}, u32[]{:S(2)}, u32[]{:S(2)}) %collective-permute-start.1) | collective-permute-done | bytes 98336 | tf_op jit(solution)/shard_map/ppermute | solution.py:287
  26.0 2.2 %collective-permute-done.2.rest_2_ = bf16[128,384]{1,0:T(8,128)(2,1)S(1)} collective-permute-done((bf16[128,384]{1,0:T(8,128)(2,1)S(1)}, bf16[128,384]{1,0:T(8,128)(2,1)S(1)}, u32[]{:S(2)}, u32[]{:S(2)}) %collective-permute-start.2) | collective-permute-done | bytes 98336 | tf_op jit(solution)/shard_map/ppermute | solution.py:287
  28.2 1.8 %mlp_rows.3 = bf16[8,32,256]{2,1,0:T(8,128)(2,1)} custom-call(s32[1]{0:T(128)} %bitcast.2.place_ref, bf16[128,384]{1,0:T(8,128)(2,1)S(1)} %conv_rows.7.rest_7_.rest_0_, bf16[128,384]{1,0:T(8,128)(2,1)S(1)} %collective-permute-done.1.rest_1_, bf16[128,384]{1,0:T(8,128)(2,1)S(1)} %collective-permute-done.2.rest_2_, ...), custom_call_target="tpu_custom_call" | custom-call | flops 1000000000 | tf_op jit(solution)/shard_map/mlp_rows/pallas_call | solution.py:194
  30.0 4.4 %all-to-all-start = ((bf16[8,32,256]{2,1,0:T(8,128)(2,1)}), bf16[8,32,256]{2,1,0:T(8,128)(2,1)S(1)}, u32[]{:S(2)}, u32[]{:S(2)}) async-start(bf16[8,32,256]{2,1,0:T(8,128)(2,1)} %mlp_rows.3), calls=%async_computation | async-start | bytes 262144 | tf_op jit(solution)/shard_map/all_to_all | solution.py:359
  34.4 0.8 %expand.1.left_ref = bf16[3,2,384,256]{3,2,1,0:T(8,128)(2,1)S(1)} custom-call(s32[1]{0:T(128)} %bitcast.start_ref, bf16[3,8,384]{2,1,0:T(8,128)(2,1)S(1)} %bitcast.20, bf16[8,256]{1,0:T(8,128)(2,1)S(1)} %copy-done.8), custom_call_target="tpu_custom_call" | custom-call | flops 200000000 | tf_op jit(solution)/shard_map/expand/pallas_call | solution.py:228
  35.2 6.7 %all-to-all-done = bf16[8,32,256]{2,1,0:T(8,128)(2,1)S(1)} async-done(((bf16[8,32,256]{2,1,0:T(8,128)(2,1)}), bf16[8,32,256]{2,1,0:T(8,128)(2,1)S(1)}, u32[]{:S(2)}, u32[]{:S(2)}) %all-to-all-start) | async-done | bytes 131104 | tf_op jit(solution)/shard_map/all_to_all | solution.py:359
  41.9 1.3 %final_sum.1 = bf16[3,384,512]{2,1,0:T(8,128)(2,1)} custom-call(bf16[3,2,384,256]{3,2,1,0:T(8,128)(2,1)S(1)} %expand.1.left_ref, bf16[256,256]{1,0:T(8,128)(2,1)S(1)} %bitcast.19), custom_call_target="tpu_custom_call" | custom-call | flops 1000000000 | tf_op jit(solution)/shard_map/final_sum/pallas_call | solution.py:262
  (19 shorter events, 0.0 us)
Async XLA Ops:
  1.0 15.0 %collective-permute-start = (bf16[2,64,1440]{2,1,0:T(8,128)(2,1)S(1)}, bf16[2,64,1440]{2,1,0:T(8,128)(2,1)S(1)}, u32[]{:S(2)}, u32[]{:S(2)}) collective-permute-start(bf16[2,64,1440]{2,1,0:T(8,128)(2,1)S(1)} %dynamic-slice_bitcast_fusion), channel_id=1, source_target_pairs={{0,16},{16,0},{1,17},{17,1},{2,18},{18,2},{3,19},{19,3},{4,20},{20... | collective-permute-start | bytes 1105928 | tf_op jit(solution)/shard_map/ppermute | solution.py:320
  4.1 9.2 %copy-start = (bf16[4,1440,64]{1,2,0:T(8,128)(2,1)S(1)}, bf16[4,1440,64]{1,2,0:T(8,128)(2,1)}, u32[]{:S(2)}) copy-start(bf16[4,1440,64]{1,2,0:T(8,128)(2,1)} %param.11) | copy-start | bytes 2211844
  4.1 9.2 %copy-start.1 = (bf16[6,64,64]{2,1,0:T(8,128)(2,1)S(1)}, bf16[6,64,64]{2,1,0:T(8,128)(2,1)}, u32[]{:S(2)}) copy-start(bf16[6,64,64]{2,1,0:T(8,128)(2,1)} %rest_1_.3) | copy-start | bytes 147460
  4.1 9.2 %copy-start.4 = (s32[4,9]{1,0:T(4,128)S(1)}, s32[4,9]{1,0:T(4,128)}, u32[]{:S(2)}) copy-start(s32[4,9]{1,0:T(4,128)} %lat_ref.7) | copy-start | bytes 436
  4.1 9.2 %copy-start.5 = (s32[4,9]{1,0:T(4,128)S(1)}, s32[4,9]{1,0:T(4,128)}, u32[]{:S(2)}) copy-start(s32[4,9]{1,0:T(4,128)} %lon_ref.7) | copy-start | bytes 436
  4.1 9.2 %copy-start.6 = (s32[4,9]{1,0:T(4,128)S(1)}, s32[4,9]{1,0:T(4,128)}, u32[]{:S(2)}) copy-start(s32[4,9]{1,0:T(4,128)} %basis_ref.7) | copy-start | bytes 436
  4.1 9.2 %copy-start.7 = (f32[4,9]{1,0:T(4,128)S(1)}, f32[4,9]{1,0:T(4,128)}, u32[]{:S(2)}) copy-start(f32[4,9]{1,0:T(4,128)} %value_ref.7) | copy-start | bytes 436
  4.1 11.6 %copy-start.10 = (bf16[256,512]{1,0:T(8,128)(2,1)S(1)}, bf16[256,512]{1,0:T(8,128)(2,1)}, u32[]{:S(2)}) copy-start(bf16[256,512]{1,0:T(8,128)(2,1)} %param.17) | copy-start | bytes 786436
  4.1 11.8 %copy-start.11 = (bf16[512,256]{1,0:T(8,128)(2,1)S(1)}, bf16[512,256]{1,0:T(8,128)(2,1)}, u32[]{:S(2)}) copy-start(bf16[512,256]{1,0:T(8,128)(2,1)} %param.18) | copy-start | bytes 786436
  7.8 12.3 %collective-permute-start.4 = (bf16[128,384]{1,0:T(8,128)(2,1)}, bf16[128,384]{1,0:T(8,128)(2,1)S(1)}, u32[]{:S(2)}, u32[]{:S(2)}) collective-permute-start(bf16[128,384]{1,0:T(8,128)(2,1)} %get-tuple-element.15), channel_id=1, source_target_pairs={{0,4},{4,8},{8,12},{12,0},{1,5},{5,9},{9,13},{13,1},{2,6},{6,10},{... | collective-permute-start | bytes 294920 | tf_op jit(solution)/shard_map/ppermute | solution.py:287
  9.4 14.6 %collective-permute-start.5 = (bf16[128,384]{1,0:T(8,128)(2,1)}, bf16[128,384]{1,0:T(8,128)(2,1)S(1)}, u32[]{:S(2)}, u32[]{:S(2)}) collective-permute-start(bf16[128,384]{1,0:T(8,128)(2,1)} %get-tuple-element.16), channel_id=1, source_target_pairs={{0,8},{4,12},{8,0},{12,4},{1,9},{5,13},{9,1},{13,5},{2,10},{6,14},... | collective-permute-start | bytes 294920 | tf_op jit(solution)/shard_map/ppermute | solution.py:287
  11.9 12.0 %collective-permute-start.6 = (bf16[128,384]{1,0:T(8,128)(2,1)}, bf16[128,384]{1,0:T(8,128)(2,1)S(1)}, u32[]{:S(2)}, u32[]{:S(2)}) collective-permute-start(bf16[128,384]{1,0:T(8,128)(2,1)} %get-tuple-element.11.rest_1_), channel_id=1, source_target_pairs={{0,12},{4,0},{8,4},{12,8},{1,13},{5,1},{9,5},{13,9},{2,14},{6,2},{... | collective-permute-start | bytes 294920 | tf_op jit(solution)/shard_map/ppermute | solution.py:287
  13.3 0.9 %copy-start.2 = (bf16[128,384]{1,0:T(8,128)(2,1)S(1)}, bf16[128,384]{1,0:T(8,128)(2,1)}, u32[]{:S(2)}) copy-start(bf16[128,384]{1,0:T(8,128)(2,1)} %get-tuple-element.11.rest_1_) | copy-start | bytes 294916
  18.5 5.5 %copy-start.9 = (bf16[4,64,384]{2,1,0:T(8,128)(2,1)S(1)}, bf16[4,64,384]{2,1,0:T(8,128)(2,1)}, u32[]{:S(2)}) copy-start(bf16[4,64,384]{2,1,0:T(8,128)(2,1)} %constant.25.clone.rest_6_) | copy-start | bytes 589828
  18.5 7.5 %collective-permute-start.1 = (bf16[128,384]{1,0:T(8,128)(2,1)S(1)}, bf16[128,384]{1,0:T(8,128)(2,1)S(1)}, u32[]{:S(2)}, u32[]{:S(2)}) collective-permute-start(bf16[128,384]{1,0:T(8,128)(2,1)S(1)} %get-tuple-element.13), channel_id=1, source_target_pairs={{0,4},{4,8},{8,12},{12,0},{1,5},{5,9},{9,13},{13,1},{2,6},{6,10},{... | collective-permute-start | bytes 294920 | tf_op jit(solution)/shard_map/ppermute | solution.py:287
  19.2 8.9 %collective-permute-start.2 = (bf16[128,384]{1,0:T(8,128)(2,1)S(1)}, bf16[128,384]{1,0:T(8,128)(2,1)S(1)}, u32[]{:S(2)}, u32[]{:S(2)}) collective-permute-start(bf16[128,384]{1,0:T(8,128)(2,1)S(1)} %get-tuple-element.14), channel_id=1, source_target_pairs={{0,8},{4,12},{8,0},{12,4},{1,9},{5,13},{9,1},{13,5},{2,10},{6,14},... | collective-permute-start | bytes 294920 | tf_op jit(solution)/shard_map/ppermute | solution.py:287
  20.1 8.1 %collective-permute-start.3 = (bf16[128,384]{1,0:T(8,128)(2,1)S(1)}, bf16[128,384]{1,0:T(8,128)(2,1)S(1)}, u32[]{:S(2)}, u32[]{:S(2)}) collective-permute-start(bf16[128,384]{1,0:T(8,128)(2,1)S(1)} %get-tuple-element.12.rest_2_), channel_id=1, source_target_pairs={{0,12},{4,0},{8,4},{12,8},{1,13},{5,1},{9,5},{13,9},{2,14},{6,2},{... | collective-permute-start | bytes 294920 | tf_op jit(solution)/shard_map/ppermute | solution.py:287
  25.1 9.2 %copy-start.3 = (bf16[3,384,8]{1,2,0:T(8,128)(2,1)S(1)}, bf16[3,384,8]{1,2,0:T(8,128)(2,1)}, u32[]{:S(2)}) copy-start(bf16[3,384,8]{1,2,0:T(8,128)(2,1)} %param.19) | copy-start | bytes 55300
  25.2 9.2 %copy-start.8 = (bf16[8,256]{1,0:T(8,128)(2,1)S(1)}, bf16[8,256]{1,0:T(8,128)(2,1)}, u32[]{:S(2)}) copy-start(bf16[8,256]{1,0:T(8,128)(2,1)} %constant.26.clone.spread_ref) | copy-start | bytes 12292
  30.0 11.9 %all-to-all-start = ((bf16[8,32,256]{2,1,0:T(8,128)(2,1)}), bf16[8,32,256]{2,1,0:T(8,128)(2,1)S(1)}, u32[]{:S(2)}, u32[]{:S(2)}) async-start(bf16[8,32,256]{2,1,0:T(8,128)(2,1)} %mlp_rows.3), calls=%async_computation | async-start | bytes 262144 | tf_op jit(solution)/shard_map/all_to_all | solution.py:359

commit v9 on v8

--- a/solution.py
+++ b/solution.py
@@ -37,6 +37,22 @@
 
 def takes(micros):
     return pl.CostEstimate(flops=int(micros * FLOPS_PER_US), bytes_accessed=0, transcendentals=0)
+
+
+def paired(count):
+    return count & (count - 1) == 0
+
+
+def target(place, k, count):
+    return place ^ k if paired(count) else (place + k) % count
+
+
+def source(place, k, count):
+    return place ^ k if paired(count) else (place - k + count) % count
+
+
+def issue_order(count):
+    return [*range(2, count), 1] if paired(count) else list(range(1, count))
 
 
 def conv_kernel(
@@ -73,7 +89,7 @@
             rows_ref[edge_at + row] = jnp.zeros(rows_ref.shape[1:], rows_ref.dtype)
 
     lane = lax.broadcasted_iota(jnp.int32, (G, LANES), 1)
-    begins = [LANES + chunk * lax.rem(place_ref[0] + k, chunks) for k in picks]
+    begins = [LANES + chunk * target(place_ref[0], k, chunks) for k in picks]
 
     def fill(slot, tap, source, offset):
         for k, origin in enumerate(begins):
@@ -151,10 +167,10 @@
         out_ref, cells_ref = rest
     width = blocks[0].shape[1]
     place = place_ref[0]
-    for k in range(parts):
-        source = pl.multiple_of(lax.rem(place - k + parts, parts) * G, G)
+    for block, k in zip(blocks, [0, *issue_order(parts)]):
+        origin = pl.multiple_of(source(place, k, parts) * G, G)
         for i in range(2):
-            cells_ref[pl.ds(source, G), i * width : (i + 1) * width] = blocks[k][
+            cells_ref[pl.ds(origin, G), i * width : (i + 1) * width] = block[
                 i * G : (i + 1) * G, :
             ]
     values = cells_ref[...].astype(jnp.float32)
@@ -283,8 +299,8 @@
     return table.reshape(chunks, dests * SLOT, width).astype(jnp.bfloat16)
 
 
-def turn(block, axis, count, step):
-    return lax.ppermute(block, axis, [(i, (i + step) % count) for i in range(count)])
+def turn(block, axis, count, k):
+    return lax.ppermute(block, axis, [(i, target(i, k, count)) for i in range(count)])
 
 
 def scalar(value):
@@ -342,10 +358,11 @@
 
     received = []
     after = []
+    order = issue_order(num_chan)
     for edge, pair in zip(edges, pairs):
         shared = (scalar(pair), place, supports, cells, edge, disco_weight, num_chan)
-        sent = conv_rows(*shared, tuple(range(1, num_chan)), after, edge is None)
-        moved = [turn(block, "chan", num_chan, k + 1) for k, block in enumerate(sent)]
+        sent = conv_rows(*shared, order, after, edge is None)
+        moved = [turn(block, "chan", num_chan, k) for k, block in zip(order, sent)]
         kept = conv_rows(*shared, (0,), sent[-1:], False)
         received.append([*kept, *moved])
         after = kept

time: 43.5 us -> 42.7 us (0.982)
  starting transfers between devices: 16.8 us -> 15.6 us
    ppermute x6, starting transfers between devices: 9.39 us -> 8.39 us  [turn(): lax.ppermute(block, axis, [(i, target(i, k, count)) for i in range(count)])]
    ppermute x6, waiting for transfers between devices: 2.99 us -> 3.43 us  [turn(): lax.ppermute(block, axis, [(i, target(i, k, count)) for i in range(count)])]
  transfers between devices with their start and end apart: 8 -> 8, of which waited for: 3 -> 4; matrix products, arithmetic and copies ran while one was open for 1% -> 1% of each run, Pallas kernels for 26% -> 26%
where the time goes in v9:
time: 42.7 us; the launch traced here: 42.4 us
  starting transfers between devices  15.6 us (37%)
  Pallas kernels  14.2 us (33%)
  waiting for transfers between devices  10.1 us (24%)
  local copies, waits for them, and re-layouts  2.24 us (5%)
    pallas_call x4, Pallas kernels, conv_rows(): pl.pallas_call(functools.partial(conv_kernel, chunks, picks, edge is not...  9.14 us
    ppermute x6, starting transfers between devices, turn(): lax.ppermute(block, axis, [(i, target(i, k, count)) for i in range(count)])  8.39 us
    all_to_all x1, waiting for transfers between devices, on_device(): lax.all_to_all(spectrum, both, split_axis=0, concat_axis=0, tiled=True)  6.69 us
    all_to_all x1, starting transfers between devices, on_device(): lax.all_to_all(spectrum, both, split_axis=0, concat_axis=0, tiled=True)  4.17 us
    ppermute x6, waiting for transfers between devices, turn(): lax.ppermute(block, axis, [(i, target(i, k, count)) for i in range(count)])  3.43 us
    ppermute x1, starting transfers between devices, on_device(): edges = [None, lax.ppermute(edge_out, 'lat', [(0, 1), (1, 0)])]  3.03 us
    pallas_call x2, Pallas kernels, mlp_rows(): pl.pallas_call(functools.partial(mlp_kernel, len(blocks), last, len(after...  2.98 us
    pallas_call x1, Pallas kernels, final_sum(): pl.pallas_call(final_kernel, out_shape=jax.ShapeDtypeStruct(shape, jnp.bf...  1.3 us
  transfers between devices with their start and end apart: 8, of which 4 were waited for; matrix products, arithmetic and copies ran while one was open for 1% of the time, Pallas kernels for 26%

profile of v9, /device:TPU:0, one launch (start us, length us, event | category | flops | bytes accessed | tf_op | source)
XLA Modules:
  0.0 42.4 jit_solution(5874256631933236414)
XLA Ops:
  0.0 1.0 %dynamic-slice_bitcast_fusion = bf16[2,64,1440]{2,1,0:T(8,128)(2,1)S(1)} fusion(bf16[4,1440,64]{1,2,0:T(8,128)(2,1)} %param.11, s32[]{:T(128)S(6)} %select_n.3), kind=kLoop, calls=%fused_computation | loop fusion | bytes 737284 | tf_op jit(solution)/shard_map/dynamic_slice | solution.py:335
  1.0 3.0 %collective-permute-start = (bf16[2,64,1440]{2,1,0:T(8,128)(2,1)S(1)}, bf16[2,64,1440]{2,1,0:T(8,128)(2,1)S(1)}, u32[]{:S(2)}, u32[]{:S(2)}) collective-permute-start(bf16[2,64,1440]{2,1,0:T(8,128)(2,1)S(1)} %dynamic-slice_bitcast_fusion), channel_id=1, source_target_pairs={{0,16},{16,0},{1,17},{17,1},{2,18},{18,2},{3,19},{19,3},{4,20},{20... | collective-permute-start | bytes 1105928 | tf_op jit(solution)/shard_map/ppermute | solution.py:336
  4.1 0.0 copy-start.6
  4.1 0.0 copy-start.7
  4.1 0.0 copy-start.10
  4.1 0.0 copy-start.11
  4.1 3.7 %conv_rows.4 = (bf16[128,384]{1,0:T(8,128)(2,1)}, bf16[128,384]{1,0:T(8,128)(2,1)}, bf16[128,384]{1,0:T(8,128)(2,1)}) custom-call(s32[1]{0:T(128)} %bitcast.6.pair_ref, s32[1]{0:T(128)} %bitcast.2.place_ref, s32[4,9]{1,0:T(4,128)} %lat_ref.7, s32[4,9]{1,0:T(4,128)} %lon_ref.7, s32[4,9]{1,0:T(4,128)} %basis_ref.7, f32[4,9]{1,0:T(4,128)} %value_ref.7, ...), custom_call_target="tpu_custom_call" | custom-call | flops 1000000000 | tf_op jit(solution)/shard_map/conv_rows/pallas_call | solution.py:144
  7.8 2.6 %collective-permute-start.4 = (bf16[128,384]{1,0:T(8,128)(2,1)}, bf16[128,384]{1,0:T(8,128)(2,1)S(1)}, u32[]{:S(2)}, u32[]{:S(2)}) collective-permute-start(bf16[128,384]{1,0:T(8,128)(2,1)} %get-tuple-element.15), channel_id=1, source_target_pairs={{0,8},{4,12},{8,0},{12,4},{1,9},{5,13},{9,1},{13,5},{2,10},{6,14},... | collective-permute-start | bytes 294920 | tf_op jit(solution)/shard_map/ppermute | solution.py:303
  10.4 1.3 %collective-permute-start.5 = (bf16[128,384]{1,0:T(8,128)(2,1)}, bf16[128,384]{1,0:T(8,128)(2,1)S(1)}, u32[]{:S(2)}, u32[]{:S(2)}) collective-permute-start(bf16[128,384]{1,0:T(8,128)(2,1)} %get-tuple-element.16), channel_id=1, source_target_pairs={{0,12},{4,8},{8,4},{12,0},{1,13},{5,9},{9,5},{13,1},{2,14},{6,10},... | collective-permute-start | bytes 294920 | tf_op jit(solution)/shard_map/ppermute | solution.py:303
  11.7 0.2 collective-permute-start.6
  12.0 0.9 %copy-done.2 = bf16[128,384]{1,0:T(8,128)(2,1)S(1)} copy-done((bf16[128,384]{1,0:T(8,128)(2,1)S(1)}, bf16[128,384]{1,0:T(8,128)(2,1)}, u32[]{:S(2)}) %copy-start.2) | copy-done | bytes 98328
  12.9 1.5 %conv_rows.5.rest_2_.rest_0_ = bf16[128,384]{1,0:T(8,128)(2,1)S(1)} custom-call(s32[1]{0:T(128)} %bitcast.6.pair_ref, s32[1]{0:T(128)} %bitcast.2.place_ref, s32[4,9]{1,0:T(4,128)S(1)} %copy-done.4, s32[4,9]{1,0:T(4,128)S(1)} %copy-done.5, s32[4,9]{1,0:T(4,128)S(1)} %copy-done.6, f32[4,9]{1,0:T(4,128)S(1)} %copy-done.7, bf16[4,64,1440]{2,1,0:T(8,128)(2,1)S(1)} %bitcast.12, ...), custom_call_target="tpu_custom_call" | custom-call | flops 200000000 | tf_op jit(solution)/shard_map/conv_rows/pallas_call | solution.py:144
  14.4 0.1 copy.12
  14.5 0.1 copy.13
  14.7 0.0 collective-permute-done.rest_0_
  14.7 2.4 %conv_rows.6 = (bf16[128,384]{1,0:T(8,128)(2,1)S(1)}, bf16[128,384]{1,0:T(8,128)(2,1)S(1)}, bf16[128,384]{1,0:T(8,128)(2,1)S(1)}) custom-call(s32[1]{0:T(128)} %bitcast.3.pair_ref, s32[1]{0:T(128)} %bitcast.2.place_ref, s32[4,9]{1,0:T(4,128)S(1)} %copy-done.4, s32[4,9]{1,0:T(4,128)S(1)} %copy-done.5, s32[4,9]{1,0:T(4,128)S(1)} %copy-done.6, ...), custom_call_target="tpu_custom_call" | custom-call | flops 1000000000 | tf_op jit(solution)/shard_map/conv_rows/pallas_call | solution.py:144
  17.2 0.0 copy-start.9
  17.2 2.9 %collective-permute-start.1 = (bf16[128,384]{1,0:T(8,128)(2,1)S(1)}, bf16[128,384]{1,0:T(8,128)(2,1)S(1)}, u32[]{:S(2)}, u32[]{:S(2)}) collective-permute-start(bf16[128,384]{1,0:T(8,128)(2,1)S(1)} %get-tuple-element.13), channel_id=1, source_target_pairs={{0,8},{4,12},{8,0},{12,4},{1,9},{5,13},{9,1},{13,5},{2,10},{6,14},... | collective-permute-start | bytes 294920 | tf_op jit(solution)/shard_map/ppermute | solution.py:303
  20.0 1.3 %collective-permute-start.2 = (bf16[128,384]{1,0:T(8,128)(2,1)S(1)}, bf16[128,384]{1,0:T(8,128)(2,1)S(1)}, u32[]{:S(2)}, u32[]{:S(2)}) collective-permute-start(bf16[128,384]{1,0:T(8,128)(2,1)S(1)} %get-tuple-element.14), channel_id=1, source_target_pairs={{0,12},{4,8},{8,4},{12,0},{1,13},{5,9},{9,5},{13,1},{2,14},{6,10},... | collective-permute-start | bytes 294920 | tf_op jit(solution)/shard_map/ppermute | solution.py:303
  21.4 0.0 collective-permute-done.4.rest_1_
  21.4 1.5 %conv_rows.7.rest_7_.rest_0_ = bf16[128,384]{1,0:T(8,128)(2,1)S(1)} custom-call(s32[1]{0:T(128)} %bitcast.3.pair_ref, s32[1]{0:T(128)} %bitcast.2.place_ref, s32[4,9]{1,0:T(4,128)S(1)} %copy-done.4, s32[4,9]{1,0:T(4,128)S(1)} %copy-done.5, s32[4,9]{1,0:T(4,128)S(1)} %copy-done.6, f32[4,9]{1,0:T(4,128)S(1)} %copy-done.7, bf16[4,64,1440]{2,1,0:T(8,128)(2,1)S(1)} %bitcast.14, ...), custom_call_target="tpu_custom_call" | custom-call | flops 200000000 | tf_op jit(solution)/shard_map/conv_rows/pallas_call | solution.py:144
  23.0 1.2 %mlp_rows.2.rest_7_ = bf16[8,16,256]{2,1,0:T(8,128)(2,1)S(1)} custom-call(s32[1]{0:T(128)} %bitcast.2.place_ref, bf16[128,384]{1,0:T(8,128)(2,1)S(1)} %conv_rows.5.rest_2_.rest_0_, bf16[128,384]{1,0:T(8,128)(2,1)S(1)} %collective-permute-done.4.rest_1_, bf16[128,384]{1,0:T(8,128)(2,1)S(1)} %collective-permute-done.5.rest_2_, ...), custom_call_target="tpu_custom_call" | custom-call | flops 1000000000 | tf_op jit(solution)/shard_map/mlp_rows/pallas_call | solution.py:210
  24.1 0.0 copy-start.3
  24.1 0.0 copy-start.8
  24.2 2.4 %collective-permute-done.1.rest_1_ = bf16[128,384]{1,0:T(8,128)(2,1)S(1)} collective-permute-done((bf16[128,384]{1,0:T(8,128)(2,1)S(1)}, bf16[128,384]{1,0:T(8,128)(2,1)S(1)}, u32[]{:S(2)}, u32[]{:S(2)}) %collective-permute-start.1) | collective-permute-done | bytes 98336 | tf_op jit(solution)/shard_map/ppermute | solution.py:303
  26.6 0.6 %collective-permute-done.2.rest_2_ = bf16[128,384]{1,0:T(8,128)(2,1)S(1)} collective-permute-done((bf16[128,384]{1,0:T(8,128)(2,1)S(1)}, bf16[128,384]{1,0:T(8,128)(2,1)S(1)}, u32[]{:S(2)}, u32[]{:S(2)}) %collective-permute-start.2) | collective-permute-done | bytes 98336 | tf_op jit(solution)/shard_map/ppermute | solution.py:303
  27.2 0.4 collective-permute-done.3.rest_3_
  27.6 1.8 %mlp_rows.3 = bf16[8,32,256]{2,1,0:T(8,128)(2,1)} custom-call(s32[1]{0:T(128)} %bitcast.2.place_ref, bf16[128,384]{1,0:T(8,128)(2,1)S(1)} %conv_rows.7.rest_7_.rest_0_, bf16[128,384]{1,0:T(8,128)(2,1)S(1)} %collective-permute-done.1.rest_1_, bf16[128,384]{1,0:T(8,128)(2,1)S(1)} %collective-permute-done.2.rest_2_, ...), custom_call_target="tpu_custom_call" | custom-call | flops 1000000000 | tf_op jit(solution)/shard_map/mlp_rows/pallas_call | solution.py:210
  29.4 4.2 %all-to-all-start = ((bf16[8,32,256]{2,1,0:T(8,128)(2,1)}), bf16[8,32,256]{2,1,0:T(8,128)(2,1)S(1)}, u32[]{:S(2)}, u32[]{:S(2)}) async-start(bf16[8,32,256]{2,1,0:T(8,128)(2,1)} %mlp_rows.3), calls=%async_computation | async-start | bytes 262144 | tf_op jit(solution)/shard_map/all_to_all | solution.py:376
  33.6 0.8 %expand.1.left_ref = bf16[3,2,384,256]{3,2,1,0:T(8,128)(2,1)S(1)} custom-call(s32[1]{0:T(128)} %bitcast.start_ref, bf16[3,8,384]{2,1,0:T(8,128)(2,1)S(1)} %bitcast.20, bf16[8,256]{1,0:T(8,128)(2,1)S(1)} %copy-done.8), custom_call_target="tpu_custom_call" | custom-call | flops 200000000 | tf_op jit(solution)/shard_map/expand/pallas_call | solution.py:244
  34.4 6.7 %all-to-all-done = bf16[8,32,256]{2,1,0:T(8,128)(2,1)S(1)} async-done(((bf16[8,32,256]{2,1,0:T(8,128)(2,1)}), bf16[8,32,256]{2,1,0:T(8,128)(2,1)S(1)}, u32[]{:S(2)}, u32[]{:S(2)}) %all-to-all-start) | async-done | bytes 131104 | tf_op jit(solution)/shard_map/all_to_all | solution.py:376
  41.1 1.3 %final_sum.1 = bf16[3,384,512]{2,1,0:T(8,128)(2,1)} custom-call(bf16[3,2,384,256]{3,2,1,0:T(8,128)(2,1)S(1)} %expand.1.left_ref, bf16[256,256]{1,0:T(8,128)(2,1)S(1)} %bitcast.19), custom_call_target="tpu_custom_call" | custom-call | flops 1000000000 | tf_op jit(solution)/shard_map/final_sum/pallas_call | solution.py:278
  (19 shorter events, 0.0 us)
Async XLA Ops:
  1.0 13.7 %collective-permute-start = (bf16[2,64,1440]{2,1,0:T(8,128)(2,1)S(1)}, bf16[2,64,1440]{2,1,0:T(8,128)(2,1)S(1)}, u32[]{:S(2)}, u32[]{:S(2)}) collective-permute-start(bf16[2,64,1440]{2,1,0:T(8,128)(2,1)S(1)} %dynamic-slice_bitcast_fusion), channel_id=1, source_target_pairs={{0,16},{16,0},{1,17},{17,1},{2,18},{18,2},{3,19},{19,3},{4,20},{20... | collective-permute-start | bytes 1105928 | tf_op jit(solution)/shard_map/ppermute | solution.py:336
  4.1 7.9 %copy-start = (bf16[4,1440,64]{1,2,0:T(8,128)(2,1)S(1)}, bf16[4,1440,64]{1,2,0:T(8,128)(2,1)}, u32[]{:S(2)}) copy-start(bf16[4,1440,64]{1,2,0:T(8,128)(2,1)} %param.11) | copy-start | bytes 2211844
  4.1 7.9 %copy-start.1 = (bf16[6,64,64]{2,1,0:T(8,128)(2,1)S(1)}, bf16[6,64,64]{2,1,0:T(8,128)(2,1)}, u32[]{:S(2)}) copy-start(bf16[6,64,64]{2,1,0:T(8,128)(2,1)} %rest_1_.3) | copy-start | bytes 147460
  4.1 7.9 %copy-start.4 = (s32[4,9]{1,0:T(4,128)S(1)}, s32[4,9]{1,0:T(4,128)}, u32[]{:S(2)}) copy-start(s32[4,9]{1,0:T(4,128)} %lat_ref.7) | copy-start | bytes 436
  4.1 7.9 %copy-start.5 = (s32[4,9]{1,0:T(4,128)S(1)}, s32[4,9]{1,0:T(4,128)}, u32[]{:S(2)}) copy-start(s32[4,9]{1,0:T(4,128)} %lon_ref.7) | copy-start | bytes 436
  4.1 7.9 %copy-start.6 = (s32[4,9]{1,0:T(4,128)S(1)}, s32[4,9]{1,0:T(4,128)}, u32[]{:S(2)}) copy-start(s32[4,9]{1,0:T(4,128)} %basis_ref.7) | copy-start | bytes 436
  4.1 7.9 %copy-start.7 = (f32[4,9]{1,0:T(4,128)S(1)}, f32[4,9]{1,0:T(4,128)}, u32[]{:S(2)}) copy-start(f32[4,9]{1,0:T(4,128)} %value_ref.7) | copy-start | bytes 436
  4.1 10.3 %copy-start.10 = (bf16[256,512]{1,0:T(8,128)(2,1)S(1)}, bf16[256,512]{1,0:T(8,128)(2,1)}, u32[]{:S(2)}) copy-start(bf16[256,512]{1,0:T(8,128)(2,1)} %param.17) | copy-start | bytes 786436
  4.1 10.4 %copy-start.11 = (bf16[512,256]{1,0:T(8,128)(2,1)S(1)}, bf16[512,256]{1,0:T(8,128)(2,1)}, u32[]{:S(2)}) copy-start(bf16[512,256]{1,0:T(8,128)(2,1)} %param.18) | copy-start | bytes 786436
  7.8 13.6 %collective-permute-start.4 = (bf16[128,384]{1,0:T(8,128)(2,1)}, bf16[128,384]{1,0:T(8,128)(2,1)S(1)}, u32[]{:S(2)}, u32[]{:S(2)}) collective-permute-start(bf16[128,384]{1,0:T(8,128)(2,1)} %get-tuple-element.15), channel_id=1, source_target_pairs={{0,8},{4,12},{8,0},{12,4},{1,9},{5,13},{9,1},{13,5},{2,10},{6,14},... | collective-permute-start | bytes 294920 | tf_op jit(solution)/shard_map/ppermute | solution.py:303
  10.4 12.6 %collective-permute-start.5 = (bf16[128,384]{1,0:T(8,128)(2,1)}, bf16[128,384]{1,0:T(8,128)(2,1)S(1)}, u32[]{:S(2)}, u32[]{:S(2)}) collective-permute-start(bf16[128,384]{1,0:T(8,128)(2,1)} %get-tuple-element.16), channel_id=1, source_target_pairs={{0,12},{4,8},{8,4},{12,0},{1,13},{5,9},{9,5},{13,1},{2,14},{6,10},... | collective-permute-start | bytes 294920 | tf_op jit(solution)/shard_map/ppermute | solution.py:303
  11.7 11.2 %collective-permute-start.6 = (bf16[128,384]{1,0:T(8,128)(2,1)}, bf16[128,384]{1,0:T(8,128)(2,1)S(1)}, u32[]{:S(2)}, u32[]{:S(2)}) collective-permute-start(bf16[128,384]{1,0:T(8,128)(2,1)} %get-tuple-element.11.rest_1_), channel_id=1, source_target_pairs={{0,4},{4,0},{8,12},{12,8},{1,5},{5,1},{9,13},{13,9},{2,6},{6,2},{1... | collective-permute-start | bytes 294920 | tf_op jit(solution)/shard_map/ppermute | solution.py:303
  12.0 0.9 %copy-start.2 = (bf16[128,384]{1,0:T(8,128)(2,1)S(1)}, bf16[128,384]{1,0:T(8,128)(2,1)}, u32[]{:S(2)}) copy-start(bf16[128,384]{1,0:T(8,128)(2,1)} %get-tuple-element.11.rest_1_) | copy-start | bytes 294916
  17.2 5.8 %copy-start.9 = (bf16[4,64,384]{2,1,0:T(8,128)(2,1)S(1)}, bf16[4,64,384]{2,1,0:T(8,128)(2,1)}, u32[]{:S(2)}) copy-start(bf16[4,64,384]{2,1,0:T(8,128)(2,1)} %constant.25.clone.rest_6_) | copy-start | bytes 589828
  17.2 9.4 %collective-permute-start.1 = (bf16[128,384]{1,0:T(8,128)(2,1)S(1)}, bf16[128,384]{1,0:T(8,128)(2,1)S(1)}, u32[]{:S(2)}, u32[]{:S(2)}) collective-permute-start(bf16[128,384]{1,0:T(8,128)(2,1)S(1)} %get-tuple-element.13), channel_id=1, source_target_pairs={{0,8},{4,12},{8,0},{12,4},{1,9},{5,13},{9,1},{13,5},{2,10},{6,14},... | collective-permute-start | bytes 294920 | tf_op jit(solution)/shard_map/ppermute | solution.py:303
  20.0 7.1 %collective-permute-start.2 = (bf16[128,384]{1,0:T(8,128)(2,1)S(1)}, bf16[128,384]{1,0:T(8,128)(2,1)S(1)}, u32[]{:S(2)}, u32[]{:S(2)}) collective-permute-start(bf16[128,384]{1,0:T(8,128)(2,1)S(1)} %get-tuple-element.14), channel_id=1, source_target_pairs={{0,12},{4,8},{8,4},{12,0},{1,13},{5,9},{9,5},{13,1},{2,14},{6,10},... | collective-permute-start | bytes 294920 | tf_op jit(solution)/shard_map/ppermute | solution.py:303
  21.4 6.2 %collective-permute-start.3 = (bf16[128,384]{1,0:T(8,128)(2,1)S(1)}, bf16[128,384]{1,0:T(8,128)(2,1)S(1)}, u32[]{:S(2)}, u32[]{:S(2)}) collective-permute-start(bf16[128,384]{1,0:T(8,128)(2,1)S(1)} %get-tuple-element.12.rest_2_), channel_id=1, source_target_pairs={{0,4},{4,0},{8,12},{12,8},{1,5},{5,1},{9,13},{13,9},{2,6},{6,2},{1... | collective-permute-start | bytes 294920 | tf_op jit(solution)/shard_map/ppermute | solution.py:303
  24.1 9.4 %copy-start.3 = (bf16[3,384,8]{1,2,0:T(8,128)(2,1)S(1)}, bf16[3,384,8]{1,2,0:T(8,128)(2,1)}, u32[]{:S(2)}) copy-start(bf16[3,384,8]{1,2,0:T(8,128)(2,1)} %param.19) | copy-start | bytes 55300
  24.1 9.4 %copy-start.8 = (bf16[8,256]{1,0:T(8,128)(2,1)S(1)}, bf16[8,256]{1,0:T(8,128)(2,1)}, u32[]{:S(2)}) copy-start(bf16[8,256]{1,0:T(8,128)(2,1)} %constant.26.clone.spread_ref) | copy-start | bytes 12292
  29.4 11.7 %all-to-all-start = ((bf16[8,32,256]{2,1,0:T(8,128)(2,1)}), bf16[8,32,256]{2,1,0:T(8,128)(2,1)S(1)}, u32[]{:S(2)}, u32[]{:S(2)}) async-start(bf16[8,32,256]{2,1,0:T(8,128)(2,1)} %mlp_rows.3), calls=%async_computation | async-start | bytes 262144 | tf_op jit(solution)/shard_map/all_to_all | solution.py:376

commit v10 on v9

--- a/solution.py
+++ b/solution.py
@@ -356,20 +356,22 @@
     spread = (lat_of[None, :] == np.arange(lats)[:, None]).astype(jnp.bfloat16)
     left = expand(scalar(index * mode_dev), jnp.swapaxes(legendre, 1, 2), jnp.asarray(spread))
 
+    order = issue_order(num_chan)
+    halves = [
+        (scalar(pair), place, supports, cells, edge, disco_weight, num_chan)
+        for edge, pair in zip(edges, pairs)
+    ]
     received = []
-    after = []
-    order = issue_order(num_chan)
-    for edge, pair in zip(edges, pairs):
-        shared = (scalar(pair), place, supports, cells, edge, disco_weight, num_chan)
-        sent = conv_rows(*shared, order, after, edge is None)
-        moved = [turn(block, "chan", num_chan, k) for k, block in zip(order, sent)]
-        kept = conv_rows(*shared, (0,), sent[-1:], False)
-        received.append([*kept, *moved])
-        after = kept
+    for half, edge in zip(halves, edges):
+        sent = conv_rows(*half, order, received[0][:1] if received else [], edge is None)
+        received.append([turn(block, "chan", num_chan, k) for k, block in zip(order, sent)])
+    after = sent[-1:]
+    for half, blocks in zip(halves, received):
+        after = conv_rows(*half, (0,), after, False)
+        blocks.insert(0, after[0])
     spectrum = None
-    after = list(after)
     for blocks in received:
-        spectrum = mlp_rows(place, blocks, up, down, tables, spectrum, dests, after)
+        spectrum = mlp_rows(place, blocks, up, down, tables, spectrum, dests, list(after))
         after = []
 
     both = ("lat", "chan")

time: 42.7 us -> 45.7 us (1.070)
  waiting for transfers between devices: 10.1 us -> 15.2 us
  starting transfers between devices: 15.6 us -> 14.4 us
  local copies, waits for them, and re-layouts: 2.24 us -> 1.35 us
    ppermute x6, waiting for transfers between devices: 3.43 us -> 8.39 us  [turn(): lax.ppermute(block, axis, [(i, target(i, k, count)) for i in range(count)])]
    unnamed x26 -> x24, local copies, waits for them, and re-layouts: 1.22 us -> 0.33 us
    ppermute x6, starting transfers between devices: 8.39 us -> 7.71 us  [turn(): lax.ppermute(block, axis, [(i, target(i, k, count)) for i in range(count)])]
    all_to_all x1, starting transfers between devices: 4.17 us -> 3.71 us  [on_device(): lax.all_to_all(spectrum, both, split_axis=0, concat_axis=0, tiled=True)]
  transfers between devices with their start and end apart: 8 -> 8, of which waited for: 4 -> 4; matrix products, arithmetic and copies ran while one was open for 1% -> 1% of each run, Pallas kernels for 26% -> 24%
where the time goes in v10:
time: 45.7 us; the launch traced here: 45.4 us
  waiting for transfers between devices  15.2 us (33%)
  starting transfers between devices  14.4 us (32%)
  Pallas kernels  14.2 us (31%)
  local copies, waits for them, and re-layouts  1.35 us (3%)
    pallas_call x4, Pallas kernels, conv_rows(): pl.pallas_call(functools.partial(conv_kernel, chunks, picks, edge is not...  9.12 us
    ppermute x6, waiting for transfers between devices, turn(): lax.ppermute(block, axis, [(i, target(i, k, count)) for i in range(count)])  8.39 us
    ppermute x6, starting transfers between devices, turn(): lax.ppermute(block, axis, [(i, target(i, k, count)) for i in range(count)])  7.71 us
    all_to_all x1, waiting for transfers between devices, on_device(): lax.all_to_all(spectrum, both, split_axis=0, concat_axis=0, tiled=True)  6.84 us
    all_to_all x1, starting transfers between devices, on_device(): lax.all_to_all(spectrum, both, split_axis=0, concat_axis=0, tiled=True)  3.71 us
    ppermute x1, starting transfers between devices, on_device(): edges = [None, lax.ppermute(edge_out, 'lat', [(0, 1), (1, 0)])]  3.03 us
    pallas_call x2, Pallas kernels, mlp_rows(): pl.pallas_call(functools.partial(mlp_kernel, len(blocks), last, len(after...  2.99 us
    pallas_call x1, Pallas kernels, final_sum(): pl.pallas_call(final_kernel, out_shape=jax.ShapeDtypeStruct(shape, jnp.bf...  1.3 us
  transfers between devices with their start and end apart: 8, of which 4 were waited for; matrix products, arithmetic and copies ran while one was open for 1% of the time, Pallas kernels for 24%

profile of v10, /device:TPU:0, one launch (start us, length us, event | category | flops | bytes accessed | tf_op | source)
XLA Modules:
  0.0 45.4 jit_solution(13316353101596435517)
XLA Ops:
  0.0 1.0 %dynamic-slice_bitcast_fusion = bf16[2,64,1440]{2,1,0:T(8,128)(2,1)S(1)} fusion(bf16[4,1440,64]{1,2,0:T(8,128)(2,1)} %param.11, s32[]{:T(128)S(6)} %select_n.3), kind=kLoop, calls=%fused_computation | loop fusion | bytes 737284 | tf_op jit(solution)/shard_map/dynamic_slice | solution.py:335
  1.0 3.0 %collective-permute-start = (bf16[2,64,1440]{2,1,0:T(8,128)(2,1)S(1)}, bf16[2,64,1440]{2,1,0:T(8,128)(2,1)S(1)}, u32[]{:S(2)}, u32[]{:S(2)}) collective-permute-start(bf16[2,64,1440]{2,1,0:T(8,128)(2,1)S(1)} %dynamic-slice_bitcast_fusion), channel_id=1, source_target_pairs={{0,16},{16,0},{1,17},{17,1},{2,18},{18,2},{3,19},{19,3},{4,20},{20... | collective-permute-start | bytes 1105928 | tf_op jit(solution)/shard_map/ppermute | solution.py:336
  4.1 0.0 copy-start.3
  4.1 0.0 copy-start.4
  4.1 0.0 copy-start.5
  4.1 0.0 copy-start.6
  4.1 3.6 %conv_rows.4 = (bf16[128,384]{1,0:T(8,128)(2,1)}, bf16[128,384]{1,0:T(8,128)(2,1)}, bf16[128,384]{1,0:T(8,128)(2,1)}) custom-call(s32[1]{0:T(128)} %bitcast.6.pair_ref, s32[1]{0:T(128)} %bitcast.2.place_ref, s32[4,9]{1,0:T(4,128)} %lat_ref.7, s32[4,9]{1,0:T(4,128)} %lon_ref.7, s32[4,9]{1,0:T(4,128)} %basis_ref.7, f32[4,9]{1,0:T(4,128)} %value_ref.7, ...), custom_call_target="tpu_custom_call" | custom-call | flops 1000000000 | tf_op jit(solution)/shard_map/conv_rows/pallas_call | solution.py:144
  7.8 2.6 %collective-permute-start.1 = (bf16[128,384]{1,0:T(8,128)(2,1)}, bf16[128,384]{1,0:T(8,128)(2,1)S(1)}, u32[]{:S(2)}, u32[]{:S(2)}) collective-permute-start(bf16[128,384]{1,0:T(8,128)(2,1)} %get-tuple-element.11), channel_id=1, source_target_pairs={{0,8},{4,12},{8,0},{12,4},{1,9},{5,13},{9,1},{13,5},{2,10},{6,14},... | collective-permute-start | bytes 294920 | tf_op jit(solution)/shard_map/ppermute | solution.py:303
  10.3 1.3 %collective-permute-start.5 = (bf16[128,384]{1,0:T(8,128)(2,1)}, bf16[128,384]{1,0:T(8,128)(2,1)S(1)}, u32[]{:S(2)}, u32[]{:S(2)}) collective-permute-start(bf16[128,384]{1,0:T(8,128)(2,1)} %get-tuple-element.15), channel_id=1, source_target_pairs={{0,12},{4,8},{8,4},{12,0},{1,13},{5,9},{9,5},{13,1},{2,14},{6,10},... | collective-permute-start | bytes 294920 | tf_op jit(solution)/shard_map/ppermute | solution.py:303
  11.7 0.2 collective-permute-start.6
  11.9 0.1 copy.12
  12.1 0.1 copy.13
  12.2 5.9 %collective-permute-done.1.rest_2_.rest_1_ = bf16[128,384]{1,0:T(8,128)(2,1)S(1)} collective-permute-done((bf16[128,384]{1,0:T(8,128)(2,1)}, bf16[128,384]{1,0:T(8,128)(2,1)S(1)}, u32[]{:S(2)}, u32[]{:S(2)}) %collective-permute-start.1) | collective-permute-done | bytes 98336 | tf_op jit(solution)/shard_map/ppermute | solution.py:303
  18.1 0.0 collective-permute-done.rest_0_
  18.1 2.4 %conv_rows.5 = (bf16[128,384]{1,0:T(8,128)(2,1)S(1)}, bf16[128,384]{1,0:T(8,128)(2,1)S(1)}, bf16[128,384]{1,0:T(8,128)(2,1)S(1)}) custom-call(s32[1]{0:T(128)} %bitcast.3.pair_ref, s32[1]{0:T(128)} %bitcast.2.place_ref, s32[4,9]{1,0:T(4,128)S(1)} %copy-done.3, s32[4,9]{1,0:T(4,128)S(1)} %copy-done.4, s32[4,9]{1,0:T(4,128)S(1)} %copy-done.5, ...), custom_call_target="tpu_custom_call" | custom-call | flops 1000000000 | tf_op jit(solution)/shard_map/conv_rows/pallas_call | solution.py:144
  20.6 0.1 collective-permute-start.2
  20.7 2.9 %collective-permute-start.3 = (bf16[128,384]{1,0:T(8,128)(2,1)S(1)}, bf16[128,384]{1,0:T(8,128)(2,1)S(1)}, u32[]{:S(2)}, u32[]{:S(2)}) collective-permute-start(bf16[128,384]{1,0:T(8,128)(2,1)S(1)} %get-tuple-element.14), channel_id=1, source_target_pairs={{0,12},{4,8},{8,4},{12,0},{1,13},{5,9},{9,5},{13,1},{2,14},{6,10},... | collective-permute-start | bytes 294920 | tf_op jit(solution)/shard_map/ppermute | solution.py:303
  23.6 0.6 %collective-permute-start.4 = (bf16[128,384]{1,0:T(8,128)(2,1)S(1)}, bf16[128,384]{1,0:T(8,128)(2,1)S(1)}, u32[]{:S(2)}, u32[]{:S(2)}) collective-permute-start(bf16[128,384]{1,0:T(8,128)(2,1)S(1)} %get-tuple-element.12.rest_1_), channel_id=1, source_target_pairs={{0,4},{4,0},{8,12},{12,8},{1,5},{5,1},{9,13},{13,9},{2,6},{6,2},{1... | collective-permute-start | bytes 294920 | tf_op jit(solution)/shard_map/ppermute | solution.py:303
  24.1 1.5 %conv_rows.6.rest_2_.rest_0_ = bf16[128,384]{1,0:T(8,128)(2,1)S(1)} custom-call(s32[1]{0:T(128)} %bitcast.6.pair_ref, s32[1]{0:T(128)} %bitcast.2.place_ref, s32[4,9]{1,0:T(4,128)S(1)} %copy-done.3, s32[4,9]{1,0:T(4,128)S(1)} %copy-done.4, s32[4,9]{1,0:T(4,128)S(1)} %copy-done.5, f32[4,9]{1,0:T(4,128)S(1)} %copy-done.6, bf16[4,64,1440]{2,1,0:T(8,128)(2,1)S(1)} %bitcast.13, ...), custom_call_target="tpu_custom_call" | custom-call | flops 200000000 | tf_op jit(solution)/shard_map/conv_rows/pallas_call | solution.py:144
  25.7 1.5 %conv_rows.7.rest_7_.rest_0_ = bf16[128,384]{1,0:T(8,128)(2,1)S(1)} custom-call(s32[1]{0:T(128)} %bitcast.3.pair_ref, s32[1]{0:T(128)} %bitcast.2.place_ref, s32[4,9]{1,0:T(4,128)S(1)} %copy-done.3, s32[4,9]{1,0:T(4,128)S(1)} %copy-done.4, s32[4,9]{1,0:T(4,128)S(1)} %copy-done.5, f32[4,9]{1,0:T(4,128)S(1)} %copy-done.6, bf16[4,64,1440]{2,1,0:T(8,128)(2,1)S(1)} %bitcast.14, ...), custom_call_target="tpu_custom_call" | custom-call | flops 200000000 | tf_op jit(solution)/shard_map/conv_rows/pallas_call | solution.py:144
  27.2 0.0 collective-permute-done.5.rest_2_
  27.2 0.0 collective-permute-done.6.rest_3_
  27.2 1.2 %mlp_rows.2.rest_7_ = bf16[8,16,256]{2,1,0:T(8,128)(2,1)S(1)} custom-call(s32[1]{0:T(128)} %bitcast.2.place_ref, bf16[128,384]{1,0:T(8,128)(2,1)S(1)} %conv_rows.6.rest_2_.rest_0_, bf16[128,384]{1,0:T(8,128)(2,1)S(1)} %collective-permute-done.1.rest_2_.rest_1_, bf16[128,384]{1,0:T(8,128)(2,1)S(1)} %collective-permute-done.5.rest_2_, ...), custom_call_target="tpu_custom_call" | custom-call | flops 1000000000 | tf_op jit(solution)/shard_map/mlp_rows/pallas_call | solution.py:210
  28.4 0.0 copy-start.2
  28.4 0.0 copy-start.7
  28.4 2.1 %collective-permute-done.2.rest_1_ = bf16[128,384]{1,0:T(8,128)(2,1)S(1)} collective-permute-done((bf16[128,384]{1,0:T(8,128)(2,1)S(1)}, bf16[128,384]{1,0:T(8,128)(2,1)S(1)}, u32[]{:S(2)}, u32[]{:S(2)}) %collective-permute-start.2) | collective-permute-done | bytes 98336 | tf_op jit(solution)/shard_map/ppermute | solution.py:303
  30.5 0.4 collective-permute-done.4.rest_3_
  30.9 1.8 %mlp_rows.3 = bf16[8,32,256]{2,1,0:T(8,128)(2,1)} custom-call(s32[1]{0:T(128)} %bitcast.2.place_ref, bf16[128,384]{1,0:T(8,128)(2,1)S(1)} %conv_rows.7.rest_7_.rest_0_, bf16[128,384]{1,0:T(8,128)(2,1)S(1)} %collective-permute-done.2.rest_1_, bf16[128,384]{1,0:T(8,128)(2,1)S(1)} %collective-permute-done.3.rest_2_, ...), custom_call_target="tpu_custom_call" | custom-call | flops 1000000000 | tf_op jit(solution)/shard_map/mlp_rows/pallas_call | solution.py:210
  32.8 3.7 %all-to-all-start = ((bf16[8,32,256]{2,1,0:T(8,128)(2,1)}), bf16[8,32,256]{2,1,0:T(8,128)(2,1)S(1)}, u32[]{:S(2)}, u32[]{:S(2)}) async-start(bf16[8,32,256]{2,1,0:T(8,128)(2,1)} %mlp_rows.3), calls=%async_computation | async-start | bytes 262144 | tf_op jit(solution)/shard_map/all_to_all | solution.py:378
  36.5 0.8 %expand.1.left_ref = bf16[3,2,384,256]{3,2,1,0:T(8,128)(2,1)S(1)} custom-call(s32[1]{0:T(128)} %bitcast.start_ref, bf16[3,8,384]{2,1,0:T(8,128)(2,1)S(1)} %bitcast.20, bf16[8,256]{1,0:T(8,128)(2,1)S(1)} %copy-done.7), custom_call_target="tpu_custom_call" | custom-call | flops 200000000 | tf_op jit(solution)/shard_map/expand/pallas_call | solution.py:244
  37.3 6.8 %all-to-all-done = bf16[8,32,256]{2,1,0:T(8,128)(2,1)S(1)} async-done(((bf16[8,32,256]{2,1,0:T(8,128)(2,1)}), bf16[8,32,256]{2,1,0:T(8,128)(2,1)S(1)}, u32[]{:S(2)}, u32[]{:S(2)}) %all-to-all-start) | async-done | bytes 131104 | tf_op jit(solution)/shard_map/all_to_all | solution.py:378
  44.1 1.3 %final_sum.1 = bf16[3,384,512]{2,1,0:T(8,128)(2,1)} custom-call(bf16[3,2,384,256]{3,2,1,0:T(8,128)(2,1)S(1)} %expand.1.left_ref, bf16[256,256]{1,0:T(8,128)(2,1)S(1)} %bitcast.19), custom_call_target="tpu_custom_call" | custom-call | flops 1000000000 | tf_op jit(solution)/shard_map/final_sum/pallas_call | solution.py:278
  (17 shorter events, 0.0 us)
Async XLA Ops:
  1.0 17.1 %collective-permute-start = (bf16[2,64,1440]{2,1,0:T(8,128)(2,1)S(1)}, bf16[2,64,1440]{2,1,0:T(8,128)(2,1)S(1)}, u32[]{:S(2)}, u32[]{:S(2)}) collective-permute-start(bf16[2,64,1440]{2,1,0:T(8,128)(2,1)S(1)} %dynamic-slice_bitcast_fusion), channel_id=1, source_target_pairs={{0,16},{16,0},{1,17},{17,1},{2,18},{18,2},{3,19},{19,3},{4,20},{20... | collective-permute-start | bytes 1105928 | tf_op jit(solution)/shard_map/ppermute | solution.py:336
  4.1 7.9 %copy-start.9 = (bf16[256,512]{1,0:T(8,128)(2,1)S(1)}, bf16[256,512]{1,0:T(8,128)(2,1)}, u32[]{:S(2)}) copy-start(bf16[256,512]{1,0:T(8,128)(2,1)} %param.17) | copy-start | bytes 786436
  4.1 8.0 %copy-start.10 = (bf16[512,256]{1,0:T(8,128)(2,1)S(1)}, bf16[512,256]{1,0:T(8,128)(2,1)}, u32[]{:S(2)}) copy-start(bf16[512,256]{1,0:T(8,128)(2,1)} %param.18) | copy-start | bytes 786436
  4.1 14.0 %copy-start = (bf16[4,1440,64]{1,2,0:T(8,128)(2,1)S(1)}, bf16[4,1440,64]{1,2,0:T(8,128)(2,1)}, u32[]{:S(2)}) copy-start(bf16[4,1440,64]{1,2,0:T(8,128)(2,1)} %param.11) | copy-start | bytes 2211844
  4.1 14.0 %copy-start.1 = (bf16[6,64,64]{2,1,0:T(8,128)(2,1)S(1)}, bf16[6,64,64]{2,1,0:T(8,128)(2,1)}, u32[]{:S(2)}) copy-start(bf16[6,64,64]{2,1,0:T(8,128)(2,1)} %rest_1_.3) | copy-start | bytes 147460
  4.1 14.0 %copy-start.3 = (s32[4,9]{1,0:T(4,128)S(1)}, s32[4,9]{1,0:T(4,128)}, u32[]{:S(2)}) copy-start(s32[4,9]{1,0:T(4,128)} %lat_ref.7) | copy-start | bytes 436
  4.1 14.0 %copy-start.4 = (s32[4,9]{1,0:T(4,128)S(1)}, s32[4,9]{1,0:T(4,128)}, u32[]{:S(2)}) copy-start(s32[4,9]{1,0:T(4,128)} %lon_ref.7) | copy-start | bytes 436
  4.1 14.0 %copy-start.5 = (s32[4,9]{1,0:T(4,128)S(1)}, s32[4,9]{1,0:T(4,128)}, u32[]{:S(2)}) copy-start(s32[4,9]{1,0:T(4,128)} %basis_ref.7) | copy-start | bytes 436
  4.1 14.0 %copy-start.6 = (f32[4,9]{1,0:T(4,128)S(1)}, f32[4,9]{1,0:T(4,128)}, u32[]{:S(2)}) copy-start(f32[4,9]{1,0:T(4,128)} %value_ref.7) | copy-start | bytes 436
  7.8 10.3 %collective-permute-start.1 = (bf16[128,384]{1,0:T(8,128)(2,1)}, bf16[128,384]{1,0:T(8,128)(2,1)S(1)}, u32[]{:S(2)}, u32[]{:S(2)}) collective-permute-start(bf16[128,384]{1,0:T(8,128)(2,1)} %get-tuple-element.11), channel_id=1, source_target_pairs={{0,8},{4,12},{8,0},{12,4},{1,9},{5,13},{9,1},{13,5},{2,10},{6,14},... | collective-permute-start | bytes 294920 | tf_op jit(solution)/shard_map/ppermute | solution.py:303
  10.3 16.9 %collective-permute-start.5 = (bf16[128,384]{1,0:T(8,128)(2,1)}, bf16[128,384]{1,0:T(8,128)(2,1)S(1)}, u32[]{:S(2)}, u32[]{:S(2)}) collective-permute-start(bf16[128,384]{1,0:T(8,128)(2,1)} %get-tuple-element.15), channel_id=1, source_target_pairs={{0,12},{4,8},{8,4},{12,0},{1,13},{5,9},{9,5},{13,1},{2,14},{6,10},... | collective-permute-start | bytes 294920 | tf_op jit(solution)/shard_map/ppermute | solution.py:303
  11.7 15.5 %collective-permute-start.6 = (bf16[128,384]{1,0:T(8,128)(2,1)}, bf16[128,384]{1,0:T(8,128)(2,1)S(1)}, u32[]{:S(2)}, u32[]{:S(2)}) collective-permute-start(bf16[128,384]{1,0:T(8,128)(2,1)} %get-tuple-element.16), channel_id=1, source_target_pairs={{0,4},{4,0},{8,12},{12,8},{1,5},{5,1},{9,13},{13,9},{2,6},{6,2},{1... | collective-permute-start | bytes 294920 | tf_op jit(solution)/shard_map/ppermute | solution.py:303
  20.6 9.9 %collective-permute-start.2 = (bf16[128,384]{1,0:T(8,128)(2,1)S(1)}, bf16[128,384]{1,0:T(8,128)(2,1)S(1)}, u32[]{:S(2)}, u32[]{:S(2)}) collective-permute-start(bf16[128,384]{1,0:T(8,128)(2,1)S(1)} %get-tuple-element.13), channel_id=1, source_target_pairs={{0,8},{4,12},{8,0},{12,4},{1,9},{5,13},{9,1},{13,5},{2,10},{6,14},... | collective-permute-start | bytes 294920 | tf_op jit(solution)/shard_map/ppermute | solution.py:303
  20.7 9.9 %collective-permute-start.3 = (bf16[128,384]{1,0:T(8,128)(2,1)S(1)}, bf16[128,384]{1,0:T(8,128)(2,1)S(1)}, u32[]{:S(2)}, u32[]{:S(2)}) collective-permute-start(bf16[128,384]{1,0:T(8,128)(2,1)S(1)} %get-tuple-element.14), channel_id=1, source_target_pairs={{0,12},{4,8},{8,4},{12,0},{1,13},{5,9},{9,5},{13,1},{2,14},{6,10},... | collective-permute-start | bytes 294920 | tf_op jit(solution)/shard_map/ppermute | solution.py:303
  23.6 3.7 %copy-start.8 = (bf16[4,64,384]{2,1,0:T(8,128)(2,1)S(1)}, bf16[4,64,384]{2,1,0:T(8,128)(2,1)}, u32[]{:S(2)}) copy-start(bf16[4,64,384]{2,1,0:T(8,128)(2,1)} %constant.25.clone.rest_6_) | copy-start | bytes 589828
  23.6 7.4 %collective-permute-start.4 = (bf16[128,384]{1,0:T(8,128)(2,1)S(1)}, bf16[128,384]{1,0:T(8,128)(2,1)S(1)}, u32[]{:S(2)}, u32[]{:S(2)}) collective-permute-start(bf16[128,384]{1,0:T(8,128)(2,1)S(1)} %get-tuple-element.12.rest_1_), channel_id=1, source_target_pairs={{0,4},{4,0},{8,12},{12,8},{1,5},{5,1},{9,13},{13,9},{2,6},{6,2},{1... | collective-permute-start | bytes 294920 | tf_op jit(solution)/shard_map/ppermute | solution.py:303
  28.4 8.1 %copy-start.2 = (bf16[3,384,8]{1,2,0:T(8,128)(2,1)S(1)}, bf16[3,384,8]{1,2,0:T(8,128)(2,1)}, u32[]{:S(2)}) copy-start(bf16[3,384,8]{1,2,0:T(8,128)(2,1)} %param.19) | copy-start | bytes 55300
  28.4 8.1 %copy-start.7 = (bf16[8,256]{1,0:T(8,128)(2,1)S(1)}, bf16[8,256]{1,0:T(8,128)(2,1)}, u32[]{:S(2)}) copy-start(bf16[8,256]{1,0:T(8,128)(2,1)} %constant.26.clone.spread_ref) | copy-start | bytes 12292
  32.8 11.4 %all-to-all-start = ((bf16[8,32,256]{2,1,0:T(8,128)(2,1)}), bf16[8,32,256]{2,1,0:T(8,128)(2,1)S(1)}, u32[]{:S(2)}, u32[]{:S(2)}) async-start(bf16[8,32,256]{2,1,0:T(8,128)(2,1)} %mlp_rows.3), calls=%async_computation | async-start | bytes 262144 | tf_op jit(solution)/shard_map/all_to_all | solution.py:378

commit v11 on v10

--- a/solution.py
+++ b/solution.py
@@ -363,9 +363,9 @@
     ]
     received = []
     for half, edge in zip(halves, edges):
-        sent = conv_rows(*half, order, received[0][:1] if received else [], edge is None)
+        sent = conv_rows(*half, order, [], edge is None)
         received.append([turn(block, "chan", num_chan, k) for k, block in zip(order, sent)])
-    after = sent[-1:]
+    after = sent[1:2]
     for half, blocks in zip(halves, received):
         after = conv_rows(*half, (0,), after, False)
         blocks.insert(0, after[0])

time: 45.7 us -> 43.3 us (0.947)
  waiting for transfers between devices: 15.2 us -> 10.6 us
  starting transfers between devices: 14.4 us -> 16.7 us
    ppermute x6, waiting for transfers between devices: 8.39 us -> 2.93 us  [turn(): lax.ppermute(block, axis, [(i, target(i, k, count)) for i in range(count)])]
    all_to_all x1, starting transfers between devices: 3.71 us -> 4.94 us  [on_device(): lax.all_to_all(spectrum, both, split_axis=0, concat_axis=0, tiled=True)]
    ppermute x6, starting transfers between devices: 7.71 us -> 8.68 us  [turn(): lax.ppermute(block, axis, [(i, target(i, k, count)) for i in range(count)])]
    ppermute x1, waiting for transfers between devices: 0.01 us -> 0.96 us  [on_device(): edges = [None, lax.ppermute(edge_out, 'lat', [(0, 1), (1, 0)])]]
  transfers between devices with their start and end apart: 8 -> 8, of which waited for: 4 -> 4; matrix products, arithmetic and copies ran while one was open for 1% -> 1% of each run, Pallas kernels for 24% -> 26%
where the time goes in v11:
time: 43.3 us; the launch traced here: 43 us
  starting transfers between devices  16.7 us (39%)
  Pallas kernels  14.2 us (33%)
  waiting for transfers between devices  10.6 us (24%)
  local copies, waits for them, and re-layouts  1.35 us (3%)
    pallas_call x4, Pallas kernels, conv_rows(): pl.pallas_call(functools.partial(conv_kernel, chunks, picks, edge is not...  9.12 us
    ppermute x6, starting transfers between devices, turn(): lax.ppermute(block, axis, [(i, target(i, k, count)) for i in range(count)])  8.68 us
    all_to_all x1, waiting for transfers between devices, on_device(): lax.all_to_all(spectrum, both, split_axis=0, concat_axis=0, tiled=True)  6.69 us
    all_to_all x1, starting transfers between devices, on_device(): lax.all_to_all(spectrum, both, split_axis=0, concat_axis=0, tiled=True)  4.94 us
    ppermute x1, starting transfers between devices, on_device(): edges = [None, lax.ppermute(edge_out, 'lat', [(0, 1), (1, 0)])]  3.03 us
    pallas_call x2, Pallas kernels, mlp_rows(): pl.pallas_call(functools.partial(mlp_kernel, len(blocks), last, len(after...  2.99 us
    ppermute x6, waiting for transfers between devices, turn(): lax.ppermute(block, axis, [(i, target(i, k, count)) for i in range(count)])  2.93 us
    pallas_call x1, Pallas kernels, final_sum(): pl.pallas_call(final_kernel, out_shape=jax.ShapeDtypeStruct(shape, jnp.bf...  1.3 us
  transfers between devices with their start and end apart: 8, of which 4 were waited for; matrix products, arithmetic and copies ran while one was open for 1% of the time, Pallas kernels for 26%

profile of v11, /device:TPU:0, one launch (start us, length us, event | category | flops | bytes accessed | tf_op | source)
XLA Modules:
  0.0 43.0 jit_solution(16233996531635072187)
XLA Ops:
  0.0 1.0 %dynamic-slice_bitcast_fusion = bf16[2,64,1440]{2,1,0:T(8,128)(2,1)S(1)} fusion(bf16[4,1440,64]{1,2,0:T(8,128)(2,1)} %param.11, s32[]{:T(128)S(6)} %select_n.3), kind=kLoop, calls=%fused_computation | loop fusion | bytes 737284 | tf_op jit(solution)/shard_map/dynamic_slice | solution.py:335
  1.0 3.0 %collective-permute-start = (bf16[2,64,1440]{2,1,0:T(8,128)(2,1)S(1)}, bf16[2,64,1440]{2,1,0:T(8,128)(2,1)S(1)}, u32[]{:S(2)}, u32[]{:S(2)}) collective-permute-start(bf16[2,64,1440]{2,1,0:T(8,128)(2,1)S(1)} %dynamic-slice_bitcast_fusion), channel_id=1, source_target_pairs={{0,16},{16,0},{1,17},{17,1},{2,18},{18,2},{3,19},{19,3},{4,20},{20... | collective-permute-start | bytes 1105928 | tf_op jit(solution)/shard_map/ppermute | solution.py:336
  4.1 0.0 copy-start.3
  4.1 0.0 copy-start.4
  4.1 0.0 copy-start.5
  4.1 0.0 copy-start.6
  4.1 3.6 %conv_rows.7 = (bf16[128,384]{1,0:T(8,128)(2,1)}, bf16[128,384]{1,0:T(8,128)(2,1)}, bf16[128,384]{1,0:T(8,128)(2,1)}) custom-call(s32[1]{0:T(128)} %bitcast.6.pair_ref, s32[1]{0:T(128)} %bitcast.2.place_ref, s32[4,9]{1,0:T(4,128)} %lat_ref.7, s32[4,9]{1,0:T(4,128)} %lon_ref.7, s32[4,9]{1,0:T(4,128)} %basis_ref.7, f32[4,9]{1,0:T(4,128)} %value_ref.7, ...), custom_call_target="tpu_custom_call" | custom-call | flops 1000000000 | tf_op jit(solution)/shard_map/conv_rows/pallas_call | solution.py:144
  7.8 2.6 %collective-permute-start.4 = (bf16[128,384]{1,0:T(8,128)(2,1)}, bf16[128,384]{1,0:T(8,128)(2,1)S(1)}, u32[]{:S(2)}, u32[]{:S(2)}) collective-permute-start(bf16[128,384]{1,0:T(8,128)(2,1)} %get-tuple-element.14), channel_id=1, source_target_pairs={{0,8},{4,12},{8,0},{12,4},{1,9},{5,13},{9,1},{13,5},{2,10},{6,14},... | collective-permute-start | bytes 294920 | tf_op jit(solution)/shard_map/ppermute | solution.py:303
  10.3 1.3 %collective-permute-start.5 = (bf16[128,384]{1,0:T(8,128)(2,1)}, bf16[128,384]{1,0:T(8,128)(2,1)S(1)}, u32[]{:S(2)}, u32[]{:S(2)}) collective-permute-start(bf16[128,384]{1,0:T(8,128)(2,1)} %get-tuple-element.15), channel_id=1, source_target_pairs={{0,12},{4,8},{8,4},{12,0},{1,13},{5,9},{9,5},{13,1},{2,14},{6,10},... | collective-permute-start | bytes 294920 | tf_op jit(solution)/shard_map/ppermute | solution.py:303
  11.7 0.2 collective-permute-start.6
  11.9 0.1 copy.12
  12.1 0.1 copy.13
  12.2 1.0 %collective-permute-done.rest_0_ = bf16[2,64,1440]{2,1,0:T(8,128)(2,1)S(1)} collective-permute-done((bf16[2,64,1440]{2,1,0:T(8,128)(2,1)S(1)}, bf16[2,64,1440]{2,1,0:T(8,128)(2,1)S(1)}, u32[]{:S(2)}, u32[]{:S(2)}) %collective-permute-start) | collective-permute-done | bytes 368672 | tf_op jit(solution)/shard_map/ppermute | solution.py:336
  13.2 2.4 %conv_rows.4 = (bf16[128,384]{1,0:T(8,128)(2,1)S(1)}, bf16[128,384]{1,0:T(8,128)(2,1)S(1)}, bf16[128,384]{1,0:T(8,128)(2,1)S(1)}) custom-call(s32[1]{0:T(128)} %bitcast.3.pair_ref, s32[1]{0:T(128)} %bitcast.2.place_ref, s32[4,9]{1,0:T(4,128)S(1)} %copy-done.3, s32[4,9]{1,0:T(4,128)S(1)} %copy-done.4, s32[4,9]{1,0:T(4,128)S(1)} %copy-done.5, ...), custom_call_target="tpu_custom_call" | custom-call | flops 1000000000 | tf_op jit(solution)/shard_map/conv_rows/pallas_call | solution.py:144
  15.7 2.9 %collective-permute-start.1 = (bf16[128,384]{1,0:T(8,128)(2,1)S(1)}, bf16[128,384]{1,0:T(8,128)(2,1)S(1)}, u32[]{:S(2)}, u32[]{:S(2)}) collective-permute-start(bf16[128,384]{1,0:T(8,128)(2,1)S(1)} %get-tuple-element.12), channel_id=1, source_target_pairs={{0,8},{4,12},{8,0},{12,4},{1,9},{5,13},{9,1},{13,5},{2,10},{6,14},... | collective-permute-start | bytes 294920 | tf_op jit(solution)/shard_map/ppermute | solution.py:303
  18.5 1.3 %collective-permute-start.2 = (bf16[128,384]{1,0:T(8,128)(2,1)S(1)}, bf16[128,384]{1,0:T(8,128)(2,1)S(1)}, u32[]{:S(2)}, u32[]{:S(2)}) collective-permute-start(bf16[128,384]{1,0:T(8,128)(2,1)S(1)} %get-tuple-element.11.rest_1_), channel_id=1, source_target_pairs={{0,12},{4,8},{8,4},{12,0},{1,13},{5,9},{9,5},{13,1},{2,14},{6,10},... | collective-permute-start | bytes 294920 | tf_op jit(solution)/shard_map/ppermute | solution.py:303
  19.9 1.5 %conv_rows.5.rest_2_.rest_0_ = bf16[128,384]{1,0:T(8,128)(2,1)S(1)} custom-call(s32[1]{0:T(128)} %bitcast.6.pair_ref, s32[1]{0:T(128)} %bitcast.2.place_ref, s32[4,9]{1,0:T(4,128)S(1)} %copy-done.3, s32[4,9]{1,0:T(4,128)S(1)} %copy-done.4, s32[4,9]{1,0:T(4,128)S(1)} %copy-done.5, f32[4,9]{1,0:T(4,128)S(1)} %copy-done.6, bf16[4,64,1440]{2,1,0:T(8,128)(2,1)S(1)} %bitcast.13, ...), custom_call_target="tpu_custom_call" | custom-call | flops 200000000 | tf_op jit(solution)/shard_map/conv_rows/pallas_call | solution.py:144
  21.4 0.0 collective-permute-done.4.rest_1_
  21.4 0.3 collective-permute-start.3
  21.7 1.5 %conv_rows.6.rest_7_.rest_0_ = bf16[128,384]{1,0:T(8,128)(2,1)S(1)} custom-call(s32[1]{0:T(128)} %bitcast.3.pair_ref, s32[1]{0:T(128)} %bitcast.2.place_ref, s32[4,9]{1,0:T(4,128)S(1)} %copy-done.3, s32[4,9]{1,0:T(4,128)S(1)} %copy-done.4, s32[4,9]{1,0:T(4,128)S(1)} %copy-done.5, f32[4,9]{1,0:T(4,128)S(1)} %copy-done.6, bf16[4,64,1440]{2,1,0:T(8,128)(2,1)S(1)} %bitcast.14, ...), custom_call_target="tpu_custom_call" | custom-call | flops 200000000 | tf_op jit(solution)/shard_map/conv_rows/pallas_call | solution.py:144
  23.2 0.0 collective-permute-done.5.rest_2_
  23.3 1.2 %mlp_rows.2.rest_7_ = bf16[8,16,256]{2,1,0:T(8,128)(2,1)S(1)} custom-call(s32[1]{0:T(128)} %bitcast.2.place_ref, bf16[128,384]{1,0:T(8,128)(2,1)S(1)} %conv_rows.5.rest_2_.rest_0_, bf16[128,384]{1,0:T(8,128)(2,1)S(1)} %collective-permute-done.4.rest_1_, bf16[128,384]{1,0:T(8,128)(2,1)S(1)} %collective-permute-done.5.rest_2_, ...), custom_call_target="tpu_custom_call" | custom-call | flops 1000000000 | tf_op jit(solution)/shard_map/mlp_rows/pallas_call | solution.py:210
  24.5 0.0 copy-start.2
  24.5 0.0 copy-start.7
  24.5 2.0 %collective-permute-done.1.rest_1_ = bf16[128,384]{1,0:T(8,128)(2,1)S(1)} collective-permute-done((bf16[128,384]{1,0:T(8,128)(2,1)S(1)}, bf16[128,384]{1,0:T(8,128)(2,1)S(1)}, u32[]{:S(2)}, u32[]{:S(2)}) %collective-permute-start.1) | collective-permute-done | bytes 98336 | tf_op jit(solution)/shard_map/ppermute | solution.py:303
  26.5 0.9 %collective-permute-done.3.rest_3_ = bf16[128,384]{1,0:T(8,128)(2,1)S(1)} collective-permute-done((bf16[128,384]{1,0:T(8,128)(2,1)S(1)}, bf16[128,384]{1,0:T(8,128)(2,1)S(1)}, u32[]{:S(2)}, u32[]{:S(2)}) %collective-permute-start.3) | collective-permute-done | bytes 98336 | tf_op jit(solution)/shard_map/ppermute | solution.py:303
  27.4 0.0 collective-permute-done.2.rest_2_
  27.4 1.8 %mlp_rows.3 = bf16[8,32,256]{2,1,0:T(8,128)(2,1)} custom-call(s32[1]{0:T(128)} %bitcast.2.place_ref, bf16[128,384]{1,0:T(8,128)(2,1)S(1)} %conv_rows.6.rest_7_.rest_0_, bf16[128,384]{1,0:T(8,128)(2,1)S(1)} %collective-permute-done.1.rest_1_, bf16[128,384]{1,0:T(8,128)(2,1)S(1)} %collective-permute-done.2.rest_2_, ...), custom_call_target="tpu_custom_call" | custom-call | flops 1000000000 | tf_op jit(solution)/shard_map/mlp_rows/pallas_call | solution.py:210
  29.2 4.9 %all-to-all-start = ((bf16[8,32,256]{2,1,0:T(8,128)(2,1)}), bf16[8,32,256]{2,1,0:T(8,128)(2,1)S(1)}, u32[]{:S(2)}, u32[]{:S(2)}) async-start(bf16[8,32,256]{2,1,0:T(8,128)(2,1)} %mlp_rows.3), calls=%async_computation | async-start | bytes 262144 | tf_op jit(solution)/shard_map/all_to_all | solution.py:378
  34.2 0.8 %expand.1.left_ref = bf16[3,2,384,256]{3,2,1,0:T(8,128)(2,1)S(1)} custom-call(s32[1]{0:T(128)} %bitcast.start_ref, bf16[3,8,384]{2,1,0:T(8,128)(2,1)S(1)} %bitcast.20, bf16[8,256]{1,0:T(8,128)(2,1)S(1)} %copy-done.7), custom_call_target="tpu_custom_call" | custom-call | flops 200000000 | tf_op jit(solution)/shard_map/expand/pallas_call | solution.py:244
  35.0 6.7 %all-to-all-done = bf16[8,32,256]{2,1,0:T(8,128)(2,1)S(1)} async-done(((bf16[8,32,256]{2,1,0:T(8,128)(2,1)}), bf16[8,32,256]{2,1,0:T(8,128)(2,1)S(1)}, u32[]{:S(2)}, u32[]{:S(2)}) %all-to-all-start) | async-done | bytes 131104 | tf_op jit(solution)/shard_map/all_to_all | solution.py:378
  41.7 1.3 %final_sum.1 = bf16[3,384,512]{2,1,0:T(8,128)(2,1)} custom-call(bf16[3,2,384,256]{3,2,1,0:T(8,128)(2,1)S(1)} %expand.1.left_ref, bf16[256,256]{1,0:T(8,128)(2,1)S(1)} %bitcast.19), custom_call_target="tpu_custom_call" | custom-call | flops 1000000000 | tf_op jit(solution)/shard_map/final_sum/pallas_call | solution.py:278
  (17 shorter events, 0.0 us)
Async XLA Ops:
  1.0 12.1 %collective-permute-start = (bf16[2,64,1440]{2,1,0:T(8,128)(2,1)S(1)}, bf16[2,64,1440]{2,1,0:T(8,128)(2,1)S(1)}, u32[]{:S(2)}, u32[]{:S(2)}) collective-permute-start(bf16[2,64,1440]{2,1,0:T(8,128)(2,1)S(1)} %dynamic-slice_bitcast_fusion), channel_id=1, source_target_pairs={{0,16},{16,0},{1,17},{17,1},{2,18},{18,2},{3,19},{19,3},{4,20},{20... | collective-permute-start | bytes 1105928 | tf_op jit(solution)/shard_map/ppermute | solution.py:336
  4.1 7.9 %copy-start.9 = (bf16[256,512]{1,0:T(8,128)(2,1)S(1)}, bf16[256,512]{1,0:T(8,128)(2,1)}, u32[]{:S(2)}) copy-start(bf16[256,512]{1,0:T(8,128)(2,1)} %param.17) | copy-start | bytes 786436
  4.1 8.0 %copy-start.10 = (bf16[512,256]{1,0:T(8,128)(2,1)S(1)}, bf16[512,256]{1,0:T(8,128)(2,1)}, u32[]{:S(2)}) copy-start(bf16[512,256]{1,0:T(8,128)(2,1)} %param.18) | copy-start | bytes 786436
  4.1 9.1 %copy-start = (bf16[4,1440,64]{1,2,0:T(8,128)(2,1)S(1)}, bf16[4,1440,64]{1,2,0:T(8,128)(2,1)}, u32[]{:S(2)}) copy-start(bf16[4,1440,64]{1,2,0:T(8,128)(2,1)} %param.11) | copy-start | bytes 2211844
  4.1 9.1 %copy-start.1 = (bf16[6,64,64]{2,1,0:T(8,128)(2,1)S(1)}, bf16[6,64,64]{2,1,0:T(8,128)(2,1)}, u32[]{:S(2)}) copy-start(bf16[6,64,64]{2,1,0:T(8,128)(2,1)} %rest_0_.3) | copy-start | bytes 147460
  4.1 9.1 %copy-start.3 = (s32[4,9]{1,0:T(4,128)S(1)}, s32[4,9]{1,0:T(4,128)}, u32[]{:S(2)}) copy-start(s32[4,9]{1,0:T(4,128)} %lat_ref.7) | copy-start | bytes 436
  4.1 9.1 %copy-start.4 = (s32[4,9]{1,0:T(4,128)S(1)}, s32[4,9]{1,0:T(4,128)}, u32[]{:S(2)}) copy-start(s32[4,9]{1,0:T(4,128)} %lon_ref.7) | copy-start | bytes 436
  4.1 9.1 %copy-start.5 = (s32[4,9]{1,0:T(4,128)S(1)}, s32[4,9]{1,0:T(4,128)}, u32[]{:S(2)}) copy-start(s32[4,9]{1,0:T(4,128)} %basis_ref.7) | copy-start | bytes 436
  4.1 9.1 %copy-start.6 = (f32[4,9]{1,0:T(4,128)S(1)}, f32[4,9]{1,0:T(4,128)}, u32[]{:S(2)}) copy-start(f32[4,9]{1,0:T(4,128)} %value_ref.7) | copy-start | bytes 436
  7.8 13.7 %collective-permute-start.4 = (bf16[128,384]{1,0:T(8,128)(2,1)}, bf16[128,384]{1,0:T(8,128)(2,1)S(1)}, u32[]{:S(2)}, u32[]{:S(2)}) collective-permute-start(bf16[128,384]{1,0:T(8,128)(2,1)} %get-tuple-element.14), channel_id=1, source_target_pairs={{0,8},{4,12},{8,0},{12,4},{1,9},{5,13},{9,1},{13,5},{2,10},{6,14},... | collective-permute-start | bytes 294920 | tf_op jit(solution)/shard_map/ppermute | solution.py:303
  10.3 12.9 %collective-permute-start.5 = (bf16[128,384]{1,0:T(8,128)(2,1)}, bf16[128,384]{1,0:T(8,128)(2,1)S(1)}, u32[]{:S(2)}, u32[]{:S(2)}) collective-permute-start(bf16[128,384]{1,0:T(8,128)(2,1)} %get-tuple-element.15), channel_id=1, source_target_pairs={{0,12},{4,8},{8,4},{12,0},{1,13},{5,9},{9,5},{13,1},{2,14},{6,10},... | collective-permute-start | bytes 294920 | tf_op jit(solution)/shard_map/ppermute | solution.py:303
  11.7 11.6 %collective-permute-start.6 = (bf16[128,384]{1,0:T(8,128)(2,1)}, bf16[128,384]{1,0:T(8,128)(2,1)S(1)}, u32[]{:S(2)}, u32[]{:S(2)}) collective-permute-start(bf16[128,384]{1,0:T(8,128)(2,1)} %get-tuple-element.16), channel_id=1, source_target_pairs={{0,4},{4,0},{8,12},{12,8},{1,5},{5,1},{9,13},{13,9},{2,6},{6,2},{1... | collective-permute-start | bytes 294920 | tf_op jit(solution)/shard_map/ppermute | solution.py:303
  15.7 10.8 %collective-permute-start.1 = (bf16[128,384]{1,0:T(8,128)(2,1)S(1)}, bf16[128,384]{1,0:T(8,128)(2,1)S(1)}, u32[]{:S(2)}, u32[]{:S(2)}) collective-permute-start(bf16[128,384]{1,0:T(8,128)(2,1)S(1)} %get-tuple-element.12), channel_id=1, source_target_pairs={{0,8},{4,12},{8,0},{12,4},{1,9},{5,13},{9,1},{13,5},{2,10},{6,14},... | collective-permute-start | bytes 294920 | tf_op jit(solution)/shard_map/ppermute | solution.py:303
  18.5 4.7 %copy-start.8 = (bf16[4,64,384]{2,1,0:T(8,128)(2,1)S(1)}, bf16[4,64,384]{2,1,0:T(8,128)(2,1)}, u32[]{:S(2)}) copy-start(bf16[4,64,384]{2,1,0:T(8,128)(2,1)} %constant.25.clone.rest_6_) | copy-start | bytes 589828
  18.5 8.9 %collective-permute-start.2 = (bf16[128,384]{1,0:T(8,128)(2,1)S(1)}, bf16[128,384]{1,0:T(8,128)(2,1)S(1)}, u32[]{:S(2)}, u32[]{:S(2)}) collective-permute-start(bf16[128,384]{1,0:T(8,128)(2,1)S(1)} %get-tuple-element.11.rest_1_), channel_id=1, source_target_pairs={{0,12},{4,8},{8,4},{12,0},{1,13},{5,9},{9,5},{13,1},{2,14},{6,10},... | collective-permute-start | bytes 294920 | tf_op jit(solution)/shard_map/ppermute | solution.py:303
  21.4 6.0 %collective-permute-start.3 = (bf16[128,384]{1,0:T(8,128)(2,1)S(1)}, bf16[128,384]{1,0:T(8,128)(2,1)S(1)}, u32[]{:S(2)}, u32[]{:S(2)}) collective-permute-start(bf16[128,384]{1,0:T(8,128)(2,1)S(1)} %get-tuple-element.13), channel_id=1, source_target_pairs={{0,4},{4,0},{8,12},{12,8},{1,5},{5,1},{9,13},{13,9},{2,6},{6,2},{1... | collective-permute-start | bytes 294920 | tf_op jit(solution)/shard_map/ppermute | solution.py:303
  24.5 9.7 %copy-start.2 = (bf16[3,384,8]{1,2,0:T(8,128)(2,1)S(1)}, bf16[3,384,8]{1,2,0:T(8,128)(2,1)}, u32[]{:S(2)}) copy-start(bf16[3,384,8]{1,2,0:T(8,128)(2,1)} %param.19) | copy-start | bytes 55300
  24.5 9.7 %copy-start.7 = (bf16[8,256]{1,0:T(8,128)(2,1)S(1)}, bf16[8,256]{1,0:T(8,128)(2,1)}, u32[]{:S(2)}) copy-start(bf16[8,256]{1,0:T(8,128)(2,1)} %constant.26.clone.spread_ref) | copy-start | bytes 12292
  29.2 12.5 %all-to-all-start = ((bf16[8,32,256]{2,1,0:T(8,128)(2,1)}), bf16[8,32,256]{2,1,0:T(8,128)(2,1)S(1)}, u32[]{:S(2)}, u32[]{:S(2)}) async-start(bf16[8,32,256]{2,1,0:T(8,128)(2,1)} %mlp_rows.3), calls=%async_computation | async-start | bytes 262144 | tf_op jit(solution)/shard_map/all_to_all | solution.py:378

commit v12 on v11

--- a/solution.py
+++ b/solution.py
@@ -363,7 +363,11 @@
     ]
     received = []
     for half, edge in zip(halves, edges):
-        sent = conv_rows(*half, order, [], edge is None)
+        if edge is None:
+            sent = conv_rows(*half, order[:1], [], True)
+            sent = [*sent, *conv_rows(*half, order[1:], sent, True)]
+        else:
+            sent = conv_rows(*half, order, [], False)
         received.append([turn(block, "chan", num_chan, k) for k, block in zip(order, sent)])
     after = sent[1:2]
     for half, blocks in zip(halves, received):

time: 43.3 us -> 43.1 us (level)
  Pallas kernels: 14.2 us -> 16.3 us
  waiting for transfers between devices: 10.6 us -> 9.21 us
  starting transfers between devices: 16.7 us -> 15.7 us
    pallas_call x4 -> x5, Pallas kernels: 9.12 us -> 11.2 us  [conv_rows(): pl.pallas_call(functools.partial(conv_kernel, chunks, picks, edge is not...]
    ppermute x1, waiting for transfers between devices: 0.96 us -> 0.01 us  [on_device(): edges = [None, lax.ppermute(edge_out, 'lat', [(0, 1), (1, 0)])]]
    all_to_all x1, starting transfers between devices: 4.94 us -> 4.15 us  [on_device(): lax.all_to_all(spectrum, both, split_axis=0, concat_axis=0, tiled=True)]
  transfers between devices with their start and end apart: 8 -> 8, of which waited for: 4 -> 3; matrix products, arithmetic and copies ran while one was open for 1% -> 1% of each run, Pallas kernels for 26% -> 31%
where the time goes in v12:
time: 43.1 us; the launch traced here: 42.8 us
  Pallas kernels  16.3 us (38%)
  starting transfers between devices  15.7 us (36%)
  waiting for transfers between devices  9.21 us (21%)
  local copies, waits for them, and re-layouts  1.35 us (3%)
    pallas_call x5, Pallas kernels, conv_rows(): pl.pallas_call(functools.partial(conv_kernel, chunks, picks, edge is not...  11.2 us
    ppermute x6, starting transfers between devices, turn(): lax.ppermute(block, axis, [(i, target(i, k, count)) for i in range(count)])  8.54 us
    all_to_all x1, waiting for transfers between devices, on_device(): lax.all_to_all(spectrum, both, split_axis=0, concat_axis=0, tiled=True)  6.69 us
    all_to_all x1, starting transfers between devices, on_device(): lax.all_to_all(spectrum, both, split_axis=0, concat_axis=0, tiled=True)  4.15 us
    ppermute x1, starting transfers between devices, on_device(): edges = [None, lax.ppermute(edge_out, 'lat', [(0, 1), (1, 0)])]  3.03 us
    pallas_call x2, Pallas kernels, mlp_rows(): pl.pallas_call(functools.partial(mlp_kernel, len(blocks), last, len(after...  2.98 us
    ppermute x6, waiting for transfers between devices, turn(): lax.ppermute(block, axis, [(i, target(i, k, count)) for i in range(count)])  2.52 us
    pallas_call x1, Pallas kernels, final_sum(): pl.pallas_call(final_kernel, out_shape=jax.ShapeDtypeStruct(shape, jnp.bf...  1.3 us
  transfers between devices with their start and end apart: 8, of which 3 were waited for; matrix products, arithmetic and copies ran while one was open for 1% of the time, Pallas kernels for 31%

profile of v12, /device:TPU:0, one launch (start us, length us, event | category | flops | bytes accessed | tf_op | source)
XLA Modules:
  0.0 42.8 jit_solution(9887869216979384888)
XLA Ops:
  0.0 1.0 %dynamic-slice_bitcast_fusion = bf16[2,64,1440]{2,1,0:T(8,128)(2,1)S(1)} fusion(bf16[4,1440,64]{1,2,0:T(8,128)(2,1)} %param.11, s32[]{:T(128)S(6)} %select_n.3), kind=kLoop, calls=%fused_computation | loop fusion | bytes 737284 | tf_op jit(solution)/shard_map/dynamic_slice | solution.py:335
  1.0 3.0 %collective-permute-start = (bf16[2,64,1440]{2,1,0:T(8,128)(2,1)S(1)}, bf16[2,64,1440]{2,1,0:T(8,128)(2,1)S(1)}, u32[]{:S(2)}, u32[]{:S(2)}) collective-permute-start(bf16[2,64,1440]{2,1,0:T(8,128)(2,1)S(1)} %dynamic-slice_bitcast_fusion), channel_id=1, source_target_pairs={{0,16},{16,0},{1,17},{17,1},{2,18},{18,2},{3,19},{19,3},{4,20},{20... | collective-permute-start | bytes 1105928 | tf_op jit(solution)/shard_map/ppermute | solution.py:336
  4.1 2.6 %conv_rows.8.rest_1_ = bf16[128,384]{1,0:T(8,128)(2,1)} custom-call(s32[1]{0:T(128)} %bitcast.6.pair_ref, s32[1]{0:T(128)} %bitcast.2.place_ref, s32[4,9]{1,0:T(4,128)} %lat_ref.9, s32[4,9]{1,0:T(4,128)} %lon_ref.9, s32[4,9]{1,0:T(4,128)} %basis_ref.9, f32[4,9]{1,0:T(4,128)} %value_ref.9, bf16[4,64,1440]{2,1,0:T(8,128)(2,1)} %bitcast.11, ...), custom_call_target="tpu_custom_call" | custom-call | flops 200000000 | tf_op jit(solution)/shard_map/conv_rows/pallas_call | solution.py:144
  6.7 0.0 copy-start.1
  6.7 0.0 copy-start.2
  6.7 0.0 copy-start.3
  6.7 0.0 copy-start.4
  6.8 0.0 copy-start.5
  6.8 2.7 %collective-permute-start.4 = (bf16[128,384]{1,0:T(8,128)(2,1)}, bf16[128,384]{1,0:T(8,128)(2,1)S(1)}, u32[]{:S(2)}, u32[]{:S(2)}) collective-permute-start(bf16[128,384]{1,0:T(8,128)(2,1)} %conv_rows.8.rest_1_), channel_id=1, source_target_pairs={{0,8},{4,12},{8,0},{12,4},{1,9},{5,13},{9,1},{13,5},{2,10},{6,14},... | collective-permute-start | bytes 294920 | tf_op jit(solution)/shard_map/ppermute | solution.py:303
  9.4 3.1 %conv_rows.9 = (bf16[128,384]{1,0:T(8,128)(2,1)}, bf16[128,384]{1,0:T(8,128)(2,1)}) custom-call(s32[1]{0:T(128)} %bitcast.6.pair_ref, s32[1]{0:T(128)} %bitcast.2.place_ref, s32[4,9]{1,0:T(4,128)} %lat_ref.9, s32[4,9]{1,0:T(4,128)} %lon_ref.9, s32[4,9]{1,0:T(4,128)} %basis_ref.9, f32[4,9]{1,0:T(4,128)} %value_ref.9, bf16[4,64,1440]{2,1,0:T(8,128)(2,1)} %bitcast.12, ...), custom_call_target="tpu_custom_call" | custom-call | flops 1000000000 | tf_op jit(solution)/shard_map/conv_rows/pallas_call | solution.py:144
  12.5 1.4 %collective-permute-start.5 = (bf16[128,384]{1,0:T(8,128)(2,1)}, bf16[128,384]{1,0:T(8,128)(2,1)S(1)}, u32[]{:S(2)}, u32[]{:S(2)}) collective-permute-start(bf16[128,384]{1,0:T(8,128)(2,1)} %get-tuple-element.13), channel_id=1, source_target_pairs={{0,12},{4,8},{8,4},{12,0},{1,13},{5,9},{9,5},{13,1},{2,14},{6,10},... | collective-permute-start | bytes 294920 | tf_op jit(solution)/shard_map/ppermute | solution.py:303
  13.9 0.2 collective-permute-start.6
  14.1 0.1 copy.12
  14.3 0.1 copy.13
  14.4 0.0 collective-permute-done.rest_0_
  14.5 2.4 %conv_rows.5 = (bf16[128,384]{1,0:T(8,128)(2,1)S(1)}, bf16[128,384]{1,0:T(8,128)(2,1)S(1)}, bf16[128,384]{1,0:T(8,128)(2,1)S(1)}) custom-call(s32[1]{0:T(128)} %bitcast.3.pair_ref, s32[1]{0:T(128)} %bitcast.2.place_ref, s32[4,9]{1,0:T(4,128)S(1)} %copy-done.2, s32[4,9]{1,0:T(4,128)S(1)} %copy-done.3, s32[4,9]{1,0:T(4,128)S(1)} %copy-done.4, ...), custom_call_target="tpu_custom_call" | custom-call | flops 1000000000 | tf_op jit(solution)/shard_map/conv_rows/pallas_call | solution.py:144
  16.9 2.9 %collective-permute-start.1 = (bf16[128,384]{1,0:T(8,128)(2,1)S(1)}, bf16[128,384]{1,0:T(8,128)(2,1)S(1)}, u32[]{:S(2)}, u32[]{:S(2)}) collective-permute-start(bf16[128,384]{1,0:T(8,128)(2,1)S(1)} %get-tuple-element.11), channel_id=1, source_target_pairs={{0,8},{4,12},{8,0},{12,4},{1,9},{5,13},{9,1},{13,5},{2,10},{6,14},... | collective-permute-start | bytes 294920 | tf_op jit(solution)/shard_map/ppermute | solution.py:303
  19.8 1.4 %collective-permute-start.2 = (bf16[128,384]{1,0:T(8,128)(2,1)S(1)}, bf16[128,384]{1,0:T(8,128)(2,1)S(1)}, u32[]{:S(2)}, u32[]{:S(2)}) collective-permute-start(bf16[128,384]{1,0:T(8,128)(2,1)S(1)} %get-tuple-element.10.rest_1_), channel_id=1, source_target_pairs={{0,12},{4,8},{8,4},{12,0},{1,13},{5,9},{9,5},{13,1},{2,14},{6,10},... | collective-permute-start | bytes 294920 | tf_op jit(solution)/shard_map/ppermute | solution.py:303
  21.2 1.5 %conv_rows.6.rest_2_.rest_0_ = bf16[128,384]{1,0:T(8,128)(2,1)S(1)} custom-call(s32[1]{0:T(128)} %bitcast.6.pair_ref, s32[1]{0:T(128)} %bitcast.2.place_ref, s32[4,9]{1,0:T(4,128)S(1)} %copy-done.2, s32[4,9]{1,0:T(4,128)S(1)} %copy-done.3, s32[4,9]{1,0:T(4,128)S(1)} %copy-done.4, f32[4,9]{1,0:T(4,128)S(1)} %copy-done.5, bf16[4,64,1440]{2,1,0:T(8,128)(2,1)S(1)} %bitcast.14, ...), custom_call_target="tpu_custom_call" | custom-call | flops 200000000 | tf_op jit(solution)/shard_map/conv_rows/pallas_call | solution.py:144
  22.7 0.0 collective-permute-done.4.rest_1_
  22.7 0.1 collective-permute-start.3
  22.8 1.5 %conv_rows.7.rest_7_.rest_0_ = bf16[128,384]{1,0:T(8,128)(2,1)S(1)} custom-call(s32[1]{0:T(128)} %bitcast.3.pair_ref, s32[1]{0:T(128)} %bitcast.2.place_ref, s32[4,9]{1,0:T(4,128)S(1)} %copy-done.2, s32[4,9]{1,0:T(4,128)S(1)} %copy-done.3, s32[4,9]{1,0:T(4,128)S(1)} %copy-done.4, f32[4,9]{1,0:T(4,128)S(1)} %copy-done.5, bf16[4,64,1440]{2,1,0:T(8,128)(2,1)S(1)} %bitcast.15, ...), custom_call_target="tpu_custom_call" | custom-call | flops 200000000 | tf_op jit(solution)/shard_map/conv_rows/pallas_call | solution.py:144
  24.3 1.2 %mlp_rows.2.rest_7_ = bf16[8,16,256]{2,1,0:T(8,128)(2,1)S(1)} custom-call(s32[1]{0:T(128)} %bitcast.2.place_ref, bf16[128,384]{1,0:T(8,128)(2,1)S(1)} %conv_rows.6.rest_2_.rest_0_, bf16[128,384]{1,0:T(8,128)(2,1)S(1)} %collective-permute-done.4.rest_1_, bf16[128,384]{1,0:T(8,128)(2,1)S(1)} %collective-permute-done.5.rest_2_, ...), custom_call_target="tpu_custom_call" | custom-call | flops 1000000000 | tf_op jit(solution)/shard_map/mlp_rows/pallas_call | solution.py:210
  25.5 0.0 copy-start.6
  25.5 0.0 copy-start.7
  25.5 1.6 %collective-permute-done.1.rest_1_ = bf16[128,384]{1,0:T(8,128)(2,1)S(1)} collective-permute-done((bf16[128,384]{1,0:T(8,128)(2,1)S(1)}, bf16[128,384]{1,0:T(8,128)(2,1)S(1)}, u32[]{:S(2)}, u32[]{:S(2)}) %collective-permute-start.1) | collective-permute-done | bytes 98336 | tf_op jit(solution)/shard_map/ppermute | solution.py:303
  27.2 0.9 %collective-permute-done.3.rest_3_ = bf16[128,384]{1,0:T(8,128)(2,1)S(1)} collective-permute-done((bf16[128,384]{1,0:T(8,128)(2,1)S(1)}, bf16[128,384]{1,0:T(8,128)(2,1)S(1)}, u32[]{:S(2)}, u32[]{:S(2)}) %collective-permute-start.3) | collective-permute-done | bytes 98336 | tf_op jit(solution)/shard_map/ppermute | solution.py:303
  28.1 1.8 %mlp_rows.3 = bf16[8,32,256]{2,1,0:T(8,128)(2,1)} custom-call(s32[1]{0:T(128)} %bitcast.2.place_ref, bf16[128,384]{1,0:T(8,128)(2,1)S(1)} %conv_rows.7.rest_7_.rest_0_, bf16[128,384]{1,0:T(8,128)(2,1)S(1)} %collective-permute-done.1.rest_1_, bf16[128,384]{1,0:T(8,128)(2,1)S(1)} %collective-permute-done.2.rest_2_, ...), custom_call_target="tpu_custom_call" | custom-call | flops 1000000000 | tf_op jit(solution)/shard_map/mlp_rows/pallas_call | solution.py:210
  29.9 4.1 %all-to-all-start = ((bf16[8,32,256]{2,1,0:T(8,128)(2,1)}), bf16[8,32,256]{2,1,0:T(8,128)(2,1)S(1)}, u32[]{:S(2)}, u32[]{:S(2)}) async-start(bf16[8,32,256]{2,1,0:T(8,128)(2,1)} %mlp_rows.3), calls=%async_computation | async-start | bytes 262144 | tf_op jit(solution)/shard_map/all_to_all | solution.py:382
  34.0 0.8 %expand.1.left_ref = bf16[3,2,384,256]{3,2,1,0:T(8,128)(2,1)S(1)} custom-call(s32[1]{0:T(128)} %bitcast.start_ref, bf16[3,8,384]{2,1,0:T(8,128)(2,1)S(1)} %bitcast.21, bf16[8,256]{1,0:T(8,128)(2,1)S(1)} %copy-done.7), custom_call_target="tpu_custom_call" | custom-call | flops 200000000 | tf_op jit(solution)/shard_map/expand/pallas_call | solution.py:244
  34.9 6.7 %all-to-all-done = bf16[8,32,256]{2,1,0:T(8,128)(2,1)S(1)} async-done(((bf16[8,32,256]{2,1,0:T(8,128)(2,1)}), bf16[8,32,256]{2,1,0:T(8,128)(2,1)S(1)}, u32[]{:S(2)}, u32[]{:S(2)}) %all-to-all-start) | async-done | bytes 131104 | tf_op jit(solution)/shard_map/all_to_all | solution.py:382
  41.5 1.3 %final_sum.1 = bf16[3,384,512]{2,1,0:T(8,128)(2,1)} custom-call(bf16[3,2,384,256]{3,2,1,0:T(8,128)(2,1)S(1)} %expand.1.left_ref, bf16[256,256]{1,0:T(8,128)(2,1)S(1)} %bitcast.20), custom_call_target="tpu_custom_call" | custom-call | flops 1000000000 | tf_op jit(solution)/shard_map/final_sum/pallas_call | solution.py:278
  (18 shorter events, 0.0 us)
Async XLA Ops:
  1.0 13.4 %collective-permute-start = (bf16[2,64,1440]{2,1,0:T(8,128)(2,1)S(1)}, bf16[2,64,1440]{2,1,0:T(8,128)(2,1)S(1)}, u32[]{:S(2)}, u32[]{:S(2)}) collective-permute-start(bf16[2,64,1440]{2,1,0:T(8,128)(2,1)S(1)} %dynamic-slice_bitcast_fusion), channel_id=1, source_target_pairs={{0,16},{16,0},{1,17},{17,1},{2,18},{18,2},{3,19},{19,3},{4,20},{20... | collective-permute-start | bytes 1105928 | tf_op jit(solution)/shard_map/ppermute | solution.py:336
  6.7 7.4 %copy-start.9 = (bf16[256,512]{1,0:T(8,128)(2,1)S(1)}, bf16[256,512]{1,0:T(8,128)(2,1)}, u32[]{:S(2)}) copy-start(bf16[256,512]{1,0:T(8,128)(2,1)} %param.17) | copy-start | bytes 786436
  6.7 7.5 %copy-start.10 = (bf16[512,256]{1,0:T(8,128)(2,1)S(1)}, bf16[512,256]{1,0:T(8,128)(2,1)}, u32[]{:S(2)}) copy-start(bf16[512,256]{1,0:T(8,128)(2,1)} %param.18) | copy-start | bytes 786436
  6.7 7.7 %copy-start = (bf16[4,1440,64]{1,2,0:T(8,128)(2,1)S(1)}, bf16[4,1440,64]{1,2,0:T(8,128)(2,1)}, u32[]{:S(2)}) copy-start(bf16[4,1440,64]{1,2,0:T(8,128)(2,1)} %param.11) | copy-start | bytes 2211844
  6.7 7.7 %copy-start.1 = (bf16[6,64,64]{2,1,0:T(8,128)(2,1)S(1)}, bf16[6,64,64]{2,1,0:T(8,128)(2,1)}, u32[]{:S(2)}) copy-start(bf16[6,64,64]{2,1,0:T(8,128)(2,1)} %rest_0_.5) | copy-start | bytes 147460
  6.7 7.7 %copy-start.2 = (s32[4,9]{1,0:T(4,128)S(1)}, s32[4,9]{1,0:T(4,128)}, u32[]{:S(2)}) copy-start(s32[4,9]{1,0:T(4,128)} %lat_ref.9) | copy-start | bytes 436
  6.7 7.7 %copy-start.3 = (s32[4,9]{1,0:T(4,128)S(1)}, s32[4,9]{1,0:T(4,128)}, u32[]{:S(2)}) copy-start(s32[4,9]{1,0:T(4,128)} %lon_ref.9) | copy-start | bytes 436
  6.7 7.7 %copy-start.4 = (s32[4,9]{1,0:T(4,128)S(1)}, s32[4,9]{1,0:T(4,128)}, u32[]{:S(2)}) copy-start(s32[4,9]{1,0:T(4,128)} %basis_ref.9) | copy-start | bytes 436
  6.8 7.7 %copy-start.5 = (f32[4,9]{1,0:T(4,128)S(1)}, f32[4,9]{1,0:T(4,128)}, u32[]{:S(2)}) copy-start(f32[4,9]{1,0:T(4,128)} %value_ref.9) | copy-start | bytes 436
  6.8 15.9 %collective-permute-start.4 = (bf16[128,384]{1,0:T(8,128)(2,1)}, bf16[128,384]{1,0:T(8,128)(2,1)S(1)}, u32[]{:S(2)}, u32[]{:S(2)}) collective-permute-start(bf16[128,384]{1,0:T(8,128)(2,1)} %conv_rows.8.rest_1_), channel_id=1, source_target_pairs={{0,8},{4,12},{8,0},{12,4},{1,9},{5,13},{9,1},{13,5},{2,10},{6,14},... | collective-permute-start | bytes 294920 | tf_op jit(solution)/shard_map/ppermute | solution.py:303
  12.5 11.8 %collective-permute-start.5 = (bf16[128,384]{1,0:T(8,128)(2,1)}, bf16[128,384]{1,0:T(8,128)(2,1)S(1)}, u32[]{:S(2)}, u32[]{:S(2)}) collective-permute-start(bf16[128,384]{1,0:T(8,128)(2,1)} %get-tuple-element.13), channel_id=1, source_target_pairs={{0,12},{4,8},{8,4},{12,0},{1,13},{5,9},{9,5},{13,1},{2,14},{6,10},... | collective-permute-start | bytes 294920 | tf_op jit(solution)/shard_map/ppermute | solution.py:303
  13.9 10.4 %collective-permute-start.6 = (bf16[128,384]{1,0:T(8,128)(2,1)}, bf16[128,384]{1,0:T(8,128)(2,1)S(1)}, u32[]{:S(2)}, u32[]{:S(2)}) collective-permute-start(bf16[128,384]{1,0:T(8,128)(2,1)} %get-tuple-element.14), channel_id=1, source_target_pairs={{0,4},{4,0},{8,12},{12,8},{1,5},{5,1},{9,13},{13,9},{2,6},{6,2},{1... | collective-permute-start | bytes 294920 | tf_op jit(solution)/shard_map/ppermute | solution.py:303
  16.9 10.2 %collective-permute-start.1 = (bf16[128,384]{1,0:T(8,128)(2,1)S(1)}, bf16[128,384]{1,0:T(8,128)(2,1)S(1)}, u32[]{:S(2)}, u32[]{:S(2)}) collective-permute-start(bf16[128,384]{1,0:T(8,128)(2,1)S(1)} %get-tuple-element.11), channel_id=1, source_target_pairs={{0,8},{4,12},{8,0},{12,4},{1,9},{5,13},{9,1},{13,5},{2,10},{6,14},... | collective-permute-start | bytes 294920 | tf_op jit(solution)/shard_map/ppermute | solution.py:303
  19.8 4.5 %copy-start.8 = (bf16[4,64,384]{2,1,0:T(8,128)(2,1)S(1)}, bf16[4,64,384]{2,1,0:T(8,128)(2,1)}, u32[]{:S(2)}) copy-start(bf16[4,64,384]{2,1,0:T(8,128)(2,1)} %constant.25.clone.rest_6_) | copy-start | bytes 589828
  19.8 8.2 %collective-permute-start.2 = (bf16[128,384]{1,0:T(8,128)(2,1)S(1)}, bf16[128,384]{1,0:T(8,128)(2,1)S(1)}, u32[]{:S(2)}, u32[]{:S(2)}) collective-permute-start(bf16[128,384]{1,0:T(8,128)(2,1)S(1)} %get-tuple-element.10.rest_1_), channel_id=1, source_target_pairs={{0,12},{4,8},{8,4},{12,0},{1,13},{5,9},{9,5},{13,1},{2,14},{6,10},... | collective-permute-start | bytes 294920 | tf_op jit(solution)/shard_map/ppermute | solution.py:303
  22.7 5.4 %collective-permute-start.3 = (bf16[128,384]{1,0:T(8,128)(2,1)S(1)}, bf16[128,384]{1,0:T(8,128)(2,1)S(1)}, u32[]{:S(2)}, u32[]{:S(2)}) collective-permute-start(bf16[128,384]{1,0:T(8,128)(2,1)S(1)} %get-tuple-element.12), channel_id=1, source_target_pairs={{0,4},{4,0},{8,12},{12,8},{1,5},{5,1},{9,13},{13,9},{2,6},{6,2},{1... | collective-permute-start | bytes 294920 | tf_op jit(solution)/shard_map/ppermute | solution.py:303
  25.5 8.5 %copy-start.6 = (bf16[3,384,8]{1,2,0:T(8,128)(2,1)S(1)}, bf16[3,384,8]{1,2,0:T(8,128)(2,1)}, u32[]{:S(2)}) copy-start(bf16[3,384,8]{1,2,0:T(8,128)(2,1)} %param.19) | copy-start | bytes 55300
  25.5 8.5 %copy-start.7 = (bf16[8,256]{1,0:T(8,128)(2,1)S(1)}, bf16[8,256]{1,0:T(8,128)(2,1)}, u32[]{:S(2)}) copy-start(bf16[8,256]{1,0:T(8,128)(2,1)} %constant.26.clone.spread_ref) | copy-start | bytes 12292
  29.9 11.7 %all-to-all-start = ((bf16[8,32,256]{2,1,0:T(8,128)(2,1)}), bf16[8,32,256]{2,1,0:T(8,128)(2,1)S(1)}, u32[]{:S(2)}, u32[]{:S(2)}) async-start(bf16[8,32,256]{2,1,0:T(8,128)(2,1)} %mlp_rows.3), calls=%async_computation | async-start | bytes 262144 | tf_op jit(solution)/shard_map/all_to_all | solution.py:382

commit v13 on v11

--- a/solution.py
+++ b/solution.py
@@ -157,12 +157,12 @@
     )(pair, place, *supports, *arrays, *after)
 
 
-def mlp_kernel(parts, last, after, place_ref, *rest):
+def mlp_kernel(parts, last, after, place_ref, me_ref, *rest):
     blocks, rest = rest[:parts], rest[parts:]
     up_ref, down_ref, table_ref, *rest = rest
     rest = rest[after:]
     if last:
-        earlier_ref, out_ref, cells_ref = rest
+        earlier_ref, *out_refs, gather_ref, cells_ref = rest
     else:
         out_ref, cells_ref = rest
     width = blocks[0].shape[1]
@@ -194,32 +194,45 @@
         )
         found.append(modes.reshape(modes.shape[0] // SLOT, SLOT, modes.shape[1]))
     block = jnp.concatenate(found, axis=1).astype(jnp.bfloat16)
-    if last:
-        out_ref[:, 0 : 2 * SLOT, :] = earlier_ref[...]
-        out_ref[:, 2 * SLOT : 4 * SLOT, :] = block
-    else:
+    if not last:
         out_ref[...] = block
-
-
-def mlp_rows(place, blocks, up, down, tables, earlier, dests, after):
+        return
+    gather_ref[:, 0 : 2 * SLOT, :] = earlier_ref[...]
+    gather_ref[:, 2 * SLOT : 4 * SLOT, :] = block
+    if len(out_refs) == 1:
+        out_refs[0][...] = gather_ref[...]
+        return
+    for out_ref, k in zip(out_refs, [0, *issue_order(len(out_refs))]):
+        out_ref[...] = gather_ref[target(me_ref[0], k, len(out_refs))]
+
+
+def mlp_rows(place, me, blocks, up, down, tables, earlier, dests, after):
     pair_chans, width = blocks[0].shape
     chan = len(blocks) * pair_chans // 2
     last = earlier is not None
     arrays = [*blocks, up, down, tables, *after] + ([earlier] if last else [])
-    rows = (4 if last else 2) * SLOT
+    shape = (dests, (4 if last else 2) * SLOT, chan)
+    outs = jax.ShapeDtypeStruct(shape, jnp.bfloat16)
+    out_specs = VMEM
+    if last:
+        count = dests if dests <= FEW else 1
+        split = shape if count == 1 else shape[1:]
+        outs = [jax.ShapeDtypeStruct(split, jnp.bfloat16)] * count
+        out_specs = [VMEM] * count
     return pl.pallas_call(
         functools.partial(mlp_kernel, len(blocks), last, len(after)),
-        out_shape=jax.ShapeDtypeStruct((dests, rows, chan), jnp.bfloat16),
-        in_specs=[SMEM]
+        out_shape=outs,
+        in_specs=[SMEM] * 2
         + [VMEM] * (len(blocks) + 3)
         + [ANY] * len(after)
         + [VMEM] * last,
-        out_specs=VMEM,
-        scratch_shapes=[pltpu.VMEM((chan, 2 * width), jnp.bfloat16)],
+        out_specs=out_specs,
+        scratch_shapes=[pltpu.VMEM(shape, jnp.bfloat16)] * last
+        + [pltpu.VMEM((chan, 2 * width), jnp.bfloat16)],
         compiler_params=params(20 if dests <= FEW else 40),
         cost_estimate=takes(1),
         name="mlp_rows",
-    )(place, *arrays)
+    )(place, me, *arrays)
 
 
 def expand_kernel(start_ref, legendre_ref, spread_ref, out_ref):
@@ -257,9 +270,16 @@
     )(start, legendre, spread)
 
 
-def final_kernel(left_ref, spectrum_ref, out_ref, result_ref, sems):
+def final_kernel(me_ref, left_ref, *rest):
+    *blocks, out_ref, spectrum_ref, result_ref, sems = rest
     modes = left_ref.shape[0]
-    chan = spectrum_ref.shape[1]
+    depth, chan = spectrum_ref.shape
+    count = len(blocks)
+    rows = depth // count
+    order = [0, *issue_order(count)] if count > 1 else [0]
+    for block, k in zip(blocks, order):
+        origin = source(me_ref[0], k, count) * rows if count > 1 else 0
+        spectrum_ref[pl.ds(pl.multiple_of(origin, rows), rows), :] = block[...]
     copies = []
     for m in range(modes):
         for r in range(2):
@@ -272,19 +292,24 @@
         copy.wait()
 
 
-def final_sum(left, spectrum):
+def final_sum(me, left, blocks):
     modes, _, degrees, depth = left.shape
-    shape = (modes, degrees, 2 * spectrum.shape[1])
+    chan = blocks[0].shape[1]
+    shape = (modes, degrees, 2 * chan)
     return pl.pallas_call(
         final_kernel,
         out_shape=jax.ShapeDtypeStruct(shape, jnp.bfloat16),
-        in_specs=[VMEM, VMEM],
+        in_specs=[SMEM] + [VMEM] * (1 + len(blocks)),
         out_specs=HBM,
-        scratch_shapes=[pltpu.VMEM(shape, jnp.bfloat16), pltpu.SemaphoreType.DMA((modes,))],
+        scratch_shapes=[
+            pltpu.VMEM((depth, chan), jnp.bfloat16),
+            pltpu.VMEM(shape, jnp.bfloat16),
+            pltpu.SemaphoreType.DMA((modes,)),
+        ],
         compiler_params=params(8 if depth <= 512 else 48),
         cost_estimate=takes(1),
         name="final_sum",
-    )(left, spectrum)
+    )(me, left, *blocks)
 
 
 def fourier_blocks(lon, chunks, width, dests, mode_dev):
@@ -327,6 +352,7 @@
     band = lax.axis_index("lat")
     place = scalar(lax.axis_index("chan"))
     index = lax.axis_index(("lat", "chan"))
+    me = scalar(index)
     supports = (support_lat, support_lon, support_basis, support_value)
 
     two_bands = num_lat == 2
@@ -370,13 +396,20 @@
         after = conv_rows(*half, (0,), after, False)
         blocks.insert(0, after[0])
     spectrum = None
+    after = [*after, left]
     for blocks in received:
-        spectrum = mlp_rows(place, blocks, up, down, tables, spectrum, dests, list(after))
+        spectrum = mlp_rows(place, me, blocks, up, down, tables, spectrum, dests, after)
         after = []
 
     both = ("lat", "chan")
-    gathered = lax.all_to_all(spectrum, both, split_axis=0, concat_axis=0, tiled=True)
-    return final_sum(left, gathered.reshape(depth, gathered.shape[2]))
+    if dests <= FEW:
+        blocks = [spectrum[0]] + [
+            turn(block, both, dests, k) for k, block in zip(issue_order(dests), spectrum[1:])
+        ]
+    else:
+        whole = lax.all_to_all(spectrum[0], both, split_axis=0, concat_axis=0, tiled=True)
+        blocks = [whole.reshape(depth, whole.shape[2])]
+    return final_sum(me, left, blocks)
 
 
 def solution(mesh):

time: 43.3 us -> 45.5 us (1.051)
  starting transfers between devices: 16.7 us -> 22.1 us
  waiting for transfers between devices: 10.6 us -> 8.14 us
  Pallas kernels: 14.2 us -> 13.5 us
    ppermute x6 -> x13, starting transfers between devices: 8.68 us -> 19.1 us  [turn(): lax.ppermute(block, axis, [(i, target(i, k, count)) for i in range(count)])]
    all_to_all x1 -> x0, waiting for transfers between devices: 6.69 us -> none  [on_device(): lax.all_to_all(spectrum, both, split_axis=0, concat_axis=0, tiled=True)]
    ppermute x6 -> x13, waiting for transfers between devices: 2.93 us -> 8.05 us  [turn(): lax.ppermute(block, axis, [(i, target(i, k, count)) for i in range(count)])]
    all_to_all x1 -> x0, starting transfers between devices: 4.94 us -> none  [on_device(): lax.all_to_all(spectrum, both, split_axis=0, concat_axis=0, tiled=True)]
    ppermute x1, waiting for transfers between devices: 0.96 us -> 0.09 us  [on_device(): edges = [None, lax.ppermute(edge_out, 'lat', [(0, 1), (1, 0)])]]
    pallas_call x2, Pallas kernels: 2.99 us -> 2.34 us  [mlp_rows(): pl.pallas_call(functools.partial(mlp_kernel, len(blocks), last, len(after...]
  transfers between devices with their start and end apart: 8 -> 14, of which waited for: 4 -> 5; matrix products, arithmetic and copies ran while one was open for 1% -> 1% of each run, Pallas kernels for 26% -> 24%
where the time goes in v13:
time: 45.5 us; the launch traced here: 45.3 us
  starting transfers between devices  22.1 us (49%)
  Pallas kernels  13.5 us (30%)
  waiting for transfers between devices  8.14 us (18%)
  local copies, waits for them, and re-layouts  1.34 us (3%)
    ppermute x13, starting transfers between devices, turn(): lax.ppermute(block, axis, [(i, target(i, k, count)) for i in range(count)])  19.1 us
    pallas_call x4, Pallas kernels, conv_rows(): pl.pallas_call(functools.partial(conv_kernel, chunks, picks, edge is not...  9.09 us
    ppermute x13, waiting for transfers between devices, turn(): lax.ppermute(block, axis, [(i, target(i, k, count)) for i in range(count)])  8.05 us
    ppermute x1, starting transfers between devices, on_device(): edges = [None, lax.ppermute(edge_out, 'lat', [(0, 1), (1, 0)])]  3.03 us
    pallas_call x2, Pallas kernels, mlp_rows(): pl.pallas_call(functools.partial(mlp_kernel, len(blocks), last, len(after...  2.34 us
    pallas_call x1, Pallas kernels, final_sum(): pl.pallas_call(final_kernel, out_shape=jax.ShapeDtypeStruct(shape, jnp.bf...  1.31 us
    dynamic_slice x1, local copies, waits for them, and re-layouts, on_device(): edge_out = lax.dynamic_slice_in_dim(cells, HALO * (1 - band), HALO, axis=0)  1.02 us
  transfers between devices with their start and end apart: 14, of which 5 were waited for; matrix products, arithmetic and copies ran while one was open for 1% of the time, Pallas kernels for 24%

profile of v13, /device:TPU:0, one launch (start us, length us, event | category | flops | bytes accessed | tf_op | source)
XLA Modules:
  0.0 45.3 jit_solution(14055450436878373261)
XLA Ops:
  0.0 1.0 %dynamic-slice_bitcast_fusion = bf16[2,64,1440]{2,1,0:T(8,128)(2,1)S(1)} fusion(bf16[4,1440,64]{1,2,0:T(8,128)(2,1)} %param.11, s32[]{:T(128)S(6)} %select_n.3), kind=kLoop, calls=%fused_computation | loop fusion | bytes 737284 | tf_op jit(solution)/shard_map/dynamic_slice | solution.py:361
  1.0 3.0 %collective-permute-start = (bf16[2,64,1440]{2,1,0:T(8,128)(2,1)S(1)}, bf16[2,64,1440]{2,1,0:T(8,128)(2,1)S(1)}, u32[]{:S(2)}, u32[]{:S(2)}) collective-permute-start(bf16[2,64,1440]{2,1,0:T(8,128)(2,1)S(1)} %dynamic-slice_bitcast_fusion), channel_id=1, source_target_pairs={{0,16},{16,0},{1,17},{17,1},{2,18},{18,2},{3,19},{19,3},{4,20},{20... | collective-permute-start | bytes 1105928 | tf_op jit(solution)/shard_map/ppermute | solution.py:362
  4.1 3.6 %conv_rows.7 = (bf16[128,384]{1,0:T(8,128)(2,1)}, bf16[128,384]{1,0:T(8,128)(2,1)}, bf16[128,384]{1,0:T(8,128)(2,1)}) custom-call(s32[1]{0:T(128)} %bitcast.7.pair_ref, s32[1]{0:T(128)} %bitcast.3.place_ref, s32[4,9]{1,0:T(4,128)} %lat_ref.7, s32[4,9]{1,0:T(4,128)} %lon_ref.7, s32[4,9]{1,0:T(4,128)} %basis_ref.7, f32[4,9]{1,0:T(4,128)} %value_ref.7, ...), custom_call_target="tpu_custom_call" | custom-call | flops 1000000000 | tf_op jit(solution)/shard_map/conv_rows/pallas_call | solution.py:144
  7.7 0.0 copy-start.4
  7.7 0.0 copy-start.5
  7.7 0.0 copy-start.6
  7.7 2.7 %collective-permute-start.4 = (bf16[128,384]{1,0:T(8,128)(2,1)}, bf16[128,384]{1,0:T(8,128)(2,1)S(1)}, u32[]{:S(2)}, u32[]{:S(2)}) collective-permute-start(bf16[128,384]{1,0:T(8,128)(2,1)} %get-tuple-element.22), channel_id=1, source_target_pairs={{0,8},{4,12},{8,0},{12,4},{1,9},{5,13},{9,1},{13,5},{2,10},{6,14},... | collective-permute-start | bytes 294920 | tf_op jit(solution)/shard_map/ppermute | solution.py:328
  10.4 1.3 %collective-permute-start.5 = (bf16[128,384]{1,0:T(8,128)(2,1)}, bf16[128,384]{1,0:T(8,128)(2,1)S(1)}, u32[]{:S(2)}, u32[]{:S(2)}) collective-permute-start(bf16[128,384]{1,0:T(8,128)(2,1)} %get-tuple-element.23), channel_id=1, source_target_pairs={{0,12},{4,8},{8,4},{12,0},{1,13},{5,9},{9,5},{13,1},{2,14},{6,10},... | collective-permute-start | bytes 294920 | tf_op jit(solution)/shard_map/ppermute | solution.py:328
  11.7 0.2 collective-permute-start.6
  11.9 0.1 copy.12
  12.1 0.1 copy.13
  12.3 0.8 %expand.1.rest_8_.left_ref = bf16[3,2,384,256]{3,2,1,0:T(8,128)(2,1)S(1)} custom-call(s32[1]{0:T(128)} %bitcast.1.start_ref, bf16[3,8,384]{2,1,0:T(8,128)(2,1)S(1)} %bitcast.19, bf16[8,256]{1,0:T(8,128)(2,1)S(1)} %copy-done.7), custom_call_target="tpu_custom_call" | custom-call | flops 200000000 | tf_op jit(solution)/shard_map/expand/pallas_call | solution.py:257
  13.1 0.1 collective-permute-done.rest_0_
  13.2 2.4 %conv_rows.4 = (bf16[128,384]{1,0:T(8,128)(2,1)S(1)}, bf16[128,384]{1,0:T(8,128)(2,1)S(1)}, bf16[128,384]{1,0:T(8,128)(2,1)S(1)}) custom-call(s32[1]{0:T(128)} %bitcast.4.pair_ref, s32[1]{0:T(128)} %bitcast.3.place_ref, s32[4,9]{1,0:T(4,128)S(1)} %copy-done.3, s32[4,9]{1,0:T(4,128)S(1)} %copy-done.4, s32[4,9]{1,0:T(4,128)S(1)} %copy-done.5, ...), custom_call_target="tpu_custom_call" | custom-call | flops 1000000000 | tf_op jit(solution)/shard_map/conv_rows/pallas_call | solution.py:144
  15.7 2.9 %collective-permute-start.1 = (bf16[128,384]{1,0:T(8,128)(2,1)S(1)}, bf16[128,384]{1,0:T(8,128)(2,1)S(1)}, u32[]{:S(2)}, u32[]{:S(2)}) collective-permute-start(bf16[128,384]{1,0:T(8,128)(2,1)S(1)} %get-tuple-element.20), channel_id=1, source_target_pairs={{0,8},{4,12},{8,0},{12,4},{1,9},{5,13},{9,1},{13,5},{2,10},{6,14},... | collective-permute-start | bytes 294920 | tf_op jit(solution)/shard_map/ppermute | solution.py:328
  18.5 1.3 %collective-permute-start.2 = (bf16[128,384]{1,0:T(8,128)(2,1)S(1)}, bf16[128,384]{1,0:T(8,128)(2,1)S(1)}, u32[]{:S(2)}, u32[]{:S(2)}) collective-permute-start(bf16[128,384]{1,0:T(8,128)(2,1)S(1)} %get-tuple-element.19.rest_1_), channel_id=1, source_target_pairs={{0,12},{4,8},{8,4},{12,0},{1,13},{5,9},{9,5},{13,1},{2,14},{6,10},... | collective-permute-start | bytes 294920 | tf_op jit(solution)/shard_map/ppermute | solution.py:328
  19.9 1.5 %conv_rows.5.rest_2_.rest_0_ = bf16[128,384]{1,0:T(8,128)(2,1)S(1)} custom-call(s32[1]{0:T(128)} %bitcast.7.pair_ref, s32[1]{0:T(128)} %bitcast.3.place_ref, s32[4,9]{1,0:T(4,128)S(1)} %copy-done.3, s32[4,9]{1,0:T(4,128)S(1)} %copy-done.4, s32[4,9]{1,0:T(4,128)S(1)} %copy-done.5, f32[4,9]{1,0:T(4,128)S(1)} %copy-done.6, bf16[4,64,1440]{2,1,0:T(8,128)(2,1)S(1)} %bitcast.13, ...), custom_call_target="tpu_custom_call" | custom-call | flops 200000000 | tf_op jit(solution)/shard_map/conv_rows/pallas_call | solution.py:144
  21.4 0.3 collective-permute-start.3
  21.7 1.5 %conv_rows.6.rest_7_.rest_0_ = bf16[128,384]{1,0:T(8,128)(2,1)S(1)} custom-call(s32[1]{0:T(128)} %bitcast.4.pair_ref, s32[1]{0:T(128)} %bitcast.3.place_ref, s32[4,9]{1,0:T(4,128)S(1)} %copy-done.3, s32[4,9]{1,0:T(4,128)S(1)} %copy-done.4, s32[4,9]{1,0:T(4,128)S(1)} %copy-done.5, f32[4,9]{1,0:T(4,128)S(1)} %copy-done.6, bf16[4,64,1440]{2,1,0:T(8,128)(2,1)S(1)} %bitcast.14, ...), custom_call_target="tpu_custom_call" | custom-call | flops 200000000 | tf_op jit(solution)/shard_map/conv_rows/pallas_call | solution.py:144
  23.3 1.2 %mlp_rows.2.rest_7_ = bf16[8,16,256]{2,1,0:T(8,128)(2,1)S(1)} custom-call(s32[1]{0:T(128)} %bitcast.3.place_ref, s32[1]{0:T(128)} %bitcast.me_ref, bf16[128,384]{1,0:T(8,128)(2,1)S(1)} %conv_rows.5.rest_2_.rest_0_, bf16[128,384]{1,0:T(8,128)(2,1)S(1)} %collective-permute-done.4.rest_1_, bf16[128,384]{1,0:T(8,128)(2,1)S(1)} %collective-permute-done.5.rest_2_, ...), custom_call_target="tpu_custom_call" | custom-call | flops 1000000000 | tf_op jit(solution)/shard_map/mlp_rows/pallas_call | solution.py:222
  24.4 2.1 %collective-permute-done.1.rest_1_ = bf16[128,384]{1,0:T(8,128)(2,1)S(1)} collective-permute-done((bf16[128,384]{1,0:T(8,128)(2,1)S(1)}, bf16[128,384]{1,0:T(8,128)(2,1)S(1)}, u32[]{:S(2)}, u32[]{:S(2)}) %collective-permute-start.1) | collective-permute-done | bytes 98336 | tf_op jit(solution)/shard_map/ppermute | solution.py:328
  26.5 0.9 %collective-permute-done.3.rest_3_ = bf16[128,384]{1,0:T(8,128)(2,1)S(1)} collective-permute-done((bf16[128,384]{1,0:T(8,128)(2,1)S(1)}, bf16[128,384]{1,0:T(8,128)(2,1)S(1)}, u32[]{:S(2)}, u32[]{:S(2)}) %collective-permute-start.3) | collective-permute-done | bytes 98336 | tf_op jit(solution)/shard_map/ppermute | solution.py:328
  27.4 1.2 %mlp_rows.3 = (bf16[32,256]{1,0:T(8,128)(2,1)S(1)}, bf16[32,256]{1,0:T(8,128)(2,1)S(1)}, bf16[32,256]{1,0:T(8,128)(2,1)S(1)}, bf16[32,256]{1,0:T(8,128)(2,1)S(1)...) custom-call(s32[1]{0:T(128)} %bitcast.3.place_ref, ...), custom_call_target="tpu_custom_call" | custom-call | flops 1000000000 | tf_op jit(solution)/shard_map/mlp_rows/pallas_call | solution.py:222
  28.6 3.1 %collective-permute-start.7 = (bf16[32,256]{1,0:T(8,128)(2,1)S(1)}, bf16[32,256]{1,0:T(8,128)(2,1)S(1)}, u32[]{:S(2)}, u32[]{:S(2)}) collective-permute-start(bf16[32,256]{1,0:T(8,128)(2,1)S(1)} %get-tuple-element.26), channel_id=1, source_target_pairs={{0,8},{4,12},{8,0},{12,4},{16,24},{20,28},{24,16},{28,20},{1,9},{5... | collective-permute-start | bytes 49160 | tf_op jit(solution)/shard_map/ppermute | solution.py:328
  31.7 0.4 collective-permute-start.8
  32.2 0.8 %collective-permute-start.9 = (bf16[32,256]{1,0:T(8,128)(2,1)S(1)}, bf16[32,256]{1,0:T(8,128)(2,1)S(1)}, u32[]{:S(2)}, u32[]{:S(2)}) collective-permute-start(bf16[32,256]{1,0:T(8,128)(2,1)S(1)} %get-tuple-element.28), channel_id=1, source_target_pairs={{0,16},{4,20},{8,24},{12,28},{16,0},{20,4},{24,8},{28,12},{1,17},{... | collective-permute-start | bytes 49160 | tf_op jit(solution)/shard_map/ppermute | solution.py:328
  33.0 0.9 %collective-permute-start.10 = (bf16[32,256]{1,0:T(8,128)(2,1)S(1)}, bf16[32,256]{1,0:T(8,128)(2,1)S(1)}, u32[]{:S(2)}, u32[]{:S(2)}) collective-permute-start(bf16[32,256]{1,0:T(8,128)(2,1)S(1)} %get-tuple-element.29), channel_id=1, source_target_pairs={{0,20},{4,16},{8,28},{12,24},{16,4},{20,0},{24,12},{28,8},{1,21},{... | collective-permute-start | bytes 49160 | tf_op jit(solution)/shard_map/ppermute | solution.py:328
  33.9 3.7 %collective-permute-start.11 = (bf16[32,256]{1,0:T(8,128)(2,1)S(1)}, bf16[32,256]{1,0:T(8,128)(2,1)S(1)}, u32[]{:S(2)}, u32[]{:S(2)}) collective-permute-start(bf16[32,256]{1,0:T(8,128)(2,1)S(1)} %get-tuple-element.30), channel_id=1, source_target_pairs={{0,24},{4,28},{8,16},{12,20},{16,8},{20,12},{24,0},{28,4},{1,25},{... | collective-permute-start | bytes 49160 | tf_op jit(solution)/shard_map/ppermute | solution.py:328
  37.6 1.4 %collective-permute-start.12 = (bf16[32,256]{1,0:T(8,128)(2,1)S(1)}, bf16[32,256]{1,0:T(8,128)(2,1)S(1)}, u32[]{:S(2)}, u32[]{:S(2)}) collective-permute-start(bf16[32,256]{1,0:T(8,128)(2,1)S(1)} %get-tuple-element.31), channel_id=1, source_target_pairs={{0,28},{4,24},{8,20},{12,16},{16,12},{20,8},{24,4},{28,0},{1,29},{... | collective-permute-start | bytes 49160 | tf_op jit(solution)/shard_map/ppermute | solution.py:328
  39.0 0.4 collective-permute-done.11.rest_5_
  39.4 4.6 %collective-permute-done.12.rest_6_ = bf16[32,256]{1,0:T(8,128)(2,1)S(1)} collective-permute-done((bf16[32,256]{1,0:T(8,128)(2,1)S(1)}, bf16[32,256]{1,0:T(8,128)(2,1)S(1)}, u32[]{:S(2)}, u32[]{:S(2)}) %collective-permute-start.12) | collective-permute-done | bytes 16416 | tf_op jit(solution)/shard_map/ppermute | solution.py:328
  44.0 1.3 %final_sum.1 = bf16[3,384,512]{2,1,0:T(8,128)(2,1)} custom-call(s32[1]{0:T(128)} %bitcast.me_ref, bf16[3,2,384,256]{3,2,1,0:T(8,128)(2,1)S(1)} %expand.1.rest_8_.left_ref, bf16[32,256]{1,0:T(8,128)(2,1)S(1)} %get-tuple-element.25.rest_0_, bf16[32,256]{1,0:T(8,128)(2,1)S(1)} %collective-permute-done.7.rest_1_, ...), custom_call_target="tpu_custom_call" | custom-call | flops 1000000000 | tf_op jit(solution)/shard_map/final_sum/pallas_call | solution.py:299
  (29 shorter events, 0.1 us)
Async XLA Ops:
  1.0 12.1 %collective-permute-start = (bf16[2,64,1440]{2,1,0:T(8,128)(2,1)S(1)}, bf16[2,64,1440]{2,1,0:T(8,128)(2,1)S(1)}, u32[]{:S(2)}, u32[]{:S(2)}) collective-permute-start(bf16[2,64,1440]{2,1,0:T(8,128)(2,1)S(1)} %dynamic-slice_bitcast_fusion), channel_id=1, source_target_pairs={{0,16},{16,0},{1,17},{17,1},{2,18},{18,2},{3,19},{19,3},{4,20},{20... | collective-permute-start | bytes 1105928 | tf_op jit(solution)/shard_map/ppermute | solution.py:362
  4.1 7.9 %copy-start.9 = (bf16[256,512]{1,0:T(8,128)(2,1)S(1)}, bf16[256,512]{1,0:T(8,128)(2,1)}, u32[]{:S(2)}) copy-start(bf16[256,512]{1,0:T(8,128)(2,1)} %param.17) | copy-start | bytes 786436
  4.1 8.0 %copy-start.10 = (bf16[512,256]{1,0:T(8,128)(2,1)S(1)}, bf16[512,256]{1,0:T(8,128)(2,1)}, u32[]{:S(2)}) copy-start(bf16[512,256]{1,0:T(8,128)(2,1)} %param.18) | copy-start | bytes 786436
  4.1 8.2 %copy-start.2 = (bf16[3,384,8]{1,2,0:T(8,128)(2,1)S(1)}, bf16[3,384,8]{1,2,0:T(8,128)(2,1)}, u32[]{:S(2)}) copy-start(bf16[3,384,8]{1,2,0:T(8,128)(2,1)} %param.19) | copy-start | bytes 55300
  4.1 8.2 %copy-start.7 = (bf16[8,256]{1,0:T(8,128)(2,1)S(1)}, bf16[8,256]{1,0:T(8,128)(2,1)}, u32[]{:S(2)}) copy-start(bf16[8,256]{1,0:T(8,128)(2,1)} %constant.26.clone.spread_ref) | copy-start | bytes 12292
  7.7 5.5 %copy-start = (bf16[4,1440,64]{1,2,0:T(8,128)(2,1)S(1)}, bf16[4,1440,64]{1,2,0:T(8,128)(2,1)}, u32[]{:S(2)}) copy-start(bf16[4,1440,64]{1,2,0:T(8,128)(2,1)} %param.11) | copy-start | bytes 2211844
  7.7 5.5 %copy-start.1 = (bf16[6,64,64]{2,1,0:T(8,128)(2,1)S(1)}, bf16[6,64,64]{2,1,0:T(8,128)(2,1)}, u32[]{:S(2)}) copy-start(bf16[6,64,64]{2,1,0:T(8,128)(2,1)} %rest_0_.3) | copy-start | bytes 147460
  7.7 5.5 %copy-start.3 = (s32[4,9]{1,0:T(4,128)S(1)}, s32[4,9]{1,0:T(4,128)}, u32[]{:S(2)}) copy-start(s32[4,9]{1,0:T(4,128)} %lat_ref.7) | copy-start | bytes 436
  7.7 5.5 %copy-start.4 = (s32[4,9]{1,0:T(4,128)S(1)}, s32[4,9]{1,0:T(4,128)}, u32[]{:S(2)}) copy-start(s32[4,9]{1,0:T(4,128)} %lon_ref.7) | copy-start | bytes 436
  7.7 5.5 %copy-start.5 = (s32[4,9]{1,0:T(4,128)S(1)}, s32[4,9]{1,0:T(4,128)}, u32[]{:S(2)}) copy-start(s32[4,9]{1,0:T(4,128)} %basis_ref.7) | copy-start | bytes 436
  7.7 5.5 %copy-start.6 = (f32[4,9]{1,0:T(4,128)S(1)}, f32[4,9]{1,0:T(4,128)}, u32[]{:S(2)}) copy-start(f32[4,9]{1,0:T(4,128)} %value_ref.7) | copy-start | bytes 436
  7.7 13.7 %collective-permute-start.4 = (bf16[128,384]{1,0:T(8,128)(2,1)}, bf16[128,384]{1,0:T(8,128)(2,1)S(1)}, u32[]{:S(2)}, u32[]{:S(2)}) collective-permute-start(bf16[128,384]{1,0:T(8,128)(2,1)} %get-tuple-element.22), channel_id=1, source_target_pairs={{0,8},{4,12},{8,0},{12,4},{1,9},{5,13},{9,1},{13,5},{2,10},{6,14},... | collective-permute-start | bytes 294920 | tf_op jit(solution)/shard_map/ppermute | solution.py:328
  10.4 12.9 %collective-permute-start.5 = (bf16[128,384]{1,0:T(8,128)(2,1)}, bf16[128,384]{1,0:T(8,128)(2,1)S(1)}, u32[]{:S(2)}, u32[]{:S(2)}) collective-permute-start(bf16[128,384]{1,0:T(8,128)(2,1)} %get-tuple-element.23), channel_id=1, source_target_pairs={{0,12},{4,8},{8,4},{12,0},{1,13},{5,9},{9,5},{13,1},{2,14},{6,10},... | collective-permute-start | bytes 294920 | tf_op jit(solution)/shard_map/ppermute | solution.py:328
  11.7 11.5 %collective-permute-start.6 = (bf16[128,384]{1,0:T(8,128)(2,1)}, bf16[128,384]{1,0:T(8,128)(2,1)S(1)}, u32[]{:S(2)}, u32[]{:S(2)}) collective-permute-start(bf16[128,384]{1,0:T(8,128)(2,1)} %get-tuple-element.24), channel_id=1, source_target_pairs={{0,4},{4,0},{8,12},{12,8},{1,5},{5,1},{9,13},{13,9},{2,6},{6,2},{1... | collective-permute-start | bytes 294920 | tf_op jit(solution)/shard_map/ppermute | solution.py:328
  15.7 10.9 %collective-permute-start.1 = (bf16[128,384]{1,0:T(8,128)(2,1)S(1)}, bf16[128,384]{1,0:T(8,128)(2,1)S(1)}, u32[]{:S(2)}, u32[]{:S(2)}) collective-permute-start(bf16[128,384]{1,0:T(8,128)(2,1)S(1)} %get-tuple-element.20), channel_id=1, source_target_pairs={{0,8},{4,12},{8,0},{12,4},{1,9},{5,13},{9,1},{13,5},{2,10},{6,14},... | collective-permute-start | bytes 294920 | tf_op jit(solution)/shard_map/ppermute | solution.py:328
  18.5 4.7 %copy-start.8 = (bf16[4,64,384]{2,1,0:T(8,128)(2,1)S(1)}, bf16[4,64,384]{2,1,0:T(8,128)(2,1)}, u32[]{:S(2)}) copy-start(bf16[4,64,384]{2,1,0:T(8,128)(2,1)} %constant.25.clone.rest_6_) | copy-start | bytes 589828
  18.5 8.9 %collective-permute-start.2 = (bf16[128,384]{1,0:T(8,128)(2,1)S(1)}, bf16[128,384]{1,0:T(8,128)(2,1)S(1)}, u32[]{:S(2)}, u32[]{:S(2)}) collective-permute-start(bf16[128,384]{1,0:T(8,128)(2,1)S(1)} %get-tuple-element.19.rest_1_), channel_id=1, source_target_pairs={{0,12},{4,8},{8,4},{12,0},{1,13},{5,9},{9,5},{13,1},{2,14},{6,10},... | collective-permute-start | bytes 294920 | tf_op jit(solution)/shard_map/ppermute | solution.py:328
  21.4 6.0 %collective-permute-start.3 = (bf16[128,384]{1,0:T(8,128)(2,1)S(1)}, bf16[128,384]{1,0:T(8,128)(2,1)S(1)}, u32[]{:S(2)}, u32[]{:S(2)}) collective-permute-start(bf16[128,384]{1,0:T(8,128)(2,1)S(1)} %get-tuple-element.21), channel_id=1, source_target_pairs={{0,4},{4,0},{8,12},{12,8},{1,5},{5,1},{9,13},{13,9},{2,6},{6,2},{1... | collective-permute-start | bytes 294920 | tf_op jit(solution)/shard_map/ppermute | solution.py:328
  28.6 9.0 %collective-permute-start.7 = (bf16[32,256]{1,0:T(8,128)(2,1)S(1)}, bf16[32,256]{1,0:T(8,128)(2,1)S(1)}, u32[]{:S(2)}, u32[]{:S(2)}) collective-permute-start(bf16[32,256]{1,0:T(8,128)(2,1)S(1)} %get-tuple-element.26), channel_id=1, source_target_pairs={{0,8},{4,12},{8,0},{12,4},{16,24},{20,28},{24,16},{28,20},{1,9},{5... | collective-permute-start | bytes 49160 | tf_op jit(solution)/shard_map/ppermute | solution.py:328
  31.7 7.2 %collective-permute-start.8 = (bf16[32,256]{1,0:T(8,128)(2,1)S(1)}, bf16[32,256]{1,0:T(8,128)(2,1)S(1)}, u32[]{:S(2)}, u32[]{:S(2)}) collective-permute-start(bf16[32,256]{1,0:T(8,128)(2,1)S(1)} %get-tuple-element.27), channel_id=1, source_target_pairs={{0,12},{4,8},{8,4},{12,0},{16,28},{20,24},{24,20},{28,16},{1,13},{... | collective-permute-start | bytes 49160 | tf_op jit(solution)/shard_map/ppermute | solution.py:328
  32.2 6.8 %collective-permute-start.9 = (bf16[32,256]{1,0:T(8,128)(2,1)S(1)}, bf16[32,256]{1,0:T(8,128)(2,1)S(1)}, u32[]{:S(2)}, u32[]{:S(2)}) collective-permute-start(bf16[32,256]{1,0:T(8,128)(2,1)S(1)} %get-tuple-element.28), channel_id=1, source_target_pairs={{0,16},{4,20},{8,24},{12,28},{16,0},{20,4},{24,8},{28,12},{1,17},{... | collective-permute-start | bytes 49160 | tf_op jit(solution)/shard_map/ppermute | solution.py:328
  33.0 6.0 %collective-permute-start.10 = (bf16[32,256]{1,0:T(8,128)(2,1)S(1)}, bf16[32,256]{1,0:T(8,128)(2,1)S(1)}, u32[]{:S(2)}, u32[]{:S(2)}) collective-permute-start(bf16[32,256]{1,0:T(8,128)(2,1)S(1)} %get-tuple-element.29), channel_id=1, source_target_pairs={{0,20},{4,16},{8,28},{12,24},{16,4},{20,0},{24,12},{28,8},{1,21},{... | collective-permute-start | bytes 49160 | tf_op jit(solution)/shard_map/ppermute | solution.py:328
  33.9 5.5 %collective-permute-start.11 = (bf16[32,256]{1,0:T(8,128)(2,1)S(1)}, bf16[32,256]{1,0:T(8,128)(2,1)S(1)}, u32[]{:S(2)}, u32[]{:S(2)}) collective-permute-start(bf16[32,256]{1,0:T(8,128)(2,1)S(1)} %get-tuple-element.30), channel_id=1, source_target_pairs={{0,24},{4,28},{8,16},{12,20},{16,8},{20,12},{24,0},{28,4},{1,25},{... | collective-permute-start | bytes 49160 | tf_op jit(solution)/shard_map/ppermute | solution.py:328
  37.6 6.4 %collective-permute-start.12 = (bf16[32,256]{1,0:T(8,128)(2,1)S(1)}, bf16[32,256]{1,0:T(8,128)(2,1)S(1)}, u32[]{:S(2)}, u32[]{:S(2)}) collective-permute-start(bf16[32,256]{1,0:T(8,128)(2,1)S(1)} %get-tuple-element.31), channel_id=1, source_target_pairs={{0,28},{4,24},{8,20},{12,16},{16,12},{20,8},{24,4},{28,0},{1,29},{... | collective-permute-start | bytes 49160 | tf_op jit(solution)/shard_map/ppermute | solution.py:328
  38.9 5.1 %collective-permute-start.13 = (bf16[32,256]{1,0:T(8,128)(2,1)S(1)}, bf16[32,256]{1,0:T(8,128)(2,1)S(1)}, u32[]{:S(2)}, u32[]{:S(2)}) collective-permute-start(bf16[32,256]{1,0:T(8,128)(2,1)S(1)} %get-tuple-element.32), channel_id=1, source_target_pairs={{0,4},{4,0},{8,12},{12,8},{16,20},{20,16},{24,28},{28,24},{1,5},{5... | collective-permute-start | bytes 49160 | tf_op jit(solution)/shard_map/ppermute | solution.py:328

commit v14 on v11

--- a/solution.py
+++ b/solution.py
@@ -56,7 +56,7 @@
 
 
 def conv_kernel(
-    chunks, picks, has_edge, after, pair_ref, place_ref, lat_ref, lon_ref, basis_ref, value_ref, fields_ref, *rest
+    chunks, picks, has_edge, after, flip, lat_ref, lon_ref, basis_ref, value_ref, fields_ref, *rest
 ):
     if has_edge:
         edge_ref, weight_ref, *rest = rest
@@ -67,7 +67,7 @@
     chunk = lon // chunks
     width = out_refs[0].shape[1]
     total = rows_ref.shape[2]
-    pair = pair_ref[0]
+    pair = flip if isinstance(flip, int) else flip()
     own_at = HALO * (1 - pair)
     edge_at = own * pair
 
@@ -89,7 +89,7 @@
             rows_ref[edge_at + row] = jnp.zeros(rows_ref.shape[1:], rows_ref.dtype)
 
     lane = lax.broadcasted_iota(jnp.int32, (G, LANES), 1)
-    begins = [LANES + chunk * target(place_ref[0], k, chunks) for k in picks]
+    begins = [LANES + chunk * target(lax.axis_index("chan"), k, chunks) for k in picks]
 
     def fill(slot, tap, source, offset):
         for k, origin in enumerate(begins):
@@ -135,16 +135,16 @@
             out_refs[k][i * G : (i + 1) * G, :] = mixed[:, k * width : (k + 1) * width]
 
 
-def conv_rows(pair, place, supports, fields, edge, weight, chunks, picks, after, roomy):
+def conv_rows(pair, supports, fields, edge, weight, chunks, picks, after, roomy):
     own, chans, lon = fields.shape
     width = ceil_to(lon // chunks, LANES)
     highest = (LANES + lon - lon // chunks + DLON) // LANES
     total = (highest + 1) * LANES + width
     arrays = [fields] + ([] if edge is None else [edge]) + [weight]
     return pl.pallas_call(
-        functools.partial(conv_kernel, chunks, picks, edge is not None, len(after)),
+        functools.partial(conv_kernel, chunks, picks, edge is not None, len(after), pair),
         out_shape=[jax.ShapeDtypeStruct((2 * chans, width), jnp.bfloat16)] * len(picks),
-        in_specs=[SMEM] * 6 + [VMEM] * len(arrays) + [ANY] * len(after),
+        in_specs=[SMEM] * 4 + [VMEM] * len(arrays) + [ANY] * len(after),
         out_specs=[VMEM] * len(picks),
         scratch_shapes=[
             pltpu.VMEM((own + HALO, chans, total), jnp.bfloat16),
@@ -154,10 +154,10 @@
         compiler_params=params(56 if roomy else 20),
         cost_estimate=takes(1 if len(picks) > 1 else 0.2),
         name="conv_rows",
-    )(pair, place, *supports, *arrays, *after)
-
-
-def mlp_kernel(parts, last, after, place_ref, *rest):
+    )(*supports, *arrays, *after)
+
+
+def mlp_kernel(parts, last, after, *rest):
     blocks, rest = rest[:parts], rest[parts:]
     up_ref, down_ref, table_ref, *rest = rest
     rest = rest[after:]
@@ -166,7 +166,7 @@
     else:
         out_ref, cells_ref = rest
     width = blocks[0].shape[1]
-    place = place_ref[0]
+    place = lax.axis_index("chan")
     for block, k in zip(blocks, [0, *issue_order(parts)]):
         origin = pl.multiple_of(source(place, k, parts) * G, G)
         for i in range(2):
@@ -201,7 +201,7 @@
         out_ref[...] = block
 
 
-def mlp_rows(place, blocks, up, down, tables, earlier, dests, after):
+def mlp_rows(blocks, up, down, tables, earlier, dests, after):
     pair_chans, width = blocks[0].shape
     chan = len(blocks) * pair_chans // 2
     last = earlier is not None
@@ -210,8 +210,7 @@
     return pl.pallas_call(
         functools.partial(mlp_kernel, len(blocks), last, len(after)),
         out_shape=jax.ShapeDtypeStruct((dests, rows, chan), jnp.bfloat16),
-        in_specs=[SMEM]
-        + [VMEM] * (len(blocks) + 3)
+        in_specs=[VMEM] * (len(blocks) + 3)
         + [ANY] * len(after)
         + [VMEM] * last,
         out_specs=VMEM,
@@ -219,14 +218,15 @@
         compiler_params=params(20 if dests <= FEW else 40),
         cost_estimate=takes(1),
         name="mlp_rows",
-    )(place, *arrays)
-
-
-def expand_kernel(start_ref, legendre_ref, spread_ref, out_ref):
+    )(*arrays)
+
+
+def expand_kernel(legendre_ref, spread_ref, out_ref):
     _, lats, degrees = legendre_ref.shape
     m = pl.program_id(0)
+    first = lax.axis_index(("lat", "chan")) * pl.num_programs(0)
     degree = lax.broadcasted_iota(jnp.int32, (lats, degrees), 1)
-    kept = jnp.where(degree >= start_ref[0] + m, legendre_ref[0].astype(jnp.float32), 0.0)
+    kept = jnp.where(degree >= first + m, legendre_ref[0].astype(jnp.float32), 0.0)
     wide = lax.dot_general(
         kept.astype(jnp.bfloat16),
         spread_ref[...],
@@ -238,7 +238,7 @@
         out_ref[0, r] = jnp.where(slot == 2 * m + r, wide, 0.0).astype(jnp.bfloat16)
 
 
-def expand(start, legendre, spread):
+def expand(legendre, spread):
     modes, lats, degrees = legendre.shape
     depth = spread.shape[1]
     return pl.pallas_call(
@@ -246,7 +246,6 @@
         out_shape=jax.ShapeDtypeStruct((modes, 2, degrees, depth), jnp.bfloat16),
         grid=(modes,),
         in_specs=[
-            SMEM,
             pl.BlockSpec((1, lats, degrees), lambda m: (m, 0, 0)),
             pl.BlockSpec((lats, depth), lambda m: (0, 0)),
         ],
@@ -254,7 +253,7 @@
         compiler_params=params(10 if depth <= 512 else 48),
         cost_estimate=takes(0.2),
         name="expand",
-    )(start, legendre, spread)
+    )(legendre, spread)
 
 
 def final_kernel(left_ref, spectrum_ref, out_ref, result_ref, sems):
@@ -301,10 +300,6 @@
 
 def turn(block, axis, count, k):
     return lax.ppermute(block, axis, [(i, target(i, k, count)) for i in range(count)])
-
-
-def scalar(value):
-    return jnp.asarray(value, jnp.int32).reshape(1)
 
 
 def on_device(
@@ -325,8 +320,6 @@
     dests = num_lat * num_chan
     width = ceil_to(lon // num_chan, LANES)
     band = lax.axis_index("lat")
-    place = scalar(lax.axis_index("chan"))
-    index = lax.axis_index(("lat", "chan"))
     supports = (support_lat, support_lon, support_basis, support_value)
 
     two_bands = num_lat == 2
@@ -334,7 +327,7 @@
     if two_bands:
         edge_out = lax.dynamic_slice_in_dim(cells, HALO * (1 - band), HALO, axis=0)
         edges = [None, lax.ppermute(edge_out, "lat", [(0, 1), (1, 0)])]
-        pairs = [band, 1 - band]
+        pairs = [lambda: lax.axis_index("lat"), lambda: 1 - lax.axis_index("lat")]
     else:
         ends = num_lat - 1
         edges = [
@@ -354,11 +347,11 @@
     source_pair = (phase ^ source_band) if two_bands else phase
     lat_of = lat_dev * source_band + 2 * source_pair + (row // SLOT) % 2
     spread = (lat_of[None, :] == np.arange(lats)[:, None]).astype(jnp.bfloat16)
-    left = expand(scalar(index * mode_dev), jnp.swapaxes(legendre, 1, 2), jnp.asarray(spread))
+    left = expand(jnp.swapaxes(legendre, 1, 2), jnp.asarray(spread))
 
     order = issue_order(num_chan)
     halves = [
-        (scalar(pair), place, supports, cells, edge, disco_weight, num_chan)
+        (pair, supports, cells, edge, disco_weight, num_chan)
         for edge, pair in zip(edges, pairs)
     ]
     received = []
@@ -371,7 +364,7 @@
         blocks.insert(0, after[0])
     spectrum = None
     for blocks in received:
-        spectrum = mlp_rows(place, blocks, up, down, tables, spectrum, dests, list(after))
+        spectrum = mlp_rows(blocks, up, down, tables, spectrum, dests, list(after))
         after = []
 
     both = ("lat", "chan")

time: 43.3 us -> 43.3 us (level)
  no operation moved by 1% of the time
where the time goes in v14:
time: 43.3 us; the launch traced here: 43 us
  starting transfers between devices  16.6 us (38%)
  Pallas kernels  14.3 us (33%)
  waiting for transfers between devices  10.5 us (24%)
  local copies, waits for them, and re-layouts  1.35 us (3%)
    pallas_call x4, Pallas kernels, conv_rows(): pl.pallas_call(functools.partial(conv_kernel, chunks, picks, edge is not...  9.17 us
    ppermute x6, starting transfers between devices, turn(): lax.ppermute(block, axis, [(i, target(i, k, count)) for i in range(count)])  8.67 us
    all_to_all x1, waiting for transfers between devices, on_device(): lax.all_to_all(spectrum, both, split_axis=0, concat_axis=0, tiled=True)  6.66 us
    all_to_all x1, starting transfers between devices, on_device(): lax.all_to_all(spectrum, both, split_axis=0, concat_axis=0, tiled=True)  4.93 us
    ppermute x1, starting transfers between devices, on_device(): edges = [None, lax.ppermute(edge_out, 'lat', [(0, 1), (1, 0)])]  3.03 us
    pallas_call x2, Pallas kernels, mlp_rows(): pl.pallas_call(functools.partial(mlp_kernel, len(blocks), last, len(after...  3.01 us
    ppermute x6, waiting for transfers between devices, turn(): lax.ppermute(block, axis, [(i, target(i, k, count)) for i in range(count)])  2.97 us
    pallas_call x1, Pallas kernels, final_sum(): pl.pallas_call(final_kernel, out_shape=jax.ShapeDtypeStruct(shape, jnp.bf...  1.3 us
  transfers between devices with their start and end apart: 8, of which 4 were waited for; matrix products, arithmetic and copies ran while one was open for 1% of the time, Pallas kernels for 26%

profile of v14, /device:TPU:0, one launch (start us, length us, event | category | flops | bytes accessed | tf_op | source)
XLA Modules:
  0.0 43.0 jit_solution(2134914480208932554)
XLA Ops:
  0.0 1.0 %dynamic-slice_bitcast_fusion = bf16[2,64,1440]{2,1,0:T(8,128)(2,1)S(1)} fusion(bf16[4,1440,64]{1,2,0:T(8,128)(2,1)} %param.11, s32[]{:T(128)S(6)} %select_n.3), kind=kLoop, calls=%fused_computation | loop fusion | bytes 737284 | tf_op jit(solution)/shard_map/dynamic_slice | solution.py:328
  1.0 3.0 %collective-permute-start = (bf16[2,64,1440]{2,1,0:T(8,128)(2,1)S(1)}, bf16[2,64,1440]{2,1,0:T(8,128)(2,1)S(1)}, u32[]{:S(2)}, u32[]{:S(2)}) collective-permute-start(bf16[2,64,1440]{2,1,0:T(8,128)(2,1)S(1)} %dynamic-slice_bitcast_fusion), channel_id=1, source_target_pairs={{0,16},{16,0},{1,17},{17,1},{2,18},{18,2},{3,19},{19,3},{4,20},{20... | collective-permute-start | bytes 1105928 | tf_op jit(solution)/shard_map/ppermute | solution.py:329
  4.1 0.0 copy-start.3
  4.1 0.0 copy-start.4
  4.1 0.0 copy-start.5
  4.1 0.0 copy-start.6
  4.1 3.7 %conv_rows.7 = (bf16[128,384]{1,0:T(8,128)(2,1)}, bf16[128,384]{1,0:T(8,128)(2,1)}, bf16[128,384]{1,0:T(8,128)(2,1)}) custom-call(s32[4,9]{1,0:T(4,128)} %lat_ref.7, s32[4,9]{1,0:T(4,128)} %lon_ref.7, s32[4,9]{1,0:T(4,128)} %basis_ref.7, f32[4,9]{1,0:T(4,128)} %value_ref.7, bf16[4,64,1440]{2,1,0:T(8,128)(2,1)} %bitcast.7, bf16[6,64,64]{2,1,0:T(8,128)(2,1)} %rest_0_.3), custom_call_target="tpu_custom_call" | custom-call | flops 1000000000 | tf_op jit(solution)/shard_map/conv_rows/pallas_call | solution.py:144
  7.8 2.6 %collective-permute-start.4 = (bf16[128,384]{1,0:T(8,128)(2,1)}, bf16[128,384]{1,0:T(8,128)(2,1)S(1)}, u32[]{:S(2)}, u32[]{:S(2)}) collective-permute-start(bf16[128,384]{1,0:T(8,128)(2,1)} %get-tuple-element.14), channel_id=1, source_target_pairs={{0,8},{4,12},{8,0},{12,4},{1,9},{5,13},{9,1},{13,5},{2,10},{6,14},... | collective-permute-start | bytes 294920 | tf_op jit(solution)/shard_map/ppermute | solution.py:302
  10.4 1.3 %collective-permute-start.5 = (bf16[128,384]{1,0:T(8,128)(2,1)}, bf16[128,384]{1,0:T(8,128)(2,1)S(1)}, u32[]{:S(2)}, u32[]{:S(2)}) collective-permute-start(bf16[128,384]{1,0:T(8,128)(2,1)} %get-tuple-element.15), channel_id=1, source_target_pairs={{0,12},{4,8},{8,4},{12,0},{1,13},{5,9},{9,5},{13,1},{2,14},{6,10},... | collective-permute-start | bytes 294920 | tf_op jit(solution)/shard_map/ppermute | solution.py:302
  11.7 0.2 collective-permute-start.6
  12.0 0.1 copy.12
  12.1 0.1 copy.13
  12.3 0.9 %collective-permute-done.rest_0_ = bf16[2,64,1440]{2,1,0:T(8,128)(2,1)S(1)} collective-permute-done((bf16[2,64,1440]{2,1,0:T(8,128)(2,1)S(1)}, bf16[2,64,1440]{2,1,0:T(8,128)(2,1)S(1)}, u32[]{:S(2)}, u32[]{:S(2)}) %collective-permute-start) | collective-permute-done | bytes 368672 | tf_op jit(solution)/shard_map/ppermute | solution.py:329
  13.2 2.5 %conv_rows.4 = (bf16[128,384]{1,0:T(8,128)(2,1)S(1)}, bf16[128,384]{1,0:T(8,128)(2,1)S(1)}, bf16[128,384]{1,0:T(8,128)(2,1)S(1)}) custom-call(s32[4,9]{1,0:T(4,128)S(1)} %copy-done.3, s32[4,9]{1,0:T(4,128)S(1)} %copy-done.4, s32[4,9]{1,0:T(4,128)S(1)} %copy-done.5, f32[4,9]{1,0:T(4,128)S(1)} %copy-done.6, bf16[4,64,1440]{2,1,0:T(8,128)(2,1)S(1)} %bitcast.8, ...), custom_call_target="tpu_custom_call" | custom-call | flops 1000000000 | tf_op jit(solution)/shard_map/conv_rows/pallas_call | solution.py:144
  15.7 2.9 %collective-permute-start.1 = (bf16[128,384]{1,0:T(8,128)(2,1)S(1)}, bf16[128,384]{1,0:T(8,128)(2,1)S(1)}, u32[]{:S(2)}, u32[]{:S(2)}) collective-permute-start(bf16[128,384]{1,0:T(8,128)(2,1)S(1)} %get-tuple-element.12), channel_id=1, source_target_pairs={{0,8},{4,12},{8,0},{12,4},{1,9},{5,13},{9,1},{13,5},{2,10},{6,14},... | collective-permute-start | bytes 294920 | tf_op jit(solution)/shard_map/ppermute | solution.py:302
  18.5 1.4 %collective-permute-start.2 = (bf16[128,384]{1,0:T(8,128)(2,1)S(1)}, bf16[128,384]{1,0:T(8,128)(2,1)S(1)}, u32[]{:S(2)}, u32[]{:S(2)}) collective-permute-start(bf16[128,384]{1,0:T(8,128)(2,1)S(1)} %get-tuple-element.11.rest_1_), channel_id=1, source_target_pairs={{0,12},{4,8},{8,4},{12,0},{1,13},{5,9},{9,5},{13,1},{2,14},{6,10},... | collective-permute-start | bytes 294920 | tf_op jit(solution)/shard_map/ppermute | solution.py:302
  19.9 1.5 %conv_rows.5.rest_2_.rest_0_ = bf16[128,384]{1,0:T(8,128)(2,1)S(1)} custom-call(s32[4,9]{1,0:T(4,128)S(1)} %copy-done.3, s32[4,9]{1,0:T(4,128)S(1)} %copy-done.4, s32[4,9]{1,0:T(4,128)S(1)} %copy-done.5, f32[4,9]{1,0:T(4,128)S(1)} %copy-done.6, bf16[4,64,1440]{2,1,0:T(8,128)(2,1)S(1)} %bitcast.9, bf16[6,64,64]{2,1,0:T(8,128)(2,1)S(1)} %copy-done.1, ...), custom_call_target="tpu_custom_call" | custom-call | flops 200000000 | tf_op jit(solution)/shard_map/conv_rows/pallas_call | solution.py:144
  21.4 0.0 collective-permute-done.4.rest_1_
  21.4 0.3 collective-permute-start.3
  21.7 1.5 %conv_rows.6.rest_7_.rest_0_ = bf16[128,384]{1,0:T(8,128)(2,1)S(1)} custom-call(s32[4,9]{1,0:T(4,128)S(1)} %copy-done.3, s32[4,9]{1,0:T(4,128)S(1)} %copy-done.4, s32[4,9]{1,0:T(4,128)S(1)} %copy-done.5, f32[4,9]{1,0:T(4,128)S(1)} %copy-done.6, bf16[4,64,1440]{2,1,0:T(8,128)(2,1)S(1)} %bitcast.10, bf16[2,64,1440]{2,1,0:T(8,128)(2,1)S(1)} %collective-permute-done.rest_0_, ...), custom_call_target="tpu_custom_call" | custom-call | flops 200000000 | tf_op jit(solution)/shard_map/conv_rows/pallas_call | solution.py:144
  23.2 0.0 collective-permute-done.5.rest_2_
  23.3 1.2 %mlp_rows.2.rest_7_ = bf16[8,16,256]{2,1,0:T(8,128)(2,1)S(1)} custom-call(bf16[128,384]{1,0:T(8,128)(2,1)S(1)} %conv_rows.5.rest_2_.rest_0_, bf16[128,384]{1,0:T(8,128)(2,1)S(1)} %collective-permute-done.4.rest_1_, bf16[128,384]{1,0:T(8,128)(2,1)S(1)} %collective-permute-done.5.rest_2_, bf16[128,384]{1,0:T(8,128)(2,1)S(1)} %collective-permute-done.6.rest_3_, ...), custom_call_target="tpu_custom_call" | custom-call | flops 1000000000 | tf_op jit(solution)/shard_map/mlp_rows/pallas_call | solution.py:210
  24.5 0.0 copy-start.2
  24.5 0.0 copy-start.7
  24.5 2.1 %collective-permute-done.1.rest_1_ = bf16[128,384]{1,0:T(8,128)(2,1)S(1)} collective-permute-done((bf16[128,384]{1,0:T(8,128)(2,1)S(1)}, bf16[128,384]{1,0:T(8,128)(2,1)S(1)}, u32[]{:S(2)}, u32[]{:S(2)}) %collective-permute-start.1) | collective-permute-done | bytes 98336 | tf_op jit(solution)/shard_map/ppermute | solution.py:302
  26.5 0.9 %collective-permute-done.3.rest_3_ = bf16[128,384]{1,0:T(8,128)(2,1)S(1)} collective-permute-done((bf16[128,384]{1,0:T(8,128)(2,1)S(1)}, bf16[128,384]{1,0:T(8,128)(2,1)S(1)}, u32[]{:S(2)}, u32[]{:S(2)}) %collective-permute-start.3) | collective-permute-done | bytes 98336 | tf_op jit(solution)/shard_map/ppermute | solution.py:302
  27.4 0.0 collective-permute-done.2.rest_2_
  27.4 1.8 %mlp_rows.3 = bf16[8,32,256]{2,1,0:T(8,128)(2,1)} custom-call(bf16[128,384]{1,0:T(8,128)(2,1)S(1)} %conv_rows.6.rest_7_.rest_0_, bf16[128,384]{1,0:T(8,128)(2,1)S(1)} %collective-permute-done.1.rest_1_, bf16[128,384]{1,0:T(8,128)(2,1)S(1)} %collective-permute-done.2.rest_2_, bf16[128,384]{1,0:T(8,128)(2,1)S(1)} %collective-permute-done.3.rest_3_, ...), custom_call_target="tpu_custom_call" | custom-call | flops 1000000000 | tf_op jit(solution)/shard_map/mlp_rows/pallas_call | solution.py:210
  29.3 4.9 %all-to-all-start = ((bf16[8,32,256]{2,1,0:T(8,128)(2,1)}), bf16[8,32,256]{2,1,0:T(8,128)(2,1)S(1)}, u32[]{:S(2)}, u32[]{:S(2)}) async-start(bf16[8,32,256]{2,1,0:T(8,128)(2,1)} %mlp_rows.3), calls=%async_computation | async-start | bytes 262144 | tf_op jit(solution)/shard_map/all_to_all | solution.py:371
  34.2 0.8 %expand.1.left_ref = bf16[3,2,384,256]{3,2,1,0:T(8,128)(2,1)S(1)} custom-call(bf16[3,8,384]{2,1,0:T(8,128)(2,1)S(1)} %bitcast.16, bf16[8,256]{1,0:T(8,128)(2,1)S(1)} %copy-done.7), custom_call_target="tpu_custom_call" | custom-call | flops 200000000 | tf_op jit(solution)/shard_map/expand/pallas_call | solution.py:244
  35.1 6.7 %all-to-all-done = bf16[8,32,256]{2,1,0:T(8,128)(2,1)S(1)} async-done(((bf16[8,32,256]{2,1,0:T(8,128)(2,1)}), bf16[8,32,256]{2,1,0:T(8,128)(2,1)S(1)}, u32[]{:S(2)}, u32[]{:S(2)}) %all-to-all-start) | async-done | bytes 131104 | tf_op jit(solution)/shard_map/all_to_all | solution.py:371
  41.7 1.3 %final_sum.1 = bf16[3,384,512]{2,1,0:T(8,128)(2,1)} custom-call(bf16[3,2,384,256]{3,2,1,0:T(8,128)(2,1)S(1)} %expand.1.left_ref, bf16[256,256]{1,0:T(8,128)(2,1)S(1)} %bitcast.15), custom_call_target="tpu_custom_call" | custom-call | flops 1000000000 | tf_op jit(solution)/shard_map/final_sum/pallas_call | solution.py:277
  (17 shorter events, 0.0 us)
Async XLA Ops:
  1.0 12.1 %collective-permute-start = (bf16[2,64,1440]{2,1,0:T(8,128)(2,1)S(1)}, bf16[2,64,1440]{2,1,0:T(8,128)(2,1)S(1)}, u32[]{:S(2)}, u32[]{:S(2)}) collective-permute-start(bf16[2,64,1440]{2,1,0:T(8,128)(2,1)S(1)} %dynamic-slice_bitcast_fusion), channel_id=1, source_target_pairs={{0,16},{16,0},{1,17},{17,1},{2,18},{18,2},{3,19},{19,3},{4,20},{20... | collective-permute-start | bytes 1105928 | tf_op jit(solution)/shard_map/ppermute | solution.py:329
  4.1 7.9 %copy-start.9 = (bf16[256,512]{1,0:T(8,128)(2,1)S(1)}, bf16[256,512]{1,0:T(8,128)(2,1)}, u32[]{:S(2)}) copy-start(bf16[256,512]{1,0:T(8,128)(2,1)} %param.17) | copy-start | bytes 786436
  4.1 8.0 %copy-start.10 = (bf16[512,256]{1,0:T(8,128)(2,1)S(1)}, bf16[512,256]{1,0:T(8,128)(2,1)}, u32[]{:S(2)}) copy-start(bf16[512,256]{1,0:T(8,128)(2,1)} %param.18) | copy-start | bytes 786436
  4.1 9.1 %copy-start = (bf16[4,1440,64]{1,2,0:T(8,128)(2,1)S(1)}, bf16[4,1440,64]{1,2,0:T(8,128)(2,1)}, u32[]{:S(2)}) copy-start(bf16[4,1440,64]{1,2,0:T(8,128)(2,1)} %param.11) | copy-start | bytes 2211844
  4.1 9.1 %copy-start.1 = (bf16[6,64,64]{2,1,0:T(8,128)(2,1)S(1)}, bf16[6,64,64]{2,1,0:T(8,128)(2,1)}, u32[]{:S(2)}) copy-start(bf16[6,64,64]{2,1,0:T(8,128)(2,1)} %rest_0_.3) | copy-start | bytes 147460
  4.1 9.1 %copy-start.3 = (s32[4,9]{1,0:T(4,128)S(1)}, s32[4,9]{1,0:T(4,128)}, u32[]{:S(2)}) copy-start(s32[4,9]{1,0:T(4,128)} %lat_ref.7) | copy-start | bytes 436
  4.1 9.1 %copy-start.4 = (s32[4,9]{1,0:T(4,128)S(1)}, s32[4,9]{1,0:T(4,128)}, u32[]{:S(2)}) copy-start(s32[4,9]{1,0:T(4,128)} %lon_ref.7) | copy-start | bytes 436
  4.1 9.1 %copy-start.5 = (s32[4,9]{1,0:T(4,128)S(1)}, s32[4,9]{1,0:T(4,128)}, u32[]{:S(2)}) copy-start(s32[4,9]{1,0:T(4,128)} %basis_ref.7) | copy-start | bytes 436
  4.1 9.1 %copy-start.6 = (f32[4,9]{1,0:T(4,128)S(1)}, f32[4,9]{1,0:T(4,128)}, u32[]{:S(2)}) copy-start(f32[4,9]{1,0:T(4,128)} %value_ref.7) | copy-start | bytes 436
  7.8 13.6 %collective-permute-start.4 = (bf16[128,384]{1,0:T(8,128)(2,1)}, bf16[128,384]{1,0:T(8,128)(2,1)S(1)}, u32[]{:S(2)}, u32[]{:S(2)}) collective-permute-start(bf16[128,384]{1,0:T(8,128)(2,1)} %get-tuple-element.14), channel_id=1, source_target_pairs={{0,8},{4,12},{8,0},{12,4},{1,9},{5,13},{9,1},{13,5},{2,10},{6,14},... | collective-permute-start | bytes 294920 | tf_op jit(solution)/shard_map/ppermute | solution.py:302
  10.4 12.9 %collective-permute-start.5 = (bf16[128,384]{1,0:T(8,128)(2,1)}, bf16[128,384]{1,0:T(8,128)(2,1)S(1)}, u32[]{:S(2)}, u32[]{:S(2)}) collective-permute-start(bf16[128,384]{1,0:T(8,128)(2,1)} %get-tuple-element.15), channel_id=1, source_target_pairs={{0,12},{4,8},{8,4},{12,0},{1,13},{5,9},{9,5},{13,1},{2,14},{6,10},... | collective-permute-start | bytes 294920 | tf_op jit(solution)/shard_map/ppermute | solution.py:302
  11.7 11.5 %collective-permute-start.6 = (bf16[128,384]{1,0:T(8,128)(2,1)}, bf16[128,384]{1,0:T(8,128)(2,1)S(1)}, u32[]{:S(2)}, u32[]{:S(2)}) collective-permute-start(bf16[128,384]{1,0:T(8,128)(2,1)} %get-tuple-element.16), channel_id=1, source_target_pairs={{0,4},{4,0},{8,12},{12,8},{1,5},{5,1},{9,13},{13,9},{2,6},{6,2},{1... | collective-permute-start | bytes 294920 | tf_op jit(solution)/shard_map/ppermute | solution.py:302
  15.7 10.9 %collective-permute-start.1 = (bf16[128,384]{1,0:T(8,128)(2,1)S(1)}, bf16[128,384]{1,0:T(8,128)(2,1)S(1)}, u32[]{:S(2)}, u32[]{:S(2)}) collective-permute-start(bf16[128,384]{1,0:T(8,128)(2,1)S(1)} %get-tuple-element.12), channel_id=1, source_target_pairs={{0,8},{4,12},{8,0},{12,4},{1,9},{5,13},{9,1},{13,5},{2,10},{6,14},... | collective-permute-start | bytes 294920 | tf_op jit(solution)/shard_map/ppermute | solution.py:302
  18.5 4.7 %copy-start.8 = (bf16[4,64,384]{2,1,0:T(8,128)(2,1)S(1)}, bf16[4,64,384]{2,1,0:T(8,128)(2,1)}, u32[]{:S(2)}) copy-start(bf16[4,64,384]{2,1,0:T(8,128)(2,1)} %constant.18.clone.rest_6_) | copy-start | bytes 589828
  18.5 8.9 %collective-permute-start.2 = (bf16[128,384]{1,0:T(8,128)(2,1)S(1)}, bf16[128,384]{1,0:T(8,128)(2,1)S(1)}, u32[]{:S(2)}, u32[]{:S(2)}) collective-permute-start(bf16[128,384]{1,0:T(8,128)(2,1)S(1)} %get-tuple-element.11.rest_1_), channel_id=1, source_target_pairs={{0,12},{4,8},{8,4},{12,0},{1,13},{5,9},{9,5},{13,1},{2,14},{6,10},... | collective-permute-start | bytes 294920 | tf_op jit(solution)/shard_map/ppermute | solution.py:302
  21.4 6.0 %collective-permute-start.3 = (bf16[128,384]{1,0:T(8,128)(2,1)S(1)}, bf16[128,384]{1,0:T(8,128)(2,1)S(1)}, u32[]{:S(2)}, u32[]{:S(2)}) collective-permute-start(bf16[128,384]{1,0:T(8,128)(2,1)S(1)} %get-tuple-element.13), channel_id=1, source_target_pairs={{0,4},{4,0},{8,12},{12,8},{1,5},{5,1},{9,13},{13,9},{2,6},{6,2},{1... | collective-permute-start | bytes 294920 | tf_op jit(solution)/shard_map/ppermute | solution.py:302
  24.5 9.8 %copy-start.2 = (bf16[3,384,8]{1,2,0:T(8,128)(2,1)S(1)}, bf16[3,384,8]{1,2,0:T(8,128)(2,1)}, u32[]{:S(2)}) copy-start(bf16[3,384,8]{1,2,0:T(8,128)(2,1)} %param.19) | copy-start | bytes 55300
  24.5 9.7 %copy-start.7 = (bf16[8,256]{1,0:T(8,128)(2,1)S(1)}, bf16[8,256]{1,0:T(8,128)(2,1)}, u32[]{:S(2)}) copy-start(bf16[8,256]{1,0:T(8,128)(2,1)} %constant.19.clone.spread_ref) | copy-start | bytes 12292
  29.3 12.4 %all-to-all-start = ((bf16[8,32,256]{2,1,0:T(8,128)(2,1)}), bf16[8,32,256]{2,1,0:T(8,128)(2,1)S(1)}, u32[]{:S(2)}, u32[]{:S(2)}) async-start(bf16[8,32,256]{2,1,0:T(8,128)(2,1)} %mlp_rows.3), calls=%async_computation | async-start | bytes 262144 | tf_op jit(solution)/shard_map/all_to_all | solution.py:371

commit v15 on v14

--- a/solution.py
+++ b/solution.py
@@ -39,20 +39,12 @@
     return pl.CostEstimate(flops=int(micros * FLOPS_PER_US), bytes_accessed=0, transcendentals=0)
 
 
-def paired(count):
-    return count & (count - 1) == 0
-
-
 def target(place, k, count):
-    return place ^ k if paired(count) else (place + k) % count
+    return lax.rem(place + k, count)
 
 
 def source(place, k, count):
-    return place ^ k if paired(count) else (place - k + count) % count
-
-
-def issue_order(count):
-    return [*range(2, count), 1] if paired(count) else list(range(1, count))
+    return lax.rem(place - k + count, count)
 
 
 def conv_kernel(
@@ -167,7 +159,7 @@
         out_ref, cells_ref = rest
     width = blocks[0].shape[1]
     place = lax.axis_index("chan")
-    for block, k in zip(blocks, [0, *issue_order(parts)]):
+    for block, k in zip(blocks, range(parts)):
         origin = pl.multiple_of(source(place, k, parts) * G, G)
         for i in range(2):
             cells_ref[pl.ds(origin, G), i * width : (i + 1) * width] = block[
@@ -299,7 +291,7 @@
 
 
 def turn(block, axis, count, k):
-    return lax.ppermute(block, axis, [(i, target(i, k, count)) for i in range(count)])
+    return lax.ppermute(block, axis, [(i, (i + k) % count) for i in range(count)])
 
 
 def on_device(
@@ -349,7 +341,7 @@
     spread = (lat_of[None, :] == np.arange(lats)[:, None]).astype(jnp.bfloat16)
     left = expand(jnp.swapaxes(legendre, 1, 2), jnp.asarray(spread))
 
-    order = issue_order(num_chan)
+    order = list(range(1, num_chan))
     halves = [
         (pair, supports, cells, edge, disco_weight, num_chan)
         for edge, pair in zip(edges, pairs)
@@ -358,7 +350,7 @@
     for half, edge in zip(halves, edges):
         sent = conv_rows(*half, order, [], edge is None)
         received.append([turn(block, "chan", num_chan, k) for k, block in zip(order, sent)])
-    after = sent[1:2]
+    after = [sent[1], received[0][0]]
     for half, blocks in zip(halves, received):
         after = conv_rows(*half, (0,), after, False)
         blocks.insert(0, after[0])

time: 43.3 us -> 43.5 us (level)
    ppermute x6, starting transfers between devices: 8.67 us -> 9.93 us  [turn(): lax.ppermute(block, axis, [(i, (i + k) % count) for i in range(count)])]
    all_to_all x1, starting transfers between devices: 4.93 us -> 3.73 us  [on_device(): lax.all_to_all(spectrum, both, split_axis=0, concat_axis=0, tiled=True)]
    ppermute x6, waiting for transfers between devices: 2.97 us -> 3.99 us  [turn(): lax.ppermute(block, axis, [(i, (i + k) % count) for i in range(count)])]
    ppermute x1, waiting for transfers between devices: 0.91 us -> 0.01 us  [on_device(): edges = [None, lax.ppermute(edge_out, 'lat', [(0, 1), (1, 0)])]]
  transfers between devices with their start and end apart: 8 -> 8, of which waited for: 4 -> 2; matrix products, arithmetic and copies ran while one was open for 1% -> 1% of each run, Pallas kernels for 26% -> 26%
where the time goes in v15:
time: 43.5 us; the launch traced here: 43.2 us
  starting transfers between devices  16.7 us (38%)
  Pallas kernels  14.3 us (33%)
  waiting for transfers between devices  10.7 us (25%)
  local copies, waits for them, and re-layouts  1.35 us (3%)
    ppermute x6, starting transfers between devices, turn(): lax.ppermute(block, axis, [(i, (i + k) % count) for i in range(count)])  9.93 us
    pallas_call x4, Pallas kernels, conv_rows(): pl.pallas_call(functools.partial(conv_kernel, chunks, picks, edge is not...  9.18 us
    all_to_all x1, waiting for transfers between devices, on_device(): lax.all_to_all(spectrum, both, split_axis=0, concat_axis=0, tiled=True)  6.66 us
    ppermute x6, waiting for transfers between devices, turn(): lax.ppermute(block, axis, [(i, (i + k) % count) for i in range(count)])  3.99 us
    all_to_all x1, starting transfers between devices, on_device(): lax.all_to_all(spectrum, both, split_axis=0, concat_axis=0, tiled=True)  3.73 us
    ppermute x1, starting transfers between devices, on_device(): edges = [None, lax.ppermute(edge_out, 'lat', [(0, 1), (1, 0)])]  3.03 us
    pallas_call x2, Pallas kernels, mlp_rows(): pl.pallas_call(functools.partial(mlp_kernel, len(blocks), last, len(after...  3 us
    pallas_call x1, Pallas kernels, final_sum(): pl.pallas_call(final_kernel, out_shape=jax.ShapeDtypeStruct(shape, jnp.bf...  1.3 us
  transfers between devices with their start and end apart: 8, of which 2 were waited for; matrix products, arithmetic and copies ran while one was open for 1% of the time, Pallas kernels for 26%

profile of v15, /device:TPU:0, one launch (start us, length us, event | category | flops | bytes accessed | tf_op | source)
XLA Modules:
  0.0 43.2 jit_solution(11299671194734970543)
XLA Ops:
  0.0 1.0 %dynamic-slice_bitcast_fusion = bf16[2,64,1440]{2,1,0:T(8,128)(2,1)S(1)} fusion(bf16[4,1440,64]{1,2,0:T(8,128)(2,1)} %param.11, s32[]{:T(128)S(6)} %select_n.3), kind=kLoop, calls=%fused_computation | loop fusion | bytes 737284 | tf_op jit(solution)/shard_map/dynamic_slice | solution.py:320
  1.0 3.0 %collective-permute-start = (bf16[2,64,1440]{2,1,0:T(8,128)(2,1)S(1)}, bf16[2,64,1440]{2,1,0:T(8,128)(2,1)S(1)}, u32[]{:S(2)}, u32[]{:S(2)}) collective-permute-start(bf16[2,64,1440]{2,1,0:T(8,128)(2,1)S(1)} %dynamic-slice_bitcast_fusion), channel_id=1, source_target_pairs={{0,16},{16,0},{1,17},{17,1},{2,18},{18,2},{3,19},{19,3},{4,20},{20... | collective-permute-start | bytes 1105928 | tf_op jit(solution)/shard_map/ppermute | solution.py:321
  4.1 0.0 copy-start.3
  4.1 0.0 copy-start.4
  4.1 0.0 copy-start.5
  4.1 0.0 copy-start.6
  4.1 3.7 %conv_rows.5 = (bf16[128,384]{1,0:T(8,128)(2,1)}, bf16[128,384]{1,0:T(8,128)(2,1)}, bf16[128,384]{1,0:T(8,128)(2,1)}) custom-call(s32[4,9]{1,0:T(4,128)} %lat_ref.7, s32[4,9]{1,0:T(4,128)} %lon_ref.7, s32[4,9]{1,0:T(4,128)} %basis_ref.7, f32[4,9]{1,0:T(4,128)} %value_ref.7, bf16[4,64,1440]{2,1,0:T(8,128)(2,1)} %bitcast.7, bf16[6,64,64]{2,1,0:T(8,128)(2,1)} %rest_1_.3), custom_call_target="tpu_custom_call" | custom-call | flops 1000000000 | tf_op jit(solution)/shard_map/conv_rows/pallas_call | solution.py:136
  7.8 1.6 %collective-permute-start.1 = (bf16[128,384]{1,0:T(8,128)(2,1)}, bf16[128,384]{1,0:T(8,128)(2,1)S(1)}, u32[]{:S(2)}, u32[]{:S(2)}) collective-permute-start(bf16[128,384]{1,0:T(8,128)(2,1)} %get-tuple-element.12), channel_id=1, source_target_pairs={{0,4},{4,8},{8,12},{12,0},{1,5},{5,9},{9,13},{13,1},{2,6},{6,10},{... | collective-permute-start | bytes 294920 | tf_op jit(solution)/shard_map/ppermute | solution.py:294
  9.4 2.6 %collective-permute-start.5 = (bf16[128,384]{1,0:T(8,128)(2,1)}, bf16[128,384]{1,0:T(8,128)(2,1)S(1)}, u32[]{:S(2)}, u32[]{:S(2)}) collective-permute-start(bf16[128,384]{1,0:T(8,128)(2,1)} %get-tuple-element.15), channel_id=1, source_target_pairs={{0,8},{4,12},{8,0},{12,4},{1,9},{5,13},{9,1},{13,5},{2,10},{6,14},... | collective-permute-start | bytes 294920 | tf_op jit(solution)/shard_map/ppermute | solution.py:294
  12.0 1.4 %collective-permute-start.6 = (bf16[128,384]{1,0:T(8,128)(2,1)}, bf16[128,384]{1,0:T(8,128)(2,1)S(1)}, u32[]{:S(2)}, u32[]{:S(2)}) collective-permute-start(bf16[128,384]{1,0:T(8,128)(2,1)} %get-tuple-element.16), channel_id=1, source_target_pairs={{0,12},{4,0},{8,4},{12,8},{1,13},{5,1},{9,5},{13,9},{2,14},{6,2},{... | collective-permute-start | bytes 294920 | tf_op jit(solution)/shard_map/ppermute | solution.py:294
  13.3 0.1 copy.12
  13.5 0.1 copy.13
  13.6 0.0 collective-permute-done.rest_0_
  13.7 2.5 %conv_rows.4 = (bf16[128,384]{1,0:T(8,128)(2,1)S(1)}, bf16[128,384]{1,0:T(8,128)(2,1)S(1)}, bf16[128,384]{1,0:T(8,128)(2,1)S(1)}) custom-call(s32[4,9]{1,0:T(4,128)S(1)} %copy-done.3, s32[4,9]{1,0:T(4,128)S(1)} %copy-done.4, s32[4,9]{1,0:T(4,128)S(1)} %copy-done.5, f32[4,9]{1,0:T(4,128)S(1)} %copy-done.6, bf16[4,64,1440]{2,1,0:T(8,128)(2,1)S(1)} %bitcast.8, ...), custom_call_target="tpu_custom_call" | custom-call | flops 1000000000 | tf_op jit(solution)/shard_map/conv_rows/pallas_call | solution.py:136
  16.1 1.4 %collective-permute-start.2 = (bf16[128,384]{1,0:T(8,128)(2,1)S(1)}, bf16[128,384]{1,0:T(8,128)(2,1)S(1)}, u32[]{:S(2)}, u32[]{:S(2)}) collective-permute-start(bf16[128,384]{1,0:T(8,128)(2,1)S(1)} %get-tuple-element.13), channel_id=1, source_target_pairs={{0,4},{4,8},{8,12},{12,0},{1,5},{5,9},{9,13},{13,1},{2,6},{6,10},{... | collective-permute-start | bytes 294920 | tf_op jit(solution)/shard_map/ppermute | solution.py:294
  17.5 2.5 %collective-permute-start.4 = (bf16[128,384]{1,0:T(8,128)(2,1)S(1)}, bf16[128,384]{1,0:T(8,128)(2,1)S(1)}, u32[]{:S(2)}, u32[]{:S(2)}) collective-permute-start(bf16[128,384]{1,0:T(8,128)(2,1)S(1)} %get-tuple-element.14), channel_id=1, source_target_pairs={{0,12},{4,0},{8,4},{12,8},{1,13},{5,1},{9,5},{13,9},{2,14},{6,2},{... | collective-permute-start | bytes 294920 | tf_op jit(solution)/shard_map/ppermute | solution.py:294
  20.0 0.0 collective-permute-done.1.rest_2_.rest_1_
  20.0 0.5 %collective-permute-start.3 = (bf16[128,384]{1,0:T(8,128)(2,1)S(1)}, bf16[128,384]{1,0:T(8,128)(2,1)S(1)}, u32[]{:S(2)}, u32[]{:S(2)}) collective-permute-start(bf16[128,384]{1,0:T(8,128)(2,1)S(1)} %get-tuple-element.11.rest_1_), channel_id=1, source_target_pairs={{0,8},{4,12},{8,0},{12,4},{1,9},{5,13},{9,1},{13,5},{2,10},{6,14},... | collective-permute-start | bytes 294920 | tf_op jit(solution)/shard_map/ppermute | solution.py:294
  20.6 1.5 %conv_rows.6.rest_2_.rest_0_ = bf16[128,384]{1,0:T(8,128)(2,1)S(1)} custom-call(s32[4,9]{1,0:T(4,128)S(1)} %copy-done.3, s32[4,9]{1,0:T(4,128)S(1)} %copy-done.4, s32[4,9]{1,0:T(4,128)S(1)} %copy-done.5, f32[4,9]{1,0:T(4,128)S(1)} %copy-done.6, bf16[4,64,1440]{2,1,0:T(8,128)(2,1)S(1)} %bitcast.9, bf16[6,64,64]{2,1,0:T(8,128)(2,1)S(1)} %copy-done.1, ...), custom_call_target="tpu_custom_call" | custom-call | flops 200000000 | tf_op jit(solution)/shard_map/conv_rows/pallas_call | solution.py:136
  22.1 1.5 %conv_rows.7.rest_7_.rest_0_ = bf16[128,384]{1,0:T(8,128)(2,1)S(1)} custom-call(s32[4,9]{1,0:T(4,128)S(1)} %copy-done.3, s32[4,9]{1,0:T(4,128)S(1)} %copy-done.4, s32[4,9]{1,0:T(4,128)S(1)} %copy-done.5, f32[4,9]{1,0:T(4,128)S(1)} %copy-done.6, bf16[4,64,1440]{2,1,0:T(8,128)(2,1)S(1)} %bitcast.10, bf16[2,64,1440]{2,1,0:T(8,128)(2,1)S(1)} %collective-permute-done.rest_0_, ...), custom_call_target="tpu_custom_call" | custom-call | flops 200000000 | tf_op jit(solution)/shard_map/conv_rows/pallas_call | solution.py:136
  23.6 0.0 collective-permute-done.5.rest_2_
  23.7 1.2 %mlp_rows.2.rest_7_ = bf16[8,16,256]{2,1,0:T(8,128)(2,1)S(1)} custom-call(bf16[128,384]{1,0:T(8,128)(2,1)S(1)} %conv_rows.6.rest_2_.rest_0_, bf16[128,384]{1,0:T(8,128)(2,1)S(1)} %collective-permute-done.1.rest_2_.rest_1_, bf16[128,384]{1,0:T(8,128)(2,1)S(1)} %collective-permute-done.5.rest_2_, bf16[128,384]{1,0:T(8,128)(2,1)S(1)} %collective-permute-done.6.rest_3_, ...), custom_call_target="tpu_custom_call" | custom-call | flops 1000000000 | tf_op jit(solution)/shard_map/mlp_rows/pallas_call | solution.py:202
  24.8 0.0 copy-start.2
  24.8 0.0 copy-start.7
  24.9 0.0 collective-permute-done.2.rest_1_
  24.9 0.0 collective-permute-done.4.rest_3_
  24.9 4.0 %collective-permute-done.3.rest_2_ = bf16[128,384]{1,0:T(8,128)(2,1)S(1)} collective-permute-done((bf16[128,384]{1,0:T(8,128)(2,1)S(1)}, bf16[128,384]{1,0:T(8,128)(2,1)S(1)}, u32[]{:S(2)}, u32[]{:S(2)}) %collective-permute-start.3) | collective-permute-done | bytes 98336 | tf_op jit(solution)/shard_map/ppermute | solution.py:294
  28.9 1.8 %mlp_rows.3 = bf16[8,32,256]{2,1,0:T(8,128)(2,1)} custom-call(bf16[128,384]{1,0:T(8,128)(2,1)S(1)} %conv_rows.7.rest_7_.rest_0_, bf16[128,384]{1,0:T(8,128)(2,1)S(1)} %collective-permute-done.2.rest_1_, bf16[128,384]{1,0:T(8,128)(2,1)S(1)} %collective-permute-done.3.rest_2_, bf16[128,384]{1,0:T(8,128)(2,1)S(1)} %collective-permute-done.4.rest_3_, ...), custom_call_target="tpu_custom_call" | custom-call | flops 1000000000 | tf_op jit(solution)/shard_map/mlp_rows/pallas_call | solution.py:202
  30.7 3.7 %all-to-all-start = ((bf16[8,32,256]{2,1,0:T(8,128)(2,1)}), bf16[8,32,256]{2,1,0:T(8,128)(2,1)S(1)}, u32[]{:S(2)}, u32[]{:S(2)}) async-start(bf16[8,32,256]{2,1,0:T(8,128)(2,1)} %mlp_rows.3), calls=%async_computation | async-start | bytes 262144 | tf_op jit(solution)/shard_map/all_to_all | solution.py:363
  34.4 0.8 %expand.1.left_ref = bf16[3,2,384,256]{3,2,1,0:T(8,128)(2,1)S(1)} custom-call(bf16[3,8,384]{2,1,0:T(8,128)(2,1)S(1)} %bitcast.16, bf16[8,256]{1,0:T(8,128)(2,1)S(1)} %copy-done.7), custom_call_target="tpu_custom_call" | custom-call | flops 200000000 | tf_op jit(solution)/shard_map/expand/pallas_call | solution.py:236
  35.3 6.7 %all-to-all-done = bf16[8,32,256]{2,1,0:T(8,128)(2,1)S(1)} async-done(((bf16[8,32,256]{2,1,0:T(8,128)(2,1)}), bf16[8,32,256]{2,1,0:T(8,128)(2,1)S(1)}, u32[]{:S(2)}, u32[]{:S(2)}) %all-to-all-start) | async-done | bytes 131104 | tf_op jit(solution)/shard_map/all_to_all | solution.py:363
  41.9 1.3 %final_sum.1 = bf16[3,384,512]{2,1,0:T(8,128)(2,1)} custom-call(bf16[3,2,384,256]{3,2,1,0:T(8,128)(2,1)S(1)} %expand.1.left_ref, bf16[256,256]{1,0:T(8,128)(2,1)S(1)} %bitcast.15), custom_call_target="tpu_custom_call" | custom-call | flops 1000000000 | tf_op jit(solution)/shard_map/final_sum/pallas_call | solution.py:269
  (17 shorter events, 0.0 us)
Async XLA Ops:
  1.0 12.6 %collective-permute-start = (bf16[2,64,1440]{2,1,0:T(8,128)(2,1)S(1)}, bf16[2,64,1440]{2,1,0:T(8,128)(2,1)S(1)}, u32[]{:S(2)}, u32[]{:S(2)}) collective-permute-start(bf16[2,64,1440]{2,1,0:T(8,128)(2,1)S(1)} %dynamic-slice_bitcast_fusion), channel_id=1, source_target_pairs={{0,16},{16,0},{1,17},{17,1},{2,18},{18,2},{3,19},{19,3},{4,20},{20... | collective-permute-start | bytes 1105928 | tf_op jit(solution)/shard_map/ppermute | solution.py:321
  4.1 9.3 %copy-start.9 = (bf16[256,512]{1,0:T(8,128)(2,1)S(1)}, bf16[256,512]{1,0:T(8,128)(2,1)}, u32[]{:S(2)}) copy-start(bf16[256,512]{1,0:T(8,128)(2,1)} %param.17) | copy-start | bytes 786436
  4.1 9.4 %copy-start.10 = (bf16[512,256]{1,0:T(8,128)(2,1)S(1)}, bf16[512,256]{1,0:T(8,128)(2,1)}, u32[]{:S(2)}) copy-start(bf16[512,256]{1,0:T(8,128)(2,1)} %param.18) | copy-start | bytes 786436
  4.1 9.6 %copy-start = (bf16[4,1440,64]{1,2,0:T(8,128)(2,1)S(1)}, bf16[4,1440,64]{1,2,0:T(8,128)(2,1)}, u32[]{:S(2)}) copy-start(bf16[4,1440,64]{1,2,0:T(8,128)(2,1)} %param.11) | copy-start | bytes 2211844
  4.1 9.6 %copy-start.1 = (bf16[6,64,64]{2,1,0:T(8,128)(2,1)S(1)}, bf16[6,64,64]{2,1,0:T(8,128)(2,1)}, u32[]{:S(2)}) copy-start(bf16[6,64,64]{2,1,0:T(8,128)(2,1)} %rest_1_.3) | copy-start | bytes 147460
  4.1 9.6 %copy-start.3 = (s32[4,9]{1,0:T(4,128)S(1)}, s32[4,9]{1,0:T(4,128)}, u32[]{:S(2)}) copy-start(s32[4,9]{1,0:T(4,128)} %lat_ref.7) | copy-start | bytes 436
  4.1 9.6 %copy-start.4 = (s32[4,9]{1,0:T(4,128)S(1)}, s32[4,9]{1,0:T(4,128)}, u32[]{:S(2)}) copy-start(s32[4,9]{1,0:T(4,128)} %lon_ref.7) | copy-start | bytes 436
  4.1 9.6 %copy-start.5 = (s32[4,9]{1,0:T(4,128)S(1)}, s32[4,9]{1,0:T(4,128)}, u32[]{:S(2)}) copy-start(s32[4,9]{1,0:T(4,128)} %basis_ref.7) | copy-start | bytes 436
  4.1 9.6 %copy-start.6 = (f32[4,9]{1,0:T(4,128)S(1)}, f32[4,9]{1,0:T(4,128)}, u32[]{:S(2)}) copy-start(f32[4,9]{1,0:T(4,128)} %value_ref.7) | copy-start | bytes 436
  7.8 12.2 %collective-permute-start.1 = (bf16[128,384]{1,0:T(8,128)(2,1)}, bf16[128,384]{1,0:T(8,128)(2,1)S(1)}, u32[]{:S(2)}, u32[]{:S(2)}) collective-permute-start(bf16[128,384]{1,0:T(8,128)(2,1)} %get-tuple-element.12), channel_id=1, source_target_pairs={{0,4},{4,8},{8,12},{12,0},{1,5},{5,9},{9,13},{13,1},{2,6},{6,10},{... | collective-permute-start | bytes 294920 | tf_op jit(solution)/shard_map/ppermute | solution.py:294
  9.4 14.3 %collective-permute-start.5 = (bf16[128,384]{1,0:T(8,128)(2,1)}, bf16[128,384]{1,0:T(8,128)(2,1)S(1)}, u32[]{:S(2)}, u32[]{:S(2)}) collective-permute-start(bf16[128,384]{1,0:T(8,128)(2,1)} %get-tuple-element.15), channel_id=1, source_target_pairs={{0,8},{4,12},{8,0},{12,4},{1,9},{5,13},{9,1},{13,5},{2,10},{6,14},... | collective-permute-start | bytes 294920 | tf_op jit(solution)/shard_map/ppermute | solution.py:294
  12.0 11.7 %collective-permute-start.6 = (bf16[128,384]{1,0:T(8,128)(2,1)}, bf16[128,384]{1,0:T(8,128)(2,1)S(1)}, u32[]{:S(2)}, u32[]{:S(2)}) collective-permute-start(bf16[128,384]{1,0:T(8,128)(2,1)} %get-tuple-element.16), channel_id=1, source_target_pairs={{0,12},{4,0},{8,4},{12,8},{1,13},{5,1},{9,5},{13,9},{2,14},{6,2},{... | collective-permute-start | bytes 294920 | tf_op jit(solution)/shard_map/ppermute | solution.py:294
  16.1 8.7 %collective-permute-start.2 = (bf16[128,384]{1,0:T(8,128)(2,1)S(1)}, bf16[128,384]{1,0:T(8,128)(2,1)S(1)}, u32[]{:S(2)}, u32[]{:S(2)}) collective-permute-start(bf16[128,384]{1,0:T(8,128)(2,1)S(1)} %get-tuple-element.13), channel_id=1, source_target_pairs={{0,4},{4,8},{8,12},{12,0},{1,5},{5,9},{9,13},{13,1},{2,6},{6,10},{... | collective-permute-start | bytes 294920 | tf_op jit(solution)/shard_map/ppermute | solution.py:294
  17.5 7.4 %collective-permute-start.4 = (bf16[128,384]{1,0:T(8,128)(2,1)S(1)}, bf16[128,384]{1,0:T(8,128)(2,1)S(1)}, u32[]{:S(2)}, u32[]{:S(2)}) collective-permute-start(bf16[128,384]{1,0:T(8,128)(2,1)S(1)} %get-tuple-element.14), channel_id=1, source_target_pairs={{0,12},{4,0},{8,4},{12,8},{1,13},{5,1},{9,5},{13,9},{2,14},{6,2},{... | collective-permute-start | bytes 294920 | tf_op jit(solution)/shard_map/ppermute | solution.py:294
  20.0 3.6 %copy-start.8 = (bf16[4,64,384]{2,1,0:T(8,128)(2,1)S(1)}, bf16[4,64,384]{2,1,0:T(8,128)(2,1)}, u32[]{:S(2)}) copy-start(bf16[4,64,384]{2,1,0:T(8,128)(2,1)} %constant.18.clone.rest_6_) | copy-start | bytes 589828
  20.0 8.8 %collective-permute-start.3 = (bf16[128,384]{1,0:T(8,128)(2,1)S(1)}, bf16[128,384]{1,0:T(8,128)(2,1)S(1)}, u32[]{:S(2)}, u32[]{:S(2)}) collective-permute-start(bf16[128,384]{1,0:T(8,128)(2,1)S(1)} %get-tuple-element.11.rest_1_), channel_id=1, source_target_pairs={{0,8},{4,12},{8,0},{12,4},{1,9},{5,13},{9,1},{13,5},{2,10},{6,14},... | collective-permute-start | bytes 294920 | tf_op jit(solution)/shard_map/ppermute | solution.py:294
  24.8 9.6 %copy-start.2 = (bf16[3,384,8]{1,2,0:T(8,128)(2,1)S(1)}, bf16[3,384,8]{1,2,0:T(8,128)(2,1)}, u32[]{:S(2)}) copy-start(bf16[3,384,8]{1,2,0:T(8,128)(2,1)} %param.19) | copy-start | bytes 55300
  24.8 9.6 %copy-start.7 = (bf16[8,256]{1,0:T(8,128)(2,1)S(1)}, bf16[8,256]{1,0:T(8,128)(2,1)}, u32[]{:S(2)}) copy-start(bf16[8,256]{1,0:T(8,128)(2,1)} %constant.19.clone.spread_ref) | copy-start | bytes 12292
  30.7 11.2 %all-to-all-start = ((bf16[8,32,256]{2,1,0:T(8,128)(2,1)}), bf16[8,32,256]{2,1,0:T(8,128)(2,1)S(1)}, u32[]{:S(2)}, u32[]{:S(2)}) async-start(bf16[8,32,256]{2,1,0:T(8,128)(2,1)} %mlp_rows.3), calls=%async_computation | async-start | bytes 262144 | tf_op jit(solution)/shard_map/all_to_all | solution.py:363

commit v16 on v14

--- a/solution.py
+++ b/solution.py
@@ -55,14 +55,25 @@
     return [*range(2, count), 1] if paired(count) else list(range(1, count))
 
 
-def conv_kernel(
-    chunks, picks, has_edge, after, flip, lat_ref, lon_ref, basis_ref, value_ref, fields_ref, *rest
-):
-    if has_edge:
-        edge_ref, weight_ref, *rest = rest
+def conv_kernel(chunks, picks, has_edge, after, flip, manual, *refs):
+    count = len(picks)
+    if manual:
+        sources, outs, refs = refs[:6], refs[6 : 6 + count], refs[6 + count :]
+        *scratch, held, sems, out_sems, rows_ref, taps_ref, filt_ref = refs
+        copies = [
+            pltpu.make_async_copy(sources[k], scratch[k], sems.at[k]) for k in range(len(sources))
+        ]
+        for copy in reversed(copies):
+            copy.start()
+        for copy in copies[:-1]:
+            copy.wait()
+        lat_ref, lon_ref, basis_ref, value_ref, weight_ref, fields_ref = scratch
+        out_refs = [held.at[k] for k in range(count)]
+        edge_ref = None
     else:
-        edge_ref, (weight_ref, *rest) = None, rest
-    *out_refs, rows_ref, taps_ref, filt_ref = rest[after:]
+        lat_ref, lon_ref, basis_ref, value_ref, weight_ref, fields_ref, *refs = refs
+        edge_ref, refs = (refs[0], refs[1:]) if has_edge else (None, refs)
+        *out_refs, rows_ref, taps_ref, filt_ref = refs[after:]
     own, _, lon = fields_ref.shape
     chunk = lon // chunks
     width = out_refs[0].shape[1]
@@ -70,6 +81,25 @@
     pair = flip if isinstance(flip, int) else flip()
     own_at = HALO * (1 - pair)
     edge_at = own * pair
+
+    eye = jnp.where(
+        lax.broadcasted_iota(jnp.int32, (G, G), 0) == lax.broadcasted_iota(jnp.int32, (G, G), 1),
+        1.0,
+        0.0,
+    ).astype(jnp.bfloat16)
+    for i in range(2):
+        row = 2 * pair + i
+        pieces = []
+        for tap in range(S):
+            picked = weight_ref[basis_ref[row, tap]].astype(jnp.float32) * value_ref[row, tap]
+            pieces.append(picked.astype(jnp.bfloat16))
+        pieces.append(eye)
+        for k in range(TAPS // 2):
+            filt_ref[i, :, k * 2 * G : (k + 1) * 2 * G] = jnp.concatenate(
+                [pieces[2 * k], pieces[2 * k + 1]], axis=1
+            )
+    if manual:
+        copies[-1].wait()
 
     def put(slot, cells):
         rows_ref[slot, :, LANES : LANES + lon] = cells
@@ -109,22 +139,8 @@
                     keep, turned[t], turned[t + 1]
                 )
 
-    eye = jnp.where(
-        lax.broadcasted_iota(jnp.int32, (G, G), 0) == lax.broadcasted_iota(jnp.int32, (G, G), 1),
-        1.0,
-        0.0,
-    ).astype(jnp.bfloat16)
     for i in range(2):
         row = 2 * pair + i
-        pieces = []
-        for tap in range(S):
-            picked = weight_ref[basis_ref[row, tap]].astype(jnp.float32) * value_ref[row, tap]
-            pieces.append(picked.astype(jnp.bfloat16))
-        pieces.append(eye)
-        for k in range(TAPS // 2):
-            filt_ref[i, :, k * 2 * G : (k + 1) * 2 * G] = jnp.concatenate(
-                [pieces[2 * k], pieces[2 * k + 1]], axis=1
-            )
         for tap in range(S):
             fill(i, tap, HALO + i + lat_ref[row, tap], lon_ref[row, tap])
         fill(i, S, HALO + i, 0)
@@ -133,28 +149,54 @@
         )
         for k in range(len(picks)):
             out_refs[k][i * G : (i + 1) * G, :] = mixed[:, k * width : (k + 1) * width]
-
-
-def conv_rows(pair, supports, fields, edge, weight, chunks, picks, after, roomy):
+    if manual:
+        copies = [
+            pltpu.make_async_copy(out_refs[k], outs[k], out_sems.at[k]) for k in range(count)
+        ]
+        for copy in copies:
+            copy.start()
+        for copy in copies:
+            copy.wait()
+
+
+def conv_rows(pair, supports, fields, edge, weight, chunks, picks, after, manual):
     own, chans, lon = fields.shape
     width = ceil_to(lon // chunks, LANES)
     highest = (LANES + lon - lon // chunks + DLON) // LANES
     total = (highest + 1) * LANES + width
-    arrays = [fields] + ([] if edge is None else [edge]) + [weight]
+    count = len(picks)
+    arrays = [*supports, weight, fields] + ([] if edge is None else [edge])
+    outs = [jax.ShapeDtypeStruct((2 * chans, width), jnp.bfloat16)] * count
+    scratch = [
+        pltpu.VMEM((own + HALO, chans, total), jnp.bfloat16),
+        pltpu.VMEM((2, TAPS * G, count * width), jnp.bfloat16),
+        pltpu.VMEM((2, G, TAPS * G), jnp.bfloat16),
+    ]
+    if manual:
+        in_specs, out_specs = [ANY] * len(arrays), [ANY] * count
+        spaces = [pltpu.SMEM] * len(supports) + [pltpu.VMEM] * 2
+        scratch = [
+            *(space(array.shape, array.dtype) for space, array in zip(spaces, arrays)),
+            pltpu.VMEM((count, 2 * chans, width), jnp.bfloat16),
+            pltpu.SemaphoreType.DMA((len(arrays),)),
+            pltpu.SemaphoreType.DMA((count,)),
+            *scratch,
+        ]
+    else:
+        in_specs = [SMEM] * len(supports) + [VMEM] * (len(arrays) - len(supports))
+        in_specs, out_specs = in_specs + [ANY] * len(after), [VMEM] * count
     return pl.pallas_call(
-        functools.partial(conv_kernel, chunks, picks, edge is not None, len(after), pair),
-        out_shape=[jax.ShapeDtypeStruct((2 * chans, width), jnp.bfloat16)] * len(picks),
-        in_specs=[SMEM] * 4 + [VMEM] * len(arrays) + [ANY] * len(after),
-        out_specs=[VMEM] * len(picks),
-        scratch_shapes=[
-            pltpu.VMEM((own + HALO, chans, total), jnp.bfloat16),
-            pltpu.VMEM((2, TAPS * G, len(picks) * width), jnp.bfloat16),
-            pltpu.VMEM((2, G, TAPS * G), jnp.bfloat16),
-        ],
-        compiler_params=params(56 if roomy else 20),
-        cost_estimate=takes(1 if len(picks) > 1 else 0.2),
+        functools.partial(
+            conv_kernel, chunks, picks, edge is not None, len(after), pair, manual
+        ),
+        out_shape=outs,
+        in_specs=in_specs,
+        out_specs=out_specs,
+        scratch_shapes=scratch,
+        compiler_params=params(56 if manual else 20),
+        cost_estimate=takes(1 if count > 1 else 0.2),
         name="conv_rows",
-    )(*supports, *arrays, *after)
+    )(*arrays, *after)
 
 
 def mlp_kernel(parts, last, after, *rest):

time: 43.3 us -> 43.4 us (level)
  no operation moved by 1% of the time
where the time goes in v16:
time: 43.4 us; the launch traced here: 43.1 us
  starting transfers between devices  16.7 us (38%)
  Pallas kernels  14.4 us (33%)
  waiting for transfers between devices  10.4 us (24%)
  local copies, waits for them, and re-layouts  1.35 us (3%)
    pallas_call x4, Pallas kernels, conv_rows(): pl.pallas_call(functools.partial(conv_kernel, chunks, picks, edge is not...  9.3 us
    ppermute x6, starting transfers between devices, turn(): lax.ppermute(block, axis, [(i, target(i, k, count)) for i in range(count)])  8.75 us
    all_to_all x1, waiting for transfers between devices, on_device(): lax.all_to_all(spectrum, both, split_axis=0, concat_axis=0, tiled=True)  6.66 us
    all_to_all x1, starting transfers between devices, on_device(): lax.all_to_all(spectrum, both, split_axis=0, concat_axis=0, tiled=True)  4.93 us
    ppermute x1, starting transfers between devices, on_device(): edges = [None, lax.ppermute(edge_out, 'lat', [(0, 1), (1, 0)])]  3.03 us
    pallas_call x2, Pallas kernels, mlp_rows(): pl.pallas_call(functools.partial(mlp_kernel, len(blocks), last, len(after...  3 us
    ppermute x6, waiting for transfers between devices, turn(): lax.ppermute(block, axis, [(i, target(i, k, count)) for i in range(count)])  3 us
    pallas_call x1, Pallas kernels, final_sum(): pl.pallas_call(final_kernel, out_shape=jax.ShapeDtypeStruct(shape, jnp.bf...  1.3 us
  transfers between devices with their start and end apart: 8, of which 4 were waited for; matrix products, arithmetic and copies ran while one was open for 1% of the time, Pallas kernels for 26%

profile of v16, /device:TPU:0, one launch (start us, length us, event | category | flops | bytes accessed | tf_op | source)
XLA Modules:
  0.0 43.1 jit_solution(17368921095090169340)
XLA Ops:
  0.0 1.0 %dynamic-slice_bitcast_fusion = bf16[2,64,1440]{2,1,0:T(8,128)(2,1)S(1)} fusion(bf16[4,1440,64]{1,2,0:T(8,128)(2,1)} %param.11, s32[]{:T(128)S(6)} %select_n.3), kind=kLoop, calls=%fused_computation | loop fusion | bytes 737284 | tf_op jit(solution)/shard_map/dynamic_slice | solution.py:370
  1.0 3.0 %collective-permute-start = (bf16[2,64,1440]{2,1,0:T(8,128)(2,1)S(1)}, bf16[2,64,1440]{2,1,0:T(8,128)(2,1)S(1)}, u32[]{:S(2)}, u32[]{:S(2)}) collective-permute-start(bf16[2,64,1440]{2,1,0:T(8,128)(2,1)S(1)} %dynamic-slice_bitcast_fusion), channel_id=1, source_target_pairs={{0,16},{16,0},{1,17},{17,1},{2,18},{18,2},{3,19},{19,3},{4,20},{20... | collective-permute-start | bytes 1105928 | tf_op jit(solution)/shard_map/ppermute | solution.py:371
  4.1 0.0 copy-start.3
  4.1 0.0 copy-start.4
  4.1 0.0 copy-start.5
  4.1 0.0 copy-start.6
  4.1 3.7 %conv_rows.7 = (bf16[128,384]{1,0:T(8,128)(2,1)}, bf16[128,384]{1,0:T(8,128)(2,1)}, bf16[128,384]{1,0:T(8,128)(2,1)}) custom-call(s32[4,9]{1,0:T(4,128)} %refs_0_.7, s32[4,9]{1,0:T(4,128)} %refs_1_.7, s32[4,9]{1,0:T(4,128)} %refs_2_.7, f32[4,9]{1,0:T(4,128)} %refs_3_.7, bf16[6,64,64]{2,1,0:T(8,128)(2,1)} %refs_4_.7, bf16[4,64,1440]{2,1,0:T(8,128)(2,1)} %bitcast.7), custom_call_target="tpu_custom_call" | custom-call | flops 1000000000 | tf_op jit(solution)/shard_map/conv_rows/pallas_call | solution.py:188
  7.8 2.7 %collective-permute-start.4 = (bf16[128,384]{1,0:T(8,128)(2,1)}, bf16[128,384]{1,0:T(8,128)(2,1)S(1)}, u32[]{:S(2)}, u32[]{:S(2)}) collective-permute-start(bf16[128,384]{1,0:T(8,128)(2,1)} %get-tuple-element.14), channel_id=1, source_target_pairs={{0,8},{4,12},{8,0},{12,4},{1,9},{5,13},{9,1},{13,5},{2,10},{6,14},... | collective-permute-start | bytes 294920 | tf_op jit(solution)/shard_map/ppermute | solution.py:344
  10.5 1.3 %collective-permute-start.5 = (bf16[128,384]{1,0:T(8,128)(2,1)}, bf16[128,384]{1,0:T(8,128)(2,1)S(1)}, u32[]{:S(2)}, u32[]{:S(2)}) collective-permute-start(bf16[128,384]{1,0:T(8,128)(2,1)} %get-tuple-element.15), channel_id=1, source_target_pairs={{0,12},{4,8},{8,4},{12,0},{1,13},{5,9},{9,5},{13,1},{2,14},{6,10},... | collective-permute-start | bytes 294920 | tf_op jit(solution)/shard_map/ppermute | solution.py:344
  11.8 0.2 collective-permute-start.6
  12.1 0.1 copy.12
  12.2 0.1 copy.13
  12.4 0.8 %collective-permute-done.refs_6_ = bf16[2,64,1440]{2,1,0:T(8,128)(2,1)S(1)} collective-permute-done((bf16[2,64,1440]{2,1,0:T(8,128)(2,1)S(1)}, bf16[2,64,1440]{2,1,0:T(8,128)(2,1)S(1)}, u32[]{:S(2)}, u32[]{:S(2)}) %collective-permute-start) | collective-permute-done | bytes 368672 | tf_op jit(solution)/shard_map/ppermute | solution.py:371
  13.2 2.5 %conv_rows.4 = (bf16[128,384]{1,0:T(8,128)(2,1)S(1)}, bf16[128,384]{1,0:T(8,128)(2,1)S(1)}, bf16[128,384]{1,0:T(8,128)(2,1)S(1)}) custom-call(s32[4,9]{1,0:T(4,128)S(1)} %copy-done.3, s32[4,9]{1,0:T(4,128)S(1)} %copy-done.4, s32[4,9]{1,0:T(4,128)S(1)} %copy-done.5, f32[4,9]{1,0:T(4,128)S(1)} %copy-done.6, bf16[6,64,64]{2,1,0:T(8,128)(2,1)S(1)} %copy-done.1, ...), custom_call_target="tpu_custom_call" | custom-call | flops 1000000000 | tf_op jit(solution)/shard_map/conv_rows/pallas_call | solution.py:188
  15.7 2.9 %collective-permute-start.1 = (bf16[128,384]{1,0:T(8,128)(2,1)S(1)}, bf16[128,384]{1,0:T(8,128)(2,1)S(1)}, u32[]{:S(2)}, u32[]{:S(2)}) collective-permute-start(bf16[128,384]{1,0:T(8,128)(2,1)S(1)} %get-tuple-element.12), channel_id=1, source_target_pairs={{0,8},{4,12},{8,0},{12,4},{1,9},{5,13},{9,1},{13,5},{2,10},{6,14},... | collective-permute-start | bytes 294920 | tf_op jit(solution)/shard_map/ppermute | solution.py:344
  18.6 1.4 %collective-permute-start.2 = (bf16[128,384]{1,0:T(8,128)(2,1)S(1)}, bf16[128,384]{1,0:T(8,128)(2,1)S(1)}, u32[]{:S(2)}, u32[]{:S(2)}) collective-permute-start(bf16[128,384]{1,0:T(8,128)(2,1)S(1)} %get-tuple-element.11.refs_6_), channel_id=1, source_target_pairs={{0,12},{4,8},{8,4},{12,0},{1,13},{5,9},{9,5},{13,1},{2,14},{6,10},... | collective-permute-start | bytes 294920 | tf_op jit(solution)/shard_map/ppermute | solution.py:344
  19.9 1.5 %conv_rows.5.refs_7_.rest_0_ = bf16[128,384]{1,0:T(8,128)(2,1)S(1)} custom-call(s32[4,9]{1,0:T(4,128)S(1)} %copy-done.3, s32[4,9]{1,0:T(4,128)S(1)} %copy-done.4, s32[4,9]{1,0:T(4,128)S(1)} %copy-done.5, f32[4,9]{1,0:T(4,128)S(1)} %copy-done.6, bf16[6,64,64]{2,1,0:T(8,128)(2,1)S(1)} %copy-done.1, bf16[4,64,1440]{2,1,0:T(8,128)(2,1)S(1)} %bitcast.9, ...), custom_call_target="tpu_custom_call" | custom-call | flops 200000000 | tf_op jit(solution)/shard_map/conv_rows/pallas_call | solution.py:188
  21.5 0.0 collective-permute-done.4.rest_1_
  21.5 0.3 collective-permute-start.3
  21.8 1.6 %conv_rows.6.rest_7_.rest_0_ = bf16[128,384]{1,0:T(8,128)(2,1)S(1)} custom-call(s32[4,9]{1,0:T(4,128)S(1)} %copy-done.3, s32[4,9]{1,0:T(4,128)S(1)} %copy-done.4, s32[4,9]{1,0:T(4,128)S(1)} %copy-done.5, f32[4,9]{1,0:T(4,128)S(1)} %copy-done.6, bf16[6,64,64]{2,1,0:T(8,128)(2,1)S(1)} %copy-done.1, bf16[4,64,1440]{2,1,0:T(8,128)(2,1)S(1)} %bitcast.10, ...), custom_call_target="tpu_custom_call" | custom-call | flops 200000000 | tf_op jit(solution)/shard_map/conv_rows/pallas_call | solution.py:188
  23.3 0.0 collective-permute-done.5.rest_2_
  23.4 1.2 %mlp_rows.2.rest_7_ = bf16[8,16,256]{2,1,0:T(8,128)(2,1)S(1)} custom-call(bf16[128,384]{1,0:T(8,128)(2,1)S(1)} %conv_rows.5.refs_7_.rest_0_, bf16[128,384]{1,0:T(8,128)(2,1)S(1)} %collective-permute-done.4.rest_1_, bf16[128,384]{1,0:T(8,128)(2,1)S(1)} %collective-permute-done.5.rest_2_, bf16[128,384]{1,0:T(8,128)(2,1)S(1)} %collective-permute-done.6.rest_3_, ...), custom_call_target="tpu_custom_call" | custom-call | flops 1000000000 | tf_op jit(solution)/shard_map/mlp_rows/pallas_call | solution.py:252
  24.6 0.0 copy-start.2
  24.6 0.0 copy-start.7
  24.6 2.1 %collective-permute-done.1.rest_1_ = bf16[128,384]{1,0:T(8,128)(2,1)S(1)} collective-permute-done((bf16[128,384]{1,0:T(8,128)(2,1)S(1)}, bf16[128,384]{1,0:T(8,128)(2,1)S(1)}, u32[]{:S(2)}, u32[]{:S(2)}) %collective-permute-start.1) | collective-permute-done | bytes 98336 | tf_op jit(solution)/shard_map/ppermute | solution.py:344
  26.7 0.9 %collective-permute-done.3.rest_3_ = bf16[128,384]{1,0:T(8,128)(2,1)S(1)} collective-permute-done((bf16[128,384]{1,0:T(8,128)(2,1)S(1)}, bf16[128,384]{1,0:T(8,128)(2,1)S(1)}, u32[]{:S(2)}, u32[]{:S(2)}) %collective-permute-start.3) | collective-permute-done | bytes 98336 | tf_op jit(solution)/shard_map/ppermute | solution.py:344
  27.6 0.0 collective-permute-done.2.rest_2_
  27.6 1.8 %mlp_rows.3 = bf16[8,32,256]{2,1,0:T(8,128)(2,1)} custom-call(bf16[128,384]{1,0:T(8,128)(2,1)S(1)} %conv_rows.6.rest_7_.rest_0_, bf16[128,384]{1,0:T(8,128)(2,1)S(1)} %collective-permute-done.1.rest_1_, bf16[128,384]{1,0:T(8,128)(2,1)S(1)} %collective-permute-done.2.rest_2_, bf16[128,384]{1,0:T(8,128)(2,1)S(1)} %collective-permute-done.3.rest_3_, ...), custom_call_target="tpu_custom_call" | custom-call | flops 1000000000 | tf_op jit(solution)/shard_map/mlp_rows/pallas_call | solution.py:252
  29.4 4.9 %all-to-all-start = ((bf16[8,32,256]{2,1,0:T(8,128)(2,1)}), bf16[8,32,256]{2,1,0:T(8,128)(2,1)S(1)}, u32[]{:S(2)}, u32[]{:S(2)}) async-start(bf16[8,32,256]{2,1,0:T(8,128)(2,1)} %mlp_rows.3), calls=%async_computation | async-start | bytes 262144 | tf_op jit(solution)/shard_map/all_to_all | solution.py:413
  34.3 0.8 %expand.1.left_ref = bf16[3,2,384,256]{3,2,1,0:T(8,128)(2,1)S(1)} custom-call(bf16[3,8,384]{2,1,0:T(8,128)(2,1)S(1)} %bitcast.16, bf16[8,256]{1,0:T(8,128)(2,1)S(1)} %copy-done.7), custom_call_target="tpu_custom_call" | custom-call | flops 200000000 | tf_op jit(solution)/shard_map/expand/pallas_call | solution.py:286
  35.2 6.7 %all-to-all-done = bf16[8,32,256]{2,1,0:T(8,128)(2,1)S(1)} async-done(((bf16[8,32,256]{2,1,0:T(8,128)(2,1)}), bf16[8,32,256]{2,1,0:T(8,128)(2,1)S(1)}, u32[]{:S(2)}, u32[]{:S(2)}) %all-to-all-start) | async-done | bytes 131104 | tf_op jit(solution)/shard_map/all_to_all | solution.py:413
  41.8 1.3 %final_sum.1 = bf16[3,384,512]{2,1,0:T(8,128)(2,1)} custom-call(bf16[3,2,384,256]{3,2,1,0:T(8,128)(2,1)S(1)} %expand.1.left_ref, bf16[256,256]{1,0:T(8,128)(2,1)S(1)} %bitcast.15), custom_call_target="tpu_custom_call" | custom-call | flops 1000000000 | tf_op jit(solution)/shard_map/final_sum/pallas_call | solution.py:319
  (17 shorter events, 0.0 us)
Async XLA Ops:
  1.0 12.1 %collective-permute-start = (bf16[2,64,1440]{2,1,0:T(8,128)(2,1)S(1)}, bf16[2,64,1440]{2,1,0:T(8,128)(2,1)S(1)}, u32[]{:S(2)}, u32[]{:S(2)}) collective-permute-start(bf16[2,64,1440]{2,1,0:T(8,128)(2,1)S(1)} %dynamic-slice_bitcast_fusion), channel_id=1, source_target_pairs={{0,16},{16,0},{1,17},{17,1},{2,18},{18,2},{3,19},{19,3},{4,20},{20... | collective-permute-start | bytes 1105928 | tf_op jit(solution)/shard_map/ppermute | solution.py:371
  4.1 8.0 %copy-start.9 = (bf16[256,512]{1,0:T(8,128)(2,1)S(1)}, bf16[256,512]{1,0:T(8,128)(2,1)}, u32[]{:S(2)}) copy-start(bf16[256,512]{1,0:T(8,128)(2,1)} %param.17) | copy-start | bytes 786436
  4.1 8.2 %copy-start.10 = (bf16[512,256]{1,0:T(8,128)(2,1)S(1)}, bf16[512,256]{1,0:T(8,128)(2,1)}, u32[]{:S(2)}) copy-start(bf16[512,256]{1,0:T(8,128)(2,1)} %param.18) | copy-start | bytes 786436
  4.1 9.1 %copy-start = (bf16[4,1440,64]{1,2,0:T(8,128)(2,1)S(1)}, bf16[4,1440,64]{1,2,0:T(8,128)(2,1)}, u32[]{:S(2)}) copy-start(bf16[4,1440,64]{1,2,0:T(8,128)(2,1)} %param.11) | copy-start | bytes 2211844
  4.1 9.1 %copy-start.1 = (bf16[6,64,64]{2,1,0:T(8,128)(2,1)S(1)}, bf16[6,64,64]{2,1,0:T(8,128)(2,1)}, u32[]{:S(2)}) copy-start(bf16[6,64,64]{2,1,0:T(8,128)(2,1)} %refs_4_.7) | copy-start | bytes 147460
  4.1 9.1 %copy-start.3 = (s32[4,9]{1,0:T(4,128)S(1)}, s32[4,9]{1,0:T(4,128)}, u32[]{:S(2)}) copy-start(s32[4,9]{1,0:T(4,128)} %refs_0_.7) | copy-start | bytes 436
  4.1 9.1 %copy-start.4 = (s32[4,9]{1,0:T(4,128)S(1)}, s32[4,9]{1,0:T(4,128)}, u32[]{:S(2)}) copy-start(s32[4,9]{1,0:T(4,128)} %refs_1_.7) | copy-start | bytes 436
  4.1 9.1 %copy-start.5 = (s32[4,9]{1,0:T(4,128)S(1)}, s32[4,9]{1,0:T(4,128)}, u32[]{:S(2)}) copy-start(s32[4,9]{1,0:T(4,128)} %refs_2_.7) | copy-start | bytes 436
  4.1 9.1 %copy-start.6 = (f32[4,9]{1,0:T(4,128)S(1)}, f32[4,9]{1,0:T(4,128)}, u32[]{:S(2)}) copy-start(f32[4,9]{1,0:T(4,128)} %refs_3_.7) | copy-start | bytes 436
  7.8 13.6 %collective-permute-start.4 = (bf16[128,384]{1,0:T(8,128)(2,1)}, bf16[128,384]{1,0:T(8,128)(2,1)S(1)}, u32[]{:S(2)}, u32[]{:S(2)}) collective-permute-start(bf16[128,384]{1,0:T(8,128)(2,1)} %get-tuple-element.14), channel_id=1, source_target_pairs={{0,8},{4,12},{8,0},{12,4},{1,9},{5,13},{9,1},{13,5},{2,10},{6,14},... | collective-permute-start | bytes 294920 | tf_op jit(solution)/shard_map/ppermute | solution.py:344
  10.5 12.8 %collective-permute-start.5 = (bf16[128,384]{1,0:T(8,128)(2,1)}, bf16[128,384]{1,0:T(8,128)(2,1)S(1)}, u32[]{:S(2)}, u32[]{:S(2)}) collective-permute-start(bf16[128,384]{1,0:T(8,128)(2,1)} %get-tuple-element.15), channel_id=1, source_target_pairs={{0,12},{4,8},{8,4},{12,0},{1,13},{5,9},{9,5},{13,1},{2,14},{6,10},... | collective-permute-start | bytes 294920 | tf_op jit(solution)/shard_map/ppermute | solution.py:344
  11.8 11.5 %collective-permute-start.6 = (bf16[128,384]{1,0:T(8,128)(2,1)}, bf16[128,384]{1,0:T(8,128)(2,1)S(1)}, u32[]{:S(2)}, u32[]{:S(2)}) collective-permute-start(bf16[128,384]{1,0:T(8,128)(2,1)} %get-tuple-element.16), channel_id=1, source_target_pairs={{0,4},{4,0},{8,12},{12,8},{1,5},{5,1},{9,13},{13,9},{2,6},{6,2},{1... | collective-permute-start | bytes 294920 | tf_op jit(solution)/shard_map/ppermute | solution.py:344
  15.7 11.0 %collective-permute-start.1 = (bf16[128,384]{1,0:T(8,128)(2,1)S(1)}, bf16[128,384]{1,0:T(8,128)(2,1)S(1)}, u32[]{:S(2)}, u32[]{:S(2)}) collective-permute-start(bf16[128,384]{1,0:T(8,128)(2,1)S(1)} %get-tuple-element.12), channel_id=1, source_target_pairs={{0,8},{4,12},{8,0},{12,4},{1,9},{5,13},{9,1},{13,5},{2,10},{6,14},... | collective-permute-start | bytes 294920 | tf_op jit(solution)/shard_map/ppermute | solution.py:344
  18.6 4.8 %copy-start.8 = (bf16[4,64,384]{2,1,0:T(8,128)(2,1)S(1)}, bf16[4,64,384]{2,1,0:T(8,128)(2,1)}, u32[]{:S(2)}) copy-start(bf16[4,64,384]{2,1,0:T(8,128)(2,1)} %constant.18.clone.rest_6_) | copy-start | bytes 589828
  18.6 9.0 %collective-permute-start.2 = (bf16[128,384]{1,0:T(8,128)(2,1)S(1)}, bf16[128,384]{1,0:T(8,128)(2,1)S(1)}, u32[]{:S(2)}, u32[]{:S(2)}) collective-permute-start(bf16[128,384]{1,0:T(8,128)(2,1)S(1)} %get-tuple-element.11.refs_6_), channel_id=1, source_target_pairs={{0,12},{4,8},{8,4},{12,0},{1,13},{5,9},{9,5},{13,1},{2,14},{6,10},... | collective-permute-start | bytes 294920 | tf_op jit(solution)/shard_map/ppermute | solution.py:344
  21.5 6.1 %collective-permute-start.3 = (bf16[128,384]{1,0:T(8,128)(2,1)S(1)}, bf16[128,384]{1,0:T(8,128)(2,1)S(1)}, u32[]{:S(2)}, u32[]{:S(2)}) collective-permute-start(bf16[128,384]{1,0:T(8,128)(2,1)S(1)} %get-tuple-element.13), channel_id=1, source_target_pairs={{0,4},{4,0},{8,12},{12,8},{1,5},{5,1},{9,13},{13,9},{2,6},{6,2},{1... | collective-permute-start | bytes 294920 | tf_op jit(solution)/shard_map/ppermute | solution.py:344
  24.6 9.8 %copy-start.2 = (bf16[3,384,8]{1,2,0:T(8,128)(2,1)S(1)}, bf16[3,384,8]{1,2,0:T(8,128)(2,1)}, u32[]{:S(2)}) copy-start(bf16[3,384,8]{1,2,0:T(8,128)(2,1)} %param.19) | copy-start | bytes 55300
  24.6 9.8 %copy-start.7 = (bf16[8,256]{1,0:T(8,128)(2,1)S(1)}, bf16[8,256]{1,0:T(8,128)(2,1)}, u32[]{:S(2)}) copy-start(bf16[8,256]{1,0:T(8,128)(2,1)} %constant.19.clone.spread_ref) | copy-start | bytes 12292
  29.4 12.4 %all-to-all-start = ((bf16[8,32,256]{2,1,0:T(8,128)(2,1)}), bf16[8,32,256]{2,1,0:T(8,128)(2,1)S(1)}, u32[]{:S(2)}, u32[]{:S(2)}) async-start(bf16[8,32,256]{2,1,0:T(8,128)(2,1)} %mlp_rows.3), calls=%async_computation | async-start | bytes 262144 | tf_op jit(solution)/shard_map/all_to_all | solution.py:413

commit v17 on v14

--- a/solution.py
+++ b/solution.py
@@ -19,6 +19,7 @@
 EPS = 1e-05
 FEW = 8
 MIB = 1024 * 1024
+EDGE_COST = 4
 FLOPS_PER_US = 1_000_000_000
 
 SMEM = pl.BlockSpec(memory_space=pltpu.SMEM)
@@ -53,6 +54,26 @@
 
 def issue_order(count):
     return [*range(2, count), 1] if paired(count) else list(range(1, count))
+
+
+def edge_kernel(fields_ref, same_ref, out_ref):
+    start = HALO * (1 - lax.axis_index("lat"))
+    for k in range(HALO):
+        out_ref[k] = fields_ref[start + k]
+    same_ref[...] = fields_ref[...]
+
+
+def edge_rows(fields):
+    shapes = [fields.shape, (HALO, *fields.shape[1:])]
+    return pl.pallas_call(
+        edge_kernel,
+        out_shape=[jax.ShapeDtypeStruct(shape, fields.dtype) for shape in shapes],
+        in_specs=[VMEM],
+        out_specs=[VMEM] * 2,
+        compiler_params=params(8),
+        cost_estimate=takes(EDGE_COST),
+        name="edge_rows",
+    )(fields)
 
 
 def conv_kernel(
@@ -151,7 +172,7 @@
             pltpu.VMEM((2, TAPS * G, len(picks) * width), jnp.bfloat16),
             pltpu.VMEM((2, G, TAPS * G), jnp.bfloat16),
         ],
-        compiler_params=params(56 if roomy else 20),
+        compiler_params=params(20),
         cost_estimate=takes(1 if len(picks) > 1 else 0.2),
         name="conv_rows",
     )(*supports, *arrays, *after)
@@ -319,13 +340,12 @@
     mode_dev, _, lats = legendre.shape
     dests = num_lat * num_chan
     width = ceil_to(lon // num_chan, LANES)
-    band = lax.axis_index("lat")
     supports = (support_lat, support_lon, support_basis, support_value)
 
     two_bands = num_lat == 2
     cells = jnp.swapaxes(fields, 1, 2)
     if two_bands:
-        edge_out = lax.dynamic_slice_in_dim(cells, HALO * (1 - band), HALO, axis=0)
+        cells, edge_out = edge_rows(cells)
         edges = [None, lax.ppermute(edge_out, "lat", [(0, 1), (1, 0)])]
         pairs = [lambda: lax.axis_index("lat"), lambda: 1 - lax.axis_index("lat")]
     else:

time: 43.3 us -> 42.9 us (level)
  waiting for transfers between devices: 10.5 us -> 11.7 us
  Pallas kernels: 14.3 us -> 13.2 us
    pallas_call x4, Pallas kernels: 9.17 us -> 7.94 us  [conv_rows(): pl.pallas_call(functools.partial(conv_kernel, chunks, picks, edge is not...]
    ppermute x1, waiting for transfers between devices: 0.91 us -> 2.07 us  [on_device(): edges = [None, lax.ppermute(edge_out, 'lat', [(0, 1), (1, 0)])]]
    unnamed x24, local copies, waits for them, and re-layouts: 0.33 us -> 1.45 us
    dynamic_slice x1 -> x0, local copies, waits for them, and re-layouts: 1.02 us -> none  [on_device(): edge_out = lax.dynamic_slice_in_dim(cells, HALO * (1 - band), HALO, axis=0)]
    all_to_all x1, starting transfers between devices: 4.93 us -> 4.35 us  [on_device(): lax.all_to_all(spectrum, both, split_axis=0, concat_axis=0, tiled=True)]
  transfers between devices with their start and end apart: 8 -> 8, of which waited for: 4 -> 4; matrix products, arithmetic and copies ran while one was open for 1% -> 1% of each run, Pallas kernels for 26% -> 23%
where the time goes in v17:
time: 42.9 us; the launch traced here: 42.7 us
  starting transfers between devices  16.2 us (38%)
  Pallas kernels  13.2 us (31%)
  waiting for transfers between devices  11.7 us (27%)
  local copies, waits for them, and re-layouts  1.45 us (3%)
    ppermute x6, starting transfers between devices, turn(): lax.ppermute(block, axis, [(i, target(i, k, count)) for i in range(count)])  8.82 us
    pallas_call x4, Pallas kernels, conv_rows(): pl.pallas_call(functools.partial(conv_kernel, chunks, picks, edge is not...  7.94 us
    all_to_all x1, waiting for transfers between devices, on_device(): lax.all_to_all(spectrum, both, split_axis=0, concat_axis=0, tiled=True)  6.66 us
    all_to_all x1, starting transfers between devices, on_device(): lax.all_to_all(spectrum, both, split_axis=0, concat_axis=0, tiled=True)  4.35 us
    ppermute x1, starting transfers between devices, on_device(): edges = [None, lax.ppermute(edge_out, 'lat', [(0, 1), (1, 0)])]  3.03 us
    pallas_call x2, Pallas kernels, mlp_rows(): pl.pallas_call(functools.partial(mlp_kernel, len(blocks), last, len(after...  3 us
    ppermute x6, waiting for transfers between devices, turn(): lax.ppermute(block, axis, [(i, target(i, k, count)) for i in range(count)])  2.92 us
    ppermute x1, waiting for transfers between devices, on_device(): edges = [None, lax.ppermute(edge_out, 'lat', [(0, 1), (1, 0)])]  2.07 us
  transfers between devices with their start and end apart: 8, of which 4 were waited for; matrix products, arithmetic and copies ran while one was open for 1% of the time, Pallas kernels for 23%

profile of v17, /device:TPU:0, one launch (start us, length us, event | category | flops | bytes accessed | tf_op | source)
XLA Modules:
  0.0 42.7 jit_solution(8045915528257922313)
XLA Ops:
  0.0 1.1 %copy-done.7 = bf16[4,1440,64]{1,2,0:T(8,128)(2,1)S(1)} copy-done((bf16[4,1440,64]{1,2,0:T(8,128)(2,1)S(1)}, bf16[4,1440,64]{1,2,0:T(8,128)(2,1)}, u32[]{:S(2)}) %copy-start.7) | copy-done | bytes 737304
  1.2 0.1 edge_rows.1
  1.2 3.0 %collective-permute-start = (bf16[2,64,1440]{2,1,0:T(8,128)(2,1)S(1)}, bf16[2,64,1440]{2,1,0:T(8,128)(2,1)S(1)}, u32[]{:S(2)}, u32[]{:S(2)}) collective-permute-start(bf16[2,64,1440]{2,1,0:T(8,128)(2,1)S(1)} %get-tuple-element.14), channel_id=1, source_target_pairs={{0,16},{16,0},{1,17},{17,1},{2,18},{18,2},{3,19},{19,3},{4,20},{20... | collective-permute-start | bytes 1105928 | tf_op jit(solution)/shard_map/ppermute | solution.py:349
  4.3 0.0 copy-start.9
  4.3 0.0 copy-start.10
  4.3 2.5 %conv_rows.7 = (bf16[128,384]{1,0:T(8,128)(2,1)S(1)}, bf16[128,384]{1,0:T(8,128)(2,1)S(1)}, bf16[128,384]{1,0:T(8,128)(2,1)S(1)}) custom-call(s32[4,9]{1,0:T(4,128)S(1)} %copy-done.2, s32[4,9]{1,0:T(4,128)S(1)} %copy-done.3, s32[4,9]{1,0:T(4,128)S(1)} %copy-done.4, f32[4,9]{1,0:T(4,128)S(1)} %copy-done.5, ...), custom_call_target="tpu_custom_call" | custom-call | flops 1000000000 | tf_op jit(solution)/shard_map/conv_rows/pallas_call | solution.py:165
  6.8 2.6 %collective-permute-start.4 = (bf16[128,384]{1,0:T(8,128)(2,1)S(1)}, bf16[128,384]{1,0:T(8,128)(2,1)S(1)}, u32[]{:S(2)}, u32[]{:S(2)}) collective-permute-start(bf16[128,384]{1,0:T(8,128)(2,1)S(1)} %get-tuple-element.18), channel_id=1, source_target_pairs={{0,8},{4,12},{8,0},{12,4},{1,9},{5,13},{9,1},{13,5},{2,10},{6,14},... | collective-permute-start | bytes 294920 | tf_op jit(solution)/shard_map/ppermute | solution.py:323
  9.4 1.4 %collective-permute-start.5 = (bf16[128,384]{1,0:T(8,128)(2,1)S(1)}, bf16[128,384]{1,0:T(8,128)(2,1)S(1)}, u32[]{:S(2)}, u32[]{:S(2)}) collective-permute-start(bf16[128,384]{1,0:T(8,128)(2,1)S(1)} %get-tuple-element.19), channel_id=1, source_target_pairs={{0,12},{4,8},{8,4},{12,0},{1,13},{5,9},{9,5},{13,1},{2,14},{6,10},... | collective-permute-start | bytes 294920 | tf_op jit(solution)/shard_map/ppermute | solution.py:323
  10.8 0.2 collective-permute-start.6
  11.0 0.1 copy.12
  11.2 0.1 copy.13
  11.3 2.1 %collective-permute-done.rest_0_ = bf16[2,64,1440]{2,1,0:T(8,128)(2,1)S(1)} collective-permute-done((bf16[2,64,1440]{2,1,0:T(8,128)(2,1)S(1)}, bf16[2,64,1440]{2,1,0:T(8,128)(2,1)S(1)}, u32[]{:S(2)}, u32[]{:S(2)}) %collective-permute-start) | collective-permute-done | bytes 368672 | tf_op jit(solution)/shard_map/ppermute | solution.py:349
  13.4 2.5 %conv_rows.4 = (bf16[128,384]{1,0:T(8,128)(2,1)S(1)}, bf16[128,384]{1,0:T(8,128)(2,1)S(1)}, bf16[128,384]{1,0:T(8,128)(2,1)S(1)}) custom-call(s32[4,9]{1,0:T(4,128)S(1)} %copy-done.2, s32[4,9]{1,0:T(4,128)S(1)} %copy-done.3, s32[4,9]{1,0:T(4,128)S(1)} %copy-done.4, f32[4,9]{1,0:T(4,128)S(1)} %copy-done.5, ...), custom_call_target="tpu_custom_call" | custom-call | flops 1000000000 | tf_op jit(solution)/shard_map/conv_rows/pallas_call | solution.py:165
  15.8 3.9 %collective-permute-start.2 = (bf16[128,384]{1,0:T(8,128)(2,1)S(1)}, bf16[128,384]{1,0:T(8,128)(2,1)S(1)}, u32[]{:S(2)}, u32[]{:S(2)}) collective-permute-start(bf16[128,384]{1,0:T(8,128)(2,1)S(1)} %get-tuple-element.15.rest_1_), channel_id=1, source_target_pairs={{0,12},{4,8},{8,4},{12,0},{1,13},{5,9},{9,5},{13,1},{2,14},{6,10},... | collective-permute-start | bytes 294920 | tf_op jit(solution)/shard_map/ppermute | solution.py:323
  19.7 0.0 collective-permute-start.1
  19.7 1.5 %conv_rows.5.rest_2_.rest_0_ = bf16[128,384]{1,0:T(8,128)(2,1)S(1)} custom-call(s32[4,9]{1,0:T(4,128)S(1)} %copy-done.2, s32[4,9]{1,0:T(4,128)S(1)} %copy-done.3, s32[4,9]{1,0:T(4,128)S(1)} %copy-done.4, f32[4,9]{1,0:T(4,128)S(1)} %copy-done.5, bf16[4,64,1440]{2,1,0:T(8,128)(2,1)S(1)} %get-tuple-element.13.fields_ref, bf16[6,64,64]{2,1,0:T(8,128)(2,1)S(1)} %copy-done, ...), custom_call_target="tpu_custom_call" | custom-call | flops 200000000 | tf_op jit(solution)/shard_map/conv_rows/pallas_call | solution.py:165
  21.2 0.0 collective-permute-done.4.rest_1_
  21.3 0.7 %collective-permute-start.3 = (bf16[128,384]{1,0:T(8,128)(2,1)S(1)}, bf16[128,384]{1,0:T(8,128)(2,1)S(1)}, u32[]{:S(2)}, u32[]{:S(2)}) collective-permute-start(bf16[128,384]{1,0:T(8,128)(2,1)S(1)} %get-tuple-element.17), channel_id=1, source_target_pairs={{0,4},{4,0},{8,12},{12,8},{1,5},{5,1},{9,13},{13,9},{2,6},{6,2},{1... | collective-permute-start | bytes 294920 | tf_op jit(solution)/shard_map/ppermute | solution.py:323
  22.0 1.5 %conv_rows.6.rest_7_.rest_0_ = bf16[128,384]{1,0:T(8,128)(2,1)S(1)} custom-call(s32[4,9]{1,0:T(4,128)S(1)} %copy-done.2, s32[4,9]{1,0:T(4,128)S(1)} %copy-done.3, s32[4,9]{1,0:T(4,128)S(1)} %copy-done.4, f32[4,9]{1,0:T(4,128)S(1)} %copy-done.5, bf16[4,64,1440]{2,1,0:T(8,128)(2,1)S(1)} %get-tuple-element.13.fields_ref, ...), custom_call_target="tpu_custom_call" | custom-call | flops 200000000 | tf_op jit(solution)/shard_map/conv_rows/pallas_call | solution.py:165
  23.5 0.0 collective-permute-done.5.rest_2_
  23.5 0.0 collective-permute-done.6.rest_3_
  23.5 1.2 %mlp_rows.2.rest_7_ = bf16[8,16,256]{2,1,0:T(8,128)(2,1)S(1)} custom-call(bf16[128,384]{1,0:T(8,128)(2,1)S(1)} %conv_rows.5.rest_2_.rest_0_, bf16[128,384]{1,0:T(8,128)(2,1)S(1)} %collective-permute-done.4.rest_1_, bf16[128,384]{1,0:T(8,128)(2,1)S(1)} %collective-permute-done.5.rest_2_, bf16[128,384]{1,0:T(8,128)(2,1)S(1)} %collective-permute-done.6.rest_3_, ...), custom_call_target="tpu_custom_call" | custom-call | flops 1000000000 | tf_op jit(solution)/shard_map/mlp_rows/pallas_call | solution.py:231
  24.7 0.0 copy-start.1
  24.7 0.0 copy-start.6
  24.7 0.0 collective-permute-done.2.rest_2_
  24.7 2.5 %collective-permute-done.1.rest_1_ = bf16[128,384]{1,0:T(8,128)(2,1)S(1)} collective-permute-done((bf16[128,384]{1,0:T(8,128)(2,1)S(1)}, bf16[128,384]{1,0:T(8,128)(2,1)S(1)}, u32[]{:S(2)}, u32[]{:S(2)}) %collective-permute-start.1) | collective-permute-done | bytes 98336 | tf_op jit(solution)/shard_map/ppermute | solution.py:323
  27.2 0.4 collective-permute-done.3.rest_3_
  27.7 1.8 %mlp_rows.3 = bf16[8,32,256]{2,1,0:T(8,128)(2,1)} custom-call(bf16[128,384]{1,0:T(8,128)(2,1)S(1)} %conv_rows.6.rest_7_.rest_0_, bf16[128,384]{1,0:T(8,128)(2,1)S(1)} %collective-permute-done.1.rest_1_, bf16[128,384]{1,0:T(8,128)(2,1)S(1)} %collective-permute-done.2.rest_2_, bf16[128,384]{1,0:T(8,128)(2,1)S(1)} %collective-permute-done.3.rest_3_, ...), custom_call_target="tpu_custom_call" | custom-call | flops 1000000000 | tf_op jit(solution)/shard_map/mlp_rows/pallas_call | solution.py:231
  29.5 4.3 %all-to-all-start = ((bf16[8,32,256]{2,1,0:T(8,128)(2,1)}), bf16[8,32,256]{2,1,0:T(8,128)(2,1)S(1)}, u32[]{:S(2)}, u32[]{:S(2)}) async-start(bf16[8,32,256]{2,1,0:T(8,128)(2,1)} %mlp_rows.3), calls=%async_computation | async-start | bytes 262144 | tf_op jit(solution)/shard_map/all_to_all | solution.py:391
  33.8 0.8 %expand.1.left_ref = bf16[3,2,384,256]{3,2,1,0:T(8,128)(2,1)S(1)} custom-call(bf16[3,8,384]{2,1,0:T(8,128)(2,1)S(1)} %bitcast.10, bf16[8,256]{1,0:T(8,128)(2,1)S(1)} %copy-done.6), custom_call_target="tpu_custom_call" | custom-call | flops 200000000 | tf_op jit(solution)/shard_map/expand/pallas_call | solution.py:265
  34.7 6.7 %all-to-all-done = bf16[8,32,256]{2,1,0:T(8,128)(2,1)S(1)} async-done(((bf16[8,32,256]{2,1,0:T(8,128)(2,1)}), bf16[8,32,256]{2,1,0:T(8,128)(2,1)S(1)}, u32[]{:S(2)}, u32[]{:S(2)}) %all-to-all-start) | async-done | bytes 131104 | tf_op jit(solution)/shard_map/all_to_all | solution.py:391
  41.4 1.3 %final_sum.1 = bf16[3,384,512]{2,1,0:T(8,128)(2,1)} custom-call(bf16[3,2,384,256]{3,2,1,0:T(8,128)(2,1)S(1)} %expand.1.left_ref, bf16[256,256]{1,0:T(8,128)(2,1)S(1)} %bitcast.9), custom_call_target="tpu_custom_call" | custom-call | flops 1000000000 | tf_op jit(solution)/shard_map/final_sum/pallas_call | solution.py:298
  (17 shorter events, 0.0 us)
Async XLA Ops:
  0.0 1.1 %copy-start.7 = (bf16[4,1440,64]{1,2,0:T(8,128)(2,1)S(1)}, bf16[4,1440,64]{1,2,0:T(8,128)(2,1)}, u32[]{:S(2)}) copy-start(bf16[4,1440,64]{1,2,0:T(8,128)(2,1)} %param.11) | copy-start | bytes 2211844
  1.1 3.1 %copy-start = (bf16[6,64,64]{2,1,0:T(8,128)(2,1)S(1)}, bf16[6,64,64]{2,1,0:T(8,128)(2,1)}, u32[]{:S(2)}) copy-start(bf16[6,64,64]{2,1,0:T(8,128)(2,1)} %rest_0_.3) | copy-start | bytes 147460
  1.1 3.1 %copy-start.2 = (s32[4,9]{1,0:T(4,128)S(1)}, s32[4,9]{1,0:T(4,128)}, u32[]{:S(2)}) copy-start(s32[4,9]{1,0:T(4,128)} %lat_ref.7) | copy-start | bytes 436
  1.1 3.1 %copy-start.3 = (s32[4,9]{1,0:T(4,128)S(1)}, s32[4,9]{1,0:T(4,128)}, u32[]{:S(2)}) copy-start(s32[4,9]{1,0:T(4,128)} %lon_ref.7) | copy-start | bytes 436
  1.1 3.1 %copy-start.4 = (s32[4,9]{1,0:T(4,128)S(1)}, s32[4,9]{1,0:T(4,128)}, u32[]{:S(2)}) copy-start(s32[4,9]{1,0:T(4,128)} %basis_ref.7) | copy-start | bytes 436
  1.1 3.1 %copy-start.5 = (f32[4,9]{1,0:T(4,128)S(1)}, f32[4,9]{1,0:T(4,128)}, u32[]{:S(2)}) copy-start(f32[4,9]{1,0:T(4,128)} %value_ref.7) | copy-start | bytes 436
  1.2 12.1 %collective-permute-start = (bf16[2,64,1440]{2,1,0:T(8,128)(2,1)S(1)}, bf16[2,64,1440]{2,1,0:T(8,128)(2,1)S(1)}, u32[]{:S(2)}, u32[]{:S(2)}) collective-permute-start(bf16[2,64,1440]{2,1,0:T(8,128)(2,1)S(1)} %get-tuple-element.14), channel_id=1, source_target_pairs={{0,16},{16,0},{1,17},{17,1},{2,18},{18,2},{3,19},{19,3},{4,20},{20... | collective-permute-start | bytes 1105928 | tf_op jit(solution)/shard_map/ppermute | solution.py:349
  4.3 6.7 %copy-start.9 = (bf16[256,512]{1,0:T(8,128)(2,1)S(1)}, bf16[256,512]{1,0:T(8,128)(2,1)}, u32[]{:S(2)}) copy-start(bf16[256,512]{1,0:T(8,128)(2,1)} %param.17) | copy-start | bytes 786436
  4.3 6.9 %copy-start.10 = (bf16[512,256]{1,0:T(8,128)(2,1)S(1)}, bf16[512,256]{1,0:T(8,128)(2,1)}, u32[]{:S(2)}) copy-start(bf16[512,256]{1,0:T(8,128)(2,1)} %param.18) | copy-start | bytes 786436
  6.8 14.5 %collective-permute-start.4 = (bf16[128,384]{1,0:T(8,128)(2,1)S(1)}, bf16[128,384]{1,0:T(8,128)(2,1)S(1)}, u32[]{:S(2)}, u32[]{:S(2)}) collective-permute-start(bf16[128,384]{1,0:T(8,128)(2,1)S(1)} %get-tuple-element.18), channel_id=1, source_target_pairs={{0,8},{4,12},{8,0},{12,4},{1,9},{5,13},{9,1},{13,5},{2,10},{6,14},... | collective-permute-start | bytes 294920 | tf_op jit(solution)/shard_map/ppermute | solution.py:323
  9.4 14.1 %collective-permute-start.5 = (bf16[128,384]{1,0:T(8,128)(2,1)S(1)}, bf16[128,384]{1,0:T(8,128)(2,1)S(1)}, u32[]{:S(2)}, u32[]{:S(2)}) collective-permute-start(bf16[128,384]{1,0:T(8,128)(2,1)S(1)} %get-tuple-element.19), channel_id=1, source_target_pairs={{0,12},{4,8},{8,4},{12,0},{1,13},{5,9},{9,5},{13,1},{2,14},{6,10},... | collective-permute-start | bytes 294920 | tf_op jit(solution)/shard_map/ppermute | solution.py:323
  10.8 12.7 %collective-permute-start.6 = (bf16[128,384]{1,0:T(8,128)(2,1)S(1)}, bf16[128,384]{1,0:T(8,128)(2,1)S(1)}, u32[]{:S(2)}, u32[]{:S(2)}) collective-permute-start(bf16[128,384]{1,0:T(8,128)(2,1)S(1)} %get-tuple-element.20), channel_id=1, source_target_pairs={{0,4},{4,0},{8,12},{12,8},{1,5},{5,1},{9,13},{13,9},{2,6},{6,2},{1... | collective-permute-start | bytes 294920 | tf_op jit(solution)/shard_map/ppermute | solution.py:323
  15.8 8.9 %collective-permute-start.2 = (bf16[128,384]{1,0:T(8,128)(2,1)S(1)}, bf16[128,384]{1,0:T(8,128)(2,1)S(1)}, u32[]{:S(2)}, u32[]{:S(2)}) collective-permute-start(bf16[128,384]{1,0:T(8,128)(2,1)S(1)} %get-tuple-element.15.rest_1_), channel_id=1, source_target_pairs={{0,12},{4,8},{8,4},{12,0},{1,13},{5,9},{9,5},{13,1},{2,14},{6,10},... | collective-permute-start | bytes 294920 | tf_op jit(solution)/shard_map/ppermute | solution.py:323
  19.7 3.8 %copy-start.8 = (bf16[4,64,384]{2,1,0:T(8,128)(2,1)S(1)}, bf16[4,64,384]{2,1,0:T(8,128)(2,1)}, u32[]{:S(2)}) copy-start(bf16[4,64,384]{2,1,0:T(8,128)(2,1)} %constant.4.clone.rest_6_) | copy-start | bytes 589828
  19.7 7.5 %collective-permute-start.1 = (bf16[128,384]{1,0:T(8,128)(2,1)S(1)}, bf16[128,384]{1,0:T(8,128)(2,1)S(1)}, u32[]{:S(2)}, u32[]{:S(2)}) collective-permute-start(bf16[128,384]{1,0:T(8,128)(2,1)S(1)} %get-tuple-element.16), channel_id=1, source_target_pairs={{0,8},{4,12},{8,0},{12,4},{1,9},{5,13},{9,1},{13,5},{2,10},{6,14},... | collective-permute-start | bytes 294920 | tf_op jit(solution)/shard_map/ppermute | solution.py:323
  21.3 6.4 %collective-permute-start.3 = (bf16[128,384]{1,0:T(8,128)(2,1)S(1)}, bf16[128,384]{1,0:T(8,128)(2,1)S(1)}, u32[]{:S(2)}, u32[]{:S(2)}) collective-permute-start(bf16[128,384]{1,0:T(8,128)(2,1)S(1)} %get-tuple-element.17), channel_id=1, source_target_pairs={{0,4},{4,0},{8,12},{12,8},{1,5},{5,1},{9,13},{13,9},{2,6},{6,2},{1... | collective-permute-start | bytes 294920 | tf_op jit(solution)/shard_map/ppermute | solution.py:323
  24.7 9.1 %copy-start.1 = (bf16[3,384,8]{1,2,0:T(8,128)(2,1)S(1)}, bf16[3,384,8]{1,2,0:T(8,128)(2,1)}, u32[]{:S(2)}) copy-start(bf16[3,384,8]{1,2,0:T(8,128)(2,1)} %param.19) | copy-start | bytes 55300
  24.7 9.1 %copy-start.6 = (bf16[8,256]{1,0:T(8,128)(2,1)S(1)}, bf16[8,256]{1,0:T(8,128)(2,1)}, u32[]{:S(2)}) copy-start(bf16[8,256]{1,0:T(8,128)(2,1)} %constant.5.clone.spread_ref) | copy-start | bytes 12292
  29.5 11.9 %all-to-all-start = ((bf16[8,32,256]{2,1,0:T(8,128)(2,1)}), bf16[8,32,256]{2,1,0:T(8,128)(2,1)S(1)}, u32[]{:S(2)}, u32[]{:S(2)}) async-start(bf16[8,32,256]{2,1,0:T(8,128)(2,1)} %mlp_rows.3), calls=%async_computation | async-start | bytes 262144 | tf_op jit(solution)/shard_map/all_to_all | solution.py:391

commit v18 on v17

--- a/solution.py
+++ b/solution.py
@@ -375,16 +375,16 @@
         for edge, pair in zip(edges, pairs)
     ]
     received = []
-    for half, edge in zip(halves, edges):
-        sent = conv_rows(*half, order, [], edge is None)
-        received.append([turn(block, "chan", num_chan, k) for k, block in zip(order, sent)])
-    after = sent[1:2]
-    for half, blocks in zip(halves, received):
-        after = conv_rows(*half, (0,), after, False)
-        blocks.insert(0, after[0])
+    for half in halves:
+        first = conv_rows(*half, order[:1], [], False)
+        rest = conv_rows(*half, [*order[1:], 0], first, False)
+        sent = [*first, *rest[:-1]]
+        moved = [turn(block, "chan", num_chan, k) for k, block in zip(order, sent)]
+        received.append([rest[-1], *moved])
+    after = [rest[-1]]
     spectrum = None
     for blocks in received:
-        spectrum = mlp_rows(blocks, up, down, tables, spectrum, dests, list(after))
+        spectrum = mlp_rows(blocks, up, down, tables, spectrum, dests, after)
         after = []
 
     both = ("lat", "chan")

time: 42.9 us -> 45.2 us (1.054)
  starting transfers between devices: 16.2 us -> 17.5 us
  waiting for transfers between devices: 11.7 us -> 12.6 us
    ppermute x6, waiting for transfers between devices: 2.92 us -> 5.22 us  [turn(): lax.ppermute(block, axis, [(i, target(i, k, count)) for i in range(count)])]
    ppermute x1, waiting for transfers between devices: 2.07 us -> 0.74 us  [on_device(): edges = [None, lax.ppermute(edge_out, 'lat', [(0, 1), (1, 0)])]]
    all_to_all x1, starting transfers between devices: 4.35 us -> 5.57 us  [on_device(): lax.all_to_all(spectrum, both, split_axis=0, concat_axis=0, tiled=True)]
  transfers between devices with their start and end apart: 8 -> 8, of which waited for: 4 -> 5; matrix products, arithmetic and copies ran while one was open for 1% -> 1% of each run, Pallas kernels for 23% -> 22%
where the time goes in v18:
time: 45.2 us; the launch traced here: 44.9 us
  starting transfers between devices  17.5 us (39%)
  Pallas kernels  13.1 us (29%)
  waiting for transfers between devices  12.6 us (28%)
  local copies, waits for them, and re-layouts  1.46 us (3%)
    ppermute x6, starting transfers between devices, turn(): lax.ppermute(block, axis, [(i, target(i, k, count)) for i in range(count)])  8.91 us
    pallas_call x4, Pallas kernels, conv_rows(): pl.pallas_call(functools.partial(conv_kernel, chunks, picks, edge is not...  7.94 us
    all_to_all x1, waiting for transfers between devices, on_device(): lax.all_to_all(spectrum, both, split_axis=0, concat_axis=0, tiled=True)  6.66 us
    all_to_all x1, starting transfers between devices, on_device(): lax.all_to_all(spectrum, both, split_axis=0, concat_axis=0, tiled=True)  5.57 us
    ppermute x6, waiting for transfers between devices, turn(): lax.ppermute(block, axis, [(i, target(i, k, count)) for i in range(count)])  5.22 us
    ppermute x1, starting transfers between devices, on_device(): edges = [None, lax.ppermute(edge_out, 'lat', [(0, 1), (1, 0)])]  3.03 us
    pallas_call x2, Pallas kernels, mlp_rows(): pl.pallas_call(functools.partial(mlp_kernel, len(blocks), last, len(after...  3 us
    unnamed x24, local copies, waits for them, and re-layouts  1.46 us
  transfers between devices with their start and end apart: 8, of which 5 were waited for; matrix products, arithmetic and copies ran while one was open for 1% of the time, Pallas kernels for 22%

profile of v18, /device:TPU:0, one launch (start us, length us, event | category | flops | bytes accessed | tf_op | source)
XLA Modules:
  0.0 44.9 jit_solution(2221748473848769455)
XLA Ops:
  0.0 1.1 %copy-done.7 = bf16[4,1440,64]{1,2,0:T(8,128)(2,1)S(1)} copy-done((bf16[4,1440,64]{1,2,0:T(8,128)(2,1)S(1)}, bf16[4,1440,64]{1,2,0:T(8,128)(2,1)}, u32[]{:S(2)}) %copy-start.7) | copy-done | bytes 737304
  1.2 0.1 edge_rows.1
  1.2 3.0 %collective-permute-start = (bf16[2,64,1440]{2,1,0:T(8,128)(2,1)S(1)}, bf16[2,64,1440]{2,1,0:T(8,128)(2,1)S(1)}, u32[]{:S(2)}, u32[]{:S(2)}) collective-permute-start(bf16[2,64,1440]{2,1,0:T(8,128)(2,1)S(1)} %get-tuple-element.14), channel_id=1, source_target_pairs={{0,16},{16,0},{1,17},{17,1},{2,18},{18,2},{3,19},{19,3},{4,20},{20... | collective-permute-start | bytes 1105928 | tf_op jit(solution)/shard_map/ppermute | solution.py:349
  4.3 1.5 %conv_rows.6.rest_1_ = bf16[128,384]{1,0:T(8,128)(2,1)S(1)} custom-call(s32[4,9]{1,0:T(4,128)S(1)} %copy-done.2, s32[4,9]{1,0:T(4,128)S(1)} %copy-done.3, s32[4,9]{1,0:T(4,128)S(1)} %copy-done.4, f32[4,9]{1,0:T(4,128)S(1)} %copy-done.5, bf16[4,64,1440]{2,1,0:T(8,128)(2,1)S(1)} %get-tuple-element.13.fields_ref, bf16[6,64,64]{2,1,0:T(8,128)(2,1)S(1)} %copy-done), custom_call_target="tpu_custom_call" | custom-call | flops 200000000 | tf_op jit(solution)/shard_map/conv_rows/pallas_call | solution.py:165
  5.8 2.7 %collective-permute-start.4 = (bf16[128,384]{1,0:T(8,128)(2,1)S(1)}, bf16[128,384]{1,0:T(8,128)(2,1)S(1)}, u32[]{:S(2)}, u32[]{:S(2)}) collective-permute-start(bf16[128,384]{1,0:T(8,128)(2,1)S(1)} %conv_rows.6.rest_1_), channel_id=1, source_target_pairs={{0,8},{4,12},{8,0},{12,4},{1,9},{5,13},{9,1},{13,5},{2,10},{6,14},... | collective-permute-start | bytes 294920 | tf_op jit(solution)/shard_map/ppermute | solution.py:323
  8.5 2.5 %conv_rows.7 = (bf16[128,384]{1,0:T(8,128)(2,1)S(1)}, bf16[128,384]{1,0:T(8,128)(2,1)S(1)}, bf16[128,384]{1,0:T(8,128)(2,1)S(1)}) custom-call(s32[4,9]{1,0:T(4,128)S(1)} %copy-done.2, s32[4,9]{1,0:T(4,128)S(1)} %copy-done.3, s32[4,9]{1,0:T(4,128)S(1)} %copy-done.4, f32[4,9]{1,0:T(4,128)S(1)} %copy-done.5, ...), custom_call_target="tpu_custom_call" | custom-call | flops 1000000000 | tf_op jit(solution)/shard_map/conv_rows/pallas_call | solution.py:165
  10.9 1.4 %collective-permute-start.5 = (bf16[128,384]{1,0:T(8,128)(2,1)S(1)}, bf16[128,384]{1,0:T(8,128)(2,1)S(1)}, u32[]{:S(2)}, u32[]{:S(2)}) collective-permute-start(bf16[128,384]{1,0:T(8,128)(2,1)S(1)} %get-tuple-element.19), channel_id=1, source_target_pairs={{0,12},{4,8},{8,4},{12,0},{1,13},{5,9},{9,5},{13,1},{2,14},{6,10},... | collective-permute-start | bytes 294920 | tf_op jit(solution)/shard_map/ppermute | solution.py:323
  12.4 0.3 collective-permute-start.6
  12.6 0.7 %collective-permute-done.rest_0_ = bf16[2,64,1440]{2,1,0:T(8,128)(2,1)S(1)} collective-permute-done((bf16[2,64,1440]{2,1,0:T(8,128)(2,1)S(1)}, bf16[2,64,1440]{2,1,0:T(8,128)(2,1)S(1)}, u32[]{:S(2)}, u32[]{:S(2)}) %collective-permute-start) | collective-permute-done | bytes 368672 | tf_op jit(solution)/shard_map/ppermute | solution.py:349
  13.4 1.5 %conv_rows.4.rest_2_ = bf16[128,384]{1,0:T(8,128)(2,1)S(1)} custom-call(s32[4,9]{1,0:T(4,128)S(1)} %copy-done.2, s32[4,9]{1,0:T(4,128)S(1)} %copy-done.3, s32[4,9]{1,0:T(4,128)S(1)} %copy-done.4, f32[4,9]{1,0:T(4,128)S(1)} %copy-done.5, bf16[4,64,1440]{2,1,0:T(8,128)(2,1)S(1)} %get-tuple-element.13.fields_ref, ...), custom_call_target="tpu_custom_call" | custom-call | flops 200000000 | tf_op jit(solution)/shard_map/conv_rows/pallas_call | solution.py:165
  14.9 0.0 copy-start.9
  14.9 0.0 copy-start.10
  14.9 0.0 copy-start.8
  15.0 2.5 %conv_rows.5 = (bf16[128,384]{1,0:T(8,128)(2,1)S(1)}, bf16[128,384]{1,0:T(8,128)(2,1)S(1)}, bf16[128,384]{1,0:T(8,128)(2,1)S(1)}) custom-call(s32[4,9]{1,0:T(4,128)S(1)} %copy-done.2, s32[4,9]{1,0:T(4,128)S(1)} %copy-done.3, s32[4,9]{1,0:T(4,128)S(1)} %copy-done.4, f32[4,9]{1,0:T(4,128)S(1)} %copy-done.5, ...), custom_call_target="tpu_custom_call" | custom-call | flops 1000000000 | tf_op jit(solution)/shard_map/conv_rows/pallas_call | solution.py:165
  17.4 3.9 %collective-permute-start.2 = (bf16[128,384]{1,0:T(8,128)(2,1)S(1)}, bf16[128,384]{1,0:T(8,128)(2,1)S(1)}, u32[]{:S(2)}, u32[]{:S(2)}) collective-permute-start(bf16[128,384]{1,0:T(8,128)(2,1)S(1)} %get-tuple-element.16), channel_id=1, source_target_pairs={{0,12},{4,8},{8,4},{12,0},{1,13},{5,9},{9,5},{13,1},{2,14},{6,10},... | collective-permute-start | bytes 294920 | tf_op jit(solution)/shard_map/ppermute | solution.py:323
  21.3 0.0 collective-permute-start.3
  21.3 0.0 collective-permute-done.5.rest_2_
  21.3 0.6 %collective-permute-start.1 = (bf16[128,384]{1,0:T(8,128)(2,1)S(1)}, bf16[128,384]{1,0:T(8,128)(2,1)S(1)}, u32[]{:S(2)}, u32[]{:S(2)}) collective-permute-start(bf16[128,384]{1,0:T(8,128)(2,1)S(1)} %conv_rows.4.rest_2_), channel_id=1, source_target_pairs={{0,8},{4,12},{8,0},{12,4},{1,9},{5,13},{9,1},{13,5},{2,10},{6,14},... | collective-permute-start | bytes 294920 | tf_op jit(solution)/shard_map/ppermute | solution.py:323
  22.0 0.1 copy.12
  22.1 0.1 copy.13
  22.3 0.0 collective-permute-done.4.rest_1_
  22.3 1.2 %mlp_rows.2.rest_7_ = bf16[8,16,256]{2,1,0:T(8,128)(2,1)S(1)} custom-call(bf16[128,384]{1,0:T(8,128)(2,1)S(1)} %get-tuple-element.18.rest_0_, bf16[128,384]{1,0:T(8,128)(2,1)S(1)} %collective-permute-done.4.rest_1_, bf16[128,384]{1,0:T(8,128)(2,1)S(1)} %collective-permute-done.5.rest_2_, bf16[128,384]{1,0:T(8,128)(2,1)S(1)} %collective-permute-done.6.rest_3_, ...), custom_call_target="tpu_custom_call" | custom-call | flops 1000000000 | tf_op jit(solution)/shard_map/mlp_rows/pallas_call | solution.py:231
  23.5 0.0 copy-start.1
  23.5 0.0 copy-start.6
  23.5 1.1 %collective-permute-done.2.rest_2_ = bf16[128,384]{1,0:T(8,128)(2,1)S(1)} collective-permute-done((bf16[128,384]{1,0:T(8,128)(2,1)S(1)}, bf16[128,384]{1,0:T(8,128)(2,1)S(1)}, u32[]{:S(2)}, u32[]{:S(2)}) %collective-permute-start.2) | collective-permute-done | bytes 98336 | tf_op jit(solution)/shard_map/ppermute | solution.py:323
  24.6 2.9 %collective-permute-done.3.rest_3_ = bf16[128,384]{1,0:T(8,128)(2,1)S(1)} collective-permute-done((bf16[128,384]{1,0:T(8,128)(2,1)S(1)}, bf16[128,384]{1,0:T(8,128)(2,1)S(1)}, u32[]{:S(2)}, u32[]{:S(2)}) %collective-permute-start.3) | collective-permute-done | bytes 98336 | tf_op jit(solution)/shard_map/ppermute | solution.py:323
  27.6 1.2 %collective-permute-done.1.rest_1_ = bf16[128,384]{1,0:T(8,128)(2,1)S(1)} collective-permute-done((bf16[128,384]{1,0:T(8,128)(2,1)S(1)}, bf16[128,384]{1,0:T(8,128)(2,1)S(1)}, u32[]{:S(2)}, u32[]{:S(2)}) %collective-permute-start.1) | collective-permute-done | bytes 98336 | tf_op jit(solution)/shard_map/ppermute | solution.py:323
  28.7 1.8 %mlp_rows.3 = bf16[8,32,256]{2,1,0:T(8,128)(2,1)} custom-call(bf16[128,384]{1,0:T(8,128)(2,1)S(1)} %get-tuple-element.15.rest_7_.rest_0_, bf16[128,384]{1,0:T(8,128)(2,1)S(1)} %collective-permute-done.1.rest_1_, bf16[128,384]{1,0:T(8,128)(2,1)S(1)} %collective-permute-done.2.rest_2_, bf16[128,384]{1,0:T(8,128)(2,1)S(1)} %collective-permute-done.3.rest_3_, ...), custom_call_target="tpu_custom_call" | custom-call | flops 1000000000 | tf_op jit(solution)/shard_map/mlp_rows/pallas_call | solution.py:231
  30.5 5.6 %all-to-all-start = ((bf16[8,32,256]{2,1,0:T(8,128)(2,1)}), bf16[8,32,256]{2,1,0:T(8,128)(2,1)S(1)}, u32[]{:S(2)}, u32[]{:S(2)}) async-start(bf16[8,32,256]{2,1,0:T(8,128)(2,1)} %mlp_rows.3), calls=%async_computation | async-start | bytes 262144 | tf_op jit(solution)/shard_map/all_to_all | solution.py:391
  36.1 0.8 %expand.1.left_ref = bf16[3,2,384,256]{3,2,1,0:T(8,128)(2,1)S(1)} custom-call(bf16[3,8,384]{2,1,0:T(8,128)(2,1)S(1)} %bitcast.10, bf16[8,256]{1,0:T(8,128)(2,1)S(1)} %copy-done.6), custom_call_target="tpu_custom_call" | custom-call | flops 200000000 | tf_op jit(solution)/shard_map/expand/pallas_call | solution.py:265
  37.0 6.7 %all-to-all-done = bf16[8,32,256]{2,1,0:T(8,128)(2,1)S(1)} async-done(((bf16[8,32,256]{2,1,0:T(8,128)(2,1)}), bf16[8,32,256]{2,1,0:T(8,128)(2,1)S(1)}, u32[]{:S(2)}, u32[]{:S(2)}) %all-to-all-start) | async-done | bytes 131104 | tf_op jit(solution)/shard_map/all_to_all | solution.py:391
  43.6 1.3 %final_sum.1 = bf16[3,384,512]{2,1,0:T(8,128)(2,1)} custom-call(bf16[3,2,384,256]{3,2,1,0:T(8,128)(2,1)S(1)} %expand.1.left_ref, bf16[256,256]{1,0:T(8,128)(2,1)S(1)} %bitcast.9), custom_call_target="tpu_custom_call" | custom-call | flops 1000000000 | tf_op jit(solution)/shard_map/final_sum/pallas_call | solution.py:298
  (17 shorter events, 0.0 us)
Async XLA Ops:
  0.0 1.1 %copy-start.7 = (bf16[4,1440,64]{1,2,0:T(8,128)(2,1)S(1)}, bf16[4,1440,64]{1,2,0:T(8,128)(2,1)}, u32[]{:S(2)}) copy-start(bf16[4,1440,64]{1,2,0:T(8,128)(2,1)} %param.11) | copy-start | bytes 2211844
  1.1 3.1 %copy-start = (bf16[6,64,64]{2,1,0:T(8,128)(2,1)S(1)}, bf16[6,64,64]{2,1,0:T(8,128)(2,1)}, u32[]{:S(2)}) copy-start(bf16[6,64,64]{2,1,0:T(8,128)(2,1)} %rest_0_.3) | copy-start | bytes 147460
  1.1 3.1 %copy-start.2 = (s32[4,9]{1,0:T(4,128)S(1)}, s32[4,9]{1,0:T(4,128)}, u32[]{:S(2)}) copy-start(s32[4,9]{1,0:T(4,128)} %lat_ref.7) | copy-start | bytes 436
  1.1 3.1 %copy-start.3 = (s32[4,9]{1,0:T(4,128)S(1)}, s32[4,9]{1,0:T(4,128)}, u32[]{:S(2)}) copy-start(s32[4,9]{1,0:T(4,128)} %lon_ref.7) | copy-start | bytes 436
  1.1 3.1 %copy-start.4 = (s32[4,9]{1,0:T(4,128)S(1)}, s32[4,9]{1,0:T(4,128)}, u32[]{:S(2)}) copy-start(s32[4,9]{1,0:T(4,128)} %basis_ref.7) | copy-start | bytes 436
  1.1 3.1 %copy-start.5 = (f32[4,9]{1,0:T(4,128)S(1)}, f32[4,9]{1,0:T(4,128)}, u32[]{:S(2)}) copy-start(f32[4,9]{1,0:T(4,128)} %value_ref.7) | copy-start | bytes 436
  1.2 12.1 %collective-permute-start = (bf16[2,64,1440]{2,1,0:T(8,128)(2,1)S(1)}, bf16[2,64,1440]{2,1,0:T(8,128)(2,1)S(1)}, u32[]{:S(2)}, u32[]{:S(2)}) collective-permute-start(bf16[2,64,1440]{2,1,0:T(8,128)(2,1)S(1)} %get-tuple-element.14), channel_id=1, source_target_pairs={{0,16},{16,0},{1,17},{17,1},{2,18},{18,2},{3,19},{19,3},{4,20},{20... | collective-permute-start | bytes 1105928 | tf_op jit(solution)/shard_map/ppermute | solution.py:349
  5.8 16.5 %collective-permute-start.4 = (bf16[128,384]{1,0:T(8,128)(2,1)S(1)}, bf16[128,384]{1,0:T(8,128)(2,1)S(1)}, u32[]{:S(2)}, u32[]{:S(2)}) collective-permute-start(bf16[128,384]{1,0:T(8,128)(2,1)S(1)} %conv_rows.6.rest_1_), channel_id=1, source_target_pairs={{0,8},{4,12},{8,0},{12,4},{1,9},{5,13},{9,1},{13,5},{2,10},{6,14},... | collective-permute-start | bytes 294920 | tf_op jit(solution)/shard_map/ppermute | solution.py:323
  10.9 10.4 %collective-permute-start.5 = (bf16[128,384]{1,0:T(8,128)(2,1)S(1)}, bf16[128,384]{1,0:T(8,128)(2,1)S(1)}, u32[]{:S(2)}, u32[]{:S(2)}) collective-permute-start(bf16[128,384]{1,0:T(8,128)(2,1)S(1)} %get-tuple-element.19), channel_id=1, source_target_pairs={{0,12},{4,8},{8,4},{12,0},{1,13},{5,9},{9,5},{13,1},{2,14},{6,10},... | collective-permute-start | bytes 294920 | tf_op jit(solution)/shard_map/ppermute | solution.py:323
  12.4 9.9 %collective-permute-start.6 = (bf16[128,384]{1,0:T(8,128)(2,1)S(1)}, bf16[128,384]{1,0:T(8,128)(2,1)S(1)}, u32[]{:S(2)}, u32[]{:S(2)}) collective-permute-start(bf16[128,384]{1,0:T(8,128)(2,1)S(1)} %get-tuple-element.20), channel_id=1, source_target_pairs={{0,4},{4,0},{8,12},{12,8},{1,5},{5,1},{9,13},{13,9},{2,6},{6,2},{1... | collective-permute-start | bytes 294920 | tf_op jit(solution)/shard_map/ppermute | solution.py:323
  14.9 7.0 %copy-start.9 = (bf16[256,512]{1,0:T(8,128)(2,1)S(1)}, bf16[256,512]{1,0:T(8,128)(2,1)}, u32[]{:S(2)}) copy-start(bf16[256,512]{1,0:T(8,128)(2,1)} %param.17) | copy-start | bytes 786436
  14.9 7.2 %copy-start.10 = (bf16[512,256]{1,0:T(8,128)(2,1)S(1)}, bf16[512,256]{1,0:T(8,128)(2,1)}, u32[]{:S(2)}) copy-start(bf16[512,256]{1,0:T(8,128)(2,1)} %param.18) | copy-start | bytes 786436
  14.9 7.3 %copy-start.8 = (bf16[4,64,384]{2,1,0:T(8,128)(2,1)S(1)}, bf16[4,64,384]{2,1,0:T(8,128)(2,1)}, u32[]{:S(2)}) copy-start(bf16[4,64,384]{2,1,0:T(8,128)(2,1)} %constant.4.clone.rest_6_) | copy-start | bytes 589828
  17.4 7.2 %collective-permute-start.2 = (bf16[128,384]{1,0:T(8,128)(2,1)S(1)}, bf16[128,384]{1,0:T(8,128)(2,1)S(1)}, u32[]{:S(2)}, u32[]{:S(2)}) collective-permute-start(bf16[128,384]{1,0:T(8,128)(2,1)S(1)} %get-tuple-element.16), channel_id=1, source_target_pairs={{0,12},{4,8},{8,4},{12,0},{1,13},{5,9},{9,5},{13,1},{2,14},{6,10},... | collective-permute-start | bytes 294920 | tf_op jit(solution)/shard_map/ppermute | solution.py:323
  21.3 6.2 %collective-permute-start.3 = (bf16[128,384]{1,0:T(8,128)(2,1)S(1)}, bf16[128,384]{1,0:T(8,128)(2,1)S(1)}, u32[]{:S(2)}, u32[]{:S(2)}) collective-permute-start(bf16[128,384]{1,0:T(8,128)(2,1)S(1)} %get-tuple-element.17), channel_id=1, source_target_pairs={{0,4},{4,0},{8,12},{12,8},{1,5},{5,1},{9,13},{13,9},{2,6},{6,2},{1... | collective-permute-start | bytes 294920 | tf_op jit(solution)/shard_map/ppermute | solution.py:323
  21.3 7.4 %collective-permute-start.1 = (bf16[128,384]{1,0:T(8,128)(2,1)S(1)}, bf16[128,384]{1,0:T(8,128)(2,1)S(1)}, u32[]{:S(2)}, u32[]{:S(2)}) collective-permute-start(bf16[128,384]{1,0:T(8,128)(2,1)S(1)} %conv_rows.4.rest_2_), channel_id=1, source_target_pairs={{0,8},{4,12},{8,0},{12,4},{1,9},{5,13},{9,1},{13,5},{2,10},{6,14},... | collective-permute-start | bytes 294920 | tf_op jit(solution)/shard_map/ppermute | solution.py:323
  23.5 12.6 %copy-start.1 = (bf16[3,384,8]{1,2,0:T(8,128)(2,1)S(1)}, bf16[3,384,8]{1,2,0:T(8,128)(2,1)}, u32[]{:S(2)}) copy-start(bf16[3,384,8]{1,2,0:T(8,128)(2,1)} %param.19) | copy-start | bytes 55300
  23.5 12.6 %copy-start.6 = (bf16[8,256]{1,0:T(8,128)(2,1)S(1)}, bf16[8,256]{1,0:T(8,128)(2,1)}, u32[]{:S(2)}) copy-start(bf16[8,256]{1,0:T(8,128)(2,1)} %constant.5.clone.spread_ref) | copy-start | bytes 12292
  30.5 13.1 %all-to-all-start = ((bf16[8,32,256]{2,1,0:T(8,128)(2,1)}), bf16[8,32,256]{2,1,0:T(8,128)(2,1)S(1)}, u32[]{:S(2)}, u32[]{:S(2)}) async-start(bf16[8,32,256]{2,1,0:T(8,128)(2,1)} %mlp_rows.3), calls=%async_computation | async-start | bytes 262144 | tf_op jit(solution)/shard_map/all_to_all | solution.py:391

commit v19 on v18

--- a/solution.py
+++ b/solution.py
@@ -376,12 +376,16 @@
     ]
     received = []
     for half in halves:
-        first = conv_rows(*half, order[:1], [], False)
-        rest = conv_rows(*half, [*order[1:], 0], first, False)
-        sent = [*first, *rest[:-1]]
+        if received:
+            sent = conv_rows(*half, order, [], False)
+            kept = conv_rows(*half, [0], sent[1:2], False)
+        else:
+            first = conv_rows(*half, order[:1], [], False)
+            *rest, own = conv_rows(*half, [*order[1:], 0], first, False)
+            sent, kept = [*first, *rest], [own]
         moved = [turn(block, "chan", num_chan, k) for k, block in zip(order, sent)]
-        received.append([rest[-1], *moved])
-    after = [rest[-1]]
+        received.append([*kept, *moved])
+    after = [*kept]
     spectrum = None
     for blocks in received:
         spectrum = mlp_rows(blocks, up, down, tables, spectrum, dests, after)

time: 45.2 us -> 43.5 us (0.962)
  starting transfers between devices: 17.5 us -> 16.2 us
    all_to_all x1, starting transfers between devices: 5.57 us -> 4.21 us  [on_device(): lax.all_to_all(spectrum, both, split_axis=0, concat_axis=0, tiled=True)]
  transfers between devices with their start and end apart: 8 -> 8, of which waited for: 5 -> 4; matrix products, arithmetic and copies ran while one was open for 1% -> 1% of each run, Pallas kernels for 22% -> 23%
where the time goes in v19:
time: 43.5 us; the launch traced here: 43.2 us
  starting transfers between devices  16.2 us (37%)
  Pallas kernels  13.2 us (30%)
  waiting for transfers between devices  12.2 us (28%)
  local copies, waits for them, and re-layouts  1.46 us (3%)
    ppermute x6, starting transfers between devices, turn(): lax.ppermute(block, axis, [(i, target(i, k, count)) for i in range(count)])  8.98 us
    pallas_call x4, Pallas kernels, conv_rows(): pl.pallas_call(functools.partial(conv_kernel, chunks, picks, edge is not...  7.94 us
    all_to_all x1, waiting for transfers between devices, on_device(): lax.all_to_all(spectrum, both, split_axis=0, concat_axis=0, tiled=True)  6.66 us
    ppermute x6, waiting for transfers between devices, turn(): lax.ppermute(block, axis, [(i, target(i, k, count)) for i in range(count)])  5.25 us
    all_to_all x1, starting transfers between devices, on_device(): lax.all_to_all(spectrum, both, split_axis=0, concat_axis=0, tiled=True)  4.21 us
    ppermute x1, starting transfers between devices, on_device(): edges = [None, lax.ppermute(edge_out, 'lat', [(0, 1), (1, 0)])]  3.03 us
    pallas_call x2, Pallas kernels, mlp_rows(): pl.pallas_call(functools.partial(mlp_kernel, len(blocks), last, len(after...  3 us
    unnamed x24, local copies, waits for them, and re-layouts  1.46 us
  transfers between devices with their start and end apart: 8, of which 4 were waited for; matrix products, arithmetic and copies ran while one was open for 1% of the time, Pallas kernels for 23%

profile of v19, /device:TPU:0, one launch (start us, length us, event | category | flops | bytes accessed | tf_op | source)
XLA Modules:
  0.0 43.2 jit_solution(4270798853739706182)
XLA Ops:
  0.0 1.1 %copy-done.7 = bf16[4,1440,64]{1,2,0:T(8,128)(2,1)S(1)} copy-done((bf16[4,1440,64]{1,2,0:T(8,128)(2,1)S(1)}, bf16[4,1440,64]{1,2,0:T(8,128)(2,1)}, u32[]{:S(2)}) %copy-start.7) | copy-done | bytes 737304
  1.2 0.1 edge_rows.1
  1.2 3.0 %collective-permute-start = (bf16[2,64,1440]{2,1,0:T(8,128)(2,1)S(1)}, bf16[2,64,1440]{2,1,0:T(8,128)(2,1)S(1)}, u32[]{:S(2)}, u32[]{:S(2)}) collective-permute-start(bf16[2,64,1440]{2,1,0:T(8,128)(2,1)S(1)} %get-tuple-element.14), channel_id=1, source_target_pairs={{0,16},{16,0},{1,17},{17,1},{2,18},{18,2},{3,19},{19,3},{4,20},{20... | collective-permute-start | bytes 1105928 | tf_op jit(solution)/shard_map/ppermute | solution.py:349
  4.3 1.5 %conv_rows.6.rest_1_ = bf16[128,384]{1,0:T(8,128)(2,1)S(1)} custom-call(s32[4,9]{1,0:T(4,128)S(1)} %copy-done.2, s32[4,9]{1,0:T(4,128)S(1)} %copy-done.3, s32[4,9]{1,0:T(4,128)S(1)} %copy-done.4, f32[4,9]{1,0:T(4,128)S(1)} %copy-done.5, bf16[4,64,1440]{2,1,0:T(8,128)(2,1)S(1)} %get-tuple-element.13.fields_ref, bf16[6,64,64]{2,1,0:T(8,128)(2,1)S(1)} %copy-done), custom_call_target="tpu_custom_call" | custom-call | flops 200000000 | tf_op jit(solution)/shard_map/conv_rows/pallas_call | solution.py:165
  5.8 0.0 copy-start.9
  5.8 0.0 copy-start.10
  5.8 2.5 %conv_rows.7 = (bf16[128,384]{1,0:T(8,128)(2,1)S(1)}, bf16[128,384]{1,0:T(8,128)(2,1)S(1)}, bf16[128,384]{1,0:T(8,128)(2,1)S(1)}) custom-call(s32[4,9]{1,0:T(4,128)S(1)} %copy-done.2, s32[4,9]{1,0:T(4,128)S(1)} %copy-done.3, s32[4,9]{1,0:T(4,128)S(1)} %copy-done.4, f32[4,9]{1,0:T(4,128)S(1)} %copy-done.5, ...), custom_call_target="tpu_custom_call" | custom-call | flops 1000000000 | tf_op jit(solution)/shard_map/conv_rows/pallas_call | solution.py:165
  8.3 3.7 %collective-permute-start.5 = (bf16[128,384]{1,0:T(8,128)(2,1)S(1)}, bf16[128,384]{1,0:T(8,128)(2,1)S(1)}, u32[]{:S(2)}, u32[]{:S(2)}) collective-permute-start(bf16[128,384]{1,0:T(8,128)(2,1)S(1)} %get-tuple-element.19), channel_id=1, source_target_pairs={{0,12},{4,8},{8,4},{12,0},{1,13},{5,9},{9,5},{13,1},{2,14},{6,10},... | collective-permute-start | bytes 294920 | tf_op jit(solution)/shard_map/ppermute | solution.py:323
  12.0 0.0 collective-permute-start.4
  12.0 0.8 %collective-permute-start.6 = (bf16[128,384]{1,0:T(8,128)(2,1)S(1)}, bf16[128,384]{1,0:T(8,128)(2,1)S(1)}, u32[]{:S(2)}, u32[]{:S(2)}) collective-permute-start(bf16[128,384]{1,0:T(8,128)(2,1)S(1)} %get-tuple-element.20), channel_id=1, source_target_pairs={{0,4},{4,0},{8,12},{12,8},{1,5},{5,1},{9,13},{13,9},{2,6},{6,2},{1... | collective-permute-start | bytes 294920 | tf_op jit(solution)/shard_map/ppermute | solution.py:323
  12.8 0.1 copy.12
  12.9 0.1 copy.13
  13.1 0.3 collective-permute-done.rest_0_
  13.4 2.5 %conv_rows.4 = (bf16[128,384]{1,0:T(8,128)(2,1)S(1)}, bf16[128,384]{1,0:T(8,128)(2,1)S(1)}, bf16[128,384]{1,0:T(8,128)(2,1)S(1)}) custom-call(s32[4,9]{1,0:T(4,128)S(1)} %copy-done.2, s32[4,9]{1,0:T(4,128)S(1)} %copy-done.3, s32[4,9]{1,0:T(4,128)S(1)} %copy-done.4, f32[4,9]{1,0:T(4,128)S(1)} %copy-done.5, ...), custom_call_target="tpu_custom_call" | custom-call | flops 1000000000 | tf_op jit(solution)/shard_map/conv_rows/pallas_call | solution.py:165
  15.8 0.0 copy-start.8
  15.9 3.9 %collective-permute-start.2 = (bf16[128,384]{1,0:T(8,128)(2,1)S(1)}, bf16[128,384]{1,0:T(8,128)(2,1)S(1)}, u32[]{:S(2)}, u32[]{:S(2)}) collective-permute-start(bf16[128,384]{1,0:T(8,128)(2,1)S(1)} %get-tuple-element.15.rest_2_), channel_id=1, source_target_pairs={{0,12},{4,8},{8,4},{12,0},{1,13},{5,9},{9,5},{13,1},{2,14},{6,10},... | collective-permute-start | bytes 294920 | tf_op jit(solution)/shard_map/ppermute | solution.py:323
  19.7 0.0 collective-permute-start.1
  19.7 0.0 collective-permute-done.5.rest_2_
  19.7 0.6 %collective-permute-start.3 = (bf16[128,384]{1,0:T(8,128)(2,1)S(1)}, bf16[128,384]{1,0:T(8,128)(2,1)S(1)}, u32[]{:S(2)}, u32[]{:S(2)}) collective-permute-start(bf16[128,384]{1,0:T(8,128)(2,1)S(1)} %get-tuple-element.17), channel_id=1, source_target_pairs={{0,4},{4,0},{8,12},{12,8},{1,5},{5,1},{9,13},{13,9},{2,6},{6,2},{1... | collective-permute-start | bytes 294920 | tf_op jit(solution)/shard_map/ppermute | solution.py:323
  20.4 1.5 %conv_rows.5.rest_7_.rest_0_ = bf16[128,384]{1,0:T(8,128)(2,1)S(1)} custom-call(s32[4,9]{1,0:T(4,128)S(1)} %copy-done.2, s32[4,9]{1,0:T(4,128)S(1)} %copy-done.3, s32[4,9]{1,0:T(4,128)S(1)} %copy-done.4, f32[4,9]{1,0:T(4,128)S(1)} %copy-done.5, bf16[4,64,1440]{2,1,0:T(8,128)(2,1)S(1)} %get-tuple-element.13.fields_ref, ...), custom_call_target="tpu_custom_call" | custom-call | flops 200000000 | tf_op jit(solution)/shard_map/conv_rows/pallas_call | solution.py:165
  21.9 0.0 collective-permute-done.6.rest_3_
  21.9 3.0 %collective-permute-done.4.rest_1_ = bf16[128,384]{1,0:T(8,128)(2,1)S(1)} collective-permute-done((bf16[128,384]{1,0:T(8,128)(2,1)S(1)}, bf16[128,384]{1,0:T(8,128)(2,1)S(1)}, u32[]{:S(2)}, u32[]{:S(2)}) %collective-permute-start.4) | collective-permute-done | bytes 98336 | tf_op jit(solution)/shard_map/ppermute | solution.py:323
  24.9 1.2 %mlp_rows.2.rest_7_ = bf16[8,16,256]{2,1,0:T(8,128)(2,1)S(1)} custom-call(bf16[128,384]{1,0:T(8,128)(2,1)S(1)} %get-tuple-element.18.rest_0_, bf16[128,384]{1,0:T(8,128)(2,1)S(1)} %collective-permute-done.4.rest_1_, bf16[128,384]{1,0:T(8,128)(2,1)S(1)} %collective-permute-done.5.rest_2_, bf16[128,384]{1,0:T(8,128)(2,1)S(1)} %collective-permute-done.6.rest_3_, ...), custom_call_target="tpu_custom_call" | custom-call | flops 1000000000 | tf_op jit(solution)/shard_map/mlp_rows/pallas_call | solution.py:231
  26.1 0.0 copy-start.1
  26.1 0.0 copy-start.6
  26.1 2.3 %collective-permute-done.1.rest_1_ = bf16[128,384]{1,0:T(8,128)(2,1)S(1)} collective-permute-done((bf16[128,384]{1,0:T(8,128)(2,1)S(1)}, bf16[128,384]{1,0:T(8,128)(2,1)S(1)}, u32[]{:S(2)}, u32[]{:S(2)}) %collective-permute-start.1) | collective-permute-done | bytes 98336 | tf_op jit(solution)/shard_map/ppermute | solution.py:323
  28.4 0.0 collective-permute-done.3.rest_3_
  28.4 1.8 %mlp_rows.3 = bf16[8,32,256]{2,1,0:T(8,128)(2,1)} custom-call(bf16[128,384]{1,0:T(8,128)(2,1)S(1)} %conv_rows.5.rest_7_.rest_0_, bf16[128,384]{1,0:T(8,128)(2,1)S(1)} %collective-permute-done.1.rest_1_, bf16[128,384]{1,0:T(8,128)(2,1)S(1)} %collective-permute-done.2.rest_2_, bf16[128,384]{1,0:T(8,128)(2,1)S(1)} %collective-permute-done.3.rest_3_, ...), custom_call_target="tpu_custom_call" | custom-call | flops 1000000000 | tf_op jit(solution)/shard_map/mlp_rows/pallas_call | solution.py:231
  30.2 4.2 %all-to-all-start = ((bf16[8,32,256]{2,1,0:T(8,128)(2,1)}), bf16[8,32,256]{2,1,0:T(8,128)(2,1)S(1)}, u32[]{:S(2)}, u32[]{:S(2)}) async-start(bf16[8,32,256]{2,1,0:T(8,128)(2,1)} %mlp_rows.3), calls=%async_computation | async-start | bytes 262144 | tf_op jit(solution)/shard_map/all_to_all | solution.py:395
  34.4 0.8 %expand.1.left_ref = bf16[3,2,384,256]{3,2,1,0:T(8,128)(2,1)S(1)} custom-call(bf16[3,8,384]{2,1,0:T(8,128)(2,1)S(1)} %bitcast.10, bf16[8,256]{1,0:T(8,128)(2,1)S(1)} %copy-done.6), custom_call_target="tpu_custom_call" | custom-call | flops 200000000 | tf_op jit(solution)/shard_map/expand/pallas_call | solution.py:265
  35.3 6.7 %all-to-all-done = bf16[8,32,256]{2,1,0:T(8,128)(2,1)S(1)} async-done(((bf16[8,32,256]{2,1,0:T(8,128)(2,1)}), bf16[8,32,256]{2,1,0:T(8,128)(2,1)S(1)}, u32[]{:S(2)}, u32[]{:S(2)}) %all-to-all-start) | async-done | bytes 131104 | tf_op jit(solution)/shard_map/all_to_all | solution.py:395
  42.0 1.3 %final_sum.1 = bf16[3,384,512]{2,1,0:T(8,128)(2,1)} custom-call(bf16[3,2,384,256]{3,2,1,0:T(8,128)(2,1)S(1)} %expand.1.left_ref, bf16[256,256]{1,0:T(8,128)(2,1)S(1)} %bitcast.9), custom_call_target="tpu_custom_call" | custom-call | flops 1000000000 | tf_op jit(solution)/shard_map/final_sum/pallas_call | solution.py:298
  (17 shorter events, 0.0 us)
Async XLA Ops:
  0.0 1.1 %copy-start.7 = (bf16[4,1440,64]{1,2,0:T(8,128)(2,1)S(1)}, bf16[4,1440,64]{1,2,0:T(8,128)(2,1)}, u32[]{:S(2)}) copy-start(bf16[4,1440,64]{1,2,0:T(8,128)(2,1)} %param.11) | copy-start | bytes 2211844
  1.1 3.1 %copy-start = (bf16[6,64,64]{2,1,0:T(8,128)(2,1)S(1)}, bf16[6,64,64]{2,1,0:T(8,128)(2,1)}, u32[]{:S(2)}) copy-start(bf16[6,64,64]{2,1,0:T(8,128)(2,1)} %rest_0_.3) | copy-start | bytes 147460
  1.1 3.1 %copy-start.2 = (s32[4,9]{1,0:T(4,128)S(1)}, s32[4,9]{1,0:T(4,128)}, u32[]{:S(2)}) copy-start(s32[4,9]{1,0:T(4,128)} %lat_ref.7) | copy-start | bytes 436
  1.1 3.1 %copy-start.3 = (s32[4,9]{1,0:T(4,128)S(1)}, s32[4,9]{1,0:T(4,128)}, u32[]{:S(2)}) copy-start(s32[4,9]{1,0:T(4,128)} %lon_ref.7) | copy-start | bytes 436
  1.1 3.1 %copy-start.4 = (s32[4,9]{1,0:T(4,128)S(1)}, s32[4,9]{1,0:T(4,128)}, u32[]{:S(2)}) copy-start(s32[4,9]{1,0:T(4,128)} %basis_ref.7) | copy-start | bytes 436
  1.1 3.1 %copy-start.5 = (f32[4,9]{1,0:T(4,128)S(1)}, f32[4,9]{1,0:T(4,128)}, u32[]{:S(2)}) copy-start(f32[4,9]{1,0:T(4,128)} %value_ref.7) | copy-start | bytes 436
  1.2 12.1 %collective-permute-start = (bf16[2,64,1440]{2,1,0:T(8,128)(2,1)S(1)}, bf16[2,64,1440]{2,1,0:T(8,128)(2,1)S(1)}, u32[]{:S(2)}, u32[]{:S(2)}) collective-permute-start(bf16[2,64,1440]{2,1,0:T(8,128)(2,1)S(1)} %get-tuple-element.14), channel_id=1, source_target_pairs={{0,16},{16,0},{1,17},{17,1},{2,18},{18,2},{3,19},{19,3},{4,20},{20... | collective-permute-start | bytes 1105928 | tf_op jit(solution)/shard_map/ppermute | solution.py:349
  5.8 6.9 %copy-start.9 = (bf16[256,512]{1,0:T(8,128)(2,1)S(1)}, bf16[256,512]{1,0:T(8,128)(2,1)}, u32[]{:S(2)}) copy-start(bf16[256,512]{1,0:T(8,128)(2,1)} %param.17) | copy-start | bytes 786436
  5.8 7.1 %copy-start.10 = (bf16[512,256]{1,0:T(8,128)(2,1)S(1)}, bf16[512,256]{1,0:T(8,128)(2,1)}, u32[]{:S(2)}) copy-start(bf16[512,256]{1,0:T(8,128)(2,1)} %param.18) | copy-start | bytes 786436
  8.3 11.4 %collective-permute-start.5 = (bf16[128,384]{1,0:T(8,128)(2,1)S(1)}, bf16[128,384]{1,0:T(8,128)(2,1)S(1)}, u32[]{:S(2)}, u32[]{:S(2)}) collective-permute-start(bf16[128,384]{1,0:T(8,128)(2,1)S(1)} %get-tuple-element.19), channel_id=1, source_target_pairs={{0,12},{4,8},{8,4},{12,0},{1,13},{5,9},{9,5},{13,1},{2,14},{6,10},... | collective-permute-start | bytes 294920 | tf_op jit(solution)/shard_map/ppermute | solution.py:323
  12.0 12.9 %collective-permute-start.4 = (bf16[128,384]{1,0:T(8,128)(2,1)S(1)}, bf16[128,384]{1,0:T(8,128)(2,1)S(1)}, u32[]{:S(2)}, u32[]{:S(2)}) collective-permute-start(bf16[128,384]{1,0:T(8,128)(2,1)S(1)} %conv_rows.6.rest_1_), channel_id=1, source_target_pairs={{0,8},{4,12},{8,0},{12,4},{1,9},{5,13},{9,1},{13,5},{2,10},{6,14},... | collective-permute-start | bytes 294920 | tf_op jit(solution)/shard_map/ppermute | solution.py:323
  12.0 10.0 %collective-permute-start.6 = (bf16[128,384]{1,0:T(8,128)(2,1)S(1)}, bf16[128,384]{1,0:T(8,128)(2,1)S(1)}, u32[]{:S(2)}, u32[]{:S(2)}) collective-permute-start(bf16[128,384]{1,0:T(8,128)(2,1)S(1)} %get-tuple-element.20), channel_id=1, source_target_pairs={{0,4},{4,0},{8,12},{12,8},{1,5},{5,1},{9,13},{13,9},{2,6},{6,2},{1... | collective-permute-start | bytes 294920 | tf_op jit(solution)/shard_map/ppermute | solution.py:323
  15.8 9.0 %copy-start.8 = (bf16[4,64,384]{2,1,0:T(8,128)(2,1)S(1)}, bf16[4,64,384]{2,1,0:T(8,128)(2,1)}, u32[]{:S(2)}) copy-start(bf16[4,64,384]{2,1,0:T(8,128)(2,1)} %constant.4.clone.rest_6_) | copy-start | bytes 589828
  15.9 10.2 %collective-permute-start.2 = (bf16[128,384]{1,0:T(8,128)(2,1)S(1)}, bf16[128,384]{1,0:T(8,128)(2,1)S(1)}, u32[]{:S(2)}, u32[]{:S(2)}) collective-permute-start(bf16[128,384]{1,0:T(8,128)(2,1)S(1)} %get-tuple-element.15.rest_2_), channel_id=1, source_target_pairs={{0,12},{4,8},{8,4},{12,0},{1,13},{5,9},{9,5},{13,1},{2,14},{6,10},... | collective-permute-start | bytes 294920 | tf_op jit(solution)/shard_map/ppermute | solution.py:323
  19.7 8.6 %collective-permute-start.1 = (bf16[128,384]{1,0:T(8,128)(2,1)S(1)}, bf16[128,384]{1,0:T(8,128)(2,1)S(1)}, u32[]{:S(2)}, u32[]{:S(2)}) collective-permute-start(bf16[128,384]{1,0:T(8,128)(2,1)S(1)} %get-tuple-element.16), channel_id=1, source_target_pairs={{0,8},{4,12},{8,0},{12,4},{1,9},{5,13},{9,1},{13,5},{2,10},{6,14},... | collective-permute-start | bytes 294920 | tf_op jit(solution)/shard_map/ppermute | solution.py:323
  19.7 8.6 %collective-permute-start.3 = (bf16[128,384]{1,0:T(8,128)(2,1)S(1)}, bf16[128,384]{1,0:T(8,128)(2,1)S(1)}, u32[]{:S(2)}, u32[]{:S(2)}) collective-permute-start(bf16[128,384]{1,0:T(8,128)(2,1)S(1)} %get-tuple-element.17), channel_id=1, source_target_pairs={{0,4},{4,0},{8,12},{12,8},{1,5},{5,1},{9,13},{13,9},{2,6},{6,2},{1... | collective-permute-start | bytes 294920 | tf_op jit(solution)/shard_map/ppermute | solution.py:323
  26.1 8.4 %copy-start.1 = (bf16[3,384,8]{1,2,0:T(8,128)(2,1)S(1)}, bf16[3,384,8]{1,2,0:T(8,128)(2,1)}, u32[]{:S(2)}) copy-start(bf16[3,384,8]{1,2,0:T(8,128)(2,1)} %param.19) | copy-start | bytes 55300
  26.1 8.4 %copy-start.6 = (bf16[8,256]{1,0:T(8,128)(2,1)S(1)}, bf16[8,256]{1,0:T(8,128)(2,1)}, u32[]{:S(2)}) copy-start(bf16[8,256]{1,0:T(8,128)(2,1)} %constant.5.clone.spread_ref) | copy-start | bytes 12292
  30.2 11.7 %all-to-all-start = ((bf16[8,32,256]{2,1,0:T(8,128)(2,1)}), bf16[8,32,256]{2,1,0:T(8,128)(2,1)S(1)}, u32[]{:S(2)}, u32[]{:S(2)}) async-start(bf16[8,32,256]{2,1,0:T(8,128)(2,1)} %mlp_rows.3), calls=%async_computation | async-start | bytes 262144 | tf_op jit(solution)/shard_map/all_to_all | solution.py:395

commit v20 on v18

--- a/solution.py
+++ b/solution.py
@@ -375,16 +375,16 @@
         for edge, pair in zip(edges, pairs)
     ]
     received = []
+    after, last = [], []
     for half in halves:
-        first = conv_rows(*half, order[:1], [], False)
-        rest = conv_rows(*half, [*order[1:], 0], first, False)
-        sent = [*first, *rest[:-1]]
+        sent = conv_rows(*half, order, after, False)
         moved = [turn(block, "chan", num_chan, k) for k, block in zip(order, sent)]
-        received.append([rest[-1], *moved])
-    after = [rest[-1]]
+        after = conv_rows(*half, [0], [sent[1], *last], False)
+        received.append([*after, *moved])
+        after, last = list(after), moved[:1]
     spectrum = None
     for blocks in received:
-        spectrum = mlp_rows(blocks, up, down, tables, spectrum, dests, after)
+        spectrum = mlp_rows(blocks, up, down, tables, spectrum, dests, list(after))
         after = []
 
     both = ("lat", "chan")

time: 45.2 us -> 42.9 us (0.949)
  waiting for transfers between devices: 12.6 us -> 11.2 us
  starting transfers between devices: 17.5 us -> 16.6 us
    ppermute x6, waiting for transfers between devices: 5.22 us -> 3.99 us  [turn(): lax.ppermute(block, axis, [(i, target(i, k, count)) for i in range(count)])]
    all_to_all x1, starting transfers between devices: 5.57 us -> 4.85 us  [on_device(): lax.all_to_all(spectrum, both, split_axis=0, concat_axis=0, tiled=True)]
  transfers between devices with their start and end apart: 8 -> 8, of which waited for: 5 -> 3; matrix products, arithmetic and copies ran while one was open for 1% -> 1% of each run, Pallas kernels for 22% -> 23%
where the time goes in v20:
time: 42.9 us; the launch traced here: 42.6 us
  starting transfers between devices  16.6 us (39%)
  Pallas kernels  13.2 us (31%)
  waiting for transfers between devices  11.2 us (26%)
  local copies, waits for them, and re-layouts  1.46 us (3%)
    ppermute x6, starting transfers between devices, turn(): lax.ppermute(block, axis, [(i, target(i, k, count)) for i in range(count)])  8.75 us
    pallas_call x4, Pallas kernels, conv_rows(): pl.pallas_call(functools.partial(conv_kernel, chunks, picks, edge is not...  7.94 us
    all_to_all x1, waiting for transfers between devices, on_device(): lax.all_to_all(spectrum, both, split_axis=0, concat_axis=0, tiled=True)  6.66 us
    all_to_all x1, starting transfers between devices, on_device(): lax.all_to_all(spectrum, both, split_axis=0, concat_axis=0, tiled=True)  4.85 us
    ppermute x6, waiting for transfers between devices, turn(): lax.ppermute(block, axis, [(i, target(i, k, count)) for i in range(count)])  3.99 us
    ppermute x1, starting transfers between devices, on_device(): edges = [None, lax.ppermute(edge_out, 'lat', [(0, 1), (1, 0)])]  3.03 us
    pallas_call x2, Pallas kernels, mlp_rows(): pl.pallas_call(functools.partial(mlp_kernel, len(blocks), last, len(after...  3 us
    unnamed x24, local copies, waits for them, and re-layouts  1.46 us
  transfers between devices with their start and end apart: 8, of which 3 were waited for; matrix products, arithmetic and copies ran while one was open for 1% of the time, Pallas kernels for 23%

profile of v20, /device:TPU:0, one launch (start us, length us, event | category | flops | bytes accessed | tf_op | source)
XLA Modules:
  0.0 42.6 jit_solution(903020982750814143)
XLA Ops:
  0.0 1.1 %copy-done.7 = bf16[4,1440,64]{1,2,0:T(8,128)(2,1)S(1)} copy-done((bf16[4,1440,64]{1,2,0:T(8,128)(2,1)S(1)}, bf16[4,1440,64]{1,2,0:T(8,128)(2,1)}, u32[]{:S(2)}) %copy-start.7) | copy-done | bytes 737304
  1.2 0.1 edge_rows.1
  1.2 3.0 %collective-permute-start = (bf16[2,64,1440]{2,1,0:T(8,128)(2,1)S(1)}, bf16[2,64,1440]{2,1,0:T(8,128)(2,1)S(1)}, u32[]{:S(2)}, u32[]{:S(2)}) collective-permute-start(bf16[2,64,1440]{2,1,0:T(8,128)(2,1)S(1)} %get-tuple-element.14), channel_id=1, source_target_pairs={{0,16},{16,0},{1,17},{17,1},{2,18},{18,2},{3,19},{19,3},{4,20},{20... | collective-permute-start | bytes 1105928 | tf_op jit(solution)/shard_map/ppermute | solution.py:349
  4.3 2.5 %conv_rows.4 = (bf16[128,384]{1,0:T(8,128)(2,1)S(1)}, bf16[128,384]{1,0:T(8,128)(2,1)S(1)}, bf16[128,384]{1,0:T(8,128)(2,1)S(1)}) custom-call(s32[4,9]{1,0:T(4,128)S(1)} %copy-done.2, s32[4,9]{1,0:T(4,128)S(1)} %copy-done.3, s32[4,9]{1,0:T(4,128)S(1)} %copy-done.4, f32[4,9]{1,0:T(4,128)S(1)} %copy-done.5, ...), custom_call_target="tpu_custom_call" | custom-call | flops 1000000000 | tf_op jit(solution)/shard_map/conv_rows/pallas_call | solution.py:165
  6.8 0.0 copy-start.9
  6.8 0.0 copy-start.10
  6.8 2.7 %collective-permute-start.1 = (bf16[128,384]{1,0:T(8,128)(2,1)S(1)}, bf16[128,384]{1,0:T(8,128)(2,1)S(1)}, u32[]{:S(2)}, u32[]{:S(2)}) collective-permute-start(bf16[128,384]{1,0:T(8,128)(2,1)S(1)} %get-tuple-element.17), channel_id=1, source_target_pairs={{0,8},{4,12},{8,0},{12,4},{1,9},{5,13},{9,1},{13,5},{2,10},{6,14},... | collective-permute-start | bytes 294920 | tf_op jit(solution)/shard_map/ppermute | solution.py:323
  9.4 1.3 %collective-permute-start.5 = (bf16[128,384]{1,0:T(8,128)(2,1)S(1)}, bf16[128,384]{1,0:T(8,128)(2,1)S(1)}, u32[]{:S(2)}, u32[]{:S(2)}) collective-permute-start(bf16[128,384]{1,0:T(8,128)(2,1)S(1)} %get-tuple-element.15.rest_1_), channel_id=1, source_target_pairs={{0,12},{4,8},{8,4},{12,0},{1,13},{5,9},{9,5},{13,1},{2,14},{6,10},... | collective-permute-start | bytes 294920 | tf_op jit(solution)/shard_map/ppermute | solution.py:323
  10.8 0.2 collective-permute-start.6
  11.0 1.5 %conv_rows.5.rest_2_.rest_0_ = bf16[128,384]{1,0:T(8,128)(2,1)S(1)} custom-call(s32[4,9]{1,0:T(4,128)S(1)} %copy-done.2, s32[4,9]{1,0:T(4,128)S(1)} %copy-done.3, s32[4,9]{1,0:T(4,128)S(1)} %copy-done.4, f32[4,9]{1,0:T(4,128)S(1)} %copy-done.5, bf16[4,64,1440]{2,1,0:T(8,128)(2,1)S(1)} %get-tuple-element.13.fields_ref, bf16[6,64,64]{2,1,0:T(8,128)(2,1)S(1)} %copy-done, ...), custom_call_target="tpu_custom_call" | custom-call | flops 200000000 | tf_op jit(solution)/shard_map/conv_rows/pallas_call | solution.py:165
  12.5 0.1 copy.12
  12.7 0.1 copy.13
  12.8 0.5 %collective-permute-done.rest_0_ = bf16[2,64,1440]{2,1,0:T(8,128)(2,1)S(1)} collective-permute-done((bf16[2,64,1440]{2,1,0:T(8,128)(2,1)S(1)}, bf16[2,64,1440]{2,1,0:T(8,128)(2,1)S(1)}, u32[]{:S(2)}, u32[]{:S(2)}) %collective-permute-start) | collective-permute-done | bytes 368672 | tf_op jit(solution)/shard_map/ppermute | solution.py:349
  13.4 2.4 %conv_rows.6 = (bf16[128,384]{1,0:T(8,128)(2,1)S(1)}, bf16[128,384]{1,0:T(8,128)(2,1)S(1)}, bf16[128,384]{1,0:T(8,128)(2,1)S(1)}) custom-call(s32[4,9]{1,0:T(4,128)S(1)} %copy-done.2, s32[4,9]{1,0:T(4,128)S(1)} %copy-done.3, s32[4,9]{1,0:T(4,128)S(1)} %copy-done.4, f32[4,9]{1,0:T(4,128)S(1)} %copy-done.5, ...), custom_call_target="tpu_custom_call" | custom-call | flops 1000000000 | tf_op jit(solution)/shard_map/conv_rows/pallas_call | solution.py:165
  15.8 0.0 copy-start.8
  15.9 3.9 %collective-permute-start.3 = (bf16[128,384]{1,0:T(8,128)(2,1)S(1)}, bf16[128,384]{1,0:T(8,128)(2,1)S(1)}, u32[]{:S(2)}, u32[]{:S(2)}) collective-permute-start(bf16[128,384]{1,0:T(8,128)(2,1)S(1)} %get-tuple-element.16.rest_2_), channel_id=1, source_target_pairs={{0,12},{4,8},{8,4},{12,0},{1,13},{5,9},{9,5},{13,1},{2,14},{6,10},... | collective-permute-start | bytes 294920 | tf_op jit(solution)/shard_map/ppermute | solution.py:323
  19.7 0.0 collective-permute-start.2
  19.7 0.0 collective-permute-done.1.rest_3_.rest_1_
  19.7 0.6 %collective-permute-start.4 = (bf16[128,384]{1,0:T(8,128)(2,1)S(1)}, bf16[128,384]{1,0:T(8,128)(2,1)S(1)}, u32[]{:S(2)}, u32[]{:S(2)}) collective-permute-start(bf16[128,384]{1,0:T(8,128)(2,1)S(1)} %get-tuple-element.19), channel_id=1, source_target_pairs={{0,4},{4,0},{8,12},{12,8},{1,5},{5,1},{9,13},{13,9},{2,6},{6,2},{1... | collective-permute-start | bytes 294920 | tf_op jit(solution)/shard_map/ppermute | solution.py:323
  20.4 1.5 %conv_rows.7.rest_7_.rest_0_ = bf16[128,384]{1,0:T(8,128)(2,1)S(1)} custom-call(s32[4,9]{1,0:T(4,128)S(1)} %copy-done.2, s32[4,9]{1,0:T(4,128)S(1)} %copy-done.3, s32[4,9]{1,0:T(4,128)S(1)} %copy-done.4, f32[4,9]{1,0:T(4,128)S(1)} %copy-done.5, bf16[4,64,1440]{2,1,0:T(8,128)(2,1)S(1)} %get-tuple-element.13.fields_ref, ...), custom_call_target="tpu_custom_call" | custom-call | flops 200000000 | tf_op jit(solution)/shard_map/conv_rows/pallas_call | solution.py:165
  21.9 0.0 collective-permute-done.5.rest_2_
  21.9 0.0 collective-permute-done.6.rest_3_
  21.9 1.2 %mlp_rows.2.rest_7_ = bf16[8,16,256]{2,1,0:T(8,128)(2,1)S(1)} custom-call(bf16[128,384]{1,0:T(8,128)(2,1)S(1)} %conv_rows.5.rest_2_.rest_0_, bf16[128,384]{1,0:T(8,128)(2,1)S(1)} %collective-permute-done.1.rest_3_.rest_1_, bf16[128,384]{1,0:T(8,128)(2,1)S(1)} %collective-permute-done.5.rest_2_, bf16[128,384]{1,0:T(8,128)(2,1)S(1)} %collective-permute-done.6.rest_3_, ...), custom_call_target="tpu_custom_call" | custom-call | flops 1000000000 | tf_op jit(solution)/shard_map/mlp_rows/pallas_call | solution.py:231
  23.1 0.0 copy-start.1
  23.1 0.0 copy-start.6
  23.2 4.0 %collective-permute-done.2.rest_1_ = bf16[128,384]{1,0:T(8,128)(2,1)S(1)} collective-permute-done((bf16[128,384]{1,0:T(8,128)(2,1)S(1)}, bf16[128,384]{1,0:T(8,128)(2,1)S(1)}, u32[]{:S(2)}, u32[]{:S(2)}) %collective-permute-start.2) | collective-permute-done | bytes 98336 | tf_op jit(solution)/shard_map/ppermute | solution.py:323
  27.1 0.0 collective-permute-done.4.rest_3_
  27.1 1.8 %mlp_rows.3 = bf16[8,32,256]{2,1,0:T(8,128)(2,1)} custom-call(bf16[128,384]{1,0:T(8,128)(2,1)S(1)} %conv_rows.7.rest_7_.rest_0_, bf16[128,384]{1,0:T(8,128)(2,1)S(1)} %collective-permute-done.2.rest_1_, bf16[128,384]{1,0:T(8,128)(2,1)S(1)} %collective-permute-done.3.rest_2_, bf16[128,384]{1,0:T(8,128)(2,1)S(1)} %collective-permute-done.4.rest_3_, ...), custom_call_target="tpu_custom_call" | custom-call | flops 1000000000 | tf_op jit(solution)/shard_map/mlp_rows/pallas_call | solution.py:231
  29.0 4.9 %all-to-all-start = ((bf16[8,32,256]{2,1,0:T(8,128)(2,1)}), bf16[8,32,256]{2,1,0:T(8,128)(2,1)S(1)}, u32[]{:S(2)}, u32[]{:S(2)}) async-start(bf16[8,32,256]{2,1,0:T(8,128)(2,1)} %mlp_rows.3), calls=%async_computation | async-start | bytes 262144 | tf_op jit(solution)/shard_map/all_to_all | solution.py:391
  33.8 0.8 %expand.1.left_ref = bf16[3,2,384,256]{3,2,1,0:T(8,128)(2,1)S(1)} custom-call(bf16[3,8,384]{2,1,0:T(8,128)(2,1)S(1)} %bitcast.10, bf16[8,256]{1,0:T(8,128)(2,1)S(1)} %copy-done.6), custom_call_target="tpu_custom_call" | custom-call | flops 200000000 | tf_op jit(solution)/shard_map/expand/pallas_call | solution.py:265
  34.7 6.7 %all-to-all-done = bf16[8,32,256]{2,1,0:T(8,128)(2,1)S(1)} async-done(((bf16[8,32,256]{2,1,0:T(8,128)(2,1)}), bf16[8,32,256]{2,1,0:T(8,128)(2,1)S(1)}, u32[]{:S(2)}, u32[]{:S(2)}) %all-to-all-start) | async-done | bytes 131104 | tf_op jit(solution)/shard_map/all_to_all | solution.py:391
  41.3 1.3 %final_sum.1 = bf16[3,384,512]{2,1,0:T(8,128)(2,1)} custom-call(bf16[3,2,384,256]{3,2,1,0:T(8,128)(2,1)S(1)} %expand.1.left_ref, bf16[256,256]{1,0:T(8,128)(2,1)S(1)} %bitcast.9), custom_call_target="tpu_custom_call" | custom-call | flops 1000000000 | tf_op jit(solution)/shard_map/final_sum/pallas_call | solution.py:298
  (17 shorter events, 0.0 us)
Async XLA Ops:
  0.0 1.1 %copy-start.7 = (bf16[4,1440,64]{1,2,0:T(8,128)(2,1)S(1)}, bf16[4,1440,64]{1,2,0:T(8,128)(2,1)}, u32[]{:S(2)}) copy-start(bf16[4,1440,64]{1,2,0:T(8,128)(2,1)} %param.11) | copy-start | bytes 2211844
  1.1 3.1 %copy-start = (bf16[6,64,64]{2,1,0:T(8,128)(2,1)S(1)}, bf16[6,64,64]{2,1,0:T(8,128)(2,1)}, u32[]{:S(2)}) copy-start(bf16[6,64,64]{2,1,0:T(8,128)(2,1)} %rest_1_.3) | copy-start | bytes 147460
  1.1 3.1 %copy-start.2 = (s32[4,9]{1,0:T(4,128)S(1)}, s32[4,9]{1,0:T(4,128)}, u32[]{:S(2)}) copy-start(s32[4,9]{1,0:T(4,128)} %lat_ref.7) | copy-start | bytes 436
  1.1 3.1 %copy-start.3 = (s32[4,9]{1,0:T(4,128)S(1)}, s32[4,9]{1,0:T(4,128)}, u32[]{:S(2)}) copy-start(s32[4,9]{1,0:T(4,128)} %lon_ref.7) | copy-start | bytes 436
  1.1 3.1 %copy-start.4 = (s32[4,9]{1,0:T(4,128)S(1)}, s32[4,9]{1,0:T(4,128)}, u32[]{:S(2)}) copy-start(s32[4,9]{1,0:T(4,128)} %basis_ref.7) | copy-start | bytes 436
  1.1 3.1 %copy-start.5 = (f32[4,9]{1,0:T(4,128)S(1)}, f32[4,9]{1,0:T(4,128)}, u32[]{:S(2)}) copy-start(f32[4,9]{1,0:T(4,128)} %value_ref.7) | copy-start | bytes 436
  1.2 12.1 %collective-permute-start = (bf16[2,64,1440]{2,1,0:T(8,128)(2,1)S(1)}, bf16[2,64,1440]{2,1,0:T(8,128)(2,1)S(1)}, u32[]{:S(2)}, u32[]{:S(2)}) collective-permute-start(bf16[2,64,1440]{2,1,0:T(8,128)(2,1)S(1)} %get-tuple-element.14), channel_id=1, source_target_pairs={{0,16},{16,0},{1,17},{17,1},{2,18},{18,2},{3,19},{19,3},{4,20},{20... | collective-permute-start | bytes 1105928 | tf_op jit(solution)/shard_map/ppermute | solution.py:349
  6.8 5.8 %copy-start.9 = (bf16[256,512]{1,0:T(8,128)(2,1)S(1)}, bf16[256,512]{1,0:T(8,128)(2,1)}, u32[]{:S(2)}) copy-start(bf16[256,512]{1,0:T(8,128)(2,1)} %param.17) | copy-start | bytes 786436
  6.8 5.9 %copy-start.10 = (bf16[512,256]{1,0:T(8,128)(2,1)S(1)}, bf16[512,256]{1,0:T(8,128)(2,1)}, u32[]{:S(2)}) copy-start(bf16[512,256]{1,0:T(8,128)(2,1)} %param.18) | copy-start | bytes 786436
  6.8 12.9 %collective-permute-start.1 = (bf16[128,384]{1,0:T(8,128)(2,1)S(1)}, bf16[128,384]{1,0:T(8,128)(2,1)S(1)}, u32[]{:S(2)}, u32[]{:S(2)}) collective-permute-start(bf16[128,384]{1,0:T(8,128)(2,1)S(1)} %get-tuple-element.17), channel_id=1, source_target_pairs={{0,8},{4,12},{8,0},{12,4},{1,9},{5,13},{9,1},{13,5},{2,10},{6,14},... | collective-permute-start | bytes 294920 | tf_op jit(solution)/shard_map/ppermute | solution.py:323
  9.4 12.5 %collective-permute-start.5 = (bf16[128,384]{1,0:T(8,128)(2,1)S(1)}, bf16[128,384]{1,0:T(8,128)(2,1)S(1)}, u32[]{:S(2)}, u32[]{:S(2)}) collective-permute-start(bf16[128,384]{1,0:T(8,128)(2,1)S(1)} %get-tuple-element.15.rest_1_), channel_id=1, source_target_pairs={{0,12},{4,8},{8,4},{12,0},{1,13},{5,9},{9,5},{13,1},{2,14},{6,10},... | collective-permute-start | bytes 294920 | tf_op jit(solution)/shard_map/ppermute | solution.py:323
  10.8 11.1 %collective-permute-start.6 = (bf16[128,384]{1,0:T(8,128)(2,1)S(1)}, bf16[128,384]{1,0:T(8,128)(2,1)S(1)}, u32[]{:S(2)}, u32[]{:S(2)}) collective-permute-start(bf16[128,384]{1,0:T(8,128)(2,1)S(1)} %get-tuple-element.20), channel_id=1, source_target_pairs={{0,4},{4,0},{8,12},{12,8},{1,5},{5,1},{9,13},{13,9},{2,6},{6,2},{1... | collective-permute-start | bytes 294920 | tf_op jit(solution)/shard_map/ppermute | solution.py:323
  15.8 6.1 %copy-start.8 = (bf16[4,64,384]{2,1,0:T(8,128)(2,1)S(1)}, bf16[4,64,384]{2,1,0:T(8,128)(2,1)}, u32[]{:S(2)}) copy-start(bf16[4,64,384]{2,1,0:T(8,128)(2,1)} %constant.4.clone.rest_6_) | copy-start | bytes 589828
  15.9 7.3 %collective-permute-start.3 = (bf16[128,384]{1,0:T(8,128)(2,1)S(1)}, bf16[128,384]{1,0:T(8,128)(2,1)S(1)}, u32[]{:S(2)}, u32[]{:S(2)}) collective-permute-start(bf16[128,384]{1,0:T(8,128)(2,1)S(1)} %get-tuple-element.16.rest_2_), channel_id=1, source_target_pairs={{0,12},{4,8},{8,4},{12,0},{1,13},{5,9},{9,5},{13,1},{2,14},{6,10},... | collective-permute-start | bytes 294920 | tf_op jit(solution)/shard_map/ppermute | solution.py:323
  19.7 7.4 %collective-permute-start.2 = (bf16[128,384]{1,0:T(8,128)(2,1)S(1)}, bf16[128,384]{1,0:T(8,128)(2,1)S(1)}, u32[]{:S(2)}, u32[]{:S(2)}) collective-permute-start(bf16[128,384]{1,0:T(8,128)(2,1)S(1)} %get-tuple-element.18), channel_id=1, source_target_pairs={{0,8},{4,12},{8,0},{12,4},{1,9},{5,13},{9,1},{13,5},{2,10},{6,14},... | collective-permute-start | bytes 294920 | tf_op jit(solution)/shard_map/ppermute | solution.py:323
  19.7 7.4 %collective-permute-start.4 = (bf16[128,384]{1,0:T(8,128)(2,1)S(1)}, bf16[128,384]{1,0:T(8,128)(2,1)S(1)}, u32[]{:S(2)}, u32[]{:S(2)}) collective-permute-start(bf16[128,384]{1,0:T(8,128)(2,1)S(1)} %get-tuple-element.19), channel_id=1, source_target_pairs={{0,4},{4,0},{8,12},{12,8},{1,5},{5,1},{9,13},{13,9},{2,6},{6,2},{1... | collective-permute-start | bytes 294920 | tf_op jit(solution)/shard_map/ppermute | solution.py:323
  23.1 10.7 %copy-start.1 = (bf16[3,384,8]{1,2,0:T(8,128)(2,1)S(1)}, bf16[3,384,8]{1,2,0:T(8,128)(2,1)}, u32[]{:S(2)}) copy-start(bf16[3,384,8]{1,2,0:T(8,128)(2,1)} %param.19) | copy-start | bytes 55300
  23.1 10.7 %copy-start.6 = (bf16[8,256]{1,0:T(8,128)(2,1)S(1)}, bf16[8,256]{1,0:T(8,128)(2,1)}, u32[]{:S(2)}) copy-start(bf16[8,256]{1,0:T(8,128)(2,1)} %constant.5.clone.spread_ref) | copy-start | bytes 12292
  29.0 12.4 %all-to-all-start = ((bf16[8,32,256]{2,1,0:T(8,128)(2,1)}), bf16[8,32,256]{2,1,0:T(8,128)(2,1)S(1)}, u32[]{:S(2)}, u32[]{:S(2)}) async-start(bf16[8,32,256]{2,1,0:T(8,128)(2,1)} %mlp_rows.3), calls=%async_computation | async-start | bytes 262144 | tf_op jit(solution)/shard_map/all_to_all | solution.py:391

commit v21 on v20

--- a/solution.py
+++ b/solution.py
@@ -20,6 +20,7 @@
 FEW = 8
 MIB = 1024 * 1024
 EDGE_COST = 4
+COLUMNS = 256
 FLOPS_PER_US = 1_000_000_000
 
 SMEM = pl.BlockSpec(memory_space=pltpu.SMEM)
@@ -194,22 +195,24 @@
             cells_ref[pl.ds(origin, G), i * width : (i + 1) * width] = block[
                 i * G : (i + 1) * G, :
             ]
-    values = cells_ref[...].astype(jnp.float32)
-    center = values - jnp.mean(values, axis=0, keepdims=True)
-    spread = jnp.mean(center * center, axis=0, keepdims=True)
-    normed = (center * lax.rsqrt(spread + EPS)).astype(jnp.bfloat16)
-    lifted = jnp.dot(up_ref[...], normed, preferred_element_type=jnp.float32)
     scale = math.sqrt(2.0 / math.pi)
-    inner = lifted * (scale + (scale * 0.044715) * (lifted * lifted))
-    half = 0.5 * lifted
-    active = (half + half * jnp.tanh(inner)).astype(jnp.bfloat16)
-    lowered = jnp.dot(down_ref[...], active, preferred_element_type=jnp.float32)
-    result = (values + lowered).astype(jnp.bfloat16)
+    for at in range(0, 2 * width, COLUMNS):
+        columns = slice(at, min(at + COLUMNS, 2 * width))
+        values = cells_ref[:, columns].astype(jnp.float32)
+        center = values - jnp.mean(values, axis=0, keepdims=True)
+        spread = jnp.mean(center * center, axis=0, keepdims=True)
+        normed = (center * lax.rsqrt(spread + EPS)).astype(jnp.bfloat16)
+        lifted = jnp.dot(up_ref[...], normed, preferred_element_type=jnp.float32)
+        inner = lifted * (scale + (scale * 0.044715) * (lifted * lifted))
+        half = 0.5 * lifted
+        active = (half + half * jnp.tanh(inner)).astype(jnp.bfloat16)
+        lowered = jnp.dot(down_ref[...], active, preferred_element_type=jnp.float32)
+        cells_ref[:, columns] = (values + lowered).astype(jnp.bfloat16)
     found = []
     for i in range(2):
         modes = lax.dot_general(
             table_ref[place],
-            result[:, i * width : (i + 1) * width],
+            cells_ref[:, i * width : (i + 1) * width],
             (((1,), (1,)), ((), ())),
             preferred_element_type=jnp.float32,
         )

time: 42.9 us -> 43 us (level)
  no operation moved by 1% of the time
where the time goes in v21:
time: 43 us; the launch traced here: 42.7 us
  starting transfers between devices  16.6 us (39%)
  Pallas kernels  13.3 us (31%)
  waiting for transfers between devices  11.1 us (26%)
  local copies, waits for them, and re-layouts  1.46 us (3%)
    ppermute x6, starting transfers between devices, turn(): lax.ppermute(block, axis, [(i, target(i, k, count)) for i in range(count)])  8.75 us
    pallas_call x4, Pallas kernels, conv_rows(): pl.pallas_call(functools.partial(conv_kernel, chunks, picks, edge is not...  7.94 us
    all_to_all x1, waiting for transfers between devices, on_device(): lax.all_to_all(spectrum, both, split_axis=0, concat_axis=0, tiled=True)  6.66 us
    all_to_all x1, starting transfers between devices, on_device(): lax.all_to_all(spectrum, both, split_axis=0, concat_axis=0, tiled=True)  4.85 us
    ppermute x6, waiting for transfers between devices, turn(): lax.ppermute(block, axis, [(i, target(i, k, count)) for i in range(count)])  3.92 us
    pallas_call x2, Pallas kernels, mlp_rows(): pl.pallas_call(functools.partial(mlp_kernel, len(blocks), last, len(after...  3.15 us
    ppermute x1, starting transfers between devices, on_device(): edges = [None, lax.ppermute(edge_out, 'lat', [(0, 1), (1, 0)])]  3.03 us
    unnamed x24, local copies, waits for them, and re-layouts  1.46 us
  transfers between devices with their start and end apart: 8, of which 3 were waited for; matrix products, arithmetic and copies ran while one was open for 1% of the time, Pallas kernels for 23%

profile of v21, /device:TPU:0, one launch (start us, length us, event | category | flops | bytes accessed | tf_op | source)
XLA Modules:
  0.0 42.7 jit_solution(14715124276149331843)
XLA Ops:
  0.0 1.1 %copy-done.7 = bf16[4,1440,64]{1,2,0:T(8,128)(2,1)S(1)} copy-done((bf16[4,1440,64]{1,2,0:T(8,128)(2,1)S(1)}, bf16[4,1440,64]{1,2,0:T(8,128)(2,1)}, u32[]{:S(2)}) %copy-start.7) | copy-done | bytes 737304
  1.2 0.1 edge_rows.1
  1.2 3.0 %collective-permute-start = (bf16[2,64,1440]{2,1,0:T(8,128)(2,1)S(1)}, bf16[2,64,1440]{2,1,0:T(8,128)(2,1)S(1)}, u32[]{:S(2)}, u32[]{:S(2)}) collective-permute-start(bf16[2,64,1440]{2,1,0:T(8,128)(2,1)S(1)} %get-tuple-element.14), channel_id=1, source_target_pairs={{0,16},{16,0},{1,17},{17,1},{2,18},{18,2},{3,19},{19,3},{4,20},{20... | collective-permute-start | bytes 1105928 | tf_op jit(solution)/shard_map/ppermute | solution.py:352
  4.3 2.5 %conv_rows.4 = (bf16[128,384]{1,0:T(8,128)(2,1)S(1)}, bf16[128,384]{1,0:T(8,128)(2,1)S(1)}, bf16[128,384]{1,0:T(8,128)(2,1)S(1)}) custom-call(s32[4,9]{1,0:T(4,128)S(1)} %copy-done.2, s32[4,9]{1,0:T(4,128)S(1)} %copy-done.3, s32[4,9]{1,0:T(4,128)S(1)} %copy-done.4, f32[4,9]{1,0:T(4,128)S(1)} %copy-done.5, ...), custom_call_target="tpu_custom_call" | custom-call | flops 1000000000 | tf_op jit(solution)/shard_map/conv_rows/pallas_call | solution.py:166
  6.8 0.0 copy-start.9
  6.8 0.0 copy-start.10
  6.8 2.7 %collective-permute-start.1 = (bf16[128,384]{1,0:T(8,128)(2,1)S(1)}, bf16[128,384]{1,0:T(8,128)(2,1)S(1)}, u32[]{:S(2)}, u32[]{:S(2)}) collective-permute-start(bf16[128,384]{1,0:T(8,128)(2,1)S(1)} %get-tuple-element.17), channel_id=1, source_target_pairs={{0,8},{4,12},{8,0},{12,4},{1,9},{5,13},{9,1},{13,5},{2,10},{6,14},... | collective-permute-start | bytes 294920 | tf_op jit(solution)/shard_map/ppermute | solution.py:326
  9.4 1.4 %collective-permute-start.5 = (bf16[128,384]{1,0:T(8,128)(2,1)S(1)}, bf16[128,384]{1,0:T(8,128)(2,1)S(1)}, u32[]{:S(2)}, u32[]{:S(2)}) collective-permute-start(bf16[128,384]{1,0:T(8,128)(2,1)S(1)} %get-tuple-element.15.rest_1_), channel_id=1, source_target_pairs={{0,12},{4,8},{8,4},{12,0},{1,13},{5,9},{9,5},{13,1},{2,14},{6,10},... | collective-permute-start | bytes 294920 | tf_op jit(solution)/shard_map/ppermute | solution.py:326
  10.8 0.2 collective-permute-start.6
  11.0 1.5 %conv_rows.5.rest_2_.rest_0_ = bf16[128,384]{1,0:T(8,128)(2,1)S(1)} custom-call(s32[4,9]{1,0:T(4,128)S(1)} %copy-done.2, s32[4,9]{1,0:T(4,128)S(1)} %copy-done.3, s32[4,9]{1,0:T(4,128)S(1)} %copy-done.4, f32[4,9]{1,0:T(4,128)S(1)} %copy-done.5, bf16[4,64,1440]{2,1,0:T(8,128)(2,1)S(1)} %get-tuple-element.13.fields_ref, bf16[6,64,64]{2,1,0:T(8,128)(2,1)S(1)} %copy-done, ...), custom_call_target="tpu_custom_call" | custom-call | flops 200000000 | tf_op jit(solution)/shard_map/conv_rows/pallas_call | solution.py:166
  12.5 0.1 copy.12
  12.7 0.1 copy.13
  12.8 0.5 %collective-permute-done.rest_0_ = bf16[2,64,1440]{2,1,0:T(8,128)(2,1)S(1)} collective-permute-done((bf16[2,64,1440]{2,1,0:T(8,128)(2,1)S(1)}, bf16[2,64,1440]{2,1,0:T(8,128)(2,1)S(1)}, u32[]{:S(2)}, u32[]{:S(2)}) %collective-permute-start) | collective-permute-done | bytes 368672 | tf_op jit(solution)/shard_map/ppermute | solution.py:352
  13.4 2.5 %conv_rows.6 = (bf16[128,384]{1,0:T(8,128)(2,1)S(1)}, bf16[128,384]{1,0:T(8,128)(2,1)S(1)}, bf16[128,384]{1,0:T(8,128)(2,1)S(1)}) custom-call(s32[4,9]{1,0:T(4,128)S(1)} %copy-done.2, s32[4,9]{1,0:T(4,128)S(1)} %copy-done.3, s32[4,9]{1,0:T(4,128)S(1)} %copy-done.4, f32[4,9]{1,0:T(4,128)S(1)} %copy-done.5, ...), custom_call_target="tpu_custom_call" | custom-call | flops 1000000000 | tf_op jit(solution)/shard_map/conv_rows/pallas_call | solution.py:166
  15.8 0.0 copy-start.8
  15.9 3.9 %collective-permute-start.3 = (bf16[128,384]{1,0:T(8,128)(2,1)S(1)}, bf16[128,384]{1,0:T(8,128)(2,1)S(1)}, u32[]{:S(2)}, u32[]{:S(2)}) collective-permute-start(bf16[128,384]{1,0:T(8,128)(2,1)S(1)} %get-tuple-element.16.rest_2_), channel_id=1, source_target_pairs={{0,12},{4,8},{8,4},{12,0},{1,13},{5,9},{9,5},{13,1},{2,14},{6,10},... | collective-permute-start | bytes 294920 | tf_op jit(solution)/shard_map/ppermute | solution.py:326
  19.7 0.0 collective-permute-start.2
  19.7 0.0 collective-permute-done.1.rest_3_.rest_1_
  19.7 0.6 %collective-permute-start.4 = (bf16[128,384]{1,0:T(8,128)(2,1)S(1)}, bf16[128,384]{1,0:T(8,128)(2,1)S(1)}, u32[]{:S(2)}, u32[]{:S(2)}) collective-permute-start(bf16[128,384]{1,0:T(8,128)(2,1)S(1)} %get-tuple-element.19), channel_id=1, source_target_pairs={{0,4},{4,0},{8,12},{12,8},{1,5},{5,1},{9,13},{13,9},{2,6},{6,2},{1... | collective-permute-start | bytes 294920 | tf_op jit(solution)/shard_map/ppermute | solution.py:326
  20.4 1.5 %conv_rows.7.rest_7_.rest_0_ = bf16[128,384]{1,0:T(8,128)(2,1)S(1)} custom-call(s32[4,9]{1,0:T(4,128)S(1)} %copy-done.2, s32[4,9]{1,0:T(4,128)S(1)} %copy-done.3, s32[4,9]{1,0:T(4,128)S(1)} %copy-done.4, f32[4,9]{1,0:T(4,128)S(1)} %copy-done.5, bf16[4,64,1440]{2,1,0:T(8,128)(2,1)S(1)} %get-tuple-element.13.fields_ref, ...), custom_call_target="tpu_custom_call" | custom-call | flops 200000000 | tf_op jit(solution)/shard_map/conv_rows/pallas_call | solution.py:166
  21.9 0.0 collective-permute-done.5.rest_2_
  21.9 0.0 collective-permute-done.6.rest_3_
  21.9 1.2 %mlp_rows.2.rest_7_ = bf16[8,16,256]{2,1,0:T(8,128)(2,1)S(1)} custom-call(bf16[128,384]{1,0:T(8,128)(2,1)S(1)} %conv_rows.5.rest_2_.rest_0_, bf16[128,384]{1,0:T(8,128)(2,1)S(1)} %collective-permute-done.1.rest_3_.rest_1_, bf16[128,384]{1,0:T(8,128)(2,1)S(1)} %collective-permute-done.5.rest_2_, bf16[128,384]{1,0:T(8,128)(2,1)S(1)} %collective-permute-done.6.rest_3_, ...), custom_call_target="tpu_custom_call" | custom-call | flops 1000000000 | tf_op jit(solution)/shard_map/mlp_rows/pallas_call | solution.py:234
  23.2 0.0 copy-start.1
  23.2 0.0 copy-start.6
  23.2 3.9 %collective-permute-done.2.rest_1_ = bf16[128,384]{1,0:T(8,128)(2,1)S(1)} collective-permute-done((bf16[128,384]{1,0:T(8,128)(2,1)S(1)}, bf16[128,384]{1,0:T(8,128)(2,1)S(1)}, u32[]{:S(2)}, u32[]{:S(2)}) %collective-permute-start.2) | collective-permute-done | bytes 98336 | tf_op jit(solution)/shard_map/ppermute | solution.py:326
  27.1 0.0 collective-permute-done.4.rest_3_
  27.1 1.9 %mlp_rows.3 = bf16[8,32,256]{2,1,0:T(8,128)(2,1)} custom-call(bf16[128,384]{1,0:T(8,128)(2,1)S(1)} %conv_rows.7.rest_7_.rest_0_, bf16[128,384]{1,0:T(8,128)(2,1)S(1)} %collective-permute-done.2.rest_1_, bf16[128,384]{1,0:T(8,128)(2,1)S(1)} %collective-permute-done.3.rest_2_, bf16[128,384]{1,0:T(8,128)(2,1)S(1)} %collective-permute-done.4.rest_3_, ...), custom_call_target="tpu_custom_call" | custom-call | flops 1000000000 | tf_op jit(solution)/shard_map/mlp_rows/pallas_call | solution.py:234
  29.0 4.9 %all-to-all-start = ((bf16[8,32,256]{2,1,0:T(8,128)(2,1)}), bf16[8,32,256]{2,1,0:T(8,128)(2,1)S(1)}, u32[]{:S(2)}, u32[]{:S(2)}) async-start(bf16[8,32,256]{2,1,0:T(8,128)(2,1)} %mlp_rows.3), calls=%async_computation | async-start | bytes 262144 | tf_op jit(solution)/shard_map/all_to_all | solution.py:394
  33.9 0.8 %expand.1.left_ref = bf16[3,2,384,256]{3,2,1,0:T(8,128)(2,1)S(1)} custom-call(bf16[3,8,384]{2,1,0:T(8,128)(2,1)S(1)} %bitcast.10, bf16[8,256]{1,0:T(8,128)(2,1)S(1)} %copy-done.6), custom_call_target="tpu_custom_call" | custom-call | flops 200000000 | tf_op jit(solution)/shard_map/expand/pallas_call | solution.py:268
  34.8 6.7 %all-to-all-done = bf16[8,32,256]{2,1,0:T(8,128)(2,1)S(1)} async-done(((bf16[8,32,256]{2,1,0:T(8,128)(2,1)}), bf16[8,32,256]{2,1,0:T(8,128)(2,1)S(1)}, u32[]{:S(2)}, u32[]{:S(2)}) %all-to-all-start) | async-done | bytes 131104 | tf_op jit(solution)/shard_map/all_to_all | solution.py:394
  41.4 1.3 %final_sum.1 = bf16[3,384,512]{2,1,0:T(8,128)(2,1)} custom-call(bf16[3,2,384,256]{3,2,1,0:T(8,128)(2,1)S(1)} %expand.1.left_ref, bf16[256,256]{1,0:T(8,128)(2,1)S(1)} %bitcast.9), custom_call_target="tpu_custom_call" | custom-call | flops 1000000000 | tf_op jit(solution)/shard_map/final_sum/pallas_call | solution.py:301
  (17 shorter events, 0.0 us)
Async XLA Ops:
  0.0 1.1 %copy-start.7 = (bf16[4,1440,64]{1,2,0:T(8,128)(2,1)S(1)}, bf16[4,1440,64]{1,2,0:T(8,128)(2,1)}, u32[]{:S(2)}) copy-start(bf16[4,1440,64]{1,2,0:T(8,128)(2,1)} %param.11) | copy-start | bytes 2211844
  1.1 3.1 %copy-start = (bf16[6,64,64]{2,1,0:T(8,128)(2,1)S(1)}, bf16[6,64,64]{2,1,0:T(8,128)(2,1)}, u32[]{:S(2)}) copy-start(bf16[6,64,64]{2,1,0:T(8,128)(2,1)} %rest_1_.3) | copy-start | bytes 147460
  1.1 3.1 %copy-start.2 = (s32[4,9]{1,0:T(4,128)S(1)}, s32[4,9]{1,0:T(4,128)}, u32[]{:S(2)}) copy-start(s32[4,9]{1,0:T(4,128)} %lat_ref.7) | copy-start | bytes 436
  1.1 3.1 %copy-start.3 = (s32[4,9]{1,0:T(4,128)S(1)}, s32[4,9]{1,0:T(4,128)}, u32[]{:S(2)}) copy-start(s32[4,9]{1,0:T(4,128)} %lon_ref.7) | copy-start | bytes 436
  1.1 3.1 %copy-start.4 = (s32[4,9]{1,0:T(4,128)S(1)}, s32[4,9]{1,0:T(4,128)}, u32[]{:S(2)}) copy-start(s32[4,9]{1,0:T(4,128)} %basis_ref.7) | copy-start | bytes 436
  1.1 3.1 %copy-start.5 = (f32[4,9]{1,0:T(4,128)S(1)}, f32[4,9]{1,0:T(4,128)}, u32[]{:S(2)}) copy-start(f32[4,9]{1,0:T(4,128)} %value_ref.7) | copy-start | bytes 436
  1.2 12.1 %collective-permute-start = (bf16[2,64,1440]{2,1,0:T(8,128)(2,1)S(1)}, bf16[2,64,1440]{2,1,0:T(8,128)(2,1)S(1)}, u32[]{:S(2)}, u32[]{:S(2)}) collective-permute-start(bf16[2,64,1440]{2,1,0:T(8,128)(2,1)S(1)} %get-tuple-element.14), channel_id=1, source_target_pairs={{0,16},{16,0},{1,17},{17,1},{2,18},{18,2},{3,19},{19,3},{4,20},{20... | collective-permute-start | bytes 1105928 | tf_op jit(solution)/shard_map/ppermute | solution.py:352
  6.8 5.8 %copy-start.9 = (bf16[256,512]{1,0:T(8,128)(2,1)S(1)}, bf16[256,512]{1,0:T(8,128)(2,1)}, u32[]{:S(2)}) copy-start(bf16[256,512]{1,0:T(8,128)(2,1)} %param.17) | copy-start | bytes 786436
  6.8 5.9 %copy-start.10 = (bf16[512,256]{1,0:T(8,128)(2,1)S(1)}, bf16[512,256]{1,0:T(8,128)(2,1)}, u32[]{:S(2)}) copy-start(bf16[512,256]{1,0:T(8,128)(2,1)} %param.18) | copy-start | bytes 786436
  6.8 13.0 %collective-permute-start.1 = (bf16[128,384]{1,0:T(8,128)(2,1)S(1)}, bf16[128,384]{1,0:T(8,128)(2,1)S(1)}, u32[]{:S(2)}, u32[]{:S(2)}) collective-permute-start(bf16[128,384]{1,0:T(8,128)(2,1)S(1)} %get-tuple-element.17), channel_id=1, source_target_pairs={{0,8},{4,12},{8,0},{12,4},{1,9},{5,13},{9,1},{13,5},{2,10},{6,14},... | collective-permute-start | bytes 294920 | tf_op jit(solution)/shard_map/ppermute | solution.py:326
  9.4 12.5 %collective-permute-start.5 = (bf16[128,384]{1,0:T(8,128)(2,1)S(1)}, bf16[128,384]{1,0:T(8,128)(2,1)S(1)}, u32[]{:S(2)}, u32[]{:S(2)}) collective-permute-start(bf16[128,384]{1,0:T(8,128)(2,1)S(1)} %get-tuple-element.15.rest_1_), channel_id=1, source_target_pairs={{0,12},{4,8},{8,4},{12,0},{1,13},{5,9},{9,5},{13,1},{2,14},{6,10},... | collective-permute-start | bytes 294920 | tf_op jit(solution)/shard_map/ppermute | solution.py:326
  10.8 11.1 %collective-permute-start.6 = (bf16[128,384]{1,0:T(8,128)(2,1)S(1)}, bf16[128,384]{1,0:T(8,128)(2,1)S(1)}, u32[]{:S(2)}, u32[]{:S(2)}) collective-permute-start(bf16[128,384]{1,0:T(8,128)(2,1)S(1)} %get-tuple-element.20), channel_id=1, source_target_pairs={{0,4},{4,0},{8,12},{12,8},{1,5},{5,1},{9,13},{13,9},{2,6},{6,2},{1... | collective-permute-start | bytes 294920 | tf_op jit(solution)/shard_map/ppermute | solution.py:326
  15.8 6.1 %copy-start.8 = (bf16[4,64,384]{2,1,0:T(8,128)(2,1)S(1)}, bf16[4,64,384]{2,1,0:T(8,128)(2,1)}, u32[]{:S(2)}) copy-start(bf16[4,64,384]{2,1,0:T(8,128)(2,1)} %constant.4.clone.rest_6_) | copy-start | bytes 589828
  15.9 7.4 %collective-permute-start.3 = (bf16[128,384]{1,0:T(8,128)(2,1)S(1)}, bf16[128,384]{1,0:T(8,128)(2,1)S(1)}, u32[]{:S(2)}, u32[]{:S(2)}) collective-permute-start(bf16[128,384]{1,0:T(8,128)(2,1)S(1)} %get-tuple-element.16.rest_2_), channel_id=1, source_target_pairs={{0,12},{4,8},{8,4},{12,0},{1,13},{5,9},{9,5},{13,1},{2,14},{6,10},... | collective-permute-start | bytes 294920 | tf_op jit(solution)/shard_map/ppermute | solution.py:326
  19.7 7.4 %collective-permute-start.2 = (bf16[128,384]{1,0:T(8,128)(2,1)S(1)}, bf16[128,384]{1,0:T(8,128)(2,1)S(1)}, u32[]{:S(2)}, u32[]{:S(2)}) collective-permute-start(bf16[128,384]{1,0:T(8,128)(2,1)S(1)} %get-tuple-element.18), channel_id=1, source_target_pairs={{0,8},{4,12},{8,0},{12,4},{1,9},{5,13},{9,1},{13,5},{2,10},{6,14},... | collective-permute-start | bytes 294920 | tf_op jit(solution)/shard_map/ppermute | solution.py:326
  19.7 7.4 %collective-permute-start.4 = (bf16[128,384]{1,0:T(8,128)(2,1)S(1)}, bf16[128,384]{1,0:T(8,128)(2,1)S(1)}, u32[]{:S(2)}, u32[]{:S(2)}) collective-permute-start(bf16[128,384]{1,0:T(8,128)(2,1)S(1)} %get-tuple-element.19), channel_id=1, source_target_pairs={{0,4},{4,0},{8,12},{12,8},{1,5},{5,1},{9,13},{13,9},{2,6},{6,2},{1... | collective-permute-start | bytes 294920 | tf_op jit(solution)/shard_map/ppermute | solution.py:326
  23.2 10.7 %copy-start.1 = (bf16[3,384,8]{1,2,0:T(8,128)(2,1)S(1)}, bf16[3,384,8]{1,2,0:T(8,128)(2,1)}, u32[]{:S(2)}) copy-start(bf16[3,384,8]{1,2,0:T(8,128)(2,1)} %param.19) | copy-start | bytes 55300
  23.2 10.7 %copy-start.6 = (bf16[8,256]{1,0:T(8,128)(2,1)S(1)}, bf16[8,256]{1,0:T(8,128)(2,1)}, u32[]{:S(2)}) copy-start(bf16[8,256]{1,0:T(8,128)(2,1)} %constant.5.clone.spread_ref) | copy-start | bytes 12292
  29.0 12.4 %all-to-all-start = ((bf16[8,32,256]{2,1,0:T(8,128)(2,1)}), bf16[8,32,256]{2,1,0:T(8,128)(2,1)S(1)}, u32[]{:S(2)}, u32[]{:S(2)}) async-start(bf16[8,32,256]{2,1,0:T(8,128)(2,1)} %mlp_rows.3), calls=%async_computation | async-start | bytes 262144 | tf_op jit(solution)/shard_map/all_to_all | solution.py:394

commit v22 on v20

--- a/solution.py
+++ b/solution.py
@@ -379,7 +379,7 @@
     for half in halves:
         sent = conv_rows(*half, order, after, False)
         moved = [turn(block, "chan", num_chan, k) for k, block in zip(order, sent)]
-        after = conv_rows(*half, [0], [sent[1], *last], False)
+        after = conv_rows(*half, [0], [sent[0], *last], False)
         received.append([*after, *moved])
         after, last = list(after), moved[:1]
     spectrum = None

time: 42.9 us -> 42.9 us (level)
  starting transfers between devices: 16.6 us -> 17.1 us
  waiting for transfers between devices: 11.2 us -> 10.7 us
    ppermute x6, waiting for transfers between devices: 3.99 us -> 3.35 us  [turn(): lax.ppermute(block, axis, [(i, target(i, k, count)) for i in range(count)])]
    all_to_all x1, starting transfers between devices: 4.85 us -> 5.43 us  [on_device(): lax.all_to_all(spectrum, both, split_axis=0, concat_axis=0, tiled=True)]
  transfers between devices with their start and end apart: 8 -> 8, of which waited for: 3 -> 5; matrix products, arithmetic and copies ran while one was open for 1% -> 1% of each run, Pallas kernels for 23% -> 23%
where the time goes in v22:
time: 42.9 us; the launch traced here: 42.6 us
  starting transfers between devices  17.1 us (40%)
  Pallas kernels  13.1 us (31%)
  waiting for transfers between devices  10.7 us (25%)
  local copies, waits for them, and re-layouts  1.46 us (3%)
    ppermute x6, starting transfers between devices, turn(): lax.ppermute(block, axis, [(i, target(i, k, count)) for i in range(count)])  8.68 us
    pallas_call x4, Pallas kernels, conv_rows(): pl.pallas_call(functools.partial(conv_kernel, chunks, picks, edge is not...  7.94 us
    all_to_all x1, waiting for transfers between devices, on_device(): lax.all_to_all(spectrum, both, split_axis=0, concat_axis=0, tiled=True)  6.82 us
    all_to_all x1, starting transfers between devices, on_device(): lax.all_to_all(spectrum, both, split_axis=0, concat_axis=0, tiled=True)  5.43 us
    ppermute x6, waiting for transfers between devices, turn(): lax.ppermute(block, axis, [(i, target(i, k, count)) for i in range(count)])  3.35 us
    ppermute x1, starting transfers between devices, on_device(): edges = [None, lax.ppermute(edge_out, 'lat', [(0, 1), (1, 0)])]  3.03 us
    pallas_call x2, Pallas kernels, mlp_rows(): pl.pallas_call(functools.partial(mlp_kernel, len(blocks), last, len(after...  3 us
    unnamed x24, local copies, waits for them, and re-layouts  1.46 us
  transfers between devices with their start and end apart: 8, of which 5 were waited for; matrix products, arithmetic and copies ran while one was open for 1% of the time, Pallas kernels for 23%

profile of v22, /device:TPU:0, one launch (start us, length us, event | category | flops | bytes accessed | tf_op | source)
XLA Modules:
  0.0 42.6 jit_solution(13313331843784524330)
XLA Ops:
  0.0 1.1 %copy-done.7 = bf16[4,1440,64]{1,2,0:T(8,128)(2,1)S(1)} copy-done((bf16[4,1440,64]{1,2,0:T(8,128)(2,1)S(1)}, bf16[4,1440,64]{1,2,0:T(8,128)(2,1)}, u32[]{:S(2)}) %copy-start.7) | copy-done | bytes 737304
  1.2 0.1 edge_rows.1
  1.2 3.0 %collective-permute-start = (bf16[2,64,1440]{2,1,0:T(8,128)(2,1)S(1)}, bf16[2,64,1440]{2,1,0:T(8,128)(2,1)S(1)}, u32[]{:S(2)}, u32[]{:S(2)}) collective-permute-start(bf16[2,64,1440]{2,1,0:T(8,128)(2,1)S(1)} %get-tuple-element.14), channel_id=1, source_target_pairs={{0,16},{16,0},{1,17},{17,1},{2,18},{18,2},{3,19},{19,3},{4,20},{20... | collective-permute-start | bytes 1105928 | tf_op jit(solution)/shard_map/ppermute | solution.py:349
  4.3 2.5 %conv_rows.4 = (bf16[128,384]{1,0:T(8,128)(2,1)S(1)}, bf16[128,384]{1,0:T(8,128)(2,1)S(1)}, bf16[128,384]{1,0:T(8,128)(2,1)S(1)}) custom-call(s32[4,9]{1,0:T(4,128)S(1)} %copy-done.2, s32[4,9]{1,0:T(4,128)S(1)} %copy-done.3, s32[4,9]{1,0:T(4,128)S(1)} %copy-done.4, f32[4,9]{1,0:T(4,128)S(1)} %copy-done.5, ...), custom_call_target="tpu_custom_call" | custom-call | flops 1000000000 | tf_op jit(solution)/shard_map/conv_rows/pallas_call | solution.py:165
  6.8 0.0 copy-start.9
  6.8 0.0 copy-start.10
  6.8 2.7 %collective-permute-start.1 = (bf16[128,384]{1,0:T(8,128)(2,1)S(1)}, bf16[128,384]{1,0:T(8,128)(2,1)S(1)}, u32[]{:S(2)}, u32[]{:S(2)}) collective-permute-start(bf16[128,384]{1,0:T(8,128)(2,1)S(1)} %get-tuple-element.15.rest_1_), channel_id=1, source_target_pairs={{0,8},{4,12},{8,0},{12,4},{1,9},{5,13},{9,1},{13,5},{2,10},{6,14},... | collective-permute-start | bytes 294920 | tf_op jit(solution)/shard_map/ppermute | solution.py:323
  9.4 1.3 %collective-permute-start.5 = (bf16[128,384]{1,0:T(8,128)(2,1)S(1)}, bf16[128,384]{1,0:T(8,128)(2,1)S(1)}, u32[]{:S(2)}, u32[]{:S(2)}) collective-permute-start(bf16[128,384]{1,0:T(8,128)(2,1)S(1)} %get-tuple-element.19), channel_id=1, source_target_pairs={{0,12},{4,8},{8,4},{12,0},{1,13},{5,9},{9,5},{13,1},{2,14},{6,10},... | collective-permute-start | bytes 294920 | tf_op jit(solution)/shard_map/ppermute | solution.py:323
  10.8 0.2 collective-permute-start.6
  11.0 1.5 %conv_rows.5.rest_2_.rest_0_ = bf16[128,384]{1,0:T(8,128)(2,1)S(1)} custom-call(s32[4,9]{1,0:T(4,128)S(1)} %copy-done.2, s32[4,9]{1,0:T(4,128)S(1)} %copy-done.3, s32[4,9]{1,0:T(4,128)S(1)} %copy-done.4, f32[4,9]{1,0:T(4,128)S(1)} %copy-done.5, bf16[4,64,1440]{2,1,0:T(8,128)(2,1)S(1)} %get-tuple-element.13.fields_ref, bf16[6,64,64]{2,1,0:T(8,128)(2,1)S(1)} %copy-done, ...), custom_call_target="tpu_custom_call" | custom-call | flops 200000000 | tf_op jit(solution)/shard_map/conv_rows/pallas_call | solution.py:165
  12.5 0.1 copy.12
  12.7 0.1 copy.13
  12.8 0.5 %collective-permute-done.rest_0_ = bf16[2,64,1440]{2,1,0:T(8,128)(2,1)S(1)} collective-permute-done((bf16[2,64,1440]{2,1,0:T(8,128)(2,1)S(1)}, bf16[2,64,1440]{2,1,0:T(8,128)(2,1)S(1)}, u32[]{:S(2)}, u32[]{:S(2)}) %collective-permute-start) | collective-permute-done | bytes 368672 | tf_op jit(solution)/shard_map/ppermute | solution.py:349
  13.4 2.4 %conv_rows.6 = (bf16[128,384]{1,0:T(8,128)(2,1)S(1)}, bf16[128,384]{1,0:T(8,128)(2,1)S(1)}, bf16[128,384]{1,0:T(8,128)(2,1)S(1)}) custom-call(s32[4,9]{1,0:T(4,128)S(1)} %copy-done.2, s32[4,9]{1,0:T(4,128)S(1)} %copy-done.3, s32[4,9]{1,0:T(4,128)S(1)} %copy-done.4, f32[4,9]{1,0:T(4,128)S(1)} %copy-done.5, ...), custom_call_target="tpu_custom_call" | custom-call | flops 1000000000 | tf_op jit(solution)/shard_map/conv_rows/pallas_call | solution.py:165
  15.8 0.0 copy-start.8
  15.9 2.9 %collective-permute-start.2 = (bf16[128,384]{1,0:T(8,128)(2,1)S(1)}, bf16[128,384]{1,0:T(8,128)(2,1)S(1)}, u32[]{:S(2)}, u32[]{:S(2)}) collective-permute-start(bf16[128,384]{1,0:T(8,128)(2,1)S(1)} %get-tuple-element.16.rest_2_), channel_id=1, source_target_pairs={{0,8},{4,12},{8,0},{12,4},{1,9},{5,13},{9,1},{13,5},{2,10},{6,14},... | collective-permute-start | bytes 294920 | tf_op jit(solution)/shard_map/ppermute | solution.py:323
  18.7 1.3 %collective-permute-start.3 = (bf16[128,384]{1,0:T(8,128)(2,1)S(1)}, bf16[128,384]{1,0:T(8,128)(2,1)S(1)}, u32[]{:S(2)}, u32[]{:S(2)}) collective-permute-start(bf16[128,384]{1,0:T(8,128)(2,1)S(1)} %get-tuple-element.17), channel_id=1, source_target_pairs={{0,12},{4,8},{8,4},{12,0},{1,13},{5,9},{9,5},{13,1},{2,14},{6,10},... | collective-permute-start | bytes 294920 | tf_op jit(solution)/shard_map/ppermute | solution.py:323
  20.1 0.0 collective-permute-done.1.rest_3_.rest_1_
  20.1 0.2 collective-permute-start.4
  20.3 1.5 %conv_rows.7.rest_7_.rest_0_ = bf16[128,384]{1,0:T(8,128)(2,1)S(1)} custom-call(s32[4,9]{1,0:T(4,128)S(1)} %copy-done.2, s32[4,9]{1,0:T(4,128)S(1)} %copy-done.3, s32[4,9]{1,0:T(4,128)S(1)} %copy-done.4, f32[4,9]{1,0:T(4,128)S(1)} %copy-done.5, bf16[4,64,1440]{2,1,0:T(8,128)(2,1)S(1)} %get-tuple-element.13.fields_ref, ...), custom_call_target="tpu_custom_call" | custom-call | flops 200000000 | tf_op jit(solution)/shard_map/conv_rows/pallas_call | solution.py:165
  21.9 0.0 collective-permute-done.6.rest_3_
  21.9 1.2 %mlp_rows.2.rest_7_ = bf16[8,16,256]{2,1,0:T(8,128)(2,1)S(1)} custom-call(bf16[128,384]{1,0:T(8,128)(2,1)S(1)} %conv_rows.5.rest_2_.rest_0_, bf16[128,384]{1,0:T(8,128)(2,1)S(1)} %collective-permute-done.1.rest_3_.rest_1_, bf16[128,384]{1,0:T(8,128)(2,1)S(1)} %collective-permute-done.5.rest_2_, bf16[128,384]{1,0:T(8,128)(2,1)S(1)} %collective-permute-done.6.rest_3_, ...), custom_call_target="tpu_custom_call" | custom-call | flops 1000000000 | tf_op jit(solution)/shard_map/mlp_rows/pallas_call | solution.py:231
  23.1 0.0 copy-start.1
  23.1 0.0 copy-start.6
  23.1 2.4 %collective-permute-done.2.rest_1_ = bf16[128,384]{1,0:T(8,128)(2,1)S(1)} collective-permute-done((bf16[128,384]{1,0:T(8,128)(2,1)S(1)}, bf16[128,384]{1,0:T(8,128)(2,1)S(1)}, u32[]{:S(2)}, u32[]{:S(2)}) %collective-permute-start.2) | collective-permute-done | bytes 98336 | tf_op jit(solution)/shard_map/ppermute | solution.py:323
  25.4 0.5 %collective-permute-done.3.rest_2_ = bf16[128,384]{1,0:T(8,128)(2,1)S(1)} collective-permute-done((bf16[128,384]{1,0:T(8,128)(2,1)S(1)}, bf16[128,384]{1,0:T(8,128)(2,1)S(1)}, u32[]{:S(2)}, u32[]{:S(2)}) %collective-permute-start.3) | collective-permute-done | bytes 98336 | tf_op jit(solution)/shard_map/ppermute | solution.py:323
  25.9 0.5 %collective-permute-done.4.rest_3_ = bf16[128,384]{1,0:T(8,128)(2,1)S(1)} collective-permute-done((bf16[128,384]{1,0:T(8,128)(2,1)S(1)}, bf16[128,384]{1,0:T(8,128)(2,1)S(1)}, u32[]{:S(2)}, u32[]{:S(2)}) %collective-permute-start.4) | collective-permute-done | bytes 98336 | tf_op jit(solution)/shard_map/ppermute | solution.py:323
  26.4 1.8 %mlp_rows.3 = bf16[8,32,256]{2,1,0:T(8,128)(2,1)} custom-call(bf16[128,384]{1,0:T(8,128)(2,1)S(1)} %conv_rows.7.rest_7_.rest_0_, bf16[128,384]{1,0:T(8,128)(2,1)S(1)} %collective-permute-done.2.rest_1_, bf16[128,384]{1,0:T(8,128)(2,1)S(1)} %collective-permute-done.3.rest_2_, bf16[128,384]{1,0:T(8,128)(2,1)S(1)} %collective-permute-done.4.rest_3_, ...), custom_call_target="tpu_custom_call" | custom-call | flops 1000000000 | tf_op jit(solution)/shard_map/mlp_rows/pallas_call | solution.py:231
  28.3 5.4 %all-to-all-start = ((bf16[8,32,256]{2,1,0:T(8,128)(2,1)}), bf16[8,32,256]{2,1,0:T(8,128)(2,1)S(1)}, u32[]{:S(2)}, u32[]{:S(2)}) async-start(bf16[8,32,256]{2,1,0:T(8,128)(2,1)} %mlp_rows.3), calls=%async_computation | async-start | bytes 262144 | tf_op jit(solution)/shard_map/all_to_all | solution.py:391
  33.7 0.8 %expand.1.left_ref = bf16[3,2,384,256]{3,2,1,0:T(8,128)(2,1)S(1)} custom-call(bf16[3,8,384]{2,1,0:T(8,128)(2,1)S(1)} %bitcast.10, bf16[8,256]{1,0:T(8,128)(2,1)S(1)} %copy-done.6), custom_call_target="tpu_custom_call" | custom-call | flops 200000000 | tf_op jit(solution)/shard_map/expand/pallas_call | solution.py:265
  34.5 6.8 %all-to-all-done = bf16[8,32,256]{2,1,0:T(8,128)(2,1)S(1)} async-done(((bf16[8,32,256]{2,1,0:T(8,128)(2,1)}), bf16[8,32,256]{2,1,0:T(8,128)(2,1)S(1)}, u32[]{:S(2)}, u32[]{:S(2)}) %all-to-all-start) | async-done | bytes 131104 | tf_op jit(solution)/shard_map/all_to_all | solution.py:391
  41.4 1.3 %final_sum.1 = bf16[3,384,512]{2,1,0:T(8,128)(2,1)} custom-call(bf16[3,2,384,256]{3,2,1,0:T(8,128)(2,1)S(1)} %expand.1.left_ref, bf16[256,256]{1,0:T(8,128)(2,1)S(1)} %bitcast.9), custom_call_target="tpu_custom_call" | custom-call | flops 1000000000 | tf_op jit(solution)/shard_map/final_sum/pallas_call | solution.py:298
  (17 shorter events, 0.0 us)
Async XLA Ops:
  0.0 1.1 %copy-start.7 = (bf16[4,1440,64]{1,2,0:T(8,128)(2,1)S(1)}, bf16[4,1440,64]{1,2,0:T(8,128)(2,1)}, u32[]{:S(2)}) copy-start(bf16[4,1440,64]{1,2,0:T(8,128)(2,1)} %param.11) | copy-start | bytes 2211844
  1.1 3.1 %copy-start = (bf16[6,64,64]{2,1,0:T(8,128)(2,1)S(1)}, bf16[6,64,64]{2,1,0:T(8,128)(2,1)}, u32[]{:S(2)}) copy-start(bf16[6,64,64]{2,1,0:T(8,128)(2,1)} %rest_1_.3) | copy-start | bytes 147460
  1.1 3.1 %copy-start.2 = (s32[4,9]{1,0:T(4,128)S(1)}, s32[4,9]{1,0:T(4,128)}, u32[]{:S(2)}) copy-start(s32[4,9]{1,0:T(4,128)} %lat_ref.7) | copy-start | bytes 436
  1.1 3.1 %copy-start.3 = (s32[4,9]{1,0:T(4,128)S(1)}, s32[4,9]{1,0:T(4,128)}, u32[]{:S(2)}) copy-start(s32[4,9]{1,0:T(4,128)} %lon_ref.7) | copy-start | bytes 436
  1.1 3.1 %copy-start.4 = (s32[4,9]{1,0:T(4,128)S(1)}, s32[4,9]{1,0:T(4,128)}, u32[]{:S(2)}) copy-start(s32[4,9]{1,0:T(4,128)} %basis_ref.7) | copy-start | bytes 436
  1.1 3.1 %copy-start.5 = (f32[4,9]{1,0:T(4,128)S(1)}, f32[4,9]{1,0:T(4,128)}, u32[]{:S(2)}) copy-start(f32[4,9]{1,0:T(4,128)} %value_ref.7) | copy-start | bytes 436
  1.2 12.1 %collective-permute-start = (bf16[2,64,1440]{2,1,0:T(8,128)(2,1)S(1)}, bf16[2,64,1440]{2,1,0:T(8,128)(2,1)S(1)}, u32[]{:S(2)}, u32[]{:S(2)}) collective-permute-start(bf16[2,64,1440]{2,1,0:T(8,128)(2,1)S(1)} %get-tuple-element.14), channel_id=1, source_target_pairs={{0,16},{16,0},{1,17},{17,1},{2,18},{18,2},{3,19},{19,3},{4,20},{20... | collective-permute-start | bytes 1105928 | tf_op jit(solution)/shard_map/ppermute | solution.py:349
  6.8 5.8 %copy-start.9 = (bf16[256,512]{1,0:T(8,128)(2,1)S(1)}, bf16[256,512]{1,0:T(8,128)(2,1)}, u32[]{:S(2)}) copy-start(bf16[256,512]{1,0:T(8,128)(2,1)} %param.17) | copy-start | bytes 786436
  6.8 5.9 %copy-start.10 = (bf16[512,256]{1,0:T(8,128)(2,1)S(1)}, bf16[512,256]{1,0:T(8,128)(2,1)}, u32[]{:S(2)}) copy-start(bf16[512,256]{1,0:T(8,128)(2,1)} %param.18) | copy-start | bytes 786436
  6.8 13.3 %collective-permute-start.1 = (bf16[128,384]{1,0:T(8,128)(2,1)S(1)}, bf16[128,384]{1,0:T(8,128)(2,1)S(1)}, u32[]{:S(2)}, u32[]{:S(2)}) collective-permute-start(bf16[128,384]{1,0:T(8,128)(2,1)S(1)} %get-tuple-element.15.rest_1_), channel_id=1, source_target_pairs={{0,8},{4,12},{8,0},{12,4},{1,9},{5,13},{9,1},{13,5},{2,10},{6,14},... | collective-permute-start | bytes 294920 | tf_op jit(solution)/shard_map/ppermute | solution.py:323
  9.4 12.4 %collective-permute-start.5 = (bf16[128,384]{1,0:T(8,128)(2,1)S(1)}, bf16[128,384]{1,0:T(8,128)(2,1)S(1)}, u32[]{:S(2)}, u32[]{:S(2)}) collective-permute-start(bf16[128,384]{1,0:T(8,128)(2,1)S(1)} %get-tuple-element.19), channel_id=1, source_target_pairs={{0,12},{4,8},{8,4},{12,0},{1,13},{5,9},{9,5},{13,1},{2,14},{6,10},... | collective-permute-start | bytes 294920 | tf_op jit(solution)/shard_map/ppermute | solution.py:323
  10.8 11.1 %collective-permute-start.6 = (bf16[128,384]{1,0:T(8,128)(2,1)S(1)}, bf16[128,384]{1,0:T(8,128)(2,1)S(1)}, u32[]{:S(2)}, u32[]{:S(2)}) collective-permute-start(bf16[128,384]{1,0:T(8,128)(2,1)S(1)} %get-tuple-element.20), channel_id=1, source_target_pairs={{0,4},{4,0},{8,12},{12,8},{1,5},{5,1},{9,13},{13,9},{2,6},{6,2},{1... | collective-permute-start | bytes 294920 | tf_op jit(solution)/shard_map/ppermute | solution.py:323
  15.8 6.0 %copy-start.8 = (bf16[4,64,384]{2,1,0:T(8,128)(2,1)S(1)}, bf16[4,64,384]{2,1,0:T(8,128)(2,1)}, u32[]{:S(2)}) copy-start(bf16[4,64,384]{2,1,0:T(8,128)(2,1)} %constant.4.clone.rest_6_) | copy-start | bytes 589828
  15.9 9.6 %collective-permute-start.2 = (bf16[128,384]{1,0:T(8,128)(2,1)S(1)}, bf16[128,384]{1,0:T(8,128)(2,1)S(1)}, u32[]{:S(2)}, u32[]{:S(2)}) collective-permute-start(bf16[128,384]{1,0:T(8,128)(2,1)S(1)} %get-tuple-element.16.rest_2_), channel_id=1, source_target_pairs={{0,8},{4,12},{8,0},{12,4},{1,9},{5,13},{9,1},{13,5},{2,10},{6,14},... | collective-permute-start | bytes 294920 | tf_op jit(solution)/shard_map/ppermute | solution.py:323
  18.7 7.2 %collective-permute-start.3 = (bf16[128,384]{1,0:T(8,128)(2,1)S(1)}, bf16[128,384]{1,0:T(8,128)(2,1)S(1)}, u32[]{:S(2)}, u32[]{:S(2)}) collective-permute-start(bf16[128,384]{1,0:T(8,128)(2,1)S(1)} %get-tuple-element.17), channel_id=1, source_target_pairs={{0,12},{4,8},{8,4},{12,0},{1,13},{5,9},{9,5},{13,1},{2,14},{6,10},... | collective-permute-start | bytes 294920 | tf_op jit(solution)/shard_map/ppermute | solution.py:323
  20.1 6.3 %collective-permute-start.4 = (bf16[128,384]{1,0:T(8,128)(2,1)S(1)}, bf16[128,384]{1,0:T(8,128)(2,1)S(1)}, u32[]{:S(2)}, u32[]{:S(2)}) collective-permute-start(bf16[128,384]{1,0:T(8,128)(2,1)S(1)} %get-tuple-element.18), channel_id=1, source_target_pairs={{0,4},{4,0},{8,12},{12,8},{1,5},{5,1},{9,13},{13,9},{2,6},{6,2},{1... | collective-permute-start | bytes 294920 | tf_op jit(solution)/shard_map/ppermute | solution.py:323
  23.1 10.6 %copy-start.1 = (bf16[3,384,8]{1,2,0:T(8,128)(2,1)S(1)}, bf16[3,384,8]{1,2,0:T(8,128)(2,1)}, u32[]{:S(2)}) copy-start(bf16[3,384,8]{1,2,0:T(8,128)(2,1)} %param.19) | copy-start | bytes 55300
  23.1 10.6 %copy-start.6 = (bf16[8,256]{1,0:T(8,128)(2,1)S(1)}, bf16[8,256]{1,0:T(8,128)(2,1)}, u32[]{:S(2)}) copy-start(bf16[8,256]{1,0:T(8,128)(2,1)} %constant.5.clone.spread_ref) | copy-start | bytes 12292
  28.3 13.1 %all-to-all-start = ((bf16[8,32,256]{2,1,0:T(8,128)(2,1)}), bf16[8,32,256]{2,1,0:T(8,128)(2,1)S(1)}, u32[]{:S(2)}, u32[]{:S(2)}) async-start(bf16[8,32,256]{2,1,0:T(8,128)(2,1)} %mlp_rows.3), calls=%async_computation | async-start | bytes 262144 | tf_op jit(solution)/shard_map/all_to_all | solution.py:391

commit v23 on v9

--- a/solution.py
+++ b/solution.py
@@ -357,15 +357,18 @@
     left = expand(scalar(index * mode_dev), jnp.swapaxes(legendre, 1, 2), jnp.asarray(spread))
 
     received = []
-    after = []
     order = issue_order(num_chan)
     for edge, pair in zip(edges, pairs):
         shared = (scalar(pair), place, supports, cells, edge, disco_weight, num_chan)
-        sent = conv_rows(*shared, order, after, edge is None)
+        if received:
+            sent = conv_rows(*shared, order, [], False)
+            kept = conv_rows(*shared, (0,), sent[-1:], False)
+        else:
+            *sent, own = conv_rows(*shared, [*order, 0], [], edge is None)
+            kept = [own]
         moved = [turn(block, "chan", num_chan, k) for k, block in zip(order, sent)]
-        kept = conv_rows(*shared, (0,), sent[-1:], False)
         received.append([*kept, *moved])
-        after = kept
+    after = kept
     spectrum = None
     after = list(after)
     for blocks in received:

time: 42.7 us -> 43.3 us (1.014)
  waiting for transfers between devices: 10.1 us -> 11.6 us
  starting transfers between devices: 15.6 us -> 16.7 us
  Pallas kernels: 14.2 us -> 13.2 us
  local copies, waits for them, and re-layouts: 2.24 us -> 1.36 us
    pallas_call x4 -> x3, Pallas kernels: 9.14 us -> 8.15 us  [conv_rows(): pl.pallas_call(functools.partial(conv_kernel, chunks, picks, edge is not...]
    ppermute x6, waiting for transfers between devices: 3.43 us -> 4.34 us  [turn(): lax.ppermute(block, axis, [(i, target(i, k, count)) for i in range(count)])]
    unnamed x26, local copies, waits for them, and re-layouts: 1.22 us -> 0.34 us
    all_to_all x1, starting transfers between devices: 4.17 us -> 5.03 us  [on_device(): lax.all_to_all(spectrum, both, split_axis=0, concat_axis=0, tiled=True)]
  transfers between devices with their start and end apart: 8 -> 8, of which waited for: 4 -> 4; matrix products, arithmetic and copies ran while one was open for 1% -> 1% of each run, Pallas kernels for 26% -> 23%
where the time goes in v23:
time: 43.3 us; the launch traced here: 43.1 us
  starting transfers between devices  16.7 us (39%)
  Pallas kernels  13.2 us (30%)
  waiting for transfers between devices  11.6 us (27%)
  local copies, waits for them, and re-layouts  1.36 us (3%)
    ppermute x6, starting transfers between devices, turn(): lax.ppermute(block, axis, [(i, target(i, k, count)) for i in range(count)])  8.62 us
    pallas_call x3, Pallas kernels, conv_rows(): pl.pallas_call(functools.partial(conv_kernel, chunks, picks, edge is not...  8.15 us
    all_to_all x1, waiting for transfers between devices, on_device(): lax.all_to_all(spectrum, both, split_axis=0, concat_axis=0, tiled=True)  6.84 us
    all_to_all x1, starting transfers between devices, on_device(): lax.all_to_all(spectrum, both, split_axis=0, concat_axis=0, tiled=True)  5.03 us
    ppermute x6, waiting for transfers between devices, turn(): lax.ppermute(block, axis, [(i, target(i, k, count)) for i in range(count)])  4.34 us
    ppermute x1, starting transfers between devices, on_device(): edges = [None, lax.ppermute(edge_out, 'lat', [(0, 1), (1, 0)])]  3.03 us
    pallas_call x2, Pallas kernels, mlp_rows(): pl.pallas_call(functools.partial(mlp_kernel, len(blocks), last, len(after...  2.99 us
    pallas_call x1, Pallas kernels, final_sum(): pl.pallas_call(final_kernel, out_shape=jax.ShapeDtypeStruct(shape, jnp.bf...  1.3 us
  transfers between devices with their start and end apart: 8, of which 4 were waited for; matrix products, arithmetic and copies ran while one was open for 1% of the time, Pallas kernels for 23%

profile of v23, /device:TPU:0, one launch (start us, length us, event | category | flops | bytes accessed | tf_op | source)
XLA Modules:
  0.0 43.1 jit_solution(10164246327374341414)
XLA Ops:
  0.0 1.0 %dynamic-slice_bitcast_fusion = bf16[2,64,1440]{2,1,0:T(8,128)(2,1)S(1)} fusion(bf16[4,1440,64]{1,2,0:T(8,128)(2,1)} %param.11, s32[]{:T(128)S(6)} %select_n.3), kind=kLoop, calls=%fused_computation | loop fusion | bytes 737284 | tf_op jit(solution)/shard_map/dynamic_slice | solution.py:335
  1.0 3.0 %collective-permute-start = (bf16[2,64,1440]{2,1,0:T(8,128)(2,1)S(1)}, bf16[2,64,1440]{2,1,0:T(8,128)(2,1)S(1)}, u32[]{:S(2)}, u32[]{:S(2)}) collective-permute-start(bf16[2,64,1440]{2,1,0:T(8,128)(2,1)S(1)} %dynamic-slice_bitcast_fusion), channel_id=1, source_target_pairs={{0,16},{16,0},{1,17},{17,1},{2,18},{18,2},{3,19},{19,3},{4,20},{20... | collective-permute-start | bytes 1105928 | tf_op jit(solution)/shard_map/ppermute | solution.py:336
  4.1 0.0 copy-start.4
  4.1 0.0 copy-start.5
  4.1 0.0 copy-start.6
  4.1 0.0 copy-start.7
  4.1 4.2 %conv_rows.5 = (bf16[128,384]{1,0:T(8,128)(2,1)}, bf16[128,384]{1,0:T(8,128)(2,1)}, bf16[128,384]{1,0:T(8,128)(2,1)}, bf16[128,384]{1,0:T(8,128)(2,1)}) custom-call(s32[1]{0:T(128)} %bitcast.8.pair_ref, s32[1]{0:T(128)} %bitcast.2.place_ref, s32[4,9]{1,0:T(4,128)} %lat_ref.5, s32[4,9]{1,0:T(4,128)} %lon_ref.5, s32[4,9]{1,0:T(4,128)} %basis_ref.5, ...), custom_call_target="tpu_custom_call" | custom-call | flops 1000000000 | tf_op jit(solution)/shard_map/conv_rows/pallas_call | solution.py:144
  8.3 2.6 %collective-permute-start.4 = (bf16[128,384]{1,0:T(8,128)(2,1)}, bf16[128,384]{1,0:T(8,128)(2,1)S(1)}, u32[]{:S(2)}, u32[]{:S(2)}) collective-permute-start(bf16[128,384]{1,0:T(8,128)(2,1)} %get-tuple-element.16), channel_id=1, source_target_pairs={{0,8},{4,12},{8,0},{12,4},{1,9},{5,13},{9,1},{13,5},{2,10},{6,14},... | collective-permute-start | bytes 294920 | tf_op jit(solution)/shard_map/ppermute | solution.py:303
  10.9 1.3 %collective-permute-start.5 = (bf16[128,384]{1,0:T(8,128)(2,1)}, bf16[128,384]{1,0:T(8,128)(2,1)S(1)}, u32[]{:S(2)}, u32[]{:S(2)}) collective-permute-start(bf16[128,384]{1,0:T(8,128)(2,1)} %get-tuple-element.17), channel_id=1, source_target_pairs={{0,12},{4,8},{8,4},{12,0},{1,13},{5,9},{9,5},{13,1},{2,14},{6,10},... | collective-permute-start | bytes 294920 | tf_op jit(solution)/shard_map/ppermute | solution.py:303
  12.2 0.2 collective-permute-start.6
  12.5 0.1 copy.12
  12.6 0.1 copy.13
  12.8 0.4 collective-permute-done.rest_0_
  13.2 2.4 %conv_rows.3 = (bf16[128,384]{1,0:T(8,128)(2,1)S(1)}, bf16[128,384]{1,0:T(8,128)(2,1)S(1)}, bf16[128,384]{1,0:T(8,128)(2,1)S(1)}) custom-call(s32[1]{0:T(128)} %bitcast.3.pair_ref, s32[1]{0:T(128)} %bitcast.2.place_ref, s32[4,9]{1,0:T(4,128)S(1)} %copy-done.4, s32[4,9]{1,0:T(4,128)S(1)} %copy-done.5, s32[4,9]{1,0:T(4,128)S(1)} %copy-done.6, ...), custom_call_target="tpu_custom_call" | custom-call | flops 1000000000 | tf_op jit(solution)/shard_map/conv_rows/pallas_call | solution.py:144
  15.7 0.0 copy-start.8
  15.7 2.9 %collective-permute-start.1 = (bf16[128,384]{1,0:T(8,128)(2,1)S(1)}, bf16[128,384]{1,0:T(8,128)(2,1)S(1)}, u32[]{:S(2)}, u32[]{:S(2)}) collective-permute-start(bf16[128,384]{1,0:T(8,128)(2,1)S(1)} %get-tuple-element.13), channel_id=1, source_target_pairs={{0,8},{4,12},{8,0},{12,4},{1,9},{5,13},{9,1},{13,5},{2,10},{6,14},... | collective-permute-start | bytes 294920 | tf_op jit(solution)/shard_map/ppermute | solution.py:303
  18.6 1.3 %collective-permute-start.2 = (bf16[128,384]{1,0:T(8,128)(2,1)S(1)}, bf16[128,384]{1,0:T(8,128)(2,1)S(1)}, u32[]{:S(2)}, u32[]{:S(2)}) collective-permute-start(bf16[128,384]{1,0:T(8,128)(2,1)S(1)} %get-tuple-element.14), channel_id=1, source_target_pairs={{0,12},{4,8},{8,4},{12,0},{1,13},{5,9},{9,5},{13,1},{2,14},{6,10},... | collective-permute-start | bytes 294920 | tf_op jit(solution)/shard_map/ppermute | solution.py:303
  19.9 0.0 collective-permute-done.4.rest_1_
  19.9 0.2 collective-permute-start.3
  20.1 1.5 %conv_rows.4.rest_7_.rest_0_ = bf16[128,384]{1,0:T(8,128)(2,1)S(1)} custom-call(s32[1]{0:T(128)} %bitcast.3.pair_ref, s32[1]{0:T(128)} %bitcast.2.place_ref, s32[4,9]{1,0:T(4,128)S(1)} %copy-done.4, s32[4,9]{1,0:T(4,128)S(1)} %copy-done.5, s32[4,9]{1,0:T(4,128)S(1)} %copy-done.6, f32[4,9]{1,0:T(4,128)S(1)} %copy-done.7, bf16[4,64,1440]{2,1,0:T(8,128)(2,1)S(1)} %bitcast.13, ...), custom_call_target="tpu_custom_call" | custom-call | flops 200000000 | tf_op jit(solution)/shard_map/conv_rows/pallas_call | solution.py:144
  21.7 0.0 collective-permute-done.5.rest_2_
  21.7 1.2 %mlp_rows.2.rest_7_ = bf16[8,16,256]{2,1,0:T(8,128)(2,1)S(1)} custom-call(s32[1]{0:T(128)} %bitcast.2.place_ref, bf16[128,384]{1,0:T(8,128)(2,1)S(1)} %copy-done.9, bf16[128,384]{1,0:T(8,128)(2,1)S(1)} %collective-permute-done.4.rest_1_, bf16[128,384]{1,0:T(8,128)(2,1)S(1)} %collective-permute-done.5.rest_2_, ...), custom_call_target="tpu_custom_call" | custom-call | flops 1000000000 | tf_op jit(solution)/shard_map/mlp_rows/pallas_call | solution.py:210
  22.9 0.0 copy-start.2
  22.9 0.0 copy-start.3
  22.9 4.1 %collective-permute-done.1.rest_1_ = bf16[128,384]{1,0:T(8,128)(2,1)S(1)} collective-permute-done((bf16[128,384]{1,0:T(8,128)(2,1)S(1)}, bf16[128,384]{1,0:T(8,128)(2,1)S(1)}, u32[]{:S(2)}, u32[]{:S(2)}) %collective-permute-start.1) | collective-permute-done | bytes 98336 | tf_op jit(solution)/shard_map/ppermute | solution.py:303
  27.0 0.0 collective-permute-done.2.rest_2_
  27.0 0.2 collective-permute-done.3.rest_3_
  27.2 1.8 %mlp_rows.3 = bf16[8,32,256]{2,1,0:T(8,128)(2,1)} custom-call(s32[1]{0:T(128)} %bitcast.2.place_ref, bf16[128,384]{1,0:T(8,128)(2,1)S(1)} %conv_rows.4.rest_7_.rest_0_, bf16[128,384]{1,0:T(8,128)(2,1)S(1)} %collective-permute-done.1.rest_1_, bf16[128,384]{1,0:T(8,128)(2,1)S(1)} %collective-permute-done.2.rest_2_, ...), custom_call_target="tpu_custom_call" | custom-call | flops 1000000000 | tf_op jit(solution)/shard_map/mlp_rows/pallas_call | solution.py:210
  29.1 5.0 %all-to-all-start = ((bf16[8,32,256]{2,1,0:T(8,128)(2,1)}), bf16[8,32,256]{2,1,0:T(8,128)(2,1)S(1)}, u32[]{:S(2)}, u32[]{:S(2)}) async-start(bf16[8,32,256]{2,1,0:T(8,128)(2,1)} %mlp_rows.3), calls=%async_computation | async-start | bytes 262144 | tf_op jit(solution)/shard_map/all_to_all | solution.py:379
  34.1 0.8 %expand.1.left_ref = bf16[3,2,384,256]{3,2,1,0:T(8,128)(2,1)S(1)} custom-call(s32[1]{0:T(128)} %bitcast.start_ref, bf16[3,8,384]{2,1,0:T(8,128)(2,1)S(1)} %bitcast.19, bf16[8,256]{1,0:T(8,128)(2,1)S(1)} %copy-done.3), custom_call_target="tpu_custom_call" | custom-call | flops 200000000 | tf_op jit(solution)/shard_map/expand/pallas_call | solution.py:244
  34.9 6.8 %all-to-all-done = bf16[8,32,256]{2,1,0:T(8,128)(2,1)S(1)} async-done(((bf16[8,32,256]{2,1,0:T(8,128)(2,1)}), bf16[8,32,256]{2,1,0:T(8,128)(2,1)S(1)}, u32[]{:S(2)}, u32[]{:S(2)}) %all-to-all-start) | async-done | bytes 131104 | tf_op jit(solution)/shard_map/all_to_all | solution.py:379
  41.8 1.3 %final_sum.1 = bf16[3,384,512]{2,1,0:T(8,128)(2,1)} custom-call(bf16[3,2,384,256]{3,2,1,0:T(8,128)(2,1)S(1)} %expand.1.left_ref, bf16[256,256]{1,0:T(8,128)(2,1)S(1)} %bitcast.18), custom_call_target="tpu_custom_call" | custom-call | flops 1000000000 | tf_op jit(solution)/shard_map/final_sum/pallas_call | solution.py:278
  (18 shorter events, 0.0 us)
Async XLA Ops:
  1.0 12.1 %collective-permute-start = (bf16[2,64,1440]{2,1,0:T(8,128)(2,1)S(1)}, bf16[2,64,1440]{2,1,0:T(8,128)(2,1)S(1)}, u32[]{:S(2)}, u32[]{:S(2)}) collective-permute-start(bf16[2,64,1440]{2,1,0:T(8,128)(2,1)S(1)} %dynamic-slice_bitcast_fusion), channel_id=1, source_target_pairs={{0,16},{16,0},{1,17},{17,1},{2,18},{18,2},{3,19},{19,3},{4,20},{20... | collective-permute-start | bytes 1105928 | tf_op jit(solution)/shard_map/ppermute | solution.py:336
  4.1 8.4 %copy-start.10 = (bf16[256,512]{1,0:T(8,128)(2,1)S(1)}, bf16[256,512]{1,0:T(8,128)(2,1)}, u32[]{:S(2)}) copy-start(bf16[256,512]{1,0:T(8,128)(2,1)} %param.17) | copy-start | bytes 786436
  4.1 8.6 %copy-start.11 = (bf16[512,256]{1,0:T(8,128)(2,1)S(1)}, bf16[512,256]{1,0:T(8,128)(2,1)}, u32[]{:S(2)}) copy-start(bf16[512,256]{1,0:T(8,128)(2,1)} %param.18) | copy-start | bytes 786436
  4.1 9.1 %copy-start = (bf16[4,1440,64]{1,2,0:T(8,128)(2,1)S(1)}, bf16[4,1440,64]{1,2,0:T(8,128)(2,1)}, u32[]{:S(2)}) copy-start(bf16[4,1440,64]{1,2,0:T(8,128)(2,1)} %param.11) | copy-start | bytes 2211844
  4.1 9.1 %copy-start.1 = (bf16[6,64,64]{2,1,0:T(8,128)(2,1)S(1)}, bf16[6,64,64]{2,1,0:T(8,128)(2,1)}, u32[]{:S(2)}) copy-start(bf16[6,64,64]{2,1,0:T(8,128)(2,1)} %rest_0_.1) | copy-start | bytes 147460
  4.1 9.1 %copy-start.4 = (s32[4,9]{1,0:T(4,128)S(1)}, s32[4,9]{1,0:T(4,128)}, u32[]{:S(2)}) copy-start(s32[4,9]{1,0:T(4,128)} %lat_ref.5) | copy-start | bytes 436
  4.1 9.1 %copy-start.5 = (s32[4,9]{1,0:T(4,128)S(1)}, s32[4,9]{1,0:T(4,128)}, u32[]{:S(2)}) copy-start(s32[4,9]{1,0:T(4,128)} %lon_ref.5) | copy-start | bytes 436
  4.1 9.1 %copy-start.6 = (s32[4,9]{1,0:T(4,128)S(1)}, s32[4,9]{1,0:T(4,128)}, u32[]{:S(2)}) copy-start(s32[4,9]{1,0:T(4,128)} %basis_ref.5) | copy-start | bytes 436
  4.1 9.1 %copy-start.7 = (f32[4,9]{1,0:T(4,128)S(1)}, f32[4,9]{1,0:T(4,128)}, u32[]{:S(2)}) copy-start(f32[4,9]{1,0:T(4,128)} %value_ref.5) | copy-start | bytes 436
  8.3 11.6 %collective-permute-start.4 = (bf16[128,384]{1,0:T(8,128)(2,1)}, bf16[128,384]{1,0:T(8,128)(2,1)S(1)}, u32[]{:S(2)}, u32[]{:S(2)}) collective-permute-start(bf16[128,384]{1,0:T(8,128)(2,1)} %get-tuple-element.16), channel_id=1, source_target_pairs={{0,8},{4,12},{8,0},{12,4},{1,9},{5,13},{9,1},{13,5},{2,10},{6,14},... | collective-permute-start | bytes 294920 | tf_op jit(solution)/shard_map/ppermute | solution.py:303
  10.9 10.8 %collective-permute-start.5 = (bf16[128,384]{1,0:T(8,128)(2,1)}, bf16[128,384]{1,0:T(8,128)(2,1)S(1)}, u32[]{:S(2)}, u32[]{:S(2)}) collective-permute-start(bf16[128,384]{1,0:T(8,128)(2,1)} %get-tuple-element.17), channel_id=1, source_target_pairs={{0,12},{4,8},{8,4},{12,0},{1,13},{5,9},{9,5},{13,1},{2,14},{6,10},... | collective-permute-start | bytes 294920 | tf_op jit(solution)/shard_map/ppermute | solution.py:303
  12.2 9.5 %collective-permute-start.6 = (bf16[128,384]{1,0:T(8,128)(2,1)}, bf16[128,384]{1,0:T(8,128)(2,1)S(1)}, u32[]{:S(2)}, u32[]{:S(2)}) collective-permute-start(bf16[128,384]{1,0:T(8,128)(2,1)} %get-tuple-element.18), channel_id=1, source_target_pairs={{0,4},{4,0},{8,12},{12,8},{1,5},{5,1},{9,13},{13,9},{2,6},{6,2},{1... | collective-permute-start | bytes 294920 | tf_op jit(solution)/shard_map/ppermute | solution.py:303
  15.7 6.0 %copy-start.8 = (bf16[4,64,384]{2,1,0:T(8,128)(2,1)S(1)}, bf16[4,64,384]{2,1,0:T(8,128)(2,1)}, u32[]{:S(2)}) copy-start(bf16[4,64,384]{2,1,0:T(8,128)(2,1)} %constant.25.clone.rest_6_) | copy-start | bytes 589828
  15.7 6.0 %copy-start.9 = (bf16[128,384]{1,0:T(8,128)(2,1)S(1)}, bf16[128,384]{1,0:T(8,128)(2,1)}, u32[]{:S(2)}) copy-start(bf16[128,384]{1,0:T(8,128)(2,1)} %get-tuple-element.15.rest_0_) | copy-start | bytes 294916
  15.7 11.3 %collective-permute-start.1 = (bf16[128,384]{1,0:T(8,128)(2,1)S(1)}, bf16[128,384]{1,0:T(8,128)(2,1)S(1)}, u32[]{:S(2)}, u32[]{:S(2)}) collective-permute-start(bf16[128,384]{1,0:T(8,128)(2,1)S(1)} %get-tuple-element.13), channel_id=1, source_target_pairs={{0,8},{4,12},{8,0},{12,4},{1,9},{5,13},{9,1},{13,5},{2,10},{6,14},... | collective-permute-start | bytes 294920 | tf_op jit(solution)/shard_map/ppermute | solution.py:303
  18.6 8.5 %collective-permute-start.2 = (bf16[128,384]{1,0:T(8,128)(2,1)S(1)}, bf16[128,384]{1,0:T(8,128)(2,1)S(1)}, u32[]{:S(2)}, u32[]{:S(2)}) collective-permute-start(bf16[128,384]{1,0:T(8,128)(2,1)S(1)} %get-tuple-element.14), channel_id=1, source_target_pairs={{0,12},{4,8},{8,4},{12,0},{1,13},{5,9},{9,5},{13,1},{2,14},{6,10},... | collective-permute-start | bytes 294920 | tf_op jit(solution)/shard_map/ppermute | solution.py:303
  19.9 7.3 %collective-permute-start.3 = (bf16[128,384]{1,0:T(8,128)(2,1)S(1)}, bf16[128,384]{1,0:T(8,128)(2,1)S(1)}, u32[]{:S(2)}, u32[]{:S(2)}) collective-permute-start(bf16[128,384]{1,0:T(8,128)(2,1)S(1)} %get-tuple-element.12.rest_2_), channel_id=1, source_target_pairs={{0,4},{4,0},{8,12},{12,8},{1,5},{5,1},{9,13},{13,9},{2,6},{6,2},{1... | collective-permute-start | bytes 294920 | tf_op jit(solution)/shard_map/ppermute | solution.py:303
  22.9 11.2 %copy-start.2 = (bf16[3,384,8]{1,2,0:T(8,128)(2,1)S(1)}, bf16[3,384,8]{1,2,0:T(8,128)(2,1)}, u32[]{:S(2)}) copy-start(bf16[3,384,8]{1,2,0:T(8,128)(2,1)} %param.19) | copy-start | bytes 55300
  22.9 11.2 %copy-start.3 = (bf16[8,256]{1,0:T(8,128)(2,1)S(1)}, bf16[8,256]{1,0:T(8,128)(2,1)}, u32[]{:S(2)}) copy-start(bf16[8,256]{1,0:T(8,128)(2,1)} %constant.26.clone.spread_ref) | copy-start | bytes 12292
  29.1 12.7 %all-to-all-start = ((bf16[8,32,256]{2,1,0:T(8,128)(2,1)}), bf16[8,32,256]{2,1,0:T(8,128)(2,1)S(1)}, u32[]{:S(2)}, u32[]{:S(2)}) async-start(bf16[8,32,256]{2,1,0:T(8,128)(2,1)} %mlp_rows.3), calls=%async_computation | async-start | bytes 262144 | tf_op jit(solution)/shard_map/all_to_all | solution.py:379

commit v24 on v9

--- a/solution.py
+++ b/solution.py
@@ -52,7 +52,7 @@
 
 
 def issue_order(count):
-    return [*range(2, count), 1] if paired(count) else list(range(1, count))
+    return list(range(count - 1, 0, -1)) if paired(count) else list(range(1, count))
 
 
 def conv_kernel(

time: 42.7 us -> 42.9 us (level)
    ppermute x6, starting transfers between devices: 8.39 us -> 8.84 us  [turn(): lax.ppermute(block, axis, [(i, target(i, k, count)) for i in range(count)])]
  transfers between devices with their start and end apart: 8 -> 8, of which waited for: 4 -> 2; matrix products, arithmetic and copies ran while one was open for 1% -> 1% of each run, Pallas kernels for 26% -> 26%
where the time goes in v24:
time: 42.9 us; the launch traced here: 42.6 us
  starting transfers between devices  15.7 us (37%)
  Pallas kernels  14.2 us (33%)
  waiting for transfers between devices  10.2 us (24%)
  local copies, waits for them, and re-layouts  2.24 us (5%)
    pallas_call x4, Pallas kernels, conv_rows(): pl.pallas_call(functools.partial(conv_kernel, chunks, picks, edge is not...  9.13 us
    ppermute x6, starting transfers between devices, turn(): lax.ppermute(block, axis, [(i, target(i, k, count)) for i in range(count)])  8.84 us
    all_to_all x1, waiting for transfers between devices, on_device(): lax.all_to_all(spectrum, both, split_axis=0, concat_axis=0, tiled=True)  6.68 us
    all_to_all x1, starting transfers between devices, on_device(): lax.all_to_all(spectrum, both, split_axis=0, concat_axis=0, tiled=True)  3.84 us
    ppermute x6, waiting for transfers between devices, turn(): lax.ppermute(block, axis, [(i, target(i, k, count)) for i in range(count)])  3.55 us
    ppermute x1, starting transfers between devices, on_device(): edges = [None, lax.ppermute(edge_out, 'lat', [(0, 1), (1, 0)])]  3.03 us
    pallas_call x2, Pallas kernels, mlp_rows(): pl.pallas_call(functools.partial(mlp_kernel, len(blocks), last, len(after...  2.98 us
    pallas_call x1, Pallas kernels, final_sum(): pl.pallas_call(final_kernel, out_shape=jax.ShapeDtypeStruct(shape, jnp.bf...  1.3 us
  transfers between devices with their start and end apart: 8, of which 2 were waited for; matrix products, arithmetic and copies ran while one was open for 1% of the time, Pallas kernels for 26%

profile of v24, /device:TPU:0, one launch (start us, length us, event | category | flops | bytes accessed | tf_op | source)
XLA Modules:
  0.0 42.6 jit_solution(8067390539694647859)
XLA Ops:
  0.0 1.0 %dynamic-slice_bitcast_fusion = bf16[2,64,1440]{2,1,0:T(8,128)(2,1)S(1)} fusion(bf16[4,1440,64]{1,2,0:T(8,128)(2,1)} %param.11, s32[]{:T(128)S(6)} %select_n.3), kind=kLoop, calls=%fused_computation | loop fusion | bytes 737284 | tf_op jit(solution)/shard_map/dynamic_slice | solution.py:335
  1.0 3.0 %collective-permute-start = (bf16[2,64,1440]{2,1,0:T(8,128)(2,1)S(1)}, bf16[2,64,1440]{2,1,0:T(8,128)(2,1)S(1)}, u32[]{:S(2)}, u32[]{:S(2)}) collective-permute-start(bf16[2,64,1440]{2,1,0:T(8,128)(2,1)S(1)} %dynamic-slice_bitcast_fusion), channel_id=1, source_target_pairs={{0,16},{16,0},{1,17},{17,1},{2,18},{18,2},{3,19},{19,3},{4,20},{20... | collective-permute-start | bytes 1105928 | tf_op jit(solution)/shard_map/ppermute | solution.py:336
  4.1 0.0 copy-start.6
  4.1 0.0 copy-start.7
  4.1 0.0 copy-start.10
  4.1 0.0 copy-start.11
  4.1 3.6 %conv_rows.4 = (bf16[128,384]{1,0:T(8,128)(2,1)}, bf16[128,384]{1,0:T(8,128)(2,1)}, bf16[128,384]{1,0:T(8,128)(2,1)}) custom-call(s32[1]{0:T(128)} %bitcast.6.pair_ref, s32[1]{0:T(128)} %bitcast.2.place_ref, s32[4,9]{1,0:T(4,128)} %lat_ref.7, s32[4,9]{1,0:T(4,128)} %lon_ref.7, s32[4,9]{1,0:T(4,128)} %basis_ref.7, f32[4,9]{1,0:T(4,128)} %value_ref.7, ...), custom_call_target="tpu_custom_call" | custom-call | flops 1000000000 | tf_op jit(solution)/shard_map/conv_rows/pallas_call | solution.py:144
  7.8 3.6 %collective-permute-start.4 = (bf16[128,384]{1,0:T(8,128)(2,1)}, bf16[128,384]{1,0:T(8,128)(2,1)S(1)}, u32[]{:S(2)}, u32[]{:S(2)}) collective-permute-start(bf16[128,384]{1,0:T(8,128)(2,1)} %get-tuple-element.15), channel_id=1, source_target_pairs={{0,12},{4,8},{8,4},{12,0},{1,13},{5,9},{9,5},{13,1},{2,14},{6,10},... | collective-permute-start | bytes 294920 | tf_op jit(solution)/shard_map/ppermute | solution.py:303
  11.4 0.0 collective-permute-start.5
  11.4 0.8 %collective-permute-start.6 = (bf16[128,384]{1,0:T(8,128)(2,1)}, bf16[128,384]{1,0:T(8,128)(2,1)S(1)}, u32[]{:S(2)}, u32[]{:S(2)}) collective-permute-start(bf16[128,384]{1,0:T(8,128)(2,1)} %get-tuple-element.11.rest_1_), channel_id=1, source_target_pairs={{0,4},{4,0},{8,12},{12,8},{1,5},{5,1},{9,13},{13,9},{2,6},{6,2},{1... | collective-permute-start | bytes 294920 | tf_op jit(solution)/shard_map/ppermute | solution.py:303
  12.2 0.9 %copy-done.2 = bf16[128,384]{1,0:T(8,128)(2,1)S(1)} copy-done((bf16[128,384]{1,0:T(8,128)(2,1)S(1)}, bf16[128,384]{1,0:T(8,128)(2,1)}, u32[]{:S(2)}) %copy-start.2) | copy-done | bytes 98328
  13.1 1.5 %conv_rows.5.rest_2_.rest_0_ = bf16[128,384]{1,0:T(8,128)(2,1)S(1)} custom-call(s32[1]{0:T(128)} %bitcast.6.pair_ref, s32[1]{0:T(128)} %bitcast.2.place_ref, s32[4,9]{1,0:T(4,128)S(1)} %copy-done.4, s32[4,9]{1,0:T(4,128)S(1)} %copy-done.5, s32[4,9]{1,0:T(4,128)S(1)} %copy-done.6, f32[4,9]{1,0:T(4,128)S(1)} %copy-done.7, bf16[4,64,1440]{2,1,0:T(8,128)(2,1)S(1)} %bitcast.12, ...), custom_call_target="tpu_custom_call" | custom-call | flops 200000000 | tf_op jit(solution)/shard_map/conv_rows/pallas_call | solution.py:144
  14.6 0.1 copy.12
  14.8 0.1 copy.13
  14.9 0.0 collective-permute-done.rest_0_
  14.9 2.4 %conv_rows.6 = (bf16[128,384]{1,0:T(8,128)(2,1)S(1)}, bf16[128,384]{1,0:T(8,128)(2,1)S(1)}, bf16[128,384]{1,0:T(8,128)(2,1)S(1)}) custom-call(s32[1]{0:T(128)} %bitcast.3.pair_ref, s32[1]{0:T(128)} %bitcast.2.place_ref, s32[4,9]{1,0:T(4,128)S(1)} %copy-done.4, s32[4,9]{1,0:T(4,128)S(1)} %copy-done.5, s32[4,9]{1,0:T(4,128)S(1)} %copy-done.6, ...), custom_call_target="tpu_custom_call" | custom-call | flops 1000000000 | tf_op jit(solution)/shard_map/conv_rows/pallas_call | solution.py:144
  17.4 0.0 copy-start.9
  17.4 3.7 %collective-permute-start.1 = (bf16[128,384]{1,0:T(8,128)(2,1)S(1)}, bf16[128,384]{1,0:T(8,128)(2,1)S(1)}, u32[]{:S(2)}, u32[]{:S(2)}) collective-permute-start(bf16[128,384]{1,0:T(8,128)(2,1)S(1)} %get-tuple-element.13), channel_id=1, source_target_pairs={{0,12},{4,8},{8,4},{12,0},{1,13},{5,9},{9,5},{13,1},{2,14},{6,10},... | collective-permute-start | bytes 294920 | tf_op jit(solution)/shard_map/ppermute | solution.py:303
  21.0 0.0 collective-permute-start.2
  21.1 0.8 %collective-permute-start.3 = (bf16[128,384]{1,0:T(8,128)(2,1)S(1)}, bf16[128,384]{1,0:T(8,128)(2,1)S(1)}, u32[]{:S(2)}, u32[]{:S(2)}) collective-permute-start(bf16[128,384]{1,0:T(8,128)(2,1)S(1)} %get-tuple-element.12.rest_2_), channel_id=1, source_target_pairs={{0,4},{4,0},{8,12},{12,8},{1,5},{5,1},{9,13},{13,9},{2,6},{6,2},{1... | collective-permute-start | bytes 294920 | tf_op jit(solution)/shard_map/ppermute | solution.py:303
  21.8 1.5 %conv_rows.7.rest_7_.rest_0_ = bf16[128,384]{1,0:T(8,128)(2,1)S(1)} custom-call(s32[1]{0:T(128)} %bitcast.3.pair_ref, s32[1]{0:T(128)} %bitcast.2.place_ref, s32[4,9]{1,0:T(4,128)S(1)} %copy-done.4, s32[4,9]{1,0:T(4,128)S(1)} %copy-done.5, s32[4,9]{1,0:T(4,128)S(1)} %copy-done.6, f32[4,9]{1,0:T(4,128)S(1)} %copy-done.7, bf16[4,64,1440]{2,1,0:T(8,128)(2,1)S(1)} %bitcast.14, ...), custom_call_target="tpu_custom_call" | custom-call | flops 200000000 | tf_op jit(solution)/shard_map/conv_rows/pallas_call | solution.py:144
  23.4 0.0 collective-permute-done.6.rest_3_
  23.4 1.2 %mlp_rows.2.rest_7_ = bf16[8,16,256]{2,1,0:T(8,128)(2,1)S(1)} custom-call(s32[1]{0:T(128)} %bitcast.2.place_ref, bf16[128,384]{1,0:T(8,128)(2,1)S(1)} %conv_rows.5.rest_2_.rest_0_, bf16[128,384]{1,0:T(8,128)(2,1)S(1)} %collective-permute-done.4.rest_1_, bf16[128,384]{1,0:T(8,128)(2,1)S(1)} %collective-permute-done.5.rest_2_, ...), custom_call_target="tpu_custom_call" | custom-call | flops 1000000000 | tf_op jit(solution)/shard_map/mlp_rows/pallas_call | solution.py:210
  24.6 0.0 copy-start.3
  24.6 0.0 copy-start.8
  24.6 0.0 collective-permute-done.1.rest_1_
  24.6 3.5 %collective-permute-done.2.rest_2_ = bf16[128,384]{1,0:T(8,128)(2,1)S(1)} collective-permute-done((bf16[128,384]{1,0:T(8,128)(2,1)S(1)}, bf16[128,384]{1,0:T(8,128)(2,1)S(1)}, u32[]{:S(2)}, u32[]{:S(2)}) %collective-permute-start.2) | collective-permute-done | bytes 98336 | tf_op jit(solution)/shard_map/ppermute | solution.py:303
  28.1 1.8 %mlp_rows.3 = bf16[8,32,256]{2,1,0:T(8,128)(2,1)} custom-call(s32[1]{0:T(128)} %bitcast.2.place_ref, bf16[128,384]{1,0:T(8,128)(2,1)S(1)} %conv_rows.7.rest_7_.rest_0_, bf16[128,384]{1,0:T(8,128)(2,1)S(1)} %collective-permute-done.1.rest_1_, bf16[128,384]{1,0:T(8,128)(2,1)S(1)} %collective-permute-done.2.rest_2_, ...), custom_call_target="tpu_custom_call" | custom-call | flops 1000000000 | tf_op jit(solution)/shard_map/mlp_rows/pallas_call | solution.py:210
  30.0 3.8 %all-to-all-start = ((bf16[8,32,256]{2,1,0:T(8,128)(2,1)}), bf16[8,32,256]{2,1,0:T(8,128)(2,1)S(1)}, u32[]{:S(2)}, u32[]{:S(2)}) async-start(bf16[8,32,256]{2,1,0:T(8,128)(2,1)} %mlp_rows.3), calls=%async_computation | async-start | bytes 262144 | tf_op jit(solution)/shard_map/all_to_all | solution.py:376
  33.8 0.8 %expand.1.left_ref = bf16[3,2,384,256]{3,2,1,0:T(8,128)(2,1)S(1)} custom-call(s32[1]{0:T(128)} %bitcast.start_ref, bf16[3,8,384]{2,1,0:T(8,128)(2,1)S(1)} %bitcast.20, bf16[8,256]{1,0:T(8,128)(2,1)S(1)} %copy-done.8), custom_call_target="tpu_custom_call" | custom-call | flops 200000000 | tf_op jit(solution)/shard_map/expand/pallas_call | solution.py:244
  34.6 6.7 %all-to-all-done = bf16[8,32,256]{2,1,0:T(8,128)(2,1)S(1)} async-done(((bf16[8,32,256]{2,1,0:T(8,128)(2,1)}), bf16[8,32,256]{2,1,0:T(8,128)(2,1)S(1)}, u32[]{:S(2)}, u32[]{:S(2)}) %all-to-all-start) | async-done | bytes 131104 | tf_op jit(solution)/shard_map/all_to_all | solution.py:376
  41.3 1.3 %final_sum.1 = bf16[3,384,512]{2,1,0:T(8,128)(2,1)} custom-call(bf16[3,2,384,256]{3,2,1,0:T(8,128)(2,1)S(1)} %expand.1.left_ref, bf16[256,256]{1,0:T(8,128)(2,1)S(1)} %bitcast.19), custom_call_target="tpu_custom_call" | custom-call | flops 1000000000 | tf_op jit(solution)/shard_map/final_sum/pallas_call | solution.py:278
  (19 shorter events, 0.0 us)
Async XLA Ops:
  1.0 13.9 %collective-permute-start = (bf16[2,64,1440]{2,1,0:T(8,128)(2,1)S(1)}, bf16[2,64,1440]{2,1,0:T(8,128)(2,1)S(1)}, u32[]{:S(2)}, u32[]{:S(2)}) collective-permute-start(bf16[2,64,1440]{2,1,0:T(8,128)(2,1)S(1)} %dynamic-slice_bitcast_fusion), channel_id=1, source_target_pairs={{0,16},{16,0},{1,17},{17,1},{2,18},{18,2},{3,19},{19,3},{4,20},{20... | collective-permute-start | bytes 1105928 | tf_op jit(solution)/shard_map/ppermute | solution.py:336
  4.1 8.1 %copy-start = (bf16[4,1440,64]{1,2,0:T(8,128)(2,1)S(1)}, bf16[4,1440,64]{1,2,0:T(8,128)(2,1)}, u32[]{:S(2)}) copy-start(bf16[4,1440,64]{1,2,0:T(8,128)(2,1)} %param.11) | copy-start | bytes 2211844
  4.1 8.1 %copy-start.1 = (bf16[6,64,64]{2,1,0:T(8,128)(2,1)S(1)}, bf16[6,64,64]{2,1,0:T(8,128)(2,1)}, u32[]{:S(2)}) copy-start(bf16[6,64,64]{2,1,0:T(8,128)(2,1)} %rest_1_.3) | copy-start | bytes 147460
  4.1 8.1 %copy-start.4 = (s32[4,9]{1,0:T(4,128)S(1)}, s32[4,9]{1,0:T(4,128)}, u32[]{:S(2)}) copy-start(s32[4,9]{1,0:T(4,128)} %lat_ref.7) | copy-start | bytes 436
  4.1 8.1 %copy-start.5 = (s32[4,9]{1,0:T(4,128)S(1)}, s32[4,9]{1,0:T(4,128)}, u32[]{:S(2)}) copy-start(s32[4,9]{1,0:T(4,128)} %lon_ref.7) | copy-start | bytes 436
  4.1 8.1 %copy-start.6 = (s32[4,9]{1,0:T(4,128)S(1)}, s32[4,9]{1,0:T(4,128)}, u32[]{:S(2)}) copy-start(s32[4,9]{1,0:T(4,128)} %basis_ref.7) | copy-start | bytes 436
  4.1 8.1 %copy-start.7 = (f32[4,9]{1,0:T(4,128)S(1)}, f32[4,9]{1,0:T(4,128)}, u32[]{:S(2)}) copy-start(f32[4,9]{1,0:T(4,128)} %value_ref.7) | copy-start | bytes 436
  4.1 10.5 %copy-start.10 = (bf16[256,512]{1,0:T(8,128)(2,1)S(1)}, bf16[256,512]{1,0:T(8,128)(2,1)}, u32[]{:S(2)}) copy-start(bf16[256,512]{1,0:T(8,128)(2,1)} %param.17) | copy-start | bytes 786436
  4.1 10.7 %copy-start.11 = (bf16[512,256]{1,0:T(8,128)(2,1)S(1)}, bf16[512,256]{1,0:T(8,128)(2,1)}, u32[]{:S(2)}) copy-start(bf16[512,256]{1,0:T(8,128)(2,1)} %param.18) | copy-start | bytes 786436
  7.8 13.3 %collective-permute-start.4 = (bf16[128,384]{1,0:T(8,128)(2,1)}, bf16[128,384]{1,0:T(8,128)(2,1)S(1)}, u32[]{:S(2)}, u32[]{:S(2)}) collective-permute-start(bf16[128,384]{1,0:T(8,128)(2,1)} %get-tuple-element.15), channel_id=1, source_target_pairs={{0,12},{4,8},{8,4},{12,0},{1,13},{5,9},{9,5},{13,1},{2,14},{6,10},... | collective-permute-start | bytes 294920 | tf_op jit(solution)/shard_map/ppermute | solution.py:303
  11.4 12.0 %collective-permute-start.5 = (bf16[128,384]{1,0:T(8,128)(2,1)}, bf16[128,384]{1,0:T(8,128)(2,1)S(1)}, u32[]{:S(2)}, u32[]{:S(2)}) collective-permute-start(bf16[128,384]{1,0:T(8,128)(2,1)} %get-tuple-element.16), channel_id=1, source_target_pairs={{0,8},{4,12},{8,0},{12,4},{1,9},{5,13},{9,1},{13,5},{2,10},{6,14},... | collective-permute-start | bytes 294920 | tf_op jit(solution)/shard_map/ppermute | solution.py:303
  11.4 12.0 %collective-permute-start.6 = (bf16[128,384]{1,0:T(8,128)(2,1)}, bf16[128,384]{1,0:T(8,128)(2,1)S(1)}, u32[]{:S(2)}, u32[]{:S(2)}) collective-permute-start(bf16[128,384]{1,0:T(8,128)(2,1)} %get-tuple-element.11.rest_1_), channel_id=1, source_target_pairs={{0,4},{4,0},{8,12},{12,8},{1,5},{5,1},{9,13},{13,9},{2,6},{6,2},{1... | collective-permute-start | bytes 294920 | tf_op jit(solution)/shard_map/ppermute | solution.py:303
  12.2 0.9 %copy-start.2 = (bf16[128,384]{1,0:T(8,128)(2,1)S(1)}, bf16[128,384]{1,0:T(8,128)(2,1)}, u32[]{:S(2)}) copy-start(bf16[128,384]{1,0:T(8,128)(2,1)} %get-tuple-element.11.rest_1_) | copy-start | bytes 294916
  17.4 6.0 %copy-start.9 = (bf16[4,64,384]{2,1,0:T(8,128)(2,1)S(1)}, bf16[4,64,384]{2,1,0:T(8,128)(2,1)}, u32[]{:S(2)}) copy-start(bf16[4,64,384]{2,1,0:T(8,128)(2,1)} %constant.25.clone.rest_6_) | copy-start | bytes 589828
  17.4 7.2 %collective-permute-start.1 = (bf16[128,384]{1,0:T(8,128)(2,1)S(1)}, bf16[128,384]{1,0:T(8,128)(2,1)S(1)}, u32[]{:S(2)}, u32[]{:S(2)}) collective-permute-start(bf16[128,384]{1,0:T(8,128)(2,1)S(1)} %get-tuple-element.13), channel_id=1, source_target_pairs={{0,12},{4,8},{8,4},{12,0},{1,13},{5,9},{9,5},{13,1},{2,14},{6,10},... | collective-permute-start | bytes 294920 | tf_op jit(solution)/shard_map/ppermute | solution.py:303
  21.0 7.1 %collective-permute-start.2 = (bf16[128,384]{1,0:T(8,128)(2,1)S(1)}, bf16[128,384]{1,0:T(8,128)(2,1)S(1)}, u32[]{:S(2)}, u32[]{:S(2)}) collective-permute-start(bf16[128,384]{1,0:T(8,128)(2,1)S(1)} %get-tuple-element.14), channel_id=1, source_target_pairs={{0,8},{4,12},{8,0},{12,4},{1,9},{5,13},{9,1},{13,5},{2,10},{6,14},... | collective-permute-start | bytes 294920 | tf_op jit(solution)/shard_map/ppermute | solution.py:303
  21.1 7.1 %collective-permute-start.3 = (bf16[128,384]{1,0:T(8,128)(2,1)S(1)}, bf16[128,384]{1,0:T(8,128)(2,1)S(1)}, u32[]{:S(2)}, u32[]{:S(2)}) collective-permute-start(bf16[128,384]{1,0:T(8,128)(2,1)S(1)} %get-tuple-element.12.rest_2_), channel_id=1, source_target_pairs={{0,4},{4,0},{8,12},{12,8},{1,5},{5,1},{9,13},{13,9},{2,6},{6,2},{1... | collective-permute-start | bytes 294920 | tf_op jit(solution)/shard_map/ppermute | solution.py:303
  24.6 9.2 %copy-start.3 = (bf16[3,384,8]{1,2,0:T(8,128)(2,1)S(1)}, bf16[3,384,8]{1,2,0:T(8,128)(2,1)}, u32[]{:S(2)}) copy-start(bf16[3,384,8]{1,2,0:T(8,128)(2,1)} %param.19) | copy-start | bytes 55300
  24.6 9.2 %copy-start.8 = (bf16[8,256]{1,0:T(8,128)(2,1)S(1)}, bf16[8,256]{1,0:T(8,128)(2,1)}, u32[]{:S(2)}) copy-start(bf16[8,256]{1,0:T(8,128)(2,1)} %constant.26.clone.spread_ref) | copy-start | bytes 12292
  30.0 11.4 %all-to-all-start = ((bf16[8,32,256]{2,1,0:T(8,128)(2,1)}), bf16[8,32,256]{2,1,0:T(8,128)(2,1)S(1)}, u32[]{:S(2)}, u32[]{:S(2)}) async-start(bf16[8,32,256]{2,1,0:T(8,128)(2,1)} %mlp_rows.3), calls=%async_computation | async-start | bytes 262144 | tf_op jit(solution)/shard_map/all_to_all | solution.py:376
